TPU v7x, 32 devices: a whole 2x2x4 slice. The times are simulated.
32 devices in a mesh: section: 4 (over z), expert: 4 (over y, x), dp: 2 (over core).
Axes of the slice: x: 2, y: 2, z: 4, core: 2. Of those that a mesh axis runs over, the one named last changes fastest.
Arguments:
- x_fwd: bfloat16 [4, 512, 3584], P('section', ('expert', 'dp')), may hold values from -6 to 6
- ids_fwd: int32 [4, 512, 2], P('section', ('expert', 'dp')), may hold values from 0 to 3, all different within a row; in each aligned block of 64 rows (0 to 63, 64 to 127, ..., all dimensions but the last counted through in order) at most 40 rows name the same one
- route_fwd: float32 [4, 512, 2], P('section', ('expert', 'dp')), may hold values from 0.1 to 1
- x_bwd: bfloat16 [4, 512, 3584], P('section', ('expert', 'dp')), may hold values from -6 to 6
- ids_bwd: int32 [4, 512, 2], P('section', ('expert', 'dp')), may hold values from 0 to 3, all different within a row; in each aligned block of 64 rows (0 to 63, 64 to 127, ..., all dimensions but the last counted through in order) at most 40 rows name the same one
- route_bwd: float32 [4, 512, 2], P('section', ('expert', 'dp')), may hold values from 0.1 to 1
- dy_bwd: bfloat16 [4, 512, 3584], P('section', ('expert', 'dp')), may hold values from -3 to 3
- w_gate: bfloat16 [4, 4, 3584, 1024], P('section', 'expert', 'dp'), may hold values from -0.09375 to 0.09375
- w_up: bfloat16 [4, 4, 3584, 1024], P('section', 'expert', 'dp'), may hold values from -0.09375 to 0.09375
- w_down: bfloat16 [4, 4, 1024, 3584], P('section', 'expert', None, 'dp'), may hold values from -0.1875 to 0.1875
Outputs:
- y_next: bfloat16 [4, 512, 3584], P('section', ('expert', 'dp'))
- dx_next: bfloat16 [4, 512, 3584], P('section', ('expert', 'dp'))
- grad_gate: bfloat16 [4, 4, 3584, 1024], P('section', 'expert', 'dp')
- grad_up: bfloat16 [4, 4, 3584, 1024], P('section', 'expert', 'dp')
- grad_down: bfloat16 [4, 4, 1024, 3584], P('section', 'expert', None, 'dp')
Inputs may be any that keep to these rules, and one draw needn't show every extreme that they name: `ids_fwd`: each row names 2 different experts. In each aligned block of 64 rows of a section (the rows of one device) no expert is named by more than 40 rows, and in some block one expert is named by exactly 40 rows. `ids_bwd`: each row names 2 different experts. In each aligned block of 64 rows of a section (the rows of one device) no expert is named by more than 40 rows, and in some block one expert is named by exactly 40 rows.
All inputs are finite; a program needn't handle non-finite values.
Results may differ from a plain program's by a relative error of at most 0.0065.
Values may be sent and summed in bfloat16 or wider, within the bound.
No kernel may reach another device: no remote copies, remote signals or barrier semaphores. Data moves between devices by JAX's collectives and lax.ppermute only.
A program may use at most 128 MiB of HBM per device.

v0:
```python
import jax
import jax.numpy as jnp
from jax import lax
from jax.sharding import PartitionSpec as P

FF = 1024
TOP = 2


def shifted(value, axis, steps):
    count = lax.axis_size(axis)
    pairs = [(source, (source + steps) % count) for source in range(count)]
    return lax.ppermute(value, axis, pairs)


def slot_tables(ids, experts, capacity):
    flat = ids.reshape(-1)
    onehot = (flat[:, None] == jnp.arange(experts, dtype=jnp.int32)[None, :]).astype(jnp.int32)
    position = jnp.sum(jnp.cumsum(onehot, axis=0) * onehot, axis=1) - 1
    pair_slot = flat * capacity + position
    table = (pair_slot[None, :] == jnp.arange(experts * capacity, dtype=jnp.int32)[:, None]).astype(
        jnp.bfloat16
    )
    return (pair_slot, table)


def combine_back(returned, pair_slot, experts, group_size, capacity):
    feature_width = returned.shape[-1]
    summed = jnp.sum(
        returned.astype(jnp.float32).reshape(experts, group_size, capacity, feature_width), axis=1
    )
    return summed.reshape(experts * capacity, feature_width)[pair_slot]


def contract_first(left, right):
    return lax.dot_general(
        left, right, (((0,), (0,)), ((), ())), preferred_element_type=jnp.float32
    )


def contract_last(left, right):
    return lax.dot_general(
        left, right, (((1,), (1,)), ((), ())), preferred_element_type=jnp.float32
    )


def local(x_fwd, ids_fwd, route_fwd, x_bwd, ids_bwd, route_bwd, dy_bwd, w_gate, w_up, w_down):
    n_expert = lax.axis_size("expert")
    slab_width = w_gate.shape[-1]
    group_size = FF // slab_width
    experts = n_expert // group_size
    tok_rows = x_fwd.shape[1]
    feature_width = x_fwd.shape[2]
    spread = 4 * experts * group_size
    capacity = group_size * ((5 * tok_rows * TOP + spread - 1) // spread)
    gate_full, up_full, down_full = (
        lax.all_gather(w_gate[0, 0], "dp", axis=0, tiled=True),
        lax.all_gather(w_up[0, 0], "dp", axis=0, tiled=True),
        lax.all_gather(w_down[0, 0], "dp", axis=1, tiled=True),
    )
    slot_fwd, table_fwd = slot_tables(ids_fwd[0], experts, capacity)
    rows_fwd = jnp.sum(table_fwd.reshape(experts * capacity, tok_rows, TOP), axis=2)
    send_f = jnp.dot(rows_fwd, x_fwd[0], preferred_element_type=jnp.float32).astype(jnp.bfloat16)
    send_f = send_f.reshape(experts, capacity, feature_width)
    slot_bwd, table_bwd = slot_tables(ids_bwd[0], experts, capacity)
    rows_bwd = jnp.sum(table_bwd.reshape(experts * capacity, tok_rows, TOP), axis=2)
    send_x = jnp.dot(rows_bwd, x_bwd[0], preferred_element_type=jnp.float32).astype(jnp.bfloat16)
    send_x = send_x.reshape(experts, capacity, feature_width)
    cotangent = (route_bwd[0][:, :, None] * dy_bwd[0][:, None, :].astype(jnp.float32)).astype(
        jnp.bfloat16
    )
    cotangent = cotangent.reshape(tok_rows * TOP, feature_width)
    send_g = jnp.dot(table_bwd, cotangent, preferred_element_type=jnp.float32).astype(jnp.bfloat16)
    send_g = send_g.reshape(experts, capacity, feature_width)
    recv_f = lax.all_to_all(
        jnp.repeat(send_f, group_size, axis=0), "expert", split_axis=0, concat_axis=0, tiled=True
    )
    recv_x, recv_g = (
        lax.all_to_all(
            jnp.repeat(send_x, group_size, axis=0),
            "expert",
            split_axis=0,
            concat_axis=0,
            tiled=True,
        ),
        lax.all_to_all(
            jnp.repeat(send_g, group_size, axis=0),
            "expert",
            split_axis=0,
            concat_axis=0,
            tiled=True,
        ),
    )
    in_rows = recv_f.reshape(-1, feature_width)
    gate_pre = jnp.dot(in_rows, gate_full, preferred_element_type=jnp.float32)
    up_proj = jnp.dot(in_rows, up_full, preferred_element_type=jnp.float32)
    hidden_f = (jax.nn.silu(gate_pre) * up_proj).astype(jnp.bfloat16)
    partial_f = jnp.dot(hidden_f, down_full, preferred_element_type=jnp.float32).astype(
        jnp.bfloat16
    )
    partial_f = partial_f.reshape(n_expert, capacity, feature_width)
    returned_f = lax.all_to_all(partial_f, "expert", split_axis=0, concat_axis=0, tiled=True)
    picked_f = combine_back(returned_f, slot_fwd, experts, group_size, capacity)
    picked_f = picked_f.reshape(tok_rows, TOP, feature_width)
    output_f = jnp.sum(route_fwd[0][:, :, None] * picked_f, axis=1).astype(jnp.bfloat16)
    y_next = shifted(output_f, "section", 1)
    rows_b = recv_x.reshape(-1, feature_width)
    cot_rows = recv_g.reshape(-1, feature_width)
    gate_b = jnp.dot(rows_b, gate_full, preferred_element_type=jnp.float32)
    up_b = jnp.dot(rows_b, up_full, preferred_element_type=jnp.float32)
    sigmoid_gate = jax.nn.sigmoid(gate_b)
    activated = gate_b * sigmoid_gate
    hidden_b = (activated * up_b).astype(jnp.bfloat16)
    d_hidden = contract_last(cot_rows, down_full)
    grad_down_part = contract_first(hidden_b, cot_rows)
    d_up = (d_hidden * activated).astype(jnp.bfloat16)
    d_gate = (d_hidden * up_b * sigmoid_gate * (1.0 + gate_b * (1.0 - sigmoid_gate))).astype(
        jnp.bfloat16
    )
    back_rows = (contract_last(d_gate, gate_full) + contract_last(d_up, up_full)).astype(
        jnp.bfloat16
    )
    back_rows = back_rows.reshape(n_expert, capacity, feature_width)
    returned_b = lax.all_to_all(back_rows, "expert", split_axis=0, concat_axis=0, tiled=True)
    picked_b = combine_back(returned_b, slot_bwd, experts, group_size, capacity)
    picked_b = picked_b.reshape(tok_rows, TOP, feature_width)
    back_sum = jnp.sum(picked_b, axis=1).astype(jnp.bfloat16)
    dx_next = shifted(back_sum, "section", 1)
    grad_gate_part = contract_first(rows_b, d_gate)
    grad_up_part = contract_first(rows_b, d_up)
    gate_share, up_share, down_share = (
        lax.psum_scatter(
            grad_gate_part.astype(jnp.bfloat16), "dp", scatter_dimension=0, tiled=True
        ).astype(jnp.float32),
        lax.psum_scatter(
            grad_up_part.astype(jnp.bfloat16), "dp", scatter_dimension=0, tiled=True
        ).astype(jnp.float32),
        lax.psum_scatter(
            grad_down_part.astype(jnp.bfloat16), "dp", scatter_dimension=1, tiled=True
        ).astype(jnp.float32),
    )
    return (
        y_next[None],
        dx_next[None],
        gate_share.astype(jnp.bfloat16)[None, None],
        up_share.astype(jnp.bfloat16)[None, None],
        down_share.astype(jnp.bfloat16)[None, None],
    )


def solution(mesh):
    return jax.shard_map(
        local,
        mesh=mesh,
        in_specs=(
            P("section", ("expert", "dp"), None),
            P("section", ("expert", "dp"), None),
            P("section", ("expert", "dp"), None),
            P("section", ("expert", "dp"), None),
            P("section", ("expert", "dp"), None),
            P("section", ("expert", "dp"), None),
            P("section", ("expert", "dp"), None),
            P("section", "expert", "dp", None),
            P("section", "expert", "dp", None),
            P("section", "expert", None, "dp"),
        ),
        out_specs=(
            P("section", ("expert", "dp"), None),
            P("section", ("expert", "dp"), None),
            P("section", "expert", "dp", None),
            P("section", "expert", "dp", None),
            P("section", "expert", None, "dp"),
        ),
        check_vma=False,
    )
```

profile of v0, /device:TPU:0, one launch (start us, length us, event | category | flops | bytes accessed | tf_op | source)
XLA Modules:
  0.0 201.2 jit_solution(10632848713278195810)
XLA Ops:
  11.6 2.6 %mul.119 = f32[128,3584]{1,0:T(8,128)S(1)} reshape(f32[64,2,3584]{2,1,0:T(2,128)} %mul.118) | data formatting | bytes 3670016 | tf_op jit(solution)/shard_map/mul | solution.py:69
  16.7 5.2 %all-to-all-start.2 = ((bf16[4,40,3584]{2,1,0:T(8,128)(2,1)}), bf16[4,40,3584]{2,1,0:T(8,128)(2,1)S(1)}, u32[]{:S(2)}, u32[]{:S(2)}) async-start(bf16[4,40,3584]{2,1,0:T(8,128)(2,1)} %bitcast.14), calls=%async_computation.2 | async-start | bytes 2293760 | tf_op jit(solution)/shard_map/all_to_all | solution.py:86
  23.7 12.9 %all-to-all-done.2 = bf16[4,40,3584]{2,1,0:T(8,128)(2,1)S(1)} async-done(((bf16[4,40,3584]{2,1,0:T(8,128)(2,1)}), bf16[4,40,3584]{2,1,0:T(8,128)(2,1)S(1)}, u32[]{:S(2)}, u32[]{:S(2)}) %all-to-all-start.2) | async-done | bytes 1146912 | tf_op jit(solution)/shard_map/all_to_all | solution.py:86
  36.5 3.6 %all-to-all-start.3 = ((bf16[4,40,3584]{2,1,0:T(8,128)(2,1)}), bf16[4,40,3584]{2,1,0:T(8,128)(2,1)S(1)}, u32[]{:S(2)}, u32[]{:S(2)}) async-start(bf16[4,40,3584]{2,1,0:T(8,128)(2,1)} %bitcast.100), calls=%async_computation.3 | async-start | bytes 2293760 | tf_op jit(solution)/shard_map/all_to_all | solution.py:79
  40.2 7.7 %fusion = f32[160,1024]{1,0:T(8,128)} fusion(bf16[160,3584]{1,0:T(8,128)(2,1)S(1)} %bitcast.96, bf16[1,1,1024,3584]{3,2,1,0:T(8,128)(2,1)} %all-gather.11.cloned.1.call-done), kind=kOutput, calls=%fused_computation.5 | convolution fusion | flops 1174405120 | bytes 9142272 | tf_op jit(solution)/shard_map/dot_general | solution.py:42
  47.9 6.3 %all-to-all-done.3 = bf16[4,40,3584]{2,1,0:T(8,128)(2,1)S(1)} async-done(((bf16[4,40,3584]{2,1,0:T(8,128)(2,1)}), bf16[4,40,3584]{2,1,0:T(8,128)(2,1)S(1)}, u32[]{:S(2)}, u32[]{:S(2)}) %all-to-all-start.3) | async-done | bytes 1146912 | tf_op jit(solution)/shard_map/all_to_all | solution.py:79
  54.2 4.4 %fusion.6 = f32[160,1024]{1,0:T(8,128)S(1)} fusion(bf16[160,3584]{1,0:T(8,128)(2,1)S(1)} %bitcast.92, bf16[1,1,3584,1024]{3,2,1,0:T(8,128)(2,1)} %all-gather.9.cloned.1.call-done), kind=kOutput, calls=%fused_computation.11 | convolution fusion | flops 1174405120 | bytes 9142272 | tf_op jit(solution)/shard_map/dot_general | solution.py:110
  58.6 14.1 %all-gather.7.cloned.1.call-done = bf16[1,1,3584,1024]{3,2,1,0:T(8,128)(2,1)} async-done(((bf16[1,1,1792,1024]{3,2,1,0:T(8,128)(2,1)}), bf16[1,1,3584,1024]{3,2,1,0:T(8,128)(2,1)}) %all-gather.7.cloned.1.call-update) | async-done | bytes 7340048 | tf_op jit(solution)/shard_map/all_gather | solution.py:57
  72.7 5.7 %multiply_convert_fusion.4 = (bf16[160,1024]{1,0:T(8,128)(2,1)S(1)}, bf16[160,1024]{1,0:T(8,128)(2,1)}, f32[160,1024]{1,0:T(8,128)}) fusion(f32[160,1024]{1,0:T(8,128)} %fusion, f32[160,1024]{1,0:T(8,128)S(1)} %fusion.6, bf16[160,3584]{1,0:T(8,128)(2,1)S(1)} %bitcast.93, bf16[1,1,3584,1024]{3,2,1,0:T(8,128)(2,1)} %all-gather.7.cloned.1.call-done), kind=kOutput, calls=%fused_computation.36 | convolution fusion | flops 1176535040 | bytes 11108352 | tf_op jit(solution)/shard_map/dot_general | solution.py:109
  78.4 5.1 %convolution_convert_fusion.2 = bf16[3584,1024]{1,0:T(8,128)(2,1)} fusion(bf16[160,3584]{1,0:T(8,128)(2,1)S(1)} %bitcast.94, bf16[160,1024]{1,0:T(8,128)(2,1)S(1)} %get-tuple-element.5), kind=kOutput, calls=%fused_computation.4 | convolution fusion | flops 1178075136 | bytes 8814592 | tf_op jit(solution)/shard_map/dot_general | solution.py:36
  83.5 6.1 %convolution_convert_fusion.1 = bf16[3584,1024]{1,0:T(8,128)(2,1)} fusion(bf16[160,3584]{1,0:T(8,128)(2,1)S(1)} %bitcast.95, bf16[160,1024]{1,0:T(8,128)(2,1)} %get-tuple-element.6), kind=kOutput, calls=%fused_computation.3 | convolution fusion | flops 1178075136 | bytes 8814592 | tf_op jit(solution)/shard_map/dot_general | solution.py:36
  90.9 6.4 %convolution_convert_fusion = bf16[1024,3584]{1,0:T(8,128)(2,1)} fusion(bf16[160,3584]{1,0:T(8,128)(2,1)S(1)} %bitcast.97, f32[160,1024]{1,0:T(8,128)S(1)} %fusion.6, f32[160,1024]{1,0:T(8,128)S(1)} %copy-done.4), kind=kOutput, calls=%fused_computation.2 | convolution fusion | flops 1179058176 | bytes 9797632 | tf_op jit(solution)/shard_map/dot_general | solution.py:36
  100.5 3.8 %all-to-all-start = ((bf16[4,40,3584]{2,1,0:T(8,128)(2,1)}), bf16[4,40,3584]{2,1,0:T(8,128)(2,1)S(1)}, u32[]{:S(2)}, u32[]{:S(2)}) async-start(bf16[4,40,3584]{2,1,0:T(8,128)(2,1)} %bitcast.3), calls=%async_computation | async-start | bytes 2293760 | tf_op jit(solution)/shard_map/all_to_all | solution.py:75
  105.0 14.6 %all-to-all-done = bf16[4,40,3584]{2,1,0:T(8,128)(2,1)S(1)} async-done(((bf16[4,40,3584]{2,1,0:T(8,128)(2,1)}), bf16[4,40,3584]{2,1,0:T(8,128)(2,1)S(1)}, u32[]{:S(2)}, u32[]{:S(2)}) %all-to-all-start) | async-done | bytes 1146912 | tf_op jit(solution)/shard_map/all_to_all | solution.py:75
  119.5 4.5 %fusion.14 = f32[160,1024]{1,0:T(8,128)S(1)} fusion(bf16[160,3584]{1,0:T(8,128)(2,1)S(1)} %bitcast.98, bf16[1,1,3584,1024]{3,2,1,0:T(8,128)(2,1)} %all-gather.7.cloned.1.call-done), kind=kOutput, calls=%fused_computation.19 | convolution fusion | flops 1174405120 | bytes 9142272 | tf_op jit(solution)/shard_map/dot_general | solution.py:95
  124.1 8.8 %fusion.22 = bf16[160,3584]{1,0:T(8,128)(2,1)} fusion(bf16[1,1,1024,3584]{3,2,1,0:T(8,128)(2,1)} %all-gather.11.cloned.1.call-done, bf16[160,3584]{1,0:T(8,128)(2,1)S(1)} %bitcast.99, bf16[1,1,3584,1024]{3,2,1,0:T(8,128)(2,1)} %all-gather.9.cloned.1.call-done, f32[160,1024]{1,0:T(8,128)S(1)} %fusion.14), kind=kOutput, calls=%fused_computation.23 | convolution fusion | flops 2350366720 | bytes 17629184 | tf_op jit(solution)/shard_map/dot_general | solution.py:98
  132.8 3.8 %all-to-all-start.1 = ((bf16[4,40,3584]{2,1,0:T(8,128)(2,1)}), bf16[4,40,3584]{2,1,0:T(8,128)(2,1)S(1)}, u32[]{:S(2)}, u32[]{:S(2)}) async-start(bf16[4,40,3584]{2,1,0:T(8,128)(2,1)} %bitcast.8), calls=%async_computation.1 | async-start | bytes 2293760 | tf_op jit(solution)/shard_map/all_to_all | solution.py:102
  136.6 6.0 %fusion.4 = f32[160,3584]{1,0:T(8,128)S(1)} fusion(bf16[160,1024]{1,0:T(8,128)(2,1)S(1)} %copy-done.3, bf16[1,1,3584,1024]{3,2,1,0:T(8,128)(2,1)} %all-gather.9.cloned.1.call-done), kind=kOutput, calls=%fused_computation.9 | convolution fusion | flops 1174405120 | bytes 9961472 | tf_op jit(solution)/shard_map/dot_general | solution.py:42
  142.7 6.8 %fusion.19 = bf16[160,3584]{1,0:T(8,128)(2,1)} fusion(f32[160,3584]{1,0:T(8,128)S(1)} %fusion.4, bf16[160,1024]{1,0:T(8,128)(2,1)S(1)} %get-tuple-element.5, bf16[1,1,3584,1024]{3,2,1,0:T(8,128)(2,1)} %all-gather.7.cloned.1.call-done), kind=kOutput, calls=%fused_computation.22 | convolution fusion | flops 1175552000 | bytes 11108352 | tf_op jit(solution)/shard_map/dot_general | solution.py:42
  152.1 4.5 %all-to-all-start.4 = ((bf16[4,40,3584]{2,1,0:T(8,128)(2,1)}), bf16[4,40,3584]{2,1,0:T(8,128)(2,1)}, u32[]{:S(2)}, u32[]{:S(2)}) async-start(bf16[4,40,3584]{2,1,0:T(8,128)(2,1)} %bitcast.20), calls=%async_computation.4 | async-start | bytes 2293760 | tf_op jit(solution)/shard_map/all_to_all | solution.py:124
  158.1 2.4 %gather_fusion = f32[128,3584]{1,0:T(8,128)} fusion(f32[160,3584]{1,0:T(8,128)S(1)} %bitcast_convert_fusion.1, s32[1024]{0:T(1024)S(1)} %pad_clamp_fusion.1), kind=kCustom, calls=%fused_computation | custom fusion | bytes 3670528 | tf_op jit(solution)/shard_map/gather | solution.py:32
  162.9 3.3 %multiply_reduce_fusion = bf16[64,3584]{1,0:T(8,128)(2,1)} fusion(f32[64,2,3584]{2,1,0:T(2,128)S(1)} %reshape.185, f32[64,2]{1,0:T(8,128)S(1)} %copy.35), kind=kLoop, calls=%fused_computation.28 | loop fusion | flops 688128 | bytes 2294272 | tf_op jit(solution)/shard_map/reduce_sum | solution.py:105
  174.5 2.5 %reshape.191 = f32[64,2,3584]{2,1,0:T(2,128)S(1)} reshape(f32[128,3584]{1,0:T(8,128)} %gather_fusion.1) | data formatting | bytes 3670016 | tf_op jit(solution)/shard_map/reshape | solution.py:126
  181.4 11.4 %collective-permute-done.1 = bf16[64,3584]{1,0:T(8,128)(2,1)S(1)} collective-permute-done((bf16[64,3584]{1,0:T(8,128)(2,1)S(1)}, bf16[64,3584]{1,0:T(8,128)(2,1)S(1)}, u32[]{:S(2)}, u32[]{:S(2)}) %collective-permute-start.1) | collective-permute-done | bytes 458784 | tf_op jit(solution)/shard_map/ppermute | solution.py:13
  (89 shorter events, 34.5 us)
Async XLA Ops:
  7.2 15.0 %copy-start = (bf16[1,64,3584]{2,1,0:T(8,128)(2,1)S(1)}, bf16[1,64,3584]{2,1,0:T(8,128)(2,1)}, u32[]{:S(2)}) copy-start(bf16[1,64,3584]{2,1,0:T(8,128)(2,1)} %param.13) | copy-start | bytes 1376260
  7.2 33.0 %all-gather.11.cloned.1.call-start = ((), (), s32[]{:S(2)}) async-start(), calls=%async_computation.13 | async-start | bytes 11010048 | tf_op jit(solution)/shard_map/all_gather | solution.py:59
  7.9 46.3 %all-gather.9.cloned.1.call-start = ((), (), s32[]{:S(2)}) async-start(), calls=%async_computation.12 | async-start | bytes 11010048 | tf_op jit(solution)/shard_map/all_gather | solution.py:58
  8.7 1.0 copy-start.6
  8.7 64.0 %all-gather.7.cloned.1.call-start = ((), (), s32[]{:S(2)}) async-start(), calls=%async_computation.11 | async-start | bytes 11010048 | tf_op jit(solution)/shard_map/all_gather | solution.py:57
  11.6 2.6 %copy-start.9 = (f32[1,64,2]{1,2,0:T(2,128)S(1)}, f32[1,64,2]{1,2,0:T(2,128)}, u32[]{:S(2)}) copy-start(f32[1,64,2]{1,2,0:T(2,128)} %param.15) | copy-start | bytes 1540
  11.6 2.9 %copy-start.8 = (s32[1,64,2]{1,2,0:T(2,128)S(1)}, s32[1,64,2]{1,2,0:T(2,128)}, u32[]{:S(2)}) copy-start(s32[1,64,2]{1,2,0:T(2,128)} %param.14) | copy-start | bytes 1540
  16.7 19.9 %all-to-all-start.2 = ((bf16[4,40,3584]{2,1,0:T(8,128)(2,1)}), bf16[4,40,3584]{2,1,0:T(8,128)(2,1)S(1)}, u32[]{:S(2)}, u32[]{:S(2)}) async-start(bf16[4,40,3584]{2,1,0:T(8,128)(2,1)} %bitcast.14), calls=%async_computation.2 | async-start | bytes 2293760 | tf_op jit(solution)/shard_map/all_to_all | solution.py:86
  36.5 17.7 %all-to-all-start.3 = ((bf16[4,40,3584]{2,1,0:T(8,128)(2,1)}), bf16[4,40,3584]{2,1,0:T(8,128)(2,1)S(1)}, u32[]{:S(2)}, u32[]{:S(2)}) async-start(bf16[4,40,3584]{2,1,0:T(8,128)(2,1)} %bitcast.100), calls=%async_computation.3 | async-start | bytes 2293760 | tf_op jit(solution)/shard_map/all_to_all | solution.py:79
  40.1 152.7 %reduce-scatter.4.cloned.1.call-start = ((), (), s32[]{:S(2)}) async-start(), calls=%async_computation.8 | async-start | bytes 11010048 | tf_op jit(solution)/shard_map/reduce_scatter | solution.py:132
  83.5 109.4 %reduce-scatter.6.cloned.1.call-start = ((), (), s32[]{:S(2)}) async-start(), calls=%async_computation.9 | async-start | bytes 11010048 | tf_op jit(solution)/shard_map/reduce_scatter | solution.py:135
  89.6 1.2 copy-start.4
  89.7 103.2 %reduce-scatter.8.cloned.1.call-start = ((), (), s32[]{:S(2)}) async-start(), calls=%async_computation.10 | async-start | bytes 11010048 | tf_op jit(solution)/shard_map/reduce_scatter | solution.py:138
  97.3 0.7 copy-start.7
  97.3 1.7 copy-start.5
  99.0 5.6 %copy-start.10 = (f32[1,64,2]{1,2,0:T(2,128)S(1)}, f32[1,64,2]{1,2,0:T(2,128)}, u32[]{:S(2)}) copy-start(f32[1,64,2]{1,2,0:T(2,128)} %param.12) | copy-start | bytes 1540
  100.5 19.0 %all-to-all-start = ((bf16[4,40,3584]{2,1,0:T(8,128)(2,1)}), bf16[4,40,3584]{2,1,0:T(8,128)(2,1)S(1)}, u32[]{:S(2)}, u32[]{:S(2)}) async-start(bf16[4,40,3584]{2,1,0:T(8,128)(2,1)} %bitcast.3), calls=%async_computation | async-start | bytes 2293760 | tf_op jit(solution)/shard_map/all_to_all | solution.py:75
  132.8 3.8 %copy-start.3 = (bf16[160,1024]{1,0:T(8,128)(2,1)S(1)}, bf16[160,1024]{1,0:T(8,128)(2,1)}, u32[]{:S(2)}) copy-start(bf16[160,1024]{1,0:T(8,128)(2,1)} %get-tuple-element.6) | copy-start | bytes 983044
  132.8 18.2 %all-to-all-start.1 = ((bf16[4,40,3584]{2,1,0:T(8,128)(2,1)}), bf16[4,40,3584]{2,1,0:T(8,128)(2,1)S(1)}, u32[]{:S(2)}, u32[]{:S(2)}) async-start(bf16[4,40,3584]{2,1,0:T(8,128)(2,1)} %bitcast.8), calls=%async_computation.1 | async-start | bytes 2293760 | tf_op jit(solution)/shard_map/all_to_all | solution.py:102
  151.0 1.0 copy-start.2
  152.1 18.5 %all-to-all-start.4 = ((bf16[4,40,3584]{2,1,0:T(8,128)(2,1)}), bf16[4,40,3584]{2,1,0:T(8,128)(2,1)}, u32[]{:S(2)}, u32[]{:S(2)}) async-start(bf16[4,40,3584]{2,1,0:T(8,128)(2,1)} %bitcast.20), calls=%async_computation.4 | async-start | bytes 2293760 | tf_op jit(solution)/shard_map/all_to_all | solution.py:124
  166.2 15.2 %collective-permute-start = (bf16[64,3584]{1,0:T(8,128)(2,1)}, bf16[64,3584]{1,0:T(8,128)(2,1)S(1)}, u32[]{:S(2)}, u32[]{:S(2)}) collective-permute-start(bf16[64,3584]{1,0:T(8,128)(2,1)} %multiply_reduce_fusion), channel_id=1, source_target_pairs={{0,8},{8,16},{16,24},{24,0},{1,9},{9,17},{17,25},{25,1},{2,10},{10... | collective-permute-start | bytes 1376264 | tf_op jit(solution)/shard_map/ppermute | solution.py:13
  174.5 19.9 %copy-start.1 = (bf16[1,64,3584]{2,1,0:T(8,128)(2,1)S(1)}, bf16[1,64,3584]{2,1,0:T(8,128)(2,1)}, u32[]{:S(2)}) copy-start(bf16[1,64,3584]{2,1,0:T(8,128)(2,1)} %param.13) | copy-start | bytes 1376260
  179.4 13.4 %collective-permute-start.1 = (bf16[64,3584]{1,0:T(8,128)(2,1)S(1)}, bf16[64,3584]{1,0:T(8,128)(2,1)S(1)}, u32[]{:S(2)}, u32[]{:S(2)}) collective-permute-start(bf16[64,3584]{1,0:T(8,128)(2,1)S(1)} %reduce_sum.73), channel_id=1, source_target_pairs={{0,8},{8,16},{16,24},{24,0},{1,9},{9,17},{17,25},{25,1},{2,10},{10... | collective-permute-start | bytes 1376264 | tf_op jit(solution)/shard_map/ppermute | solution.py:13
Sparse Core Ops, SparseCore 0:
  9.6 20.9 all-gather.10
  32.1 19.4 all-gather.8
  53.2 19.4 all-gather.6
  83.6 17.0 reduce-scatter.3
  103.5 16.8 reduce-scatter.5
  123.1 17.1 reduce-scatter.7
where the time goes:
time: 202 us; the launch traced here: 201 us
  matrix products  66 us (33%)
  waiting for transfers between devices  65.4 us (32%)
  starting transfers between devices  25.2 us (12%)
  local copies, waits for them, and re-layouts  20.4 us (10%)
  between operations  14.4 us (7%)
  other arithmetic  9.85 us (5%)
    dot_general x3, matrix products, contract_last(): lax.dot_general(left, right, (((1,), (1,)), ((), ())), preferred_element_...  20.5 us
    dot_general x3, matrix products, contract_first(): lax.dot_general(left, right, (((0,), (0,)), ((), ())), preferred_element_...  17.6 us
    all_to_all x1, waiting for transfers between devices, local(): lax.all_to_all(jnp.repeat(send_f, group_size, axis=0), 'expert', split_ax...  14.6 us
    all_gather x1, waiting for transfers between devices, local(): lax.all_gather(w_gate[0, 0], 'dp', axis=0, tiled=True)  14.1 us
    all_to_all x1, waiting for transfers between devices, local(): lax.all_to_all(jnp.repeat(send_g, group_size, axis=0), 'expert', split_ax...  12.9 us
    ppermute x2, waiting for transfers between devices, shifted(): return lax.ppermute(value, axis, pairs)  11.4 us
    dot_general x1, matrix products, local(): jnp.dot(hidden_f, down_full, preferred_element_type=jnp.float32)  8.76 us
    all_to_all x1, waiting for transfers between devices, local(): lax.all_to_all(jnp.repeat(send_x, group_size, axis=0), 'expert', split_ax...  6.31 us
  transfers between devices with their start and end apart: 13, of which 7 were waited for; matrix products, arithmetic and copies ran while one was open for 40% of the time, Pallas kernels for 0%

commit v1 on v0

v1 whole, which is shorter than its diff:
```python
import functools

import jax
import jax.numpy as jnp
from jax import lax
from jax.experimental import pallas as pl
from jax.experimental.pallas import tpu as pltpu
from jax.sharding import PartitionSpec as P

FF = 1024
TOP = 2
TILE = 256
VMEM_LIMIT = 32 * 1024 * 1024
F32 = jnp.float32
BF16 = jnp.bfloat16


def exchange(value, axis, mask):
    count = lax.axis_size(axis)
    return lax.ppermute(value, axis, [(source, source ^ mask) for source in range(count)])


def section_shift(value, flip):
    sections, cores = lax.axis_size("section"), lax.axis_size("dp")
    pairs = []
    for section in range(sections):
        for core in range(cores):
            target = ((section + 1) % sections) * cores + (core ^ flip)
            pairs.append((section * cores + core, target))
    return lax.ppermute(value, ("section", "dp"), pairs)


def dot(left, right, left_dim, right_dim):
    return lax.dot_general(
        left, right, (((left_dim,), (right_dim,)), ((), ())), preferred_element_type=F32
    )


def call(kernel, out_shape, grid, in_specs, out_specs, scratch, flops, moved):
    return pl.pallas_call(
        kernel,
        out_shape=out_shape,
        grid=grid,
        in_specs=in_specs,
        out_specs=out_specs,
        scratch_shapes=scratch,
        compiler_params=pltpu.CompilerParams(vmem_limit_bytes=VMEM_LIMIT),
        cost_estimate=pl.CostEstimate(flops=flops, bytes_accessed=moved, transcendentals=0),
    )


def whole(shape):
    return pl.BlockSpec(shape, lambda *_: (0,) * len(shape))


SCALARS = pl.BlockSpec(memory_space=pltpu.SMEM)


def slot_rows(place_ref, ids_ref, blocks, group, capacity, tokens):
    lanes = 2 * tokens
    padded = max(8, blocks)
    me, core = place_ref[0], place_ref[1]
    first, second = ids_ref[0:1, :], ids_ref[1:2, :]
    row = lax.broadcasted_iota(jnp.int32, (padded, lanes), 0)
    expert = ((row ^ me) // group).astype(F32)
    is_first, is_second = expert == first, expert == second
    named = jnp.where(is_first | is_second, 1.0, 0.0)
    before = lax.broadcasted_iota(jnp.int32, (lanes, lanes), 0)
    after = lax.broadcasted_iota(jnp.int32, (lanes, lanes), 1)
    earlier = (before < after) & ((before < tokens) == (after < tokens))
    position = dot(named.astype(BF16), jnp.where(earlier, 1.0, 0.0).astype(BF16), 1, 0)
    lane = lax.broadcasted_iota(jnp.int32, (padded, lanes), 1)
    half = jnp.where(lane < tokens, core, 1 - core).astype(F32)
    slot = jnp.where(named > 0.5, position + half * capacity, -1.0)
    return slot, is_first


def slot_table(slot, block, rows):
    lanes = slot.shape[1]
    index = lax.broadcasted_iota(jnp.int32, (rows, lanes), 0).astype(F32)
    return jnp.where(index == slot[block : block + 1, :], 1.0, 0.0)


def dispatch_kernel(
    place_ref, meta_ref, own_ref, other_ref, *refs, blocks, group, capacity, tokens, weighted
):
    outs, all_ref = refs[:blocks], refs[blocks]
    rows, width = outs[0].shape
    core = place_ref[1]
    own = own_ref[:, pl.ds(pl.multiple_of(core * width, 128), width)]
    all_ref[0:tokens, :] = own
    all_ref[tokens : 2 * tokens, :] = other_ref[...]
    slot, is_first = slot_rows(place_ref, meta_ref, blocks, group, capacity, tokens)
    for block in range(blocks):
        table = slot_table(slot, block, rows)
        if weighted:
            route = jnp.where(
                is_first[block : block + 1, :], meta_ref[2:3, :], meta_ref[3:4, :]
            )
            scale = jnp.sum(table * route, axis=1, keepdims=True)
        table = table.astype(BF16)
        for start in range(0, width, TILE):
            picked = dot(table, all_ref[:, start : start + TILE], 1, 0)
            if weighted:
                picked = picked * scale
            outs[block][:, start : start + TILE] = picked.astype(BF16)


def dispatch(place, meta, own, other, shape, weighted):
    blocks, rows, group, capacity = shape
    tokens, width = other.shape
    kernel = functools.partial(
        dispatch_kernel,
        blocks=blocks,
        group=group,
        capacity=capacity,
        tokens=tokens,
        weighted=weighted,
    )
    return call(
        kernel,
        [jax.ShapeDtypeStruct((rows, width), BF16)] * blocks,
        (1,),
        [SCALARS, whole(meta.shape), whole(own.shape), whole(other.shape)],
        [whole((rows, width))] * blocks,
        [pltpu.VMEM((2 * tokens, width), BF16)],
        2 * blocks * rows * 2 * tokens * width,
        2 * width * (3 * tokens + blocks * rows),
    )(place, meta, own, other)


def combine_kernel(place_ref, meta_ref, *refs, blocks, group, capacity, tokens, weighted):
    returned, (own_ref, other_ref) = refs[:blocks], refs[blocks:]
    rows, width = returned[0].shape
    slot, is_first = slot_rows(place_ref, meta_ref, blocks, group, capacity, tokens)
    high, low = [], []
    for block in range(blocks):
        table = slot_table(slot, block, rows)
        if weighted:
            route = jnp.where(
                is_first[block : block + 1, :], meta_ref[2:3, :], meta_ref[3:4, :]
            )
            table = table * route
        top = table.astype(BF16)
        high.append(top)
        low.append((table - top.astype(F32)).astype(BF16))
    for start in range(0, width, TILE):
        total = jnp.zeros((2 * tokens, TILE), F32)
        for block in range(blocks):
            values = returned[block][:, start : start + TILE]
            total += dot(high[block], values, 0, 0)
            if weighted:
                total += dot(low[block], values, 0, 0)
        total = total.astype(BF16)
        own_ref[:, start : start + TILE] = total[:tokens]
        other_ref[:, start : start + TILE] = total[tokens:]


def combine(place, meta, returned, shape, tokens, weighted):
    blocks, rows, group, capacity = shape
    width = returned[0].shape[1]
    kernel = functools.partial(
        combine_kernel,
        blocks=blocks,
        group=group,
        capacity=capacity,
        tokens=tokens,
        weighted=weighted,
    )
    return call(
        kernel,
        [jax.ShapeDtypeStruct((tokens, width), BF16)] * 2,
        (1,),
        [SCALARS, whole(meta.shape)] + [whole((rows, width))] * blocks,
        [whole((tokens, width))] * 2,
        [],
        4 * blocks * rows * 2 * tokens * width,
        2 * width * (2 * tokens + blocks * rows),
    )(place, meta, *returned)


def gather_blocks(refs, target):
    rows = refs[0].shape[0]
    for block, ref in enumerate(refs):
        target[block * rows : (block + 1) * rows, :] = ref[...]


def gate_up_kernel(*refs, blocks):
    gate_w, up_w, out, all_ref = refs[blocks:]

    @pl.when(pl.program_id(0) == 0)
    def _():
        gather_blocks(refs[:blocks], all_ref)

    out[0] = dot(all_ref[...], gate_w[...], 1, 0).astype(BF16)
    out[1] = dot(all_ref[...], up_w[...], 1, 0).astype(BF16)


def gate_up(inputs, gate_w, up_w):
    blocks, (rows, width) = len(inputs), inputs[0].shape
    units, total = gate_w.shape[1], len(inputs) * inputs[0].shape[0]
    weight = pl.BlockSpec((width, TILE), lambda i: (0, i))
    return call(
        functools.partial(gate_up_kernel, blocks=blocks),
        jax.ShapeDtypeStruct((2, total, units), BF16),
        (units // TILE,),
        [whole((rows, width))] * blocks + [weight, weight],
        pl.BlockSpec((2, total, TILE), lambda i: (0, 0, i)),
        [pltpu.VMEM((total, width), BF16)],
        4 * total * width * units,
        2 * (total * width + 2 * width * units + 2 * total * units),
    )(*inputs, gate_w, up_w)


def d_hidden_kernel(*refs, blocks):
    down_w, out, all_ref = refs[blocks:]

    @pl.when(pl.program_id(0) == 0)
    def _():
        gather_blocks(refs[:blocks], all_ref)

    out[...] = dot(all_ref[...], down_w[...], 1, 1).astype(BF16)


def d_hidden(inputs, down_w):
    blocks, (rows, width) = len(inputs), inputs[0].shape
    units, total = down_w.shape[0], len(inputs) * inputs[0].shape[0]
    return call(
        functools.partial(d_hidden_kernel, blocks=blocks),
        jax.ShapeDtypeStruct((total, units), BF16),
        (units // TILE,),
        [whole((rows, width))] * blocks + [pl.BlockSpec((TILE, width), lambda i: (i, 0))],
        pl.BlockSpec((total, TILE), lambda i: (0, i)),
        [pltpu.VMEM((total, width), BF16)],
        2 * total * width * units,
        2 * (total * width + width * units + total * units),
    )(*inputs, down_w)


def scatter_tile(value, outs):
    rows = outs[0].shape[0]
    for block, out in enumerate(outs):
        out[...] = value[block * rows : (block + 1) * rows]


def down_kernel(own_ref, other_ref, down_w, *refs):
    outs, hidden = refs[:-1], refs[-1]

    @pl.when(pl.program_id(0) == 0)
    def _():
        for start in range(0, hidden.shape[1], TILE):
            part = slice(start, start + TILE)
            gate = own_ref[0, :, part].astype(F32) + other_ref[0, :, part].astype(F32)
            up = own_ref[1, :, part].astype(F32) + other_ref[1, :, part].astype(F32)
            hidden[:, part] = (gate * jax.nn.sigmoid(gate) * up).astype(BF16)

    scatter_tile(dot(hidden[...], down_w[...], 1, 0).astype(BF16), outs)


def down(own, other, down_w, blocks):
    _, total, units = own.shape
    width, rows = down_w.shape[1], total // blocks
    return call(
        down_kernel,
        [jax.ShapeDtypeStruct((rows, width), BF16)] * blocks,
        (width // TILE,),
        [whole(own.shape)] * 2 + [pl.BlockSpec((units, TILE), lambda i: (0, i))],
        [pl.BlockSpec((rows, TILE), lambda i: (0, i))] * blocks,
        [pltpu.VMEM((total, units), BF16)],
        2 * total * width * units,
        2 * (total * width + width * units + 4 * total * units),
    )(own, other, down_w)


def back_kernel(own_ref, other_ref, own_d, other_d, gate_w, up_w, hidden, d_gate, d_up, *outs):
    @pl.when(pl.program_id(0) == 0)
    def _():
        for start in range(0, hidden.shape[1], TILE):
            part = slice(start, start + TILE)
            gate = own_ref[0, :, part].astype(F32) + other_ref[0, :, part].astype(F32)
            up = own_ref[1, :, part].astype(F32) + other_ref[1, :, part].astype(F32)
            d_hid = own_d[:, part].astype(F32) + other_d[:, part].astype(F32)
            sigmoid = jax.nn.sigmoid(gate)
            activated = gate * sigmoid
            hidden[:, part] = (activated * up).astype(BF16)
            d_up[:, part] = (d_hid * activated).astype(BF16)
            d_gate[:, part] = (
                d_hid * up * sigmoid * (1.0 + gate * (1.0 - sigmoid))
            ).astype(BF16)

    total = dot(d_gate[...], gate_w[...], 1, 1) + dot(d_up[...], up_w[...], 1, 1)
    scatter_tile(total.astype(BF16), outs)


def back(own, other, own_d, other_d, gate_w, up_w, blocks):
    _, total, units = own.shape
    width, rows = gate_w.shape[0], total // blocks
    weight = pl.BlockSpec((TILE, units), lambda i: (i, 0))
    return call(
        back_kernel,
        [jax.ShapeDtypeStruct((total, units), BF16)] * 3
        + [jax.ShapeDtypeStruct((rows, width), BF16)] * blocks,
        (width // TILE,),
        [whole(own.shape)] * 2 + [whole(own_d.shape)] * 2 + [weight, weight],
        [whole((total, units))] * 3 + [pl.BlockSpec((rows, TILE), lambda i: (0, i))] * blocks,
        [],
        4 * total * width * units,
        2 * (total * width + 2 * width * units + 9 * total * units),
    )(own, other, own_d, other_d, gate_w, up_w)


def grad_kernel(hidden, d_gate, d_up, *refs, blocks):
    inputs, cots = refs[:blocks], refs[blocks : 2 * blocks]
    grad_gate, grad_up, grad_down, in_all, cot_all = refs[2 * blocks :]
    gather_blocks(inputs, in_all)
    gather_blocks(cots, cot_all)
    grad_gate[...] = dot(in_all[...], d_gate[...], 0, 0).astype(BF16)
    grad_up[...] = dot(in_all[...], d_up[...], 0, 0).astype(BF16)
    grad_down[...] = dot(hidden[...], cot_all[...], 0, 0).astype(BF16)


def grads(hidden, d_gate, d_up, inputs, cots):
    blocks, (rows, width) = len(inputs), inputs[0].shape
    total, units = hidden.shape
    piece = pl.BlockSpec((rows, TILE), lambda i: (0, i))
    return call(
        functools.partial(grad_kernel, blocks=blocks),
        [
            jax.ShapeDtypeStruct((width, units), BF16),
            jax.ShapeDtypeStruct((width, units), BF16),
            jax.ShapeDtypeStruct((units, width), BF16),
        ],
        (width // TILE,),
        [whole((total, units))] * 3 + [piece] * (2 * blocks),
        [
            pl.BlockSpec((TILE, units), lambda i: (i, 0)),
            pl.BlockSpec((TILE, units), lambda i: (i, 0)),
            pl.BlockSpec((units, TILE), lambda i: (0, i)),
        ],
        [pltpu.VMEM((total, TILE), BF16)] * 2,
        6 * total * width * units,
        2 * (2 * total * width + 3 * width * units + 3 * total * units),
    )(hidden, d_gate, d_up, *inputs, *cots)


def to_experts(blocks):
    return [blocks[0]] + [
        exchange(block, "expert", mask) for mask, block in enumerate(blocks) if mask > 0
    ]


def next_section(own, other, core):
    mine, rest = section_shift(own, 0), section_shift(other, 1)
    first = jnp.where(core == 0, mine, rest)
    second = jnp.where(core == 0, rest, mine)
    return jnp.concatenate([first, second], axis=1)


def local(x_fwd, ids_fwd, route_fwd, x_bwd, ids_bwd, route_bwd, dy_bwd, w_gate, w_up, w_down):
    n_expert = lax.axis_size("expert")
    slab_width = w_gate.shape[-1]
    group = FF // slab_width
    experts = n_expert // group
    tokens = x_fwd.shape[1]
    width = w_gate.shape[2]
    spread = 4 * experts * group
    capacity = group * ((5 * tokens * TOP + spread - 1) // spread)
    rows = (2 * capacity + 15) // 16 * 16
    shape = (n_expert, rows, group, capacity)
    core = lax.axis_index("dp")
    place = jnp.stack([lax.axis_index("expert"), core]).astype(jnp.int32)
    gate_w, up_w, down_w = w_gate[0, 0], w_up[0, 0], w_down[0, 0]

    def other_half(value):
        return lax.dynamic_slice_in_dim(value, (1 - core) * width, width, axis=1)

    meta = jnp.concatenate(
        [
            ids_bwd[0].T.astype(F32),
            route_bwd[0].T,
            ids_fwd[0].T.astype(F32),
            route_fwd[0].T,
        ],
        axis=0,
    )
    meta = jnp.concatenate([meta, exchange(meta, "dp", 1)], axis=1)
    meta_b, meta_f = meta[0:4], meta[4:8]
    other_x = exchange(other_half(x_bwd[0]), "dp", 1)
    other_dy = exchange(other_half(dy_bwd[0]), "dp", 1)
    other_f = exchange(other_half(x_fwd[0]), "dp", 1)

    rows_b = to_experts(dispatch(place, meta_b, x_bwd[0], other_x, shape, False))
    cots_b = to_experts(dispatch(place, meta_b, dy_bwd[0], other_dy, shape, True))
    rows_f = to_experts(dispatch(place, meta_f, x_fwd[0], other_f, shape, False))

    part_b = gate_up(rows_b, gate_w, up_w)
    part_b_other = exchange(part_b, "dp", 1)
    part_d = d_hidden(cots_b, down_w)
    part_d_other = exchange(part_d, "dp", 1)
    hidden, d_gate, d_up, *back_blocks = back(
        part_b, part_b_other, part_d, part_d_other, gate_w, up_w, n_expert
    )
    returned_b = to_experts(back_blocks)

    part_f = gate_up(rows_f, gate_w, up_w)
    part_f_other = exchange(part_f, "dp", 1)
    returned_f = to_experts(down(part_f, part_f_other, down_w, n_expert))

    grad_gate, grad_up, grad_down = grads(hidden, d_gate, d_up, rows_b, cots_b)

    dx_next = next_section(*combine(place, meta_b, returned_b, shape, tokens, False), core)
    y_next = next_section(*combine(place, meta_f, returned_f, shape, tokens, True), core)
    return (
        y_next[None],
        dx_next[None],
        grad_gate[None, None],
        grad_up[None, None],
        grad_down[None, None],
    )


def solution(mesh):
    rows = P("section", ("expert", "dp"), None)
    by_feature = P("section", "expert", "dp", None)
    down_spec = P("section", "expert", None, "dp")
    return jax.shard_map(
        local,
        mesh=mesh,
        in_specs=(rows,) * 7 + (by_feature, by_feature, down_spec),
        out_specs=(rows, rows, by_feature, by_feature, down_spec),
        check_vma=False,
    )
```

time: 202 us -> 115 us (0.57)
  matrix products: 66 us -> 0 us
  Pallas kernels: 0 us -> 35.4 us
  waiting for transfers between devices: 65.4 us -> 31.9 us
  between operations: 14.4 us -> 0.92 us
  other arithmetic: 9.85 us -> 3.92 us
  local copies, waits for them, and re-layouts: 20.4 us -> 15.8 us
    dot_general x13 -> x0, matrix products: 66 us -> none  [the longest x3 20.5 us: contract_last(): lax.dot_general(left, right, (((1,), (1,)), ((), ())), preferred_element_...]
    all_to_all x5 -> x0, waiting for transfers between devices: 37.8 us -> none  [the longest x1 14.6 us: local(): lax.all_to_all(jnp.repeat(send_f, group_size, axis=0), 'expert', split_ax...]
    pallas_call x0 -> x11, Pallas kernels: none -> 35.4 us  [the longest x1 8.51 us: grads(): call(functools.partial(grad_kernel, blocks=blocks), [jax.ShapeDtypeStruct...]
    ppermute x2 -> x26, starting transfers between devices: 3.95 us -> 26.4 us  [the longest x22 21.8 us: exchange(): lax.ppermute(value, axis, [(source, source ^ mask) for source in range(co...]
    all_to_all x5 -> x0, starting transfers between devices: 20.8 us -> none  [the longest x1 5.16 us: local(): lax.all_to_all(jnp.repeat(send_g, group_size, axis=0), 'expert', split_ax...]
    ppermute x2 -> x26, waiting for transfers between devices: 11.4 us -> 31.9 us  [the longest x22 20.4 us: exchange(): lax.ppermute(value, axis, [(source, source ^ mask) for source in range(co...]
    all_gather x3 -> x0, waiting for transfers between devices: 14.1 us -> none  [the longest x1 14.1 us: local(): lax.all_gather(w_gate[0, 0], 'dp', axis=0, tiled=True)]
    unnamed x27 -> x54, local copies, waits for them, and re-layouts: 4.8 us -> 13 us
  transfers between devices with their start and end apart: 13 -> 26, of which waited for: 7 -> 9; matrix products, arithmetic and copies ran while one was open for 40% -> 4% of each run, Pallas kernels for 0% -> 30%
where the time goes in v1:
time: 115 us; the launch traced here: 114 us
  Pallas kernels  35.4 us (31%)
  waiting for transfers between devices  31.9 us (28%)
  starting transfers between devices  26.4 us (23%)
  local copies, waits for them, and re-layouts  15.8 us (14%)
  other arithmetic  3.92 us (3%)
    ppermute x22, starting transfers between devices, exchange(): lax.ppermute(value, axis, [(source, source ^ mask) for source in range(co...  21.8 us
    ppermute x22, waiting for transfers between devices, exchange(): lax.ppermute(value, axis, [(source, source ^ mask) for source in range(co...  20.4 us
    unnamed x54, local copies, waits for them, and re-layouts  13 us
    ppermute x4, waiting for transfers between devices, section_shift(): return lax.ppermute(value, ('section', 'dp'), pairs)  11.4 us
    pallas_call x1, Pallas kernels, grads(): call(functools.partial(grad_kernel, blocks=blocks), [jax.ShapeDtypeStruct...  8.51 us
    pallas_call x2, Pallas kernels, gate_up(): call(functools.partial(gate_up_kernel, blocks=blocks), jax.ShapeDtypeStru...  8.49 us
    pallas_call x1, Pallas kernels, back(): call(back_kernel, [jax.ShapeDtypeStruct((total, units), BF16)] * 3 + [jax...  5.8 us
    ppermute x4, starting transfers between devices, section_shift(): return lax.ppermute(value, ('section', 'dp'), pairs)  4.61 us
  transfers between devices with their start and end apart: 26, of which 9 were waited for; matrix products, arithmetic and copies ran while one was open for 4% of the time, Pallas kernels for 30%

profile of v1, /device:TPU:0, one launch (start us, length us, event | category | flops | bytes accessed | tf_op | source)
XLA Modules:
  0.0 114.3 jit_solution(11455527255587187873)
XLA Ops:
  7.2 2.7 %collective-permute-start.12 = (bf16[80,1792]{1,0:T(8,128)(2,1)S(1)}, bf16[80,1792]{1,0:T(8,128)(2,1)S(1)}, u32[]{:S(2)}, u32[]{:S(2)}) collective-permute-start(bf16[80,1792]{1,0:T(8,128)(2,1)S(1)} %get-tuple-element.46), channel_id=1, source_target_pairs={{0,2},{2,0},{4,6},{6,4},{1,3},{3,1},{5,7},{7,5},{8,10},{10,8},{12,... | collective-permute-start | bytes 860168 | tf_op jit(solution)/shard_map/ppermute | solution.py:20
  16.1 2.0 %collective-permute-start.2 = (bf16[80,1792]{1,0:T(8,128)(2,1)S(1)}, bf16[80,1792]{1,0:T(8,128)(2,1)S(1)}, u32[]{:S(2)}, u32[]{:S(2)}) collective-permute-start(bf16[80,1792]{1,0:T(8,128)(2,1)S(1)} %get-tuple-element.36), channel_id=1, source_target_pairs={{0,2},{2,0},{4,6},{6,4},{1,3},{3,1},{5,7},{7,5},{8,10},{10,8},{12,... | collective-permute-start | bytes 860168 | tf_op jit(solution)/shard_map/ppermute | solution.py:20
  19.7 5.1 %collective-permute-done.13.refs_2_ = bf16[80,1792]{1,0:T(8,128)(2,1)S(1)} collective-permute-done((bf16[80,1792]{1,0:T(8,128)(2,1)S(1)}, bf16[80,1792]{1,0:T(8,128)(2,1)S(1)}, u32[]{:S(2)}, u32[]{:S(2)}) %collective-permute-start.13) | collective-permute-done | bytes 286752 | tf_op jit(solution)/shard_map/ppermute | solution.py:20
  26.4 2.1 %copy-done = bf16[1,1,1792,1024]{3,2,1,0:T(8,128)(2,1)S(1)} copy-done((bf16[1,1,1792,1024]{3,2,1,0:T(8,128)(2,1)S(1)}, bf16[1,1,1792,1024]{3,2,1,0:T(8,128)(2,1)}, u32[]{:S(2)}) %copy-start) | copy-done | bytes 3670040
  28.5 2.0 %copy-done.2 = bf16[1,1,1792,1024]{3,2,1,0:T(8,128)(2,1)S(1)} copy-done((bf16[1,1,1792,1024]{3,2,1,0:T(8,128)(2,1)S(1)}, bf16[1,1,1792,1024]{3,2,1,0:T(8,128)(2,1)}, u32[]{:S(2)}) %copy-start.2) | copy-done | bytes 3670040
  30.5 4.2 %shard_map.142.own_ref = bf16[2,320,1024]{2,1,0:T(8,128)(2,1)S(1)} custom-call(bf16[80,1792]{1,0:T(8,128)(2,1)S(1)} %get-tuple-element.45.refs_0_, bf16[80,1792]{1,0:T(8,128)(2,1)S(1)} %collective-permute-done.12.refs_1_, bf16[80,1792]{1,0:T(8,128)(2,1)S(1)} %collective-permute-done.13.refs_2_, bf16[80,1792]{1,0:T(8,128)(2,1)S(1)} %collective-permute-done.14.refs_3_, ...), custom_call_target="tpu_custom_call" | custom-call | flops 2348810240 | bytes 9797632 | tf_op jit(solution)/shard_map/pallas_call | solution.py:203
  36.1 2.4 %collective-permute-start.17 = (bf16[80,1792]{1,0:T(8,128)(2,1)S(1)}, bf16[80,1792]{1,0:T(8,128)(2,1)S(1)}, u32[]{:S(2)}, u32[]{:S(2)}) collective-permute-start(bf16[80,1792]{1,0:T(8,128)(2,1)S(1)} %get-tuple-element.50), channel_id=1, source_target_pairs={{0,2},{2,0},{4,6},{6,4},{1,3},{3,1},{5,7},{7,5},{8,10},{10,8},{12,... | collective-permute-start | bytes 860168 | tf_op jit(solution)/shard_map/ppermute | solution.py:20
  40.0 4.2 %shard_map.138.own_ref = bf16[2,320,1024]{2,1,0:T(8,128)(2,1)S(1)} custom-call(bf16[80,1792]{1,0:T(8,128)(2,1)S(1)} %get-tuple-element.35.refs_0_, bf16[80,1792]{1,0:T(8,128)(2,1)S(1)} %collective-permute-done.2.refs_1_, bf16[80,1792]{1,0:T(8,128)(2,1)S(1)} %collective-permute-done.3.refs_2_, bf16[80,1792]{1,0:T(8,128)(2,1)S(1)} %collective-permute-done.4.refs_3_, ...), custom_call_target="tpu_custom_call" | custom-call | flops 2348810240 | bytes 9797632 | tf_op jit(solution)/shard_map/pallas_call | solution.py:203
  44.4 1.8 %collective-permute-done.17.refs_1_.refs_5_ = bf16[80,1792]{1,0:T(8,128)(2,1)S(1)} collective-permute-done((bf16[80,1792]{1,0:T(8,128)(2,1)S(1)}, bf16[80,1792]{1,0:T(8,128)(2,1)S(1)}, u32[]{:S(2)}, u32[]{:S(2)}) %collective-permute-start.17) | collective-permute-done | bytes 286752 | tf_op jit(solution)/shard_map/ppermute | solution.py:20
  46.2 7.4 %collective-permute-done.18.refs_2_.refs_6_ = bf16[80,1792]{1,0:T(8,128)(2,1)S(1)} collective-permute-done((bf16[80,1792]{1,0:T(8,128)(2,1)S(1)}, bf16[80,1792]{1,0:T(8,128)(2,1)S(1)}, u32[]{:S(2)}, u32[]{:S(2)}) %collective-permute-start.18) | collective-permute-done | bytes 286752 | tf_op jit(solution)/shard_map/ppermute | solution.py:20
  53.6 2.2 %shard_map.144.own_d = bf16[320,1024]{1,0:T(8,128)(2,1)S(1)} custom-call(bf16[80,1792]{1,0:T(8,128)(2,1)S(1)} %get-tuple-element.49.refs_0_.refs_4_, bf16[80,1792]{1,0:T(8,128)(2,1)S(1)} %collective-permute-done.17.refs_1_.refs_5_, bf16[80,1792]{1,0:T(8,128)(2,1)S(1)} %collective-permute-done.18.refs_2_.refs_6_, ...), custom_call_target="tpu_custom_call" | custom-call | flops 1174405120 | bytes 5472256 | tf_op jit(solution)/shard_map/pallas_call | solution.py:228
  57.2 2.1 %collective-permute-done.20.other_d = bf16[320,1024]{1,0:T(8,128)(2,1)S(1)} collective-permute-done((bf16[320,1024]{1,0:T(8,128)(2,1)S(1)}, bf16[320,1024]{1,0:T(8,128)(2,1)S(1)}, u32[]{:S(2)}, u32[]{:S(2)}) %collective-permute-start.20) | collective-permute-done | bytes 655392 | tf_op jit(solution)/shard_map/ppermute | solution.py:20
  59.3 5.8 %shard_map.145 = (bf16[320,1024]{1,0:T(8,128)(2,1)S(1)}, bf16[320,1024]{1,0:T(8,128)(2,1)S(1)}, bf16[320,1024]{1,0:T(8,128)(2,1)S(1)}, bf16[80,1792]{1,0:T(8,128...) custom-call(bf16[2,320,1024]{2,1,0:T(8,128)(2,1)S(1)} %shard_map.142.own_ref, ...), custom_call_target="tpu_custom_call" | custom-call | flops 2348810240 | bytes 14385152 | tf_op jit(solution)/shard_map/pallas_call | solution.py:299
  70.0 1.8 %collective-permute-start.23 = (bf16[80,1792]{1,0:T(8,128)(2,1)}, bf16[80,1792]{1,0:T(8,128)(2,1)}, u32[]{:S(2)}, u32[]{:S(2)}) collective-permute-start(bf16[80,1792]{1,0:T(8,128)(2,1)} %get-tuple-element.56), channel_id=1, source_target_pairs={{0,6},{2,4},{4,2},{6,0},{1,7},{3,5},{5,3},{7,1},{8,14},{10,12},{12... | collective-permute-start | bytes 860168 | tf_op jit(solution)/shard_map/ppermute | solution.py:20
  71.8 2.0 %copy-done.5 = bf16[1,1,1024,1792]{3,2,1,0:T(8,128)(2,1)S(1)} copy-done((bf16[1,1,1024,1792]{3,2,1,0:T(8,128)(2,1)S(1)}, bf16[1,1,1024,1792]{3,2,1,0:T(8,128)(2,1)}, u32[]{:S(2)}) %copy-start.5) | copy-done | bytes 3670040
  73.9 3.3 %shard_map.139 = (bf16[80,1792]{1,0:T(8,128)(2,1)S(1)}, bf16[80,1792]{1,0:T(8,128)(2,1)S(1)}, bf16[80,1792]{1,0:T(8,128)(2,1)S(1)}, bf16[80,1792]{1,0:T(8,128)(2,1)S(1)}) custom-call(bf16[2,320,1024]{2,1,0:T(8,128)(2,1)S(1)} %shard_map.138.own_ref, bf16[2,320,1024]{2,1,0:T(8,128)(2,1)S(1)} %collective-permute-done.5.other_ref, bf16[1024,1792]{1,0:T(8,128)(2,1)S(1)} %bitcast.42), custom_call_target="tpu_custom_call" | custom-call | flops 1174405120 | bytes 7438336 | tf_op jit(solution)/shard_map/pallas_call | solution.py:263
  79.0 1.8 %collective-permute-start.8 = (bf16[80,1792]{1,0:T(8,128)(2,1)S(1)}, bf16[80,1792]{1,0:T(8,128)(2,1)S(1)}, u32[]{:S(2)}, u32[]{:S(2)}) collective-permute-start(bf16[80,1792]{1,0:T(8,128)(2,1)S(1)} %get-tuple-element.42), channel_id=1, source_target_pairs={{0,6},{2,4},{4,2},{6,0},{1,7},{3,5},{5,3},{7,1},{8,14},{10,12},{12... | collective-permute-start | bytes 860168 | tf_op jit(solution)/shard_map/ppermute | solution.py:20
  80.8 2.8 %collective-permute-done.22.refs_2_ = bf16[80,1792]{1,0:T(8,128)(2,1)} collective-permute-done((bf16[80,1792]{1,0:T(8,128)(2,1)}, bf16[80,1792]{1,0:T(8,128)(2,1)}, u32[]{:S(2)}, u32[]{:S(2)}) %collective-permute-start.22) | collective-permute-done | bytes 286752 | tf_op jit(solution)/shard_map/ppermute | solution.py:20
  84.2 1.9 %shard_map.146 = (bf16[64,1792]{1,0:T(8,128)(2,1)S(1)}, bf16[64,1792]{1,0:T(8,128)(2,1)S(1)}) custom-call(s32[2]{0:T(128)S(1)} %pad_add_fusion.place_ref, f32[4,128]{1,0:T(4,128)S(1)} %get-tuple-element.69.meta_ref, bf16[80,1792]{1,0:T(8,128)(2,1)S(1)} %copy-done.12, bf16[80,1792]{1,0:T(8,128)(2,1)} %collective-permute-done.21.refs_1_, ...), custom_call_target="tpu_custom_call" | custom-call | flops 293601280 | bytes 1605632 | tf_op jit(solution)/shard_map/pallas_call | solution.py:170
  86.2 1.6 %collective-permute-start.24 = (bf16[64,1792]{1,0:T(8,128)(2,1)S(1)}, bf16[64,1792]{1,0:T(8,128)(2,1)S(1)}, u32[]{:S(2)}, u32[]{:S(2)}) collective-permute-start(bf16[64,1792]{1,0:T(8,128)(2,1)S(1)} %get-tuple-element.57), channel_id=1, source_target_pairs={{0,8},{1,9},{8,16},{9,17},{16,24},{17,25},{24,0},{25,1},{2,10},{3,... | collective-permute-start | bytes 688136 | tf_op jit(solution)/shard_map/ppermute | solution.py:30
  87.9 8.5 %shard_map.147 = (bf16[1792,1024]{1,0:T(8,128)(2,1)}, bf16[1792,1024]{1,0:T(8,128)(2,1)}, bf16[1024,1792]{1,0:T(8,128)(2,1)}) custom-call(bf16[320,1024]{1,0:T(8,128)(2,1)S(1)} %copy-done.22, bf16[320,1024]{1,0:T(8,128)(2,1)S(1)} %copy-done.24, bf16[320,1024]{1,0:T(8,128)(2,1)S(1)} %copy-done.26, bf16[80,1792]{1,0:T(8,128)(2,1)S(1)} %get-tuple-element.45.refs_0_, ...), custom_call_target="tpu_custom_call" | custom-call | flops 3523215360 | bytes 15269888 | tf_op jit(solution)/shard_map/pallas_call | solution.py:326
  96.4 1.8 %shard_map.140 = (bf16[64,1792]{1,0:T(8,128)(2,1)S(1)}, bf16[64,1792]{1,0:T(8,128)(2,1)S(1)}) custom-call(s32[2]{0:T(128)S(1)} %pad_add_fusion.place_ref, f32[4,128]{1,0:T(4,128)S(1)} %get-tuple-element.70.meta_ref, bf16[80,1792]{1,0:T(8,128)(2,1)S(1)} %get-tuple-element.39.refs_0_, bf16[80,1792]{1,0:T(8,128)(2,1)S(1)} %collective-permute-done.6.refs_1_, ...), custom_call_target="tpu_custom_call" | custom-call | flops 293601280 | bytes 1605632 | tf_op jit(solution)/shard_map/pallas_call | solution.py:170
  102.1 5.8 %collective-permute-done.9 = bf16[64,1792]{1,0:T(8,128)(2,1)S(1)} collective-permute-done((bf16[64,1792]{1,0:T(8,128)(2,1)S(1)}, bf16[64,1792]{1,0:T(8,128)(2,1)S(1)}, u32[]{:S(2)}, u32[]{:S(2)}) %collective-permute-start.9) | collective-permute-done | bytes 229408 | tf_op jit(solution)/shard_map/ppermute | solution.py:30
  107.9 5.6 %collective-permute-done.10 = bf16[64,1792]{1,0:T(8,128)(2,1)S(1)} collective-permute-done((bf16[64,1792]{1,0:T(8,128)(2,1)S(1)}, bf16[64,1792]{1,0:T(8,128)(2,1)S(1)}, u32[]{:S(2)}, u32[]{:S(2)}) %collective-permute-start.10) | collective-permute-done | bytes 229408 | tf_op jit(solution)/shard_map/ppermute | solution.py:30
  (105 shorter events, 32.2 us)
Async XLA Ops:
  2.0 1.7 %collective-permute-start = (f32[8,64]{1,0:T(8,128)S(1)}, f32[8,64]{1,0:T(8,128)S(1)}, u32[]{:S(2)}, u32[]{:S(2)}) collective-permute-start(f32[8,64]{1,0:T(8,128)S(1)} %pad_maximum_fusion), channel_id=1, source_target_pairs={{0,1},{1,0},{2,3},{3,2},{4,5},{5,4},{6,7},{7,6},{8,9},{9,8},{10,11... | collective-permute-start | bytes 6152 | tf_op jit(solution)/shard_map/ppermute | solution.py:20
  7.2 11.0 %collective-permute-start.12 = (bf16[80,1792]{1,0:T(8,128)(2,1)S(1)}, bf16[80,1792]{1,0:T(8,128)(2,1)S(1)}, u32[]{:S(2)}, u32[]{:S(2)}) collective-permute-start(bf16[80,1792]{1,0:T(8,128)(2,1)S(1)} %get-tuple-element.46), channel_id=1, source_target_pairs={{0,2},{2,0},{4,6},{6,4},{1,3},{3,1},{5,7},{7,5},{8,10},{10,8},{12,... | collective-permute-start | bytes 860168 | tf_op jit(solution)/shard_map/ppermute | solution.py:20
  9.9 14.9 %collective-permute-start.13 = (bf16[80,1792]{1,0:T(8,128)(2,1)S(1)}, bf16[80,1792]{1,0:T(8,128)(2,1)S(1)}, u32[]{:S(2)}, u32[]{:S(2)}) collective-permute-start(bf16[80,1792]{1,0:T(8,128)(2,1)S(1)} %get-tuple-element.47), channel_id=1, source_target_pairs={{0,4},{2,6},{4,0},{6,2},{1,5},{3,7},{5,1},{7,3},{8,12},{10,14},{12... | collective-permute-start | bytes 860168 | tf_op jit(solution)/shard_map/ppermute | solution.py:20
  11.4 14.9 %collective-permute-start.14 = (bf16[80,1792]{1,0:T(8,128)(2,1)S(1)}, bf16[80,1792]{1,0:T(8,128)(2,1)S(1)}, u32[]{:S(2)}, u32[]{:S(2)}) collective-permute-start(bf16[80,1792]{1,0:T(8,128)(2,1)S(1)} %get-tuple-element.48), channel_id=1, source_target_pairs={{0,6},{2,4},{4,2},{6,0},{1,7},{3,5},{5,3},{7,1},{8,14},{10,12},{12... | collective-permute-start | bytes 860168 | tf_op jit(solution)/shard_map/ppermute | solution.py:20
  13.4 21.4 %collective-permute-start.16 = (bf16[64,1792]{1,0:T(8,128)(2,1)S(1)}, bf16[64,1792]{1,0:T(8,128)(2,1)S(1)}, u32[]{:S(2)}, u32[]{:S(2)}) collective-permute-start(bf16[64,1792]{1,0:T(8,128)(2,1)S(1)} %dynamic-slice_bitcast_fusion), channel_id=1, source_target_pairs={{0,1},{1,0},{2,3},{3,2},{4,5},{5,4},{6,7},{7,6},{8,9},{9,8},{10,11... | collective-permute-start | bytes 688136 | tf_op jit(solution)/shard_map/ppermute | solution.py:20
  16.1 22.3 %collective-permute-start.2 = (bf16[80,1792]{1,0:T(8,128)(2,1)S(1)}, bf16[80,1792]{1,0:T(8,128)(2,1)S(1)}, u32[]{:S(2)}, u32[]{:S(2)}) collective-permute-start(bf16[80,1792]{1,0:T(8,128)(2,1)S(1)} %get-tuple-element.36), channel_id=1, source_target_pairs={{0,2},{2,0},{4,6},{6,4},{1,3},{3,1},{5,7},{7,5},{8,10},{10,8},{12,... | collective-permute-start | bytes 860168 | tf_op jit(solution)/shard_map/ppermute | solution.py:20
  18.2 20.3 %collective-permute-start.3 = (bf16[80,1792]{1,0:T(8,128)(2,1)S(1)}, bf16[80,1792]{1,0:T(8,128)(2,1)S(1)}, u32[]{:S(2)}, u32[]{:S(2)}) collective-permute-start(bf16[80,1792]{1,0:T(8,128)(2,1)S(1)} %get-tuple-element.37), channel_id=1, source_target_pairs={{0,4},{2,6},{4,0},{6,2},{1,5},{3,7},{5,1},{7,3},{8,12},{10,14},{12... | collective-permute-start | bytes 860168 | tf_op jit(solution)/shard_map/ppermute | solution.py:20
  24.8 15.3 %collective-permute-start.4 = (bf16[80,1792]{1,0:T(8,128)(2,1)S(1)}, bf16[80,1792]{1,0:T(8,128)(2,1)S(1)}, u32[]{:S(2)}, u32[]{:S(2)}) collective-permute-start(bf16[80,1792]{1,0:T(8,128)(2,1)S(1)} %get-tuple-element.38), channel_id=1, source_target_pairs={{0,6},{2,4},{4,2},{6,0},{1,7},{3,5},{5,3},{7,1},{8,14},{10,12},{12... | collective-permute-start | bytes 860168 | tf_op jit(solution)/shard_map/ppermute | solution.py:20
  34.8 24.5 %collective-permute-start.15 = (bf16[2,320,1024]{2,1,0:T(8,128)(2,1)S(1)}, bf16[2,320,1024]{2,1,0:T(8,128)(2,1)S(1)}, u32[]{:S(2)}, u32[]{:S(2)}) collective-permute-start(bf16[2,320,1024]{2,1,0:T(8,128)(2,1)S(1)} %shard_map.142.own_ref), channel_id=1, source_target_pairs={{0,1},{1,0},{2,3},{3,2},{4,5},{5,4},{6,7},{7,6},{8,9},{9,8},{10,11... | collective-permute-start | bytes 3932168 | tf_op jit(solution)/shard_map/ppermute | solution.py:20
  36.1 10.1 %collective-permute-start.17 = (bf16[80,1792]{1,0:T(8,128)(2,1)S(1)}, bf16[80,1792]{1,0:T(8,128)(2,1)S(1)}, u32[]{:S(2)}, u32[]{:S(2)}) collective-permute-start(bf16[80,1792]{1,0:T(8,128)(2,1)S(1)} %get-tuple-element.50), channel_id=1, source_target_pairs={{0,2},{2,0},{4,6},{6,4},{1,3},{3,1},{5,7},{7,5},{8,10},{10,8},{12,... | collective-permute-start | bytes 860168 | tf_op jit(solution)/shard_map/ppermute | solution.py:20
  38.5 15.1 %collective-permute-start.18 = (bf16[80,1792]{1,0:T(8,128)(2,1)S(1)}, bf16[80,1792]{1,0:T(8,128)(2,1)S(1)}, u32[]{:S(2)}, u32[]{:S(2)}) collective-permute-start(bf16[80,1792]{1,0:T(8,128)(2,1)S(1)} %get-tuple-element.51), channel_id=1, source_target_pairs={{0,4},{2,6},{4,0},{6,2},{1,5},{3,7},{5,1},{7,3},{8,12},{10,14},{12... | collective-permute-start | bytes 860168 | tf_op jit(solution)/shard_map/ppermute | solution.py:20
  38.5 15.1 %collective-permute-start.19 = (bf16[80,1792]{1,0:T(8,128)(2,1)S(1)}, bf16[80,1792]{1,0:T(8,128)(2,1)S(1)}, u32[]{:S(2)}, u32[]{:S(2)}) collective-permute-start(bf16[80,1792]{1,0:T(8,128)(2,1)S(1)} %get-tuple-element.52), channel_id=1, source_target_pairs={{0,6},{2,4},{4,2},{6,0},{1,7},{3,5},{5,3},{7,1},{8,14},{10,12},{12... | collective-permute-start | bytes 860168 | tf_op jit(solution)/shard_map/ppermute | solution.py:20
  44.3 27.5 %collective-permute-start.5 = (bf16[2,320,1024]{2,1,0:T(8,128)(2,1)S(1)}, bf16[2,320,1024]{2,1,0:T(8,128)(2,1)S(1)}, u32[]{:S(2)}, u32[]{:S(2)}) collective-permute-start(bf16[2,320,1024]{2,1,0:T(8,128)(2,1)S(1)} %shard_map.138.own_ref), channel_id=1, source_target_pairs={{0,1},{1,0},{2,3},{3,2},{4,5},{5,4},{6,7},{7,6},{8,9},{9,8},{10,11... | collective-permute-start | bytes 3932168 | tf_op jit(solution)/shard_map/ppermute | solution.py:20
  57.2 2.1 %collective-permute-start.20 = (bf16[320,1024]{1,0:T(8,128)(2,1)S(1)}, bf16[320,1024]{1,0:T(8,128)(2,1)S(1)}, u32[]{:S(2)}, u32[]{:S(2)}) collective-permute-start(bf16[320,1024]{1,0:T(8,128)(2,1)S(1)} %shard_map.144.own_d), channel_id=1, source_target_pairs={{0,1},{1,0},{2,3},{3,2},{4,5},{5,4},{6,7},{7,6},{8,9},{9,8},{10,11... | collective-permute-start | bytes 1966088 | tf_op jit(solution)/shard_map/ppermute | solution.py:20
  68.3 10.7 %collective-permute-start.21 = (bf16[80,1792]{1,0:T(8,128)(2,1)}, bf16[80,1792]{1,0:T(8,128)(2,1)}, u32[]{:S(2)}, u32[]{:S(2)}) collective-permute-start(bf16[80,1792]{1,0:T(8,128)(2,1)} %get-tuple-element.54), channel_id=1, source_target_pairs={{0,2},{2,0},{4,6},{6,4},{1,3},{3,1},{5,7},{7,5},{8,10},{10,8},{12,... | collective-permute-start | bytes 860168 | tf_op jit(solution)/shard_map/ppermute | solution.py:20
  68.7 14.9 %collective-permute-start.22 = (bf16[80,1792]{1,0:T(8,128)(2,1)}, bf16[80,1792]{1,0:T(8,128)(2,1)}, u32[]{:S(2)}, u32[]{:S(2)}) collective-permute-start(bf16[80,1792]{1,0:T(8,128)(2,1)} %get-tuple-element.55), channel_id=1, source_target_pairs={{0,4},{2,6},{4,0},{6,2},{1,5},{3,7},{5,1},{7,3},{8,12},{10,14},{12... | collective-permute-start | bytes 860168 | tf_op jit(solution)/shard_map/ppermute | solution.py:20
  70.0 14.2 %collective-permute-start.23 = (bf16[80,1792]{1,0:T(8,128)(2,1)}, bf16[80,1792]{1,0:T(8,128)(2,1)}, u32[]{:S(2)}, u32[]{:S(2)}) collective-permute-start(bf16[80,1792]{1,0:T(8,128)(2,1)} %get-tuple-element.56), channel_id=1, source_target_pairs={{0,6},{2,4},{4,2},{6,0},{1,7},{3,5},{5,3},{7,1},{8,14},{10,12},{12... | collective-permute-start | bytes 860168 | tf_op jit(solution)/shard_map/ppermute | solution.py:20
  77.2 19.2 %collective-permute-start.6 = (bf16[80,1792]{1,0:T(8,128)(2,1)S(1)}, bf16[80,1792]{1,0:T(8,128)(2,1)S(1)}, u32[]{:S(2)}, u32[]{:S(2)}) collective-permute-start(bf16[80,1792]{1,0:T(8,128)(2,1)S(1)} %get-tuple-element.40), channel_id=1, source_target_pairs={{0,2},{2,0},{4,6},{6,4},{1,3},{3,1},{5,7},{7,5},{8,10},{10,8},{12,... | collective-permute-start | bytes 860168 | tf_op jit(solution)/shard_map/ppermute | solution.py:20
  77.6 18.8 %collective-permute-start.7 = (bf16[80,1792]{1,0:T(8,128)(2,1)S(1)}, bf16[80,1792]{1,0:T(8,128)(2,1)S(1)}, u32[]{:S(2)}, u32[]{:S(2)}) collective-permute-start(bf16[80,1792]{1,0:T(8,128)(2,1)S(1)} %get-tuple-element.41), channel_id=1, source_target_pairs={{0,4},{2,6},{4,0},{6,2},{1,5},{3,7},{5,1},{7,3},{8,12},{10,14},{12... | collective-permute-start | bytes 860168 | tf_op jit(solution)/shard_map/ppermute | solution.py:20
  79.0 17.4 %collective-permute-start.8 = (bf16[80,1792]{1,0:T(8,128)(2,1)S(1)}, bf16[80,1792]{1,0:T(8,128)(2,1)S(1)}, u32[]{:S(2)}, u32[]{:S(2)}) collective-permute-start(bf16[80,1792]{1,0:T(8,128)(2,1)S(1)} %get-tuple-element.42), channel_id=1, source_target_pairs={{0,6},{2,4},{4,2},{6,0},{1,7},{3,5},{5,3},{7,1},{8,14},{10,12},{12... | collective-permute-start | bytes 860168 | tf_op jit(solution)/shard_map/ppermute | solution.py:20
  86.2 15.0 %collective-permute-start.24 = (bf16[64,1792]{1,0:T(8,128)(2,1)S(1)}, bf16[64,1792]{1,0:T(8,128)(2,1)S(1)}, u32[]{:S(2)}, u32[]{:S(2)}) collective-permute-start(bf16[64,1792]{1,0:T(8,128)(2,1)S(1)} %get-tuple-element.57), channel_id=1, source_target_pairs={{0,8},{1,9},{8,16},{9,17},{16,24},{17,25},{24,0},{25,1},{2,10},{3,... | collective-permute-start | bytes 688136 | tf_op jit(solution)/shard_map/ppermute | solution.py:30
  87.8 13.4 %collective-permute-start.25 = (bf16[64,1792]{1,0:T(8,128)(2,1)S(1)}, bf16[64,1792]{1,0:T(8,128)(2,1)S(1)}, u32[]{:S(2)}, u32[]{:S(2)}) collective-permute-start(bf16[64,1792]{1,0:T(8,128)(2,1)S(1)} %get-tuple-element.58), channel_id=1, source_target_pairs={{0,9},{1,8},{8,17},{9,16},{16,25},{17,24},{24,1},{25,0},{2,11},{3,... | collective-permute-start | bytes 688136 | tf_op jit(solution)/shard_map/ppermute | solution.py:30
  98.2 9.7 %collective-permute-start.9 = (bf16[64,1792]{1,0:T(8,128)(2,1)S(1)}, bf16[64,1792]{1,0:T(8,128)(2,1)S(1)}, u32[]{:S(2)}, u32[]{:S(2)}) collective-permute-start(bf16[64,1792]{1,0:T(8,128)(2,1)S(1)} %get-tuple-element.43), channel_id=1, source_target_pairs={{0,8},{1,9},{8,16},{9,17},{16,24},{17,25},{24,0},{25,1},{2,10},{3,... | collective-permute-start | bytes 688136 | tf_op jit(solution)/shard_map/ppermute | solution.py:30
  99.9 13.6 %collective-permute-start.10 = (bf16[64,1792]{1,0:T(8,128)(2,1)S(1)}, bf16[64,1792]{1,0:T(8,128)(2,1)S(1)}, u32[]{:S(2)}, u32[]{:S(2)}) collective-permute-start(bf16[64,1792]{1,0:T(8,128)(2,1)S(1)} %get-tuple-element.44), channel_id=1, source_target_pairs={{0,9},{1,8},{8,17},{9,16},{16,25},{17,24},{24,1},{25,0},{2,11},{3,... | collective-permute-start | bytes 688136 | tf_op jit(solution)/shard_map/ppermute | solution.py:30
  (29 other events, 225.5 us)

commit v2 on v1

v2 whole, which is shorter than its diff:
```python
import functools

import jax
import jax.numpy as jnp
from jax import lax
from jax.experimental import pallas as pl
from jax.experimental.pallas import tpu as pltpu
from jax.sharding import PartitionSpec as P

FF = 1024
TOP = 2
TILE = 256
VMEM_LIMIT = 20 * 1024 * 1024
META = 16
COST_SHARE = 1024
F32 = jnp.float32
BF16 = jnp.bfloat16


def exchange(value, axis, mask):
    count = lax.axis_size(axis)
    return lax.ppermute(value, axis, [(source, source ^ mask) for source in range(count)])


def section_shift(value, flip):
    sections, cores = lax.axis_size("section"), lax.axis_size("dp")
    pairs = []
    for section in range(sections):
        for core in range(cores):
            target = ((section + 1) % sections) * cores + (core ^ flip)
            pairs.append((section * cores + core, target))
    return lax.ppermute(value, ("section", "dp"), pairs)


def dot(left, right, left_dim, right_dim):
    return lax.dot_general(
        left, right, (((left_dim,), (right_dim,)), ((), ())), preferred_element_type=F32
    )


VMEM = pl.BlockSpec(memory_space=pltpu.VMEM)
HBM = pl.BlockSpec(memory_space=pltpu.HBM)
AFTER = pl.BlockSpec(memory_space=pl.ANY)


def call(kernel, out_shape, in_specs, out_specs, scratch, flops, moved, grid=()):
    return pl.pallas_call(
        kernel,
        out_shape=out_shape,
        grid=grid,
        in_specs=in_specs,
        out_specs=out_specs,
        scratch_shapes=scratch,
        compiler_params=pltpu.CompilerParams(vmem_limit_bytes=VMEM_LIMIT),
        cost_estimate=pl.CostEstimate(
            flops=flops // COST_SHARE, bytes_accessed=moved // COST_SHARE, transcendentals=0
        ),
    )


def array(*shape):
    return jax.ShapeDtypeStruct(shape, BF16)


def in_hbm(value):
    return pltpu.with_memory_space_constraint(value, pltpu.HBM)


def halves(value_ref, own_ref, other_ref, sems, first):
    tokens, width = value_ref.shape[0], value_ref.shape[1] // 2
    core = lax.axis_index("dp")
    copies = []
    for place, (half, target) in enumerate(((core, own_ref), (1 - core, other_ref))):
        columns = pl.ds(pl.multiple_of(half * width, 128), width)
        copies.append(
            pltpu.make_async_copy(
                value_ref.at[:, columns], target.at[0:tokens], sems.at[first + place]
            )
        )
    for copy in copies:
        copy.start()
    return copies


def pack_kernel(x_ref, *refs):
    sources, (own_ref, other_ref, packed, sems), held = refs[:4], refs[4:8], refs[8:]
    copies = halves(x_ref, own_ref, other_ref, sems, 0)
    tokens = x_ref.shape[0]
    small = [
        pltpu.make_async_copy(source, target, sems.at[2 + place])
        for place, (source, target) in enumerate(zip(sources, held))
    ]
    for copy in small:
        copy.start()
    packed[...] = jnp.zeros_like(packed)
    for copy in small:
        copy.wait()
    ids_b, route_b, ids_f, route_f = held
    for start, ids, route in ((0, ids_b, route_b), (META // 2, ids_f, route_f)):
        packed[start : start + 2, 0:tokens] = ids[...].astype(F32)
        rest = route[...]
        for piece in range(3):
            top = rest.astype(BF16).astype(F32)
            row = start + 2 + 2 * piece
            packed[row : row + 2, 0:tokens] = top
            rest = rest - top
    mine = packed[...]
    lanes = packed.shape[1]
    own_ref[tokens : tokens + META, 0:lanes] = mine.astype(BF16)
    other_ref[tokens : tokens + META, 0:lanes] = pltpu.roll(mine, tokens, 1).astype(BF16)
    for copy in copies:
        copy.wait()


def pack(x, ids_b, route_b, ids_f, route_f):
    tokens, width = x.shape[0], x.shape[1] // 2
    out = array(tokens + META, width)
    return call(
        pack_kernel,
        [out, out],
        [HBM] * 5,
        [VMEM, VMEM],
        [pltpu.VMEM((META, 2 * tokens), F32), pltpu.SemaphoreType.DMA((6,))]
        + [pltpu.VMEM(value.shape, value.dtype) for value in (ids_b, route_b, ids_f, route_f)],
        0,
        8 * x.size,
    )(x, ids_b, route_b, ids_f, route_f)


def cut_kernel(x_ref, dy_ref, own_x, other_x, own_dy, other_dy, sems):
    copies = halves(x_ref, own_x, other_x, sems, 0)
    copies += halves(dy_ref, own_dy, other_dy, sems, 2)
    for copy in copies:
        copy.wait()


def cut(x, dy):
    tokens, width = x.shape[0], x.shape[1] // 2
    return call(
        cut_kernel,
        [array(tokens, width)] * 4,
        [HBM, HBM],
        [VMEM] * 4,
        [pltpu.SemaphoreType.DMA((4,))],
        0,
        16 * x.size,
    )(x, dy)


class Plan:
    def __init__(self, blocks, rows, group, capacity, tokens, relative):
        self.blocks, self.rows, self.group = blocks, rows, group
        self.capacity, self.tokens, self.relative = capacity, tokens, relative


def slot_rows(own_meta, other_meta, plan, first_row):
    lanes = 2 * plan.tokens
    padded = max(8, plan.blocks)
    me = lax.axis_index("expert") if plan.relative else 0
    core = lax.axis_index("dp")
    meta = own_meta[plan.tokens : plan.tokens + META, 0:lanes].astype(F32)
    meta = meta + other_meta[plan.tokens : plan.tokens + META, 0:lanes].astype(F32)
    meta = meta[first_row : first_row + META // 2]
    first, second = meta[0:1], meta[1:2]
    route = meta[2:4] + meta[4:6] + meta[6:8]
    row = lax.broadcasted_iota(jnp.int32, (padded, lanes), 0)
    expert = ((row ^ me) // plan.group).astype(F32)
    is_first, is_second = expert == first, expert == second
    named = jnp.where(is_first | is_second, 1.0, 0.0)
    before = lax.broadcasted_iota(jnp.int32, (lanes, lanes), 0)
    after = lax.broadcasted_iota(jnp.int32, (lanes, lanes), 1)
    earlier = (before < after) & ((before < plan.tokens) == (after < plan.tokens))
    position = dot(named.astype(BF16), jnp.where(earlier, 1.0, 0.0).astype(BF16), 1, 0)
    lane = lax.broadcasted_iota(jnp.int32, (padded, lanes), 1)
    half = jnp.where(lane < plan.tokens, core, 1 - core).astype(F32)
    slot = jnp.where(named > 0.5, position + half * plan.capacity, -1.0)
    return slot, jnp.where(is_first, route[0:1], route[1:2])


def slot_table(slot, block, rows):
    index = lax.broadcasted_iota(jnp.int32, (rows, slot.shape[1]), 0).astype(F32)
    return jnp.where(index == slot[block : block + 1, :], 1.0, 0.0)


def dispatch_kernel(own_meta, other_meta, own_ref, other_ref, *refs, plan, first_row, weighted):
    outs = refs[-plan.blocks :]
    width, tokens = outs[0].shape[1], plan.tokens
    slot, route = slot_rows(own_meta, other_meta, plan, first_row)
    values = jnp.concatenate([own_ref[0:tokens, :], other_ref[0:tokens, :]], axis=0)
    for block in range(plan.blocks):
        table = slot_table(slot, block, plan.rows)
        if weighted:
            scale = jnp.sum(table * route[block : block + 1, :], axis=1, keepdims=True)
        table = table.astype(BF16)
        for start in range(0, width, TILE):
            picked = dot(table, values[:, start : start + TILE], 1, 0)
            if weighted:
                picked = picked * scale
            outs[block][:, start : start + TILE] = picked.astype(BF16)


def dispatch(metas, own, other, plan, first_row, weighted, after=()):
    width = own.shape[1]
    return call(
        functools.partial(
            dispatch_kernel, plan=plan, first_row=first_row, weighted=weighted
        ),
        [array(plan.rows, width)] * plan.blocks,
        [VMEM] * 4 + [AFTER] * len(after),
        [VMEM] * plan.blocks,
        [],
        4 * plan.blocks * plan.rows * plan.tokens * width,
        2 * width * (3 * plan.tokens + plan.blocks * plan.rows),
    )(*metas, own, other, *after)


def combine_kernel(own_meta, other_meta, *refs, plan, first_row, weighted):
    returned = refs[: plan.blocks]
    own_ref, other_ref = refs[-2:]
    width, tokens = returned[0].shape[1], plan.tokens
    slot, route = slot_rows(own_meta, other_meta, plan, first_row)
    high, low = [], []
    for block in range(plan.blocks):
        table = slot_table(slot, block, plan.rows)
        if weighted:
            table = table * route[block : block + 1, :]
        top = table.astype(BF16)
        high.append(top)
        low.append((table - top.astype(F32)).astype(BF16))
    high = jnp.concatenate(high, axis=0)
    low = jnp.concatenate(low, axis=0)
    for start in range(0, width, TILE):
        values = jnp.concatenate([ref[:, start : start + TILE] for ref in returned], axis=0)
        total = dot(high, values, 0, 0)
        if weighted:
            total += dot(low, values, 0, 0)
        total = total.astype(BF16)
        own_ref[:, start : start + TILE] = total[:tokens]
        other_ref[:, start : start + TILE] = total[tokens:]


def combine(metas, returned, plan, first_row, weighted, after=()):
    width = returned[0].shape[1]
    return call(
        functools.partial(combine_kernel, plan=plan, first_row=first_row, weighted=weighted),
        [array(plan.tokens, width)] * 2,
        [VMEM] * (2 + plan.blocks) + [AFTER] * len(after),
        [VMEM] * 2,
        [],
        8 * plan.blocks * plan.rows * plan.tokens * width,
        2 * width * (2 * plan.tokens + plan.blocks * plan.rows),
    )(*metas, *returned, *after)


def stream(weight_ref, held, sems, axis):
    copies = []
    for tile in range(weight_ref.shape[axis] // TILE):
        part = pl.ds(tile * TILE, TILE)
        part = (part, slice(None)) if axis == 0 else (slice(None), part)
        copy = pltpu.make_async_copy(weight_ref.at[part], held.at[part], sems.at[tile])
        copy.start()
        copies.append(copy)
    return copies


def held_weight(shape, axis):
    return [pltpu.VMEM(shape, BF16), pltpu.SemaphoreType.DMA((shape[axis] // TILE,))]


def joined(refs):
    return jnp.concatenate([ref[...] for ref in refs], axis=0)


def gate_up_kernel(*refs, blocks):
    gate_w, up_w = refs[blocks : blocks + 2]
    out, gate_held, gate_sems, up_held, up_sems, rows = refs[-6:]
    gate_copies = stream(gate_w, gate_held, gate_sems, 1)
    up_copies = stream(up_w, up_held, up_sems, 1)
    rows[...] = joined(refs[:blocks])
    for tile in range(len(gate_copies)):
        part = slice(tile * TILE, (tile + 1) * TILE)
        gate_copies[tile].wait()
        out[0, :, part] = dot(rows[...], gate_held[:, part], 1, 0).astype(BF16)
        up_copies[tile].wait()
        out[1, :, part] = dot(rows[...], up_held[:, part], 1, 0).astype(BF16)


def gate_up(inputs, gate_w, up_w, after=()):
    blocks, (rows, width) = len(inputs), inputs[0].shape
    units, total = gate_w.shape[1], blocks * rows
    return call(
        functools.partial(gate_up_kernel, blocks=blocks),
        array(2, total, units),
        [VMEM] * blocks + [HBM, HBM] + [AFTER] * len(after),
        VMEM,
        held_weight(gate_w.shape, 1) * 2 + [pltpu.VMEM((total, width), BF16)],
        4 * total * width * units,
        2 * (total * width + 2 * width * units + 2 * total * units),
    )(*inputs, gate_w, up_w, *after)


def d_hidden_kernel(*refs, blocks):
    down_w = refs[blocks]
    out, held, sems, rows = refs[-4:]
    copies = stream(down_w, held, sems, 0)
    rows[...] = joined(refs[:blocks])
    for tile, copy in enumerate(copies):
        part = slice(tile * TILE, (tile + 1) * TILE)
        copy.wait()
        out[:, part] = dot(rows[...], held[part, :], 1, 1).astype(BF16)


def d_hidden(inputs, down_w, after=()):
    blocks, (rows, width) = len(inputs), inputs[0].shape
    units, total = down_w.shape[0], blocks * rows
    return call(
        functools.partial(d_hidden_kernel, blocks=blocks),
        array(total, units),
        [VMEM] * blocks + [HBM] + [AFTER] * len(after),
        VMEM,
        held_weight(down_w.shape, 0) + [pltpu.VMEM((total, width), BF16)],
        2 * total * width * units,
        2 * (total * width + width * units + total * units),
    )(*inputs, down_w, *after)


def scatter_tile(value, outs, part):
    rows = outs[0].shape[0]
    for block, out in enumerate(outs):
        out[:, part] = value[block * rows : (block + 1) * rows]


def gate_and_up(own_ref, other_ref, part):
    gate = own_ref[0, :, part].astype(F32) + other_ref[0, :, part].astype(F32)
    up = own_ref[1, :, part].astype(F32) + other_ref[1, :, part].astype(F32)
    return gate, up


def down_kernel(own_ref, other_ref, down_w, *refs):
    outs, (held, sems, hidden) = refs[:-3], refs[-3:]
    copies = stream(down_w, held, sems, 1)
    for start in range(0, hidden.shape[1], TILE):
        part = slice(start, start + TILE)
        gate, up = gate_and_up(own_ref, other_ref, part)
        hidden[:, part] = (gate * jax.nn.sigmoid(gate) * up).astype(BF16)
    for tile, copy in enumerate(copies):
        part = slice(tile * TILE, (tile + 1) * TILE)
        copy.wait()
        scatter_tile(dot(hidden[...], held[:, part], 1, 0).astype(BF16), outs, part)


def down(own, other, down_w, blocks):
    _, total, units = own.shape
    width, rows = down_w.shape[1], total // blocks
    return call(
        down_kernel,
        [array(rows, width)] * blocks,
        [VMEM, VMEM, HBM],
        [VMEM] * blocks,
        held_weight(down_w.shape, 1) + [pltpu.VMEM((total, units), BF16)],
        2 * total * width * units,
        2 * (total * width + width * units + 4 * total * units),
    )(own, other, down_w)


def back_kernel(own_ref, other_ref, own_d, other_d, gate_w, up_w, hidden, d_gate, d_up, *refs):
    outs, (gate_held, gate_sems, up_held, up_sems) = refs[:-4], refs[-4:]
    gate_copies = stream(gate_w, gate_held, gate_sems, 0)
    up_copies = stream(up_w, up_held, up_sems, 0)
    for start in range(0, hidden.shape[1], TILE):
        part = slice(start, start + TILE)
        gate, up = gate_and_up(own_ref, other_ref, part)
        d_hid = own_d[:, part].astype(F32) + other_d[:, part].astype(F32)
        sigmoid = jax.nn.sigmoid(gate)
        activated = gate * sigmoid
        hidden[:, part] = (activated * up).astype(BF16)
        d_up[:, part] = (d_hid * activated).astype(BF16)
        d_gate[:, part] = (d_hid * up * sigmoid * (1.0 + gate * (1.0 - sigmoid))).astype(BF16)
    for tile in range(len(gate_copies)):
        part = slice(tile * TILE, (tile + 1) * TILE)
        gate_copies[tile].wait()
        total = dot(d_gate[...], gate_held[part, :], 1, 1)
        up_copies[tile].wait()
        total += dot(d_up[...], up_held[part, :], 1, 1)
        scatter_tile(total.astype(BF16), outs, part)


def back(own, other, own_d, other_d, gate_w, up_w, blocks):
    _, total, units = own.shape
    width, rows = gate_w.shape[0], total // blocks
    return call(
        back_kernel,
        [array(total, units)] * 3 + [array(rows, width)] * blocks,
        [VMEM] * 4 + [HBM] * 2,
        [VMEM] * (3 + blocks),
        held_weight(gate_w.shape, 0) * 2,
        4 * total * width * units,
        2 * (total * width + 2 * width * units + 9 * total * units),
    )(own, other, own_d, other_d, gate_w, up_w)


def grad_kernel(hidden, d_gate, d_up, *refs, blocks):
    inputs, cots = refs[:blocks], refs[blocks : 2 * blocks]
    grad_gate, grad_up, grad_down, turned, cot_all = refs[-5:]

    @pl.when(pl.program_id(0) == 0)
    def _():
        for start in range(0, turned.shape[0], TILE):
            part = slice(start, start + TILE)
            piece = jnp.concatenate([ref[:, part] for ref in inputs], axis=0)
            turned[part, :] = piece.T
        cot_all[...] = joined(cots)

    part = pl.ds(pl.multiple_of(pl.program_id(0) * TILE, TILE), TILE)
    grad_gate[...] = dot(turned[...], d_gate[:, part], 1, 0).astype(BF16)
    grad_up[...] = dot(turned[...], d_up[:, part], 1, 0).astype(BF16)
    grad_down[...] = dot(hidden[:, part], cot_all[...], 0, 0).astype(BF16)


def grads(hidden, d_gate, d_up, inputs, cots, after=()):
    blocks, (rows, width) = len(inputs), inputs[0].shape
    total, units = hidden.shape
    by_column = pl.BlockSpec((width, TILE), lambda i: (0, i))
    return call(
        functools.partial(grad_kernel, blocks=blocks),
        [
            pltpu.HBM((width, units), BF16),
            pltpu.HBM((width, units), BF16),
            pltpu.HBM((units, width), BF16),
        ],
        [VMEM] * (3 + 2 * blocks) + [AFTER] * len(after),
        [by_column, by_column, pl.BlockSpec((TILE, width), lambda i: (i, 0))],
        [pltpu.VMEM((width, total), BF16), pltpu.VMEM((total, width), BF16)],
        6 * total * width * units,
        2 * (2 * total * width + 3 * width * units + 3 * total * units),
        grid=(units // TILE,),
    )(hidden, d_gate, d_up, *inputs, *cots, *after)


def to_experts(blocks, relative):
    if not relative:
        stacked = lax.all_to_all(jnp.stack(blocks), "expert", split_axis=0, concat_axis=0)
        return [stacked[block] for block in range(len(blocks))]
    return [blocks[0]] + [
        exchange(block, "expert", mask) for mask, block in enumerate(blocks) if mask > 0
    ]


def finish_kernel(mine_ref, rest_ref, out_ref, sems):
    width = mine_ref.shape[1]
    core = lax.axis_index("dp")
    copies = []
    for place, (half, source) in enumerate(((core, mine_ref), (1 - core, rest_ref))):
        columns = pl.ds(pl.multiple_of(half * width, 128), width)
        copies.append(
            pltpu.make_async_copy(source, out_ref.at[:, columns], sems.at[place])
        )
    for copy in copies:
        copy.start()
    for copy in copies:
        copy.wait()


def next_section(own, other):
    mine, rest = section_shift(own, 0), section_shift(other, 1)
    tokens, width = mine.shape
    return call(
        finish_kernel,
        pltpu.HBM((tokens, 2 * width), BF16),
        [VMEM, VMEM],
        HBM,
        [pltpu.SemaphoreType.DMA((2,))],
        0,
        8 * tokens * width,
    )(mine, rest)


def local(x_fwd, ids_fwd, route_fwd, x_bwd, ids_bwd, route_bwd, dy_bwd, w_gate, w_up, w_down):
    n_expert = lax.axis_size("expert")
    slab_width = w_gate.shape[-1]
    group = FF // slab_width
    experts = n_expert // group
    tokens = x_fwd.shape[1]
    spread = 4 * experts * group
    capacity = group * ((5 * tokens * TOP + spread - 1) // spread)
    rows = (2 * capacity + 15) // 16 * 16
    relative = n_expert <= 8
    plan = Plan(n_expert, rows, group, capacity, tokens, relative)
    gate_w, up_w, down_w = in_hbm(w_gate[0, 0]), in_hbm(w_up[0, 0]), in_hbm(w_down[0, 0])
    row_b, row_f = 0, META // 2

    own_x, send_x = pack(
        in_hbm(x_bwd[0]),
        *[in_hbm(value[0].T) for value in (ids_bwd, route_bwd, ids_fwd, route_fwd)],
    )
    other_x = exchange(send_x, "dp", 1)
    own_f, send_f, own_dy, send_dy = cut(in_hbm(x_fwd[0]), in_hbm(dy_bwd[0]))
    other_f = exchange(send_f, "dp", 1)
    other_dy = exchange(send_dy, "dp", 1)
    metas = (own_x, other_x)
    sent_x = dispatch(metas, own_x, other_x, plan, row_b, False, after=(own_f,))
    rows_b = to_experts(sent_x, relative)
    sent_f = dispatch(metas, own_f, other_f, plan, row_f, False, after=sent_x[:1])
    rows_f = to_experts(sent_f, relative)
    sent_dy = dispatch(metas, own_dy, other_dy, plan, row_b, True, after=sent_f[:1])
    cots_b = to_experts(sent_dy, relative)

    part_b = gate_up(rows_b, gate_w, up_w, after=sent_dy[:1])
    part_b_other = exchange(part_b, "dp", 1)

    part_f = gate_up(rows_f, gate_w, up_w, after=(part_b,))
    part_f_other = exchange(part_f, "dp", 1)
    down_blocks = down(part_f, part_f_other, down_w, n_expert)
    returned_f = to_experts(down_blocks, relative)

    part_d = d_hidden(cots_b, down_w, after=down_blocks[:1])
    part_d_other = exchange(part_d, "dp", 1)
    hidden, d_gate, d_up, *back_blocks = back(
        part_b, part_b_other, part_d, part_d_other, gate_w, up_w, n_expert
    )
    returned_b = to_experts(back_blocks, relative)

    sums_f = combine(metas, returned_f, plan, row_f, True, after=back_blocks[:1])
    y_next = next_section(*sums_f)
    grad_gate, grad_up, grad_down = grads(hidden, d_gate, d_up, rows_b, cots_b, after=sums_f[:1])
    sums_b = combine(metas, returned_b, plan, row_b, False, after=(in_hbm(grad_gate),))
    dx_next = next_section(*sums_b)
    return (
        y_next[None],
        dx_next[None],
        grad_gate[None, None],
        grad_up[None, None],
        grad_down[None, None],
    )


def solution(mesh):
    rows = P("section", ("expert", "dp"), None)
    by_feature = P("section", "expert", "dp", None)
    down_spec = P("section", "expert", None, "dp")
    return jax.shard_map(
        local,
        mesh=mesh,
        in_specs=(rows,) * 7 + (by_feature, by_feature, down_spec),
        out_specs=(rows, rows, by_feature, by_feature, down_spec),
        check_vma=False,
    )
```

time: 115 us -> 106 us (0.922)
  local copies, waits for them, and re-layouts: 15.8 us -> 0 us
  Pallas kernels: 35.4 us -> 45.5 us
  other arithmetic: 3.92 us -> 0 us
    unnamed x54 -> x0, local copies, waits for them, and re-layouts: 13 us -> none
    pallas_call x11 -> x15, Pallas kernels: 35.4 us -> 45.5 us  [the longest x2 14.4 us: gate_up(): call(functools.partial(gate_up_kernel, blocks=blocks), array(2, total, un...]
    dynamic_slice x3 -> x0, local copies, waits for them, and re-layouts: 2.87 us -> none  [other_half(): return lax.dynamic_slice_in_dim(value, (1 - core) * width, width, axis=1)]
    broadcast_in_dim x2 -> x0, other arithmetic: 1.6 us -> none  [the longest x1 0.8 us: local(): dx_next[None]]
    ppermute x22 -> x21, waiting for transfers between devices: 20.4 us -> 21.9 us  [exchange(): lax.ppermute(value, axis, [(source, source ^ mask) for source in range(co...]
    concatenate x2 -> x0, other arithmetic: 1.48 us -> none  [the longest x1 0.77 us: local(): meta = jnp.concatenate([meta, exchange(meta, 'dp', 1)], axis=1)]
    ppermute x22 -> x21, starting transfers between devices: 21.8 us -> 23.1 us  [exchange(): lax.ppermute(value, axis, [(source, source ^ mask) for source in range(co...]
    ppermute x4, waiting for transfers between devices: 11.4 us -> 10.2 us  [section_shift(): return lax.ppermute(value, ('section', 'dp'), pairs)]
  transfers between devices with their start and end apart: 26 -> 25, of which waited for: 9 -> 11; matrix products, arithmetic and copies ran while one was open for 4% -> 0% of each run, Pallas kernels for 30% -> 34%
where the time goes in v2:
time: 106 us
  Pallas kernels  45.5 us (43%)
  waiting for transfers between devices  32.1 us (30%)
  starting transfers between devices  27.4 us (26%)
    ppermute x21, starting transfers between devices, exchange(): lax.ppermute(value, axis, [(source, source ^ mask) for source in range(co...  23.1 us
    ppermute x21, waiting for transfers between devices, exchange(): lax.ppermute(value, axis, [(source, source ^ mask) for source in range(co...  21.9 us
    pallas_call x2, Pallas kernels, gate_up(): call(functools.partial(gate_up_kernel, blocks=blocks), array(2, total, un...  14.4 us
    ppermute x4, waiting for transfers between devices, section_shift(): return lax.ppermute(value, ('section', 'dp'), pairs)  10.2 us
    pallas_call x1, Pallas kernels, grads(): call(functools.partial(grad_kernel, blocks=blocks), [pltpu.HBM((width, un...  7.87 us
    pallas_call x1, Pallas kernels, back(): call(back_kernel, [array(total, units)] * 3 + [array(rows, width)] * bloc...  7.46 us
    pallas_call x1, Pallas kernels, down(): call(down_kernel, [array(rows, width)] * blocks, [VMEM, VMEM, HBM], [VMEM...  4.37 us
    pallas_call x1, Pallas kernels, d_hidden(): call(functools.partial(d_hidden_kernel, blocks=blocks), array(total, unit...  4.31 us
  transfers between devices with their start and end apart: 25, of which 11 were waited for; matrix products, arithmetic and copies ran while one was open for 0% of the time, Pallas kernels for 34%

profile of v2, /device:TPU:0, one launch (start us, length us, event | category | flops | bytes accessed | tf_op | source)
XLA Modules:
  0.0 106.0 jit_solution(18203697122819668040)
XLA Ops:
  4.2 2.8 %collective-permute-start.5 = (bf16[80,1792]{1,0:T(8,128)(2,1)S(1)}, bf16[80,1792]{1,0:T(8,128)(2,1)S(1)}, u32[]{:S(2)}, u32[]{:S(2)}) collective-permute-start(bf16[80,1792]{1,0:T(8,128)(2,1)S(1)} %get-tuple-element.50), channel_id=1, source_target_pairs={{0,2},{2,0},{4,6},{6,4},{1,3},{3,1},{5,7},{7,5},{8,10},{10,8},{12,... | collective-permute-start | bytes 860168 | tf_op jit(solution)/shard_map/ppermute | solution.py:22
  7.5 1.5 %collective-permute-start.6 = (bf16[80,1792]{1,0:T(8,128)(2,1)S(1)}, bf16[80,1792]{1,0:T(8,128)(2,1)S(1)}, u32[]{:S(2)}, u32[]{:S(2)}) collective-permute-start(bf16[80,1792]{1,0:T(8,128)(2,1)S(1)} %get-tuple-element.51), channel_id=1, source_target_pairs={{0,4},{2,6},{4,0},{6,2},{1,5},{3,7},{5,1},{7,3},{8,12},{10,14},{12... | collective-permute-start | bytes 860168 | tf_op jit(solution)/shard_map/ppermute | solution.py:22
  9.6 2.0 %collective-permute-start.2 = (bf16[80,1792]{1,0:T(8,128)(2,1)S(1)}, bf16[80,1792]{1,0:T(8,128)(2,1)S(1)}, u32[]{:S(2)}, u32[]{:S(2)}) collective-permute-start(bf16[80,1792]{1,0:T(8,128)(2,1)S(1)} %get-tuple-element.47), channel_id=1, source_target_pairs={{0,2},{2,0},{4,6},{6,4},{1,3},{3,1},{5,7},{7,5},{8,10},{10,8},{12,... | collective-permute-start | bytes 860168 | tf_op jit(solution)/shard_map/ppermute | solution.py:22
  11.6 1.5 %collective-permute-start.3 = (bf16[80,1792]{1,0:T(8,128)(2,1)S(1)}, bf16[80,1792]{1,0:T(8,128)(2,1)S(1)}, u32[]{:S(2)}, u32[]{:S(2)}) collective-permute-start(bf16[80,1792]{1,0:T(8,128)(2,1)S(1)} %get-tuple-element.48), channel_id=1, source_target_pairs={{0,4},{2,6},{4,0},{6,2},{1,5},{3,7},{5,1},{7,3},{8,12},{10,14},{12... | collective-permute-start | bytes 860168 | tf_op jit(solution)/shard_map/ppermute | solution.py:22
  14.6 3.0 %collective-permute-start.4 = (bf16[80,1792]{1,0:T(8,128)(2,1)S(1)}, bf16[80,1792]{1,0:T(8,128)(2,1)S(1)}, u32[]{:S(2)}, u32[]{:S(2)}) collective-permute-start(bf16[80,1792]{1,0:T(8,128)(2,1)S(1)} %get-tuple-element.49), channel_id=1, source_target_pairs={{0,6},{2,4},{4,2},{6,0},{1,7},{3,5},{5,3},{7,1},{8,14},{10,12},{12... | collective-permute-start | bytes 860168 | tf_op jit(solution)/shard_map/ppermute | solution.py:22
  18.2 5.1 %collective-permute-done.6.refs_2_ = bf16[80,1792]{1,0:T(8,128)(2,1)S(1)} collective-permute-done((bf16[80,1792]{1,0:T(8,128)(2,1)S(1)}, bf16[80,1792]{1,0:T(8,128)(2,1)S(1)}, u32[]{:S(2)}, u32[]{:S(2)}) %collective-permute-start.6) | collective-permute-done | bytes 286752 | tf_op jit(solution)/shard_map/ppermute | solution.py:22
  23.3 7.2 %shard_map.142.refs_6_.own_ref = bf16[2,320,1024]{2,1,0:T(8,128)(2,1)S(1)} custom-call(bf16[80,1792]{1,0:T(8,128)(2,1)S(1)} %get-tuple-element.45.refs_0_, bf16[80,1792]{1,0:T(8,128)(2,1)S(1)} %collective-permute-done.5.refs_1_, bf16[80,1792]{1,0:T(8,128)(2,1)S(1)} %collective-permute-done.6.refs_2_, bf16[80,1792]{1,0:T(8,128)(2,1)S(1)} %collective-permute-done.7.refs_3_, ...), custom_call_target="tpu_custom_call" | custom-call | flops 2293760 | bytes 9568 | tf_op jit(solution)/shard_map/pallas_call | solution.py:291
  30.5 4.1 %collective-permute-done.3.refs_2_ = bf16[80,1792]{1,0:T(8,128)(2,1)S(1)} collective-permute-done((bf16[80,1792]{1,0:T(8,128)(2,1)S(1)}, bf16[80,1792]{1,0:T(8,128)(2,1)S(1)}, u32[]{:S(2)}, u32[]{:S(2)}) %collective-permute-start.3) | collective-permute-done | bytes 286752 | tf_op jit(solution)/shard_map/ppermute | solution.py:22
  34.7 7.2 %shard_map.143.own_ref = bf16[2,320,1024]{2,1,0:T(8,128)(2,1)S(1)} custom-call(bf16[80,1792]{1,0:T(8,128)(2,1)S(1)} %get-tuple-element.46.refs_0_, bf16[80,1792]{1,0:T(8,128)(2,1)S(1)} %collective-permute-done.2.refs_1_, bf16[80,1792]{1,0:T(8,128)(2,1)S(1)} %collective-permute-done.3.refs_2_, bf16[80,1792]{1,0:T(8,128)(2,1)S(1)} %collective-permute-done.4.refs_3_, ...), custom_call_target="tpu_custom_call" | custom-call | flops 2293760 | bytes 9568 | tf_op jit(solution)/shard_map/pallas_call | solution.py:291
  44.5 1.4 %collective-permute-start.16 = (bf16[80,1792]{1,0:T(8,128)(2,1)S(1)}, bf16[80,1792]{1,0:T(8,128)(2,1)S(1)}, u32[]{:S(2)}, u32[]{:S(2)}) collective-permute-start(bf16[80,1792]{1,0:T(8,128)(2,1)S(1)} %get-tuple-element.62), channel_id=1, source_target_pairs={{0,6},{2,4},{4,2},{6,0},{1,7},{3,5},{5,3},{7,1},{8,14},{10,12},{12... | collective-permute-start | bytes 860168 | tf_op jit(solution)/shard_map/ppermute | solution.py:22
  45.9 4.4 %shard_map.144 = (bf16[80,1792]{1,0:T(8,128)(2,1)S(1)}, bf16[80,1792]{1,0:T(8,128)(2,1)S(1)}, bf16[80,1792]{1,0:T(8,128)(2,1)S(1)}, bf16[80,1792]{1,0:T(8,128)(2,1)S(1)}) custom-call(bf16[2,320,1024]{2,1,0:T(8,128)(2,1)S(1)} %shard_map.143.own_ref, bf16[2,320,1024]{2,1,0:T(8,128)(2,1)S(1)} %collective-permute-done.9.other_ref, bf16[1024,1792]{1,0:T(8,128)(2,1)} %bitcast.29), custom_call_target="tpu_custom_call" | custom-call | flops 1146880 | bytes 7264 | tf_op jit(solution)/shard_map/pallas_call | solution.py:355
  50.3 1.8 %collective-permute-done.14.refs_1_.refs_5_ = bf16[80,1792]{1,0:T(8,128)(2,1)S(1)} collective-permute-done((bf16[80,1792]{1,0:T(8,128)(2,1)S(1)}, bf16[80,1792]{1,0:T(8,128)(2,1)S(1)}, u32[]{:S(2)}, u32[]{:S(2)}) %collective-permute-start.14) | collective-permute-done | bytes 286752 | tf_op jit(solution)/shard_map/ppermute | solution.py:22
  52.1 4.6 %collective-permute-done.15.refs_2_.refs_6_ = bf16[80,1792]{1,0:T(8,128)(2,1)S(1)} collective-permute-done((bf16[80,1792]{1,0:T(8,128)(2,1)S(1)}, bf16[80,1792]{1,0:T(8,128)(2,1)S(1)}, u32[]{:S(2)}, u32[]{:S(2)}) %collective-permute-start.15) | collective-permute-done | bytes 286752 | tf_op jit(solution)/shard_map/ppermute | solution.py:22
  56.7 1.6 %collective-permute-done.16.refs_3_.refs_7_ = bf16[80,1792]{1,0:T(8,128)(2,1)S(1)} collective-permute-done((bf16[80,1792]{1,0:T(8,128)(2,1)S(1)}, bf16[80,1792]{1,0:T(8,128)(2,1)S(1)}, u32[]{:S(2)}, u32[]{:S(2)}) %collective-permute-start.16) | collective-permute-done | bytes 286752 | tf_op jit(solution)/shard_map/ppermute | solution.py:22
  58.4 4.3 %shard_map.145.own_d = bf16[320,1024]{1,0:T(8,128)(2,1)S(1)} custom-call(bf16[80,1792]{1,0:T(8,128)(2,1)S(1)} %get-tuple-element.55.refs_6_.refs_0_.refs_4_, bf16[80,1792]{1,0:T(8,128)(2,1)S(1)} %collective-permute-done.14.refs_1_.refs_5_, bf16[80,1792]{1,0:T(8,128)(2,1)S(1)} %collective-permute-done.15.refs_2_.refs_6_, ...), custom_call_target="tpu_custom_call" | custom-call | flops 1146880 | bytes 5344 | tf_op jit(solution)/shard_map/pallas_call | solution.py:316
  63.6 1.5 %collective-permute-start.11 = (bf16[80,1792]{1,0:T(8,128)(2,1)S(1)}, bf16[80,1792]{1,0:T(8,128)(2,1)S(1)}, u32[]{:S(2)}, u32[]{:S(2)}) collective-permute-start(bf16[80,1792]{1,0:T(8,128)(2,1)S(1)} %get-tuple-element.58), channel_id=1, source_target_pairs={{0,4},{2,6},{4,0},{6,2},{1,5},{3,7},{5,1},{7,3},{8,12},{10,14},{12... | collective-permute-start | bytes 860168 | tf_op jit(solution)/shard_map/ppermute | solution.py:22
  66.3 7.5 %shard_map.146 = (bf16[320,1024]{1,0:T(8,128)(2,1)S(1)}, bf16[320,1024]{1,0:T(8,128)(2,1)S(1)}, bf16[320,1024]{1,0:T(8,128)(2,1)S(1)}, bf16[80,1792]{1,0:T(8,128...) custom-call(bf16[2,320,1024]{2,1,0:T(8,128)(2,1)S(1)} %shard_map.142.refs_6_.ow, ...), custom_call_target="tpu_custom_call" | custom-call | flops 2293760 | bytes 14048 | tf_op jit(solution)/shard_map/pallas_call | solution.py:391
  74.6 1.5 %collective-permute-start.21 = (bf16[80,1792]{1,0:T(8,128)(2,1)S(1)}, bf16[80,1792]{1,0:T(8,128)(2,1)S(1)}, u32[]{:S(2)}, u32[]{:S(2)}) collective-permute-start(bf16[80,1792]{1,0:T(8,128)(2,1)S(1)} %get-tuple-element.67), channel_id=1, source_target_pairs={{0,4},{2,6},{4,0},{6,2},{1,5},{3,7},{5,1},{7,3},{8,12},{10,14},{12... | collective-permute-start | bytes 860168 | tf_op jit(solution)/shard_map/ppermute | solution.py:22
  79.7 1.6 %collective-permute-start.18 = (bf16[64,1792]{1,0:T(8,128)(2,1)S(1)}, bf16[64,1792]{1,0:T(8,128)(2,1)S(1)}, u32[]{:S(2)}, u32[]{:S(2)}) collective-permute-start(bf16[64,1792]{1,0:T(8,128)(2,1)S(1)} %get-tuple-element.64.refs_8_), channel_id=1, source_target_pairs={{0,8},{1,9},{8,16},{9,17},{16,24},{17,25},{24,0},{25,1},{2,10},{3,... | collective-permute-start | bytes 688136 | tf_op jit(solution)/shard_map/ppermute | solution.py:32
  81.5 7.9 %shard_map.149 = (bf16[1792,1024]{1,0:T(8,128)(2,1)}, bf16[1792,1024]{1,0:T(8,128)(2,1)}, bf16[1024,1792]{1,0:T(8,128)(2,1)}) custom-call(bf16[320,1024]{1,0:T(8,128)(2,1)S(1)} %get-tuple-element.69.hidden, bf16[320,1024]{1,0:T(8,128)(2,1)S(1)} %get-tuple-element.70.d_gate, bf16[320,1024]{1,0:T(8,128)(2,1)S(1)} %get-tuple-element.71.d_up, ...), custom_call_target="tpu_custom_call" | custom-call | flops 3440640 | bytes 14912 | tf_op jit(solution)/shard_map/pallas_call | solution.py:424
  89.4 1.6 %collective-permute-done.21.refs_2_ = bf16[80,1792]{1,0:T(8,128)(2,1)S(1)} collective-permute-done((bf16[80,1792]{1,0:T(8,128)(2,1)S(1)}, bf16[80,1792]{1,0:T(8,128)(2,1)S(1)}, u32[]{:S(2)}, u32[]{:S(2)}) %collective-permute-start.21) | collective-permute-done | bytes 286752 | tf_op jit(solution)/shard_map/ppermute | solution.py:22
  91.5 1.6 %collective-permute-start.23 = (bf16[64,1792]{1,0:T(8,128)(2,1)S(1)}, bf16[64,1792]{1,0:T(8,128)(2,1)S(1)}, u32[]{:S(2)}, u32[]{:S(2)}) collective-permute-start(bf16[64,1792]{1,0:T(8,128)(2,1)S(1)} %get-tuple-element.73), channel_id=1, source_target_pairs={{0,8},{1,9},{8,16},{9,17},{16,24},{17,25},{24,0},{25,1},{2,10},{3,... | collective-permute-start | bytes 688136 | tf_op jit(solution)/shard_map/ppermute | solution.py:32
  94.9 7.0 %collective-permute-done.23.mine_ref = bf16[64,1792]{1,0:T(8,128)(2,1)S(1)} collective-permute-done((bf16[64,1792]{1,0:T(8,128)(2,1)S(1)}, bf16[64,1792]{1,0:T(8,128)(2,1)S(1)}, u32[]{:S(2)}, u32[]{:S(2)}) %collective-permute-start.23) | collective-permute-done | bytes 229408 | tf_op jit(solution)/shard_map/ppermute | solution.py:32
  101.8 3.2 %collective-permute-done.24.rest_ref = bf16[64,1792]{1,0:T(8,128)(2,1)S(1)} collective-permute-done((bf16[64,1792]{1,0:T(8,128)(2,1)S(1)}, bf16[64,1792]{1,0:T(8,128)(2,1)S(1)}, u32[]{:S(2)}, u32[]{:S(2)}) %collective-permute-start.24) | collective-permute-done | bytes 229408 | tf_op jit(solution)/shard_map/ppermute | solution.py:32
  (41 shorter events, 19.0 us)
Async XLA Ops:
  4.2 10.4 %collective-permute-start.5 = (bf16[80,1792]{1,0:T(8,128)(2,1)S(1)}, bf16[80,1792]{1,0:T(8,128)(2,1)S(1)}, u32[]{:S(2)}, u32[]{:S(2)}) collective-permute-start(bf16[80,1792]{1,0:T(8,128)(2,1)S(1)} %get-tuple-element.50), channel_id=1, source_target_pairs={{0,2},{2,0},{4,6},{6,4},{1,3},{3,1},{5,7},{7,5},{8,10},{10,8},{12,... | collective-permute-start | bytes 860168 | tf_op jit(solution)/shard_map/ppermute | solution.py:22
  7.0 2.1 %collective-permute-start.1 = (bf16[64,1792]{1,0:T(8,128)(2,1)S(1)}, bf16[64,1792]{1,0:T(8,128)(2,1)S(1)}, u32[]{:S(2)}, u32[]{:S(2)}) collective-permute-start(bf16[64,1792]{1,0:T(8,128)(2,1)S(1)} %get-tuple-element.44), channel_id=1, source_target_pairs={{0,1},{1,0},{2,3},{3,2},{4,5},{5,4},{6,7},{7,6},{8,9},{9,8},{10,11... | collective-permute-start | bytes 688136 | tf_op jit(solution)/shard_map/ppermute | solution.py:22
  7.0 4.7 %collective-permute-start.8 = (bf16[64,1792]{1,0:T(8,128)(2,1)S(1)}, bf16[64,1792]{1,0:T(8,128)(2,1)S(1)}, u32[]{:S(2)}, u32[]{:S(2)}) collective-permute-start(bf16[64,1792]{1,0:T(8,128)(2,1)S(1)} %get-tuple-element.54), channel_id=1, source_target_pairs={{0,1},{1,0},{2,3},{3,2},{4,5},{5,4},{6,7},{7,6},{8,9},{9,8},{10,11... | collective-permute-start | bytes 688136 | tf_op jit(solution)/shard_map/ppermute | solution.py:22
  7.5 15.8 %collective-permute-start.6 = (bf16[80,1792]{1,0:T(8,128)(2,1)S(1)}, bf16[80,1792]{1,0:T(8,128)(2,1)S(1)}, u32[]{:S(2)}, u32[]{:S(2)}) collective-permute-start(bf16[80,1792]{1,0:T(8,128)(2,1)S(1)} %get-tuple-element.51), channel_id=1, source_target_pairs={{0,4},{2,6},{4,0},{6,2},{1,5},{3,7},{5,1},{7,3},{8,12},{10,14},{12... | collective-permute-start | bytes 860168 | tf_op jit(solution)/shard_map/ppermute | solution.py:22
  9.0 14.3 %collective-permute-start.7 = (bf16[80,1792]{1,0:T(8,128)(2,1)S(1)}, bf16[80,1792]{1,0:T(8,128)(2,1)S(1)}, u32[]{:S(2)}, u32[]{:S(2)}) collective-permute-start(bf16[80,1792]{1,0:T(8,128)(2,1)S(1)} %get-tuple-element.52), channel_id=1, source_target_pairs={{0,6},{2,4},{4,2},{6,0},{1,7},{3,5},{5,3},{7,1},{8,14},{10,12},{12... | collective-permute-start | bytes 860168 | tf_op jit(solution)/shard_map/ppermute | solution.py:22
  9.6 20.9 %collective-permute-start.2 = (bf16[80,1792]{1,0:T(8,128)(2,1)S(1)}, bf16[80,1792]{1,0:T(8,128)(2,1)S(1)}, u32[]{:S(2)}, u32[]{:S(2)}) collective-permute-start(bf16[80,1792]{1,0:T(8,128)(2,1)S(1)} %get-tuple-element.47), channel_id=1, source_target_pairs={{0,2},{2,0},{4,6},{6,4},{1,3},{3,1},{5,7},{7,5},{8,10},{10,8},{12,... | collective-permute-start | bytes 860168 | tf_op jit(solution)/shard_map/ppermute | solution.py:22
  11.6 23.0 %collective-permute-start.3 = (bf16[80,1792]{1,0:T(8,128)(2,1)S(1)}, bf16[80,1792]{1,0:T(8,128)(2,1)S(1)}, u32[]{:S(2)}, u32[]{:S(2)}) collective-permute-start(bf16[80,1792]{1,0:T(8,128)(2,1)S(1)} %get-tuple-element.48), channel_id=1, source_target_pairs={{0,4},{2,6},{4,0},{6,2},{1,5},{3,7},{5,1},{7,3},{8,12},{10,14},{12... | collective-permute-start | bytes 860168 | tf_op jit(solution)/shard_map/ppermute | solution.py:22
  14.6 20.1 %collective-permute-start.4 = (bf16[80,1792]{1,0:T(8,128)(2,1)S(1)}, bf16[80,1792]{1,0:T(8,128)(2,1)S(1)}, u32[]{:S(2)}, u32[]{:S(2)}) collective-permute-start(bf16[80,1792]{1,0:T(8,128)(2,1)S(1)} %get-tuple-element.49), channel_id=1, source_target_pairs={{0,6},{2,4},{4,2},{6,0},{1,7},{3,5},{5,3},{7,1},{8,14},{10,12},{12... | collective-permute-start | bytes 860168 | tf_op jit(solution)/shard_map/ppermute | solution.py:22
  41.9 4.1 %collective-permute-start.9 = (bf16[2,320,1024]{2,1,0:T(8,128)(2,1)S(1)}, bf16[2,320,1024]{2,1,0:T(8,128)(2,1)S(1)}, u32[]{:S(2)}, u32[]{:S(2)}) collective-permute-start(bf16[2,320,1024]{2,1,0:T(8,128)(2,1)S(1)} %shard_map.143.own_ref), channel_id=1, source_target_pairs={{0,1},{1,0},{2,3},{3,2},{4,5},{5,4},{6,7},{7,6},{8,9},{9,8},{10,11... | collective-permute-start | bytes 3932168 | tf_op jit(solution)/shard_map/ppermute | solution.py:22
  41.9 24.4 %collective-permute-start.13 = (bf16[2,320,1024]{2,1,0:T(8,128)(2,1)S(1)}, bf16[2,320,1024]{2,1,0:T(8,128)(2,1)S(1)}, u32[]{:S(2)}, u32[]{:S(2)}) collective-permute-start(bf16[2,320,1024]{2,1,0:T(8,128)(2,1)S(1)} %shard_map.142.refs_6_.own_ref), channel_id=1, source_target_pairs={{0,1},{1,0},{2,3},{3,2},{4,5},{5,4},{6,7},{7,6},{8,9},{9,8},{10,11... | collective-permute-start | bytes 3932168 | tf_op jit(solution)/shard_map/ppermute | solution.py:22
  42.4 9.7 %collective-permute-start.14 = (bf16[80,1792]{1,0:T(8,128)(2,1)S(1)}, bf16[80,1792]{1,0:T(8,128)(2,1)S(1)}, u32[]{:S(2)}, u32[]{:S(2)}) collective-permute-start(bf16[80,1792]{1,0:T(8,128)(2,1)S(1)} %get-tuple-element.60), channel_id=1, source_target_pairs={{0,2},{2,0},{4,6},{6,4},{1,3},{3,1},{5,7},{7,5},{8,10},{10,8},{12,... | collective-permute-start | bytes 860168 | tf_op jit(solution)/shard_map/ppermute | solution.py:22
  43.2 13.5 %collective-permute-start.15 = (bf16[80,1792]{1,0:T(8,128)(2,1)S(1)}, bf16[80,1792]{1,0:T(8,128)(2,1)S(1)}, u32[]{:S(2)}, u32[]{:S(2)}) collective-permute-start(bf16[80,1792]{1,0:T(8,128)(2,1)S(1)} %get-tuple-element.61), channel_id=1, source_target_pairs={{0,4},{2,6},{4,0},{6,2},{1,5},{3,7},{5,1},{7,3},{8,12},{10,14},{12... | collective-permute-start | bytes 860168 | tf_op jit(solution)/shard_map/ppermute | solution.py:22
  44.5 13.9 %collective-permute-start.16 = (bf16[80,1792]{1,0:T(8,128)(2,1)S(1)}, bf16[80,1792]{1,0:T(8,128)(2,1)S(1)}, u32[]{:S(2)}, u32[]{:S(2)}) collective-permute-start(bf16[80,1792]{1,0:T(8,128)(2,1)S(1)} %get-tuple-element.62), channel_id=1, source_target_pairs={{0,6},{2,4},{4,2},{6,0},{1,7},{3,5},{5,3},{7,1},{8,14},{10,12},{12... | collective-permute-start | bytes 860168 | tf_op jit(solution)/shard_map/ppermute | solution.py:22
  62.7 3.6 %collective-permute-start.17 = (bf16[320,1024]{1,0:T(8,128)(2,1)S(1)}, bf16[320,1024]{1,0:T(8,128)(2,1)S(1)}, u32[]{:S(2)}, u32[]{:S(2)}) collective-permute-start(bf16[320,1024]{1,0:T(8,128)(2,1)S(1)} %shard_map.145.own_d), channel_id=1, source_target_pairs={{0,1},{1,0},{2,3},{3,2},{4,5},{5,4},{6,7},{7,6},{8,9},{9,8},{10,11... | collective-permute-start | bytes 1966088 | tf_op jit(solution)/shard_map/ppermute | solution.py:22
  62.7 13.4 %collective-permute-start.10 = (bf16[80,1792]{1,0:T(8,128)(2,1)S(1)}, bf16[80,1792]{1,0:T(8,128)(2,1)S(1)}, u32[]{:S(2)}, u32[]{:S(2)}) collective-permute-start(bf16[80,1792]{1,0:T(8,128)(2,1)S(1)} %get-tuple-element.57), channel_id=1, source_target_pairs={{0,2},{2,0},{4,6},{6,4},{1,3},{3,1},{5,7},{7,5},{8,10},{10,8},{12,... | collective-permute-start | bytes 860168 | tf_op jit(solution)/shard_map/ppermute | solution.py:22
  63.6 15.0 %collective-permute-start.11 = (bf16[80,1792]{1,0:T(8,128)(2,1)S(1)}, bf16[80,1792]{1,0:T(8,128)(2,1)S(1)}, u32[]{:S(2)}, u32[]{:S(2)}) collective-permute-start(bf16[80,1792]{1,0:T(8,128)(2,1)S(1)} %get-tuple-element.58), channel_id=1, source_target_pairs={{0,4},{2,6},{4,0},{6,2},{1,5},{3,7},{5,1},{7,3},{8,12},{10,14},{12... | collective-permute-start | bytes 860168 | tf_op jit(solution)/shard_map/ppermute | solution.py:22
  65.1 13.8 %collective-permute-start.12 = (bf16[80,1792]{1,0:T(8,128)(2,1)S(1)}, bf16[80,1792]{1,0:T(8,128)(2,1)S(1)}, u32[]{:S(2)}, u32[]{:S(2)}) collective-permute-start(bf16[80,1792]{1,0:T(8,128)(2,1)S(1)} %get-tuple-element.59), channel_id=1, source_target_pairs={{0,6},{2,4},{4,2},{6,0},{1,7},{3,5},{5,3},{7,1},{8,14},{10,12},{12... | collective-permute-start | bytes 860168 | tf_op jit(solution)/shard_map/ppermute | solution.py:22
  73.8 15.6 %collective-permute-start.20 = (bf16[80,1792]{1,0:T(8,128)(2,1)S(1)}, bf16[80,1792]{1,0:T(8,128)(2,1)S(1)}, u32[]{:S(2)}, u32[]{:S(2)}) collective-permute-start(bf16[80,1792]{1,0:T(8,128)(2,1)S(1)} %get-tuple-element.66), channel_id=1, source_target_pairs={{0,2},{2,0},{4,6},{6,4},{1,3},{3,1},{5,7},{7,5},{8,10},{10,8},{12,... | collective-permute-start | bytes 860168 | tf_op jit(solution)/shard_map/ppermute | solution.py:22
  74.6 16.3 %collective-permute-start.21 = (bf16[80,1792]{1,0:T(8,128)(2,1)S(1)}, bf16[80,1792]{1,0:T(8,128)(2,1)S(1)}, u32[]{:S(2)}, u32[]{:S(2)}) collective-permute-start(bf16[80,1792]{1,0:T(8,128)(2,1)S(1)} %get-tuple-element.67), channel_id=1, source_target_pairs={{0,4},{2,6},{4,0},{6,2},{1,5},{3,7},{5,1},{7,3},{8,12},{10,14},{12... | collective-permute-start | bytes 860168 | tf_op jit(solution)/shard_map/ppermute | solution.py:22
  76.2 14.8 %collective-permute-start.22 = (bf16[80,1792]{1,0:T(8,128)(2,1)S(1)}, bf16[80,1792]{1,0:T(8,128)(2,1)S(1)}, u32[]{:S(2)}, u32[]{:S(2)}) collective-permute-start(bf16[80,1792]{1,0:T(8,128)(2,1)S(1)} %get-tuple-element.68), channel_id=1, source_target_pairs={{0,6},{2,4},{4,2},{6,0},{1,7},{3,5},{5,3},{7,1},{8,14},{10,12},{12... | collective-permute-start | bytes 860168 | tf_op jit(solution)/shard_map/ppermute | solution.py:22
  79.7 14.4 %collective-permute-start.18 = (bf16[64,1792]{1,0:T(8,128)(2,1)S(1)}, bf16[64,1792]{1,0:T(8,128)(2,1)S(1)}, u32[]{:S(2)}, u32[]{:S(2)}) collective-permute-start(bf16[64,1792]{1,0:T(8,128)(2,1)S(1)} %get-tuple-element.64.refs_8_), channel_id=1, source_target_pairs={{0,8},{1,9},{8,16},{9,17},{16,24},{17,25},{24,0},{25,1},{2,10},{3,... | collective-permute-start | bytes 688136 | tf_op jit(solution)/shard_map/ppermute | solution.py:32
  81.4 12.7 %collective-permute-start.19 = (bf16[64,1792]{1,0:T(8,128)(2,1)S(1)}, bf16[64,1792]{1,0:T(8,128)(2,1)S(1)}, u32[]{:S(2)}, u32[]{:S(2)}) collective-permute-start(bf16[64,1792]{1,0:T(8,128)(2,1)S(1)} %get-tuple-element.65), channel_id=1, source_target_pairs={{0,9},{1,8},{8,17},{9,16},{16,25},{17,24},{24,1},{25,0},{2,11},{3,... | collective-permute-start | bytes 688136 | tf_op jit(solution)/shard_map/ppermute | solution.py:32
  91.5 10.3 %collective-permute-start.23 = (bf16[64,1792]{1,0:T(8,128)(2,1)S(1)}, bf16[64,1792]{1,0:T(8,128)(2,1)S(1)}, u32[]{:S(2)}, u32[]{:S(2)}) collective-permute-start(bf16[64,1792]{1,0:T(8,128)(2,1)S(1)} %get-tuple-element.73), channel_id=1, source_target_pairs={{0,8},{1,9},{8,16},{9,17},{16,24},{17,25},{24,0},{25,1},{2,10},{3,... | collective-permute-start | bytes 688136 | tf_op jit(solution)/shard_map/ppermute | solution.py:32
  93.2 11.9 %collective-permute-start.24 = (bf16[64,1792]{1,0:T(8,128)(2,1)S(1)}, bf16[64,1792]{1,0:T(8,128)(2,1)S(1)}, u32[]{:S(2)}, u32[]{:S(2)}) collective-permute-start(bf16[64,1792]{1,0:T(8,128)(2,1)S(1)} %get-tuple-element.74), channel_id=1, source_target_pairs={{0,9},{1,8},{8,17},{9,16},{16,25},{17,24},{24,1},{25,0},{2,11},{3,... | collective-permute-start | bytes 688136 | tf_op jit(solution)/shard_map/ppermute | solution.py:32
  (1 other events, 1.8 us)

commit v3 on v2

--- a/solution.py
+++ b/solution.py
@@ -12,7 +12,7 @@
 TILE = 256
 VMEM_LIMIT = 20 * 1024 * 1024
 META = 16
-COST_SHARE = 1024
+COST = 10**7
 F32 = jnp.float32
 BF16 = jnp.bfloat16
 
@@ -43,7 +43,7 @@
 AFTER = pl.BlockSpec(memory_space=pl.ANY)
 
 
-def call(kernel, out_shape, in_specs, out_specs, scratch, flops, moved, grid=()):
+def call(kernel, out_shape, in_specs, out_specs, scratch, grid=(), weight=1):
     return pl.pallas_call(
         kernel,
         out_shape=out_shape,
@@ -53,13 +53,17 @@
         scratch_shapes=scratch,
         compiler_params=pltpu.CompilerParams(vmem_limit_bytes=VMEM_LIMIT),
         cost_estimate=pl.CostEstimate(
-            flops=flops // COST_SHARE, bytes_accessed=moved // COST_SHARE, transcendentals=0
+            flops=weight * COST, bytes_accessed=1, transcendentals=0
         ),
     )
 
 
 def array(*shape):
     return jax.ShapeDtypeStruct(shape, BF16)
+
+
+def in_vmem(value):
+    return pltpu.with_memory_space_constraint(value, pltpu.VMEM)
 
 
 def in_hbm(value):
@@ -82,21 +86,23 @@
     return copies
 
 
-def pack_kernel(x_ref, *refs):
-    sources, (own_ref, other_ref, packed, sems), held = refs[:4], refs[4:8], refs[8:]
-    copies = halves(x_ref, own_ref, other_ref, sems, 0)
+def pack_kernel(x_ref, f_ref, dy_ref, *refs):
+    sources, outs, (packed, sems), held = refs[:4], refs[4:9], refs[9:11], refs[11:]
+    own_x, other_x, own_f, own_dy, other_rest = outs
     tokens = x_ref.shape[0]
+    copies = halves(x_ref, own_x, other_x, sems, 0)
     small = [
-        pltpu.make_async_copy(source, target, sems.at[2 + place])
+        pltpu.make_async_copy(source, target, sems.at[6 + place])
         for place, (source, target) in enumerate(zip(sources, held))
     ]
     for copy in small:
         copy.start()
+    copies += halves(f_ref, own_f, other_rest.at[0:tokens], sems, 2)
+    copies += halves(dy_ref, own_dy, other_rest.at[tokens : 2 * tokens], sems, 4)
     packed[...] = jnp.zeros_like(packed)
     for copy in small:
         copy.wait()
-    ids_b, route_b, ids_f, route_f = held
-    for start, ids, route in ((0, ids_b, route_b), (META // 2, ids_f, route_f)):
+    for start, ids, route in ((0, *held[:2]), (META // 2, *held[2:])):
         packed[start : start + 2, 0:tokens] = ids[...].astype(F32)
         rest = route[...]
         for piece in range(3):
@@ -106,45 +112,44 @@
             rest = rest - top
     mine = packed[...]
     lanes = packed.shape[1]
-    own_ref[tokens : tokens + META, 0:lanes] = mine.astype(BF16)
-    other_ref[tokens : tokens + META, 0:lanes] = pltpu.roll(mine, tokens, 1).astype(BF16)
+    own_x[tokens : tokens + META, 0:lanes] = mine.astype(BF16)
+    other_x[tokens : tokens + META, 0:lanes] = pltpu.roll(mine, tokens, 1).astype(BF16)
     for copy in copies:
         copy.wait()
 
 
-def pack(x, ids_b, route_b, ids_f, route_f):
+def pack(x, f, dy, *small):
     tokens, width = x.shape[0], x.shape[1] // 2
-    out = array(tokens + META, width)
     return call(
         pack_kernel,
-        [out, out],
-        [HBM] * 5,
-        [VMEM, VMEM],
-        [pltpu.VMEM((META, 2 * tokens), F32), pltpu.SemaphoreType.DMA((6,))]
-        + [pltpu.VMEM(value.shape, value.dtype) for value in (ids_b, route_b, ids_f, route_f)],
-        0,
-        8 * x.size,
-    )(x, ids_b, route_b, ids_f, route_f)
-
-
-def cut_kernel(x_ref, dy_ref, own_x, other_x, own_dy, other_dy, sems):
-    copies = halves(x_ref, own_x, other_x, sems, 0)
-    copies += halves(dy_ref, own_dy, other_dy, sems, 2)
+        [array(tokens + META, width)] * 2 + [array(tokens, width)] * 2 + [array(2 * tokens, width)],
+        [HBM] * 7,
+        [VMEM] * 5,
+        [pltpu.VMEM((META, 2 * tokens), F32), pltpu.SemaphoreType.DMA((10,))]
+        + [pltpu.VMEM(value.shape, value.dtype) for value in small],
+    )(x, f, dy, *small)
+
+
+def load_kernel(*refs, count):
+    sources, targets, sems = refs[:count], refs[-count - 1 : -1], refs[-1]
+    copies = [
+        pltpu.make_async_copy(source, target, sems.at[place])
+        for place, (source, target) in enumerate(zip(sources, targets))
+    ]
+    for copy in copies:
+        copy.start()
     for copy in copies:
         copy.wait()
 
 
-def cut(x, dy):
-    tokens, width = x.shape[0], x.shape[1] // 2
-    return call(
-        cut_kernel,
-        [array(tokens, width)] * 4,
-        [HBM, HBM],
-        [VMEM] * 4,
-        [pltpu.SemaphoreType.DMA((4,))],
-        0,
-        16 * x.size,
-    )(x, dy)
+def load(weights, after):
+    return call(
+        functools.partial(load_kernel, count=len(weights)),
+        [array(*weight.shape) for weight in weights],
+        [HBM] * len(weights) + [AFTER] * len(after),
+        [VMEM] * len(weights),
+        [pltpu.SemaphoreType.DMA((len(weights),))],
+    )(*weights, *after)
 
 
 class Plan:
@@ -182,11 +187,13 @@
     return jnp.where(index == slot[block : block + 1, :], 1.0, 0.0)
 
 
-def dispatch_kernel(own_meta, other_meta, own_ref, other_ref, *refs, plan, first_row, weighted):
+def dispatch_kernel(
+    own_meta, other_meta, own_ref, other_ref, *refs, plan, first_row, other_row, weighted
+):
     outs = refs[-plan.blocks :]
     width, tokens = outs[0].shape[1], plan.tokens
     slot, route = slot_rows(own_meta, other_meta, plan, first_row)
-    values = jnp.concatenate([own_ref[0:tokens, :], other_ref[0:tokens, :]], axis=0)
+    values = jnp.concatenate([own_ref[0:tokens, :], other_ref[other_row : other_row + tokens, :]], axis=0)
     for block in range(plan.blocks):
         table = slot_table(slot, block, plan.rows)
         if weighted:
@@ -199,18 +206,20 @@
             outs[block][:, start : start + TILE] = picked.astype(BF16)
 
 
-def dispatch(metas, own, other, plan, first_row, weighted, after=()):
+def dispatch(metas, own, other, plan, first_row, other_row, weighted, after=()):
     width = own.shape[1]
     return call(
         functools.partial(
-            dispatch_kernel, plan=plan, first_row=first_row, weighted=weighted
+            dispatch_kernel,
+            plan=plan,
+            first_row=first_row,
+            other_row=other_row,
+            weighted=weighted,
         ),
         [array(plan.rows, width)] * plan.blocks,
         [VMEM] * 4 + [AFTER] * len(after),
         [VMEM] * plan.blocks,
         [],
-        4 * plan.blocks * plan.rows * plan.tokens * width,
-        2 * width * (3 * plan.tokens + plan.blocks * plan.rows),
     )(*metas, own, other, *after)
 
 
@@ -247,24 +256,7 @@
         [VMEM] * (2 + plan.blocks) + [AFTER] * len(after),
         [VMEM] * 2,
         [],
-        8 * plan.blocks * plan.rows * plan.tokens * width,
-        2 * width * (2 * plan.tokens + plan.blocks * plan.rows),
     )(*metas, *returned, *after)
-
-
-def stream(weight_ref, held, sems, axis):
-    copies = []
-    for tile in range(weight_ref.shape[axis] // TILE):
-        part = pl.ds(tile * TILE, TILE)
-        part = (part, slice(None)) if axis == 0 else (slice(None), part)
-        copy = pltpu.make_async_copy(weight_ref.at[part], held.at[part], sems.at[tile])
-        copy.start()
-        copies.append(copy)
-    return copies
-
-
-def held_weight(shape, axis):
-    return [pltpu.VMEM(shape, BF16), pltpu.SemaphoreType.DMA((shape[axis] // TILE,))]
 
 
 def joined(refs):
@@ -273,16 +265,12 @@
 
 def gate_up_kernel(*refs, blocks):
     gate_w, up_w = refs[blocks : blocks + 2]
-    out, gate_held, gate_sems, up_held, up_sems, rows = refs[-6:]
-    gate_copies = stream(gate_w, gate_held, gate_sems, 1)
-    up_copies = stream(up_w, up_held, up_sems, 1)
+    out, rows = refs[-2:]
     rows[...] = joined(refs[:blocks])
-    for tile in range(len(gate_copies)):
-        part = slice(tile * TILE, (tile + 1) * TILE)
-        gate_copies[tile].wait()
-        out[0, :, part] = dot(rows[...], gate_held[:, part], 1, 0).astype(BF16)
-        up_copies[tile].wait()
-        out[1, :, part] = dot(rows[...], up_held[:, part], 1, 0).astype(BF16)
+    for start in range(0, out.shape[2], TILE):
+        part = slice(start, start + TILE)
+        out[0, :, part] = dot(rows[...], gate_w[:, part], 1, 0).astype(BF16)
+        out[1, :, part] = dot(rows[...], up_w[:, part], 1, 0).astype(BF16)
 
 
 def gate_up(inputs, gate_w, up_w, after=()):
@@ -291,23 +279,19 @@
     return call(
         functools.partial(gate_up_kernel, blocks=blocks),
         array(2, total, units),
-        [VMEM] * blocks + [HBM, HBM] + [AFTER] * len(after),
+        [VMEM] * (blocks + 2) + [AFTER] * len(after),
         VMEM,
-        held_weight(gate_w.shape, 1) * 2 + [pltpu.VMEM((total, width), BF16)],
-        4 * total * width * units,
-        2 * (total * width + 2 * width * units + 2 * total * units),
+        [pltpu.VMEM((total, width), BF16)],
     )(*inputs, gate_w, up_w, *after)
 
 
 def d_hidden_kernel(*refs, blocks):
     down_w = refs[blocks]
-    out, held, sems, rows = refs[-4:]
-    copies = stream(down_w, held, sems, 0)
+    out, rows = refs[-2:]
     rows[...] = joined(refs[:blocks])
-    for tile, copy in enumerate(copies):
-        part = slice(tile * TILE, (tile + 1) * TILE)
-        copy.wait()
-        out[:, part] = dot(rows[...], held[part, :], 1, 1).astype(BF16)
+    for start in range(0, out.shape[1], TILE):
+        part = slice(start, start + TILE)
+        out[:, part] = dot(rows[...], down_w[part, :], 1, 1).astype(BF16)
 
 
 def d_hidden(inputs, down_w, after=()):
@@ -316,11 +300,10 @@
     return call(
         functools.partial(d_hidden_kernel, blocks=blocks),
         array(total, units),
-        [VMEM] * blocks + [HBM] + [AFTER] * len(after),
+        [VMEM] * (blocks + 1) + [AFTER] * len(after),
         VMEM,
-        held_weight(down_w.shape, 0) + [pltpu.VMEM((total, width), BF16)],
-        2 * total * width * units,
-        2 * (total * width + width * units + total * units),
+        [pltpu.VMEM((total, width), BF16)],
+        weight=1000,
     )(*inputs, down_w, *after)
 
 
@@ -336,37 +319,32 @@
     return gate, up
 
 
-def down_kernel(own_ref, other_ref, down_w, *refs):
-    outs, (held, sems, hidden) = refs[:-3], refs[-3:]
-    copies = stream(down_w, held, sems, 1)
+def down_kernel(own_ref, other_ref, down_w, *refs, blocks):
+    outs, hidden = refs[-1 - blocks : -1], refs[-1]
     for start in range(0, hidden.shape[1], TILE):
         part = slice(start, start + TILE)
         gate, up = gate_and_up(own_ref, other_ref, part)
         hidden[:, part] = (gate * jax.nn.sigmoid(gate) * up).astype(BF16)
-    for tile, copy in enumerate(copies):
-        part = slice(tile * TILE, (tile + 1) * TILE)
-        copy.wait()
-        scatter_tile(dot(hidden[...], held[:, part], 1, 0).astype(BF16), outs, part)
-
-
-def down(own, other, down_w, blocks):
+    for start in range(0, outs[0].shape[1], TILE):
+        part = slice(start, start + TILE)
+        scatter_tile(dot(hidden[...], down_w[:, part], 1, 0).astype(BF16), outs, part)
+
+
+def down(own, other, down_w, blocks, after=()):
     _, total, units = own.shape
     width, rows = down_w.shape[1], total // blocks
     return call(
-        down_kernel,
+        functools.partial(down_kernel, blocks=blocks),
         [array(rows, width)] * blocks,
-        [VMEM, VMEM, HBM],
+        [VMEM] * 3 + [AFTER] * len(after),
         [VMEM] * blocks,
-        held_weight(down_w.shape, 1) + [pltpu.VMEM((total, units), BF16)],
-        2 * total * width * units,
-        2 * (total * width + width * units + 4 * total * units),
-    )(own, other, down_w)
-
-
-def back_kernel(own_ref, other_ref, own_d, other_d, gate_w, up_w, hidden, d_gate, d_up, *refs):
-    outs, (gate_held, gate_sems, up_held, up_sems) = refs[:-4], refs[-4:]
-    gate_copies = stream(gate_w, gate_held, gate_sems, 0)
-    up_copies = stream(up_w, up_held, up_sems, 0)
+        [pltpu.VMEM((total, units), BF16)],
+    )(own, other, down_w, *after)
+
+
+def back_kernel(
+    own_ref, other_ref, own_d, other_d, gate_w, up_w, hidden, d_gate, d_up, *outs
+):
     for start in range(0, hidden.shape[1], TILE):
         part = slice(start, start + TILE)
         gate, up = gate_and_up(own_ref, other_ref, part)
@@ -376,12 +354,10 @@
         hidden[:, part] = (activated * up).astype(BF16)
         d_up[:, part] = (d_hid * activated).astype(BF16)
         d_gate[:, part] = (d_hid * up * sigmoid * (1.0 + gate * (1.0 - sigmoid))).astype(BF16)
-    for tile in range(len(gate_copies)):
-        part = slice(tile * TILE, (tile + 1) * TILE)
-        gate_copies[tile].wait()
-        total = dot(d_gate[...], gate_held[part, :], 1, 1)
-        up_copies[tile].wait()
-        total += dot(d_up[...], up_held[part, :], 1, 1)
+    for start in range(0, outs[0].shape[1], TILE):
+        part = slice(start, start + TILE)
+        total = dot(d_gate[...], gate_w[part, :], 1, 1)
+        total += dot(d_up[...], up_w[part, :], 1, 1)
         scatter_tile(total.astype(BF16), outs, part)
 
 
@@ -391,11 +367,9 @@
     return call(
         back_kernel,
         [array(total, units)] * 3 + [array(rows, width)] * blocks,
-        [VMEM] * 4 + [HBM] * 2,
+        [VMEM] * 6,
         [VMEM] * (3 + blocks),
-        held_weight(gate_w.shape, 0) * 2,
-        4 * total * width * units,
-        2 * (total * width + 2 * width * units + 9 * total * units),
+        [],
     )(own, other, own_d, other_d, gate_w, up_w)
 
 
@@ -431,8 +405,6 @@
         [VMEM] * (3 + 2 * blocks) + [AFTER] * len(after),
         [by_column, by_column, pl.BlockSpec((TILE, width), lambda i: (i, 0))],
         [pltpu.VMEM((width, total), BF16), pltpu.VMEM((total, width), BF16)],
-        6 * total * width * units,
-        2 * (2 * total * width + 3 * width * units + 3 * total * units),
         grid=(units // TILE,),
     )(hidden, d_gate, d_up, *inputs, *cots, *after)
 
@@ -470,8 +442,6 @@
         [VMEM, VMEM],
         HBM,
         [pltpu.SemaphoreType.DMA((2,))],
-        0,
-        8 * tokens * width,
     )(mine, rest)
 
 
@@ -486,35 +456,35 @@
     rows = (2 * capacity + 15) // 16 * 16
     relative = n_expert <= 8
     plan = Plan(n_expert, rows, group, capacity, tokens, relative)
-    gate_w, up_w, down_w = in_hbm(w_gate[0, 0]), in_hbm(w_up[0, 0]), in_hbm(w_down[0, 0])
     row_b, row_f = 0, META // 2
 
-    own_x, send_x = pack(
-        in_hbm(x_bwd[0]),
+    own_x, send_x, own_f, own_dy, send_rest = pack(
+        *[in_hbm(value[0]) for value in (x_bwd, x_fwd, dy_bwd)],
         *[in_hbm(value[0].T) for value in (ids_bwd, route_bwd, ids_fwd, route_fwd)],
     )
     other_x = exchange(send_x, "dp", 1)
-    own_f, send_f, own_dy, send_dy = cut(in_hbm(x_fwd[0]), in_hbm(dy_bwd[0]))
-    other_f = exchange(send_f, "dp", 1)
-    other_dy = exchange(send_dy, "dp", 1)
+    other_rest = exchange(send_rest, "dp", 1)
     metas = (own_x, other_x)
-    sent_x = dispatch(metas, own_x, other_x, plan, row_b, False, after=(own_f,))
+    sent_x = dispatch(metas, own_x, other_x, plan, row_b, 0, False)
     rows_b = to_experts(sent_x, relative)
-    sent_f = dispatch(metas, own_f, other_f, plan, row_f, False, after=sent_x[:1])
+    sent_f = dispatch(metas, own_f, other_rest, plan, row_f, 0, False, after=sent_x[:1])
     rows_f = to_experts(sent_f, relative)
-    sent_dy = dispatch(metas, own_dy, other_dy, plan, row_b, True, after=sent_f[:1])
+    gate_w, up_w, down_w = load(
+        [in_hbm(weight[0, 0]) for weight in (w_gate, w_up, w_down)], after=sent_f[:1]
+    )
+    sent_dy = dispatch(
+        metas, own_dy, other_rest, plan, row_b, tokens, True, after=(in_vmem(down_w),)
+    )
     cots_b = to_experts(sent_dy, relative)
 
     part_b = gate_up(rows_b, gate_w, up_w, after=sent_dy[:1])
     part_b_other = exchange(part_b, "dp", 1)
-
     part_f = gate_up(rows_f, gate_w, up_w, after=(part_b,))
     part_f_other = exchange(part_f, "dp", 1)
-    down_blocks = down(part_f, part_f_other, down_w, n_expert)
+    part_d = d_hidden(cots_b, down_w, after=(part_f,))
+    part_d_other = exchange(part_d, "dp", 1)
+    down_blocks = down(part_f, part_f_other, down_w, n_expert, after=(part_d,))
     returned_f = to_experts(down_blocks, relative)
-
-    part_d = d_hidden(cots_b, down_w, after=down_blocks[:1])
-    part_d_other = exchange(part_d, "dp", 1)
     hidden, d_gate, d_up, *back_blocks = back(
         part_b, part_b_other, part_d, part_d_other, gate_w, up_w, n_expert
     )

time: 106 us -> 94.9 us (0.90)
  Pallas kernels: 45.5 us -> 29.8 us
  waiting for transfers between devices: 32.1 us -> 35.3 us
  starting transfers between devices: 27.4 us -> 28.7 us
    pallas_call x2, Pallas kernels: 14.4 us -> 5.18 us  [gate_up(): call(functools.partial(gate_up_kernel, blocks=blocks), array(2, total, un...]
    pallas_call x1, Pallas kernels: 7.46 us -> 3.2 us  [back(): call(back_kernel, [array(total, units)] * 3 + [array(rows, width)] * bloc...]
    pallas_call x1, Pallas kernels: 4.31 us -> 1.38 us  [d_hidden(): call(functools.partial(d_hidden_kernel, blocks=blocks), array(total, unit...]
    ppermute x21 -> x20, waiting for transfers between devices: 21.9 us -> 24.4 us  [exchange(): lax.ppermute(value, axis, [(source, source ^ mask) for source in range(co...]
    ppermute x21 -> x20, starting transfers between devices: 23.1 us -> 24.5 us  [exchange(): lax.ppermute(value, axis, [(source, source ^ mask) for source in range(co...]
  transfers between devices with their start and end apart: 25 -> 24, of which waited for: 11 -> 13; matrix products, arithmetic and copies ran while one was open for 0% -> 0% of each run, Pallas kernels for 34% -> 29%
where the time goes in v3:
time: 94.9 us; the launch traced here: 94.8 us
  waiting for transfers between devices  35.3 us (37%)
  Pallas kernels  29.8 us (31%)
  starting transfers between devices  28.7 us (30%)
    ppermute x20, starting transfers between devices, exchange(): lax.ppermute(value, axis, [(source, source ^ mask) for source in range(co...  24.5 us
    ppermute x20, waiting for transfers between devices, exchange(): lax.ppermute(value, axis, [(source, source ^ mask) for source in range(co...  24.4 us
    ppermute x4, waiting for transfers between devices, section_shift(): return lax.ppermute(value, ('section', 'dp'), pairs)  10.9 us
    pallas_call x1, Pallas kernels, grads(): call(functools.partial(grad_kernel, blocks=blocks), [pltpu.HBM((width, un...  7.86 us
    pallas_call x2, Pallas kernels, gate_up(): call(functools.partial(gate_up_kernel, blocks=blocks), array(2, total, un...  5.18 us
    pallas_call x1, Pallas kernels, load(): call(functools.partial(load_kernel, count=len(weights)), [array(*weight.s...  4.23 us
    ppermute x4, starting transfers between devices, section_shift(): return lax.ppermute(value, ('section', 'dp'), pairs)  4.22 us
    pallas_call x1, Pallas kernels, back(): call(back_kernel, [array(total, units)] * 3 + [array(rows, width)] * bloc...  3.2 us
  transfers between devices with their start and end apart: 24, of which 13 were waited for; matrix products, arithmetic and copies ran while one was open for 0% of the time, Pallas kernels for 29%

profile of v3, /device:TPU:0, one launch (start us, length us, event | category | flops | bytes accessed | tf_op | source)
XLA Modules:
  0.0 94.8 jit_solution(12914260938420484547)
XLA Ops:
  0.6 1.6 %shard_map.137 = (bf16[80,1792]{1,0:T(8,128)(2,1)S(1)}, bf16[80,1792]{1,0:T(8,128)(2,1)S(1)}, bf16[64,1792]{1,0:T(8,128)(2,1)S(1)}, bf16[64,1792]{1,0:T(8,128)(2,1)S(1)}, bf16[128,1792]{1,0:T(8,128)(2,1)S(1)}) custom-call(bf16[64,3584]{1,0:T(8,128)(2,1)} %bitcast.29, bf16[64,3584]{1,0:T(8,128)(2,1)} %bitcast.30, bf16[64,3584]{1,0:T(8,128)(2,1)} %bitcast.31, ...), custom_call_target="tpu_custom_call" | custom-call | flops 10000000 | bytes 1 | tf_op jit(solution)/shard_map/pallas_call | solution.py:123
  2.8 1.8 %collective-permute-done.other_meta.other_ref = bf16[80,1792]{1,0:T(8,128)(2,1)S(1)} collective-permute-done((bf16[80,1792]{1,0:T(8,128)(2,1)S(1)}, bf16[80,1792]{1,0:T(8,128)(2,1)S(1)}, u32[]{:S(2)}, u32[]{:S(2)}) %collective-permute-start) | collective-permute-done | bytes 286752 | tf_op jit(solution)/shard_map/ppermute | solution.py:22
  5.2 2.9 %collective-permute-start.5 = (bf16[80,1792]{1,0:T(8,128)(2,1)S(1)}, bf16[80,1792]{1,0:T(8,128)(2,1)S(1)}, u32[]{:S(2)}, u32[]{:S(2)}) collective-permute-start(bf16[80,1792]{1,0:T(8,128)(2,1)S(1)} %get-tuple-element.54), channel_id=1, source_target_pairs={{0,2},{2,0},{4,6},{6,4},{1,3},{3,1},{5,7},{7,5},{8,10},{10,8},{12,... | collective-permute-start | bytes 860168 | tf_op jit(solution)/shard_map/ppermute | solution.py:22
  8.1 1.5 %collective-permute-start.6 = (bf16[80,1792]{1,0:T(8,128)(2,1)S(1)}, bf16[80,1792]{1,0:T(8,128)(2,1)S(1)}, u32[]{:S(2)}, u32[]{:S(2)}) collective-permute-start(bf16[80,1792]{1,0:T(8,128)(2,1)S(1)} %get-tuple-element.55), channel_id=1, source_target_pairs={{0,4},{2,6},{4,0},{6,2},{1,5},{3,7},{5,1},{7,3},{8,12},{10,14},{12... | collective-permute-start | bytes 860168 | tf_op jit(solution)/shard_map/ppermute | solution.py:22
  10.2 2.0 %collective-permute-start.2 = (bf16[80,1792]{1,0:T(8,128)(2,1)S(1)}, bf16[80,1792]{1,0:T(8,128)(2,1)S(1)}, u32[]{:S(2)}, u32[]{:S(2)}) collective-permute-start(bf16[80,1792]{1,0:T(8,128)(2,1)S(1)} %get-tuple-element.49), channel_id=1, source_target_pairs={{0,2},{2,0},{4,6},{6,4},{1,3},{3,1},{5,7},{7,5},{8,10},{10,8},{12,... | collective-permute-start | bytes 860168 | tf_op jit(solution)/shard_map/ppermute | solution.py:22
  12.3 1.5 %collective-permute-start.3 = (bf16[80,1792]{1,0:T(8,128)(2,1)S(1)}, bf16[80,1792]{1,0:T(8,128)(2,1)S(1)}, u32[]{:S(2)}, u32[]{:S(2)}) collective-permute-start(bf16[80,1792]{1,0:T(8,128)(2,1)S(1)} %get-tuple-element.50), channel_id=1, source_target_pairs={{0,4},{2,6},{4,0},{6,2},{1,5},{3,7},{5,1},{7,3},{8,12},{10,14},{12... | collective-permute-start | bytes 860168 | tf_op jit(solution)/shard_map/ppermute | solution.py:22
  13.8 2.0 %collective-permute-done.5.refs_1_ = bf16[80,1792]{1,0:T(8,128)(2,1)S(1)} collective-permute-done((bf16[80,1792]{1,0:T(8,128)(2,1)S(1)}, bf16[80,1792]{1,0:T(8,128)(2,1)S(1)}, u32[]{:S(2)}, u32[]{:S(2)}) %collective-permute-start.5) | collective-permute-done | bytes 286752 | tf_op jit(solution)/shard_map/ppermute | solution.py:22
  15.7 3.0 %collective-permute-start.4 = (bf16[80,1792]{1,0:T(8,128)(2,1)S(1)}, bf16[80,1792]{1,0:T(8,128)(2,1)S(1)}, u32[]{:S(2)}, u32[]{:S(2)}) collective-permute-start(bf16[80,1792]{1,0:T(8,128)(2,1)S(1)} %get-tuple-element.51), channel_id=1, source_target_pairs={{0,6},{2,4},{4,2},{6,0},{1,7},{3,5},{5,3},{7,1},{8,14},{10,12},{12... | collective-permute-start | bytes 860168 | tf_op jit(solution)/shard_map/ppermute | solution.py:22
  18.7 4.2 %shard_map.140 = (bf16[1792,1024]{1,0:T(8,128)(2,1)S(1)}, bf16[1792,1024]{1,0:T(8,128)(2,1)S(1)}, bf16[1024,1792]{1,0:T(8,128)(2,1)S(1)}) custom-call(bf16[1792,1024]{1,0:T(8,128)(2,1)} %bitcast.23, bf16[1792,1024]{1,0:T(8,128)(2,1)} %bitcast.24, bf16[1024,1792]{1,0:T(8,128)(2,1)} %bitcast.25, bf16[80,1792]{1,0:T(8,128)(2,1)S(1)} %get-tuple-element.48.refs_3_.refs_0_), custom_call_target="tpu_custom_call" | custom-call | flops 10000000 | bytes 1 | tf_op jit(solution)/shard_map/pallas_call | solution.py:146
  24.2 1.8 %collective-permute-start.10 = (bf16[80,1792]{1,0:T(8,128)(2,1)S(1)}, bf16[80,1792]{1,0:T(8,128)(2,1)S(1)}, u32[]{:S(2)}, u32[]{:S(2)}) collective-permute-start(bf16[80,1792]{1,0:T(8,128)(2,1)S(1)} %get-tuple-element.61), channel_id=1, source_target_pairs={{0,4},{2,6},{4,0},{6,2},{1,5},{3,7},{5,1},{7,3},{8,12},{10,14},{12... | collective-permute-start | bytes 860168 | tf_op jit(solution)/shard_map/ppermute | solution.py:22
  26.0 2.0 %collective-permute-done.2.refs_1_ = bf16[80,1792]{1,0:T(8,128)(2,1)S(1)} collective-permute-done((bf16[80,1792]{1,0:T(8,128)(2,1)S(1)}, bf16[80,1792]{1,0:T(8,128)(2,1)S(1)}, u32[]{:S(2)}, u32[]{:S(2)}) %collective-permute-start.2) | collective-permute-done | bytes 286752 | tf_op jit(solution)/shard_map/ppermute | solution.py:22
  28.1 3.0 %collective-permute-start.11 = (bf16[80,1792]{1,0:T(8,128)(2,1)S(1)}, bf16[80,1792]{1,0:T(8,128)(2,1)S(1)}, u32[]{:S(2)}, u32[]{:S(2)}) collective-permute-start(bf16[80,1792]{1,0:T(8,128)(2,1)S(1)} %get-tuple-element.62), channel_id=1, source_target_pairs={{0,6},{2,4},{4,2},{6,0},{1,7},{3,5},{5,3},{7,1},{8,14},{10,12},{12... | collective-permute-start | bytes 860168 | tf_op jit(solution)/shard_map/ppermute | solution.py:22
  31.1 2.6 %shard_map.142.refs_6_.own_ref = bf16[2,320,1024]{2,1,0:T(8,128)(2,1)S(1)} custom-call(bf16[80,1792]{1,0:T(8,128)(2,1)S(1)} %get-tuple-element.47.refs_0_, bf16[80,1792]{1,0:T(8,128)(2,1)S(1)} %collective-permute-done.5.refs_1_, bf16[80,1792]{1,0:T(8,128)(2,1)S(1)} %collective-permute-done.6.refs_2_, bf16[80,1792]{1,0:T(8,128)(2,1)S(1)} %collective-permute-done.7.refs_3_, ...), custom_call_target="tpu_custom_call" | custom-call | flops 10000000 | bytes 1 | tf_op jit(solution)/shard_map/pallas_call | solution.py:279
  33.6 2.6 %collective-permute-done.3.refs_2_ = bf16[80,1792]{1,0:T(8,128)(2,1)S(1)} collective-permute-done((bf16[80,1792]{1,0:T(8,128)(2,1)S(1)}, bf16[80,1792]{1,0:T(8,128)(2,1)S(1)}, u32[]{:S(2)}, u32[]{:S(2)}) %collective-permute-start.3) | collective-permute-done | bytes 286752 | tf_op jit(solution)/shard_map/ppermute | solution.py:22
  36.3 2.6 %shard_map.143.refs_5_.own_ref = bf16[2,320,1024]{2,1,0:T(8,128)(2,1)S(1)} custom-call(bf16[80,1792]{1,0:T(8,128)(2,1)S(1)} %get-tuple-element.48.refs_3_.refs_0_, bf16[80,1792]{1,0:T(8,128)(2,1)S(1)} %collective-permute-done.2.refs_1_, bf16[80,1792]{1,0:T(8,128)(2,1)S(1)} %collective-permute-done.3.refs_2_, ...), custom_call_target="tpu_custom_call" | custom-call | flops 10000000 | bytes 1 | tf_op jit(solution)/shard_map/pallas_call | solution.py:279
  40.4 7.0 %collective-permute-done.10.refs_2_.refs_6_ = bf16[80,1792]{1,0:T(8,128)(2,1)S(1)} collective-permute-done((bf16[80,1792]{1,0:T(8,128)(2,1)S(1)}, bf16[80,1792]{1,0:T(8,128)(2,1)S(1)}, u32[]{:S(2)}, u32[]{:S(2)}) %collective-permute-start.10) | collective-permute-done | bytes 286752 | tf_op jit(solution)/shard_map/ppermute | solution.py:22
  48.9 1.7 %shard_map.145 = (bf16[80,1792]{1,0:T(8,128)(2,1)S(1)}, bf16[80,1792]{1,0:T(8,128)(2,1)S(1)}, bf16[80,1792]{1,0:T(8,128)(2,1)S(1)}, bf16[80,1792]{1,0:T(8,128)(2,1)S(1)}) custom-call(bf16[2,320,1024]{2,1,0:T(8,128)(2,1)S(1)} %shard_map.143.refs_5_.own_ref, bf16[2,320,1024]{2,1,0:T(8,128)(2,1)S(1)} %collective-permute-done.8.other_ref, ...), custom_call_target="tpu_custom_call" | custom-call | flops 10000000 | bytes 1 | tf_op jit(solution)/shard_map/pallas_call | solution.py:336
  54.1 3.2 %shard_map.146 = (bf16[320,1024]{1,0:T(8,128)(2,1)S(1)}, bf16[320,1024]{1,0:T(8,128)(2,1)S(1)}, bf16[320,1024]{1,0:T(8,128)(2,1)S(1)}, bf16[80,1792]{1,0:T(8,128...) custom-call(bf16[2,320,1024]{2,1,0:T(8,128)(2,1)S(1)} %shard_map.142.refs_6_.ow, ...), custom_call_target="tpu_custom_call" | custom-call | flops 10000000 | bytes 1 | tf_op jit(solution)/shard_map/pallas_call | solution.py:367
  61.7 5.5 %collective-permute-done.13.refs_2_ = bf16[80,1792]{1,0:T(8,128)(2,1)S(1)} collective-permute-done((bf16[80,1792]{1,0:T(8,128)(2,1)S(1)}, bf16[80,1792]{1,0:T(8,128)(2,1)S(1)}, u32[]{:S(2)}, u32[]{:S(2)}) %collective-permute-start.13) | collective-permute-done | bytes 286752 | tf_op jit(solution)/shard_map/ppermute | solution.py:22
  68.2 1.8 %collective-permute-start.17 = (bf16[64,1792]{1,0:T(8,128)(2,1)S(1)}, bf16[64,1792]{1,0:T(8,128)(2,1)S(1)}, u32[]{:S(2)}, u32[]{:S(2)}) collective-permute-start(bf16[64,1792]{1,0:T(8,128)(2,1)S(1)} %get-tuple-element.68.refs_8_), channel_id=1, source_target_pairs={{0,8},{1,9},{8,16},{9,17},{16,24},{17,25},{24,0},{25,1},{2,10},{3,... | collective-permute-start | bytes 688136 | tf_op jit(solution)/shard_map/ppermute | solution.py:32
  70.3 7.9 %shard_map.149 = (bf16[1792,1024]{1,0:T(8,128)(2,1)}, bf16[1792,1024]{1,0:T(8,128)(2,1)}, bf16[1024,1792]{1,0:T(8,128)(2,1)}) custom-call(bf16[320,1024]{1,0:T(8,128)(2,1)S(1)} %get-tuple-element.73.hidden, bf16[320,1024]{1,0:T(8,128)(2,1)S(1)} %get-tuple-element.74.d_gate, bf16[320,1024]{1,0:T(8,128)(2,1)S(1)} %get-tuple-element.75.d_up, ...), custom_call_target="tpu_custom_call" | custom-call | flops 10000000 | bytes 1 | tf_op jit(solution)/shard_map/pallas_call | solution.py:398
  79.9 1.6 %collective-permute-start.22 = (bf16[64,1792]{1,0:T(8,128)(2,1)S(1)}, bf16[64,1792]{1,0:T(8,128)(2,1)S(1)}, u32[]{:S(2)}, u32[]{:S(2)}) collective-permute-start(bf16[64,1792]{1,0:T(8,128)(2,1)S(1)} %get-tuple-element.77), channel_id=1, source_target_pairs={{0,8},{1,9},{8,16},{9,17},{16,24},{17,25},{24,0},{25,1},{2,10},{3,... | collective-permute-start | bytes 688136 | tf_op jit(solution)/shard_map/ppermute | solution.py:32
  82.9 7.3 %collective-permute-done.22.mine_ref = bf16[64,1792]{1,0:T(8,128)(2,1)S(1)} collective-permute-done((bf16[64,1792]{1,0:T(8,128)(2,1)S(1)}, bf16[64,1792]{1,0:T(8,128)(2,1)S(1)}, u32[]{:S(2)}, u32[]{:S(2)}) %collective-permute-start.22) | collective-permute-done | bytes 229408 | tf_op jit(solution)/shard_map/ppermute | solution.py:32
  90.2 3.6 %collective-permute-done.23.rest_ref = bf16[64,1792]{1,0:T(8,128)(2,1)S(1)} collective-permute-done((bf16[64,1792]{1,0:T(8,128)(2,1)S(1)}, bf16[64,1792]{1,0:T(8,128)(2,1)S(1)}, u32[]{:S(2)}, u32[]{:S(2)}) %collective-permute-start.23) | collective-permute-done | bytes 229408 | tf_op jit(solution)/shard_map/ppermute | solution.py:32
  (39 shorter events, 19.0 us)
Async XLA Ops:
  2.2 7.4 %collective-permute-start.1 = (bf16[128,1792]{1,0:T(8,128)(2,1)S(1)}, bf16[128,1792]{1,0:T(8,128)(2,1)S(1)}, u32[]{:S(2)}, u32[]{:S(2)}) collective-permute-start(bf16[128,1792]{1,0:T(8,128)(2,1)S(1)} %get-tuple-element.46), channel_id=1, source_target_pairs={{0,1},{1,0},{2,3},{3,2},{4,5},{5,4},{6,7},{7,6},{8,9},{9,8},{10,11... | collective-permute-start | bytes 1376264 | tf_op jit(solution)/shard_map/ppermute | solution.py:22
  2.7 1.9 %collective-permute-start = (bf16[80,1792]{1,0:T(8,128)(2,1)S(1)}, bf16[80,1792]{1,0:T(8,128)(2,1)S(1)}, u32[]{:S(2)}, u32[]{:S(2)}) collective-permute-start(bf16[80,1792]{1,0:T(8,128)(2,1)S(1)} %get-tuple-element.44), channel_id=1, source_target_pairs={{0,1},{1,0},{2,3},{3,2},{4,5},{5,4},{6,7},{7,6},{8,9},{9,8},{10,11... | collective-permute-start | bytes 860168 | tf_op jit(solution)/shard_map/ppermute | solution.py:22
  5.2 10.6 %collective-permute-start.5 = (bf16[80,1792]{1,0:T(8,128)(2,1)S(1)}, bf16[80,1792]{1,0:T(8,128)(2,1)S(1)}, u32[]{:S(2)}, u32[]{:S(2)}) collective-permute-start(bf16[80,1792]{1,0:T(8,128)(2,1)S(1)} %get-tuple-element.54), channel_id=1, source_target_pairs={{0,2},{2,0},{4,6},{6,4},{1,3},{3,1},{5,7},{7,5},{8,10},{10,8},{12,... | collective-permute-start | bytes 860168 | tf_op jit(solution)/shard_map/ppermute | solution.py:22
  8.1 15.9 %collective-permute-start.6 = (bf16[80,1792]{1,0:T(8,128)(2,1)S(1)}, bf16[80,1792]{1,0:T(8,128)(2,1)S(1)}, u32[]{:S(2)}, u32[]{:S(2)}) collective-permute-start(bf16[80,1792]{1,0:T(8,128)(2,1)S(1)} %get-tuple-element.55), channel_id=1, source_target_pairs={{0,4},{2,6},{4,0},{6,2},{1,5},{3,7},{5,1},{7,3},{8,12},{10,14},{12... | collective-permute-start | bytes 860168 | tf_op jit(solution)/shard_map/ppermute | solution.py:22
  9.6 14.6 %collective-permute-start.7 = (bf16[80,1792]{1,0:T(8,128)(2,1)S(1)}, bf16[80,1792]{1,0:T(8,128)(2,1)S(1)}, u32[]{:S(2)}, u32[]{:S(2)}) collective-permute-start(bf16[80,1792]{1,0:T(8,128)(2,1)S(1)} %get-tuple-element.56), channel_id=1, source_target_pairs={{0,6},{2,4},{4,2},{6,0},{1,7},{3,5},{5,3},{7,1},{8,14},{10,12},{12... | collective-permute-start | bytes 860168 | tf_op jit(solution)/shard_map/ppermute | solution.py:22
  10.2 17.8 %collective-permute-start.2 = (bf16[80,1792]{1,0:T(8,128)(2,1)S(1)}, bf16[80,1792]{1,0:T(8,128)(2,1)S(1)}, u32[]{:S(2)}, u32[]{:S(2)}) collective-permute-start(bf16[80,1792]{1,0:T(8,128)(2,1)S(1)} %get-tuple-element.49), channel_id=1, source_target_pairs={{0,2},{2,0},{4,6},{6,4},{1,3},{3,1},{5,7},{7,5},{8,10},{10,8},{12,... | collective-permute-start | bytes 860168 | tf_op jit(solution)/shard_map/ppermute | solution.py:22
  12.3 24.0 %collective-permute-start.3 = (bf16[80,1792]{1,0:T(8,128)(2,1)S(1)}, bf16[80,1792]{1,0:T(8,128)(2,1)S(1)}, u32[]{:S(2)}, u32[]{:S(2)}) collective-permute-start(bf16[80,1792]{1,0:T(8,128)(2,1)S(1)} %get-tuple-element.50), channel_id=1, source_target_pairs={{0,4},{2,6},{4,0},{6,2},{1,5},{3,7},{5,1},{7,3},{8,12},{10,14},{12... | collective-permute-start | bytes 860168 | tf_op jit(solution)/shard_map/ppermute | solution.py:22
  15.7 20.5 %collective-permute-start.4 = (bf16[80,1792]{1,0:T(8,128)(2,1)S(1)}, bf16[80,1792]{1,0:T(8,128)(2,1)S(1)}, u32[]{:S(2)}, u32[]{:S(2)}) collective-permute-start(bf16[80,1792]{1,0:T(8,128)(2,1)S(1)} %get-tuple-element.51), channel_id=1, source_target_pairs={{0,6},{2,4},{4,2},{6,0},{1,7},{3,5},{5,3},{7,1},{8,14},{10,12},{12... | collective-permute-start | bytes 860168 | tf_op jit(solution)/shard_map/ppermute | solution.py:22
  24.0 16.4 %collective-permute-start.9 = (bf16[80,1792]{1,0:T(8,128)(2,1)S(1)}, bf16[80,1792]{1,0:T(8,128)(2,1)S(1)}, u32[]{:S(2)}, u32[]{:S(2)}) collective-permute-start(bf16[80,1792]{1,0:T(8,128)(2,1)S(1)} %get-tuple-element.60), channel_id=1, source_target_pairs={{0,2},{2,0},{4,6},{6,4},{1,3},{3,1},{5,7},{7,5},{8,10},{10,8},{12,... | collective-permute-start | bytes 860168 | tf_op jit(solution)/shard_map/ppermute | solution.py:22
  24.2 23.2 %collective-permute-start.10 = (bf16[80,1792]{1,0:T(8,128)(2,1)S(1)}, bf16[80,1792]{1,0:T(8,128)(2,1)S(1)}, u32[]{:S(2)}, u32[]{:S(2)}) collective-permute-start(bf16[80,1792]{1,0:T(8,128)(2,1)S(1)} %get-tuple-element.61), channel_id=1, source_target_pairs={{0,4},{2,6},{4,0},{6,2},{1,5},{3,7},{5,1},{7,3},{8,12},{10,14},{12... | collective-permute-start | bytes 860168 | tf_op jit(solution)/shard_map/ppermute | solution.py:22
  28.1 19.4 %collective-permute-start.11 = (bf16[80,1792]{1,0:T(8,128)(2,1)S(1)}, bf16[80,1792]{1,0:T(8,128)(2,1)S(1)}, u32[]{:S(2)}, u32[]{:S(2)}) collective-permute-start(bf16[80,1792]{1,0:T(8,128)(2,1)S(1)} %get-tuple-element.62), channel_id=1, source_target_pairs={{0,6},{2,4},{4,2},{6,0},{1,7},{3,5},{5,3},{7,1},{8,14},{10,12},{12... | collective-permute-start | bytes 860168 | tf_op jit(solution)/shard_map/ppermute | solution.py:22
  38.9 10.0 %collective-permute-start.8 = (bf16[2,320,1024]{2,1,0:T(8,128)(2,1)S(1)}, bf16[2,320,1024]{2,1,0:T(8,128)(2,1)S(1)}, u32[]{:S(2)}, u32[]{:S(2)}) collective-permute-start(bf16[2,320,1024]{2,1,0:T(8,128)(2,1)S(1)} %shard_map.143.refs_5_.own_ref), channel_id=1, source_target_pairs={{0,1},{1,0},{2,3},{3,2},{4,5},{5,4},{6,7},{7,6},{8,9},{9,8},{10,11... | collective-permute-start | bytes 3932168 | tf_op jit(solution)/shard_map/ppermute | solution.py:22
  39.0 15.2 %collective-permute-start.15 = (bf16[2,320,1024]{2,1,0:T(8,128)(2,1)S(1)}, bf16[2,320,1024]{2,1,0:T(8,128)(2,1)S(1)}, u32[]{:S(2)}, u32[]{:S(2)}) collective-permute-start(bf16[2,320,1024]{2,1,0:T(8,128)(2,1)S(1)} %shard_map.142.refs_6_.own_ref), channel_id=1, source_target_pairs={{0,1},{1,0},{2,3},{3,2},{4,5},{5,4},{6,7},{7,6},{8,9},{9,8},{10,11... | collective-permute-start | bytes 3932168 | tf_op jit(solution)/shard_map/ppermute | solution.py:22
  48.8 5.3 %collective-permute-start.16 = (bf16[320,1024]{1,0:T(8,128)(2,1)S(1)}, bf16[320,1024]{1,0:T(8,128)(2,1)S(1)}, u32[]{:S(2)}, u32[]{:S(2)}) collective-permute-start(bf16[320,1024]{1,0:T(8,128)(2,1)S(1)} %shard_map.144.refs_0_.own_d), channel_id=1, source_target_pairs={{0,1},{1,0},{2,3},{3,2},{4,5},{5,4},{6,7},{7,6},{8,9},{9,8},{10,11... | collective-permute-start | bytes 1966088 | tf_op jit(solution)/shard_map/ppermute | solution.py:22
  50.6 9.7 %collective-permute-start.12 = (bf16[80,1792]{1,0:T(8,128)(2,1)S(1)}, bf16[80,1792]{1,0:T(8,128)(2,1)S(1)}, u32[]{:S(2)}, u32[]{:S(2)}) collective-permute-start(bf16[80,1792]{1,0:T(8,128)(2,1)S(1)} %get-tuple-element.64), channel_id=1, source_target_pairs={{0,2},{2,0},{4,6},{6,4},{1,3},{3,1},{5,7},{7,5},{8,10},{10,8},{12,... | collective-permute-start | bytes 860168 | tf_op jit(solution)/shard_map/ppermute | solution.py:22
  52.0 15.3 %collective-permute-start.13 = (bf16[80,1792]{1,0:T(8,128)(2,1)S(1)}, bf16[80,1792]{1,0:T(8,128)(2,1)S(1)}, u32[]{:S(2)}, u32[]{:S(2)}) collective-permute-start(bf16[80,1792]{1,0:T(8,128)(2,1)S(1)} %get-tuple-element.65), channel_id=1, source_target_pairs={{0,4},{2,6},{4,0},{6,2},{1,5},{3,7},{5,1},{7,3},{8,12},{10,14},{12... | collective-permute-start | bytes 860168 | tf_op jit(solution)/shard_map/ppermute | solution.py:22
  52.7 14.7 %collective-permute-start.14 = (bf16[80,1792]{1,0:T(8,128)(2,1)S(1)}, bf16[80,1792]{1,0:T(8,128)(2,1)S(1)}, u32[]{:S(2)}, u32[]{:S(2)}) collective-permute-start(bf16[80,1792]{1,0:T(8,128)(2,1)S(1)} %get-tuple-element.66), channel_id=1, source_target_pairs={{0,6},{2,4},{4,2},{6,0},{1,7},{3,5},{5,3},{7,1},{8,14},{10,12},{12... | collective-permute-start | bytes 860168 | tf_op jit(solution)/shard_map/ppermute | solution.py:22
  57.3 20.8 %collective-permute-start.19 = (bf16[80,1792]{1,0:T(8,128)(2,1)S(1)}, bf16[80,1792]{1,0:T(8,128)(2,1)S(1)}, u32[]{:S(2)}, u32[]{:S(2)}) collective-permute-start(bf16[80,1792]{1,0:T(8,128)(2,1)S(1)} %get-tuple-element.70), channel_id=1, source_target_pairs={{0,2},{2,0},{4,6},{6,4},{1,3},{3,1},{5,7},{7,5},{8,10},{10,8},{12,... | collective-permute-start | bytes 860168 | tf_op jit(solution)/shard_map/ppermute | solution.py:22
  58.7 19.4 %collective-permute-start.20 = (bf16[80,1792]{1,0:T(8,128)(2,1)S(1)}, bf16[80,1792]{1,0:T(8,128)(2,1)S(1)}, u32[]{:S(2)}, u32[]{:S(2)}) collective-permute-start(bf16[80,1792]{1,0:T(8,128)(2,1)S(1)} %get-tuple-element.71), channel_id=1, source_target_pairs={{0,4},{2,6},{4,0},{6,2},{1,5},{3,7},{5,1},{7,3},{8,12},{10,14},{12... | collective-permute-start | bytes 860168 | tf_op jit(solution)/shard_map/ppermute | solution.py:22
  60.3 19.1 %collective-permute-start.21 = (bf16[80,1792]{1,0:T(8,128)(2,1)S(1)}, bf16[80,1792]{1,0:T(8,128)(2,1)S(1)}, u32[]{:S(2)}, u32[]{:S(2)}) collective-permute-start(bf16[80,1792]{1,0:T(8,128)(2,1)S(1)} %get-tuple-element.72), channel_id=1, source_target_pairs={{0,6},{2,4},{4,2},{6,0},{1,7},{3,5},{5,3},{7,1},{8,14},{10,12},{12... | collective-permute-start | bytes 860168 | tf_op jit(solution)/shard_map/ppermute | solution.py:22
  68.2 13.9 %collective-permute-start.17 = (bf16[64,1792]{1,0:T(8,128)(2,1)S(1)}, bf16[64,1792]{1,0:T(8,128)(2,1)S(1)}, u32[]{:S(2)}, u32[]{:S(2)}) collective-permute-start(bf16[64,1792]{1,0:T(8,128)(2,1)S(1)} %get-tuple-element.68.refs_8_), channel_id=1, source_target_pairs={{0,8},{1,9},{8,16},{9,17},{16,24},{17,25},{24,0},{25,1},{2,10},{3,... | collective-permute-start | bytes 688136 | tf_op jit(solution)/shard_map/ppermute | solution.py:32
  70.1 12.1 %collective-permute-start.18 = (bf16[64,1792]{1,0:T(8,128)(2,1)S(1)}, bf16[64,1792]{1,0:T(8,128)(2,1)S(1)}, u32[]{:S(2)}, u32[]{:S(2)}) collective-permute-start(bf16[64,1792]{1,0:T(8,128)(2,1)S(1)} %get-tuple-element.69), channel_id=1, source_target_pairs={{0,9},{1,8},{8,17},{9,16},{16,25},{17,24},{24,1},{25,0},{2,11},{3,... | collective-permute-start | bytes 688136 | tf_op jit(solution)/shard_map/ppermute | solution.py:32
  79.9 10.3 %collective-permute-start.22 = (bf16[64,1792]{1,0:T(8,128)(2,1)S(1)}, bf16[64,1792]{1,0:T(8,128)(2,1)S(1)}, u32[]{:S(2)}, u32[]{:S(2)}) collective-permute-start(bf16[64,1792]{1,0:T(8,128)(2,1)S(1)} %get-tuple-element.77), channel_id=1, source_target_pairs={{0,8},{1,9},{8,16},{9,17},{16,24},{17,25},{24,0},{25,1},{2,10},{3,... | collective-permute-start | bytes 688136 | tf_op jit(solution)/shard_map/ppermute | solution.py:32
  81.5 12.3 %collective-permute-start.23 = (bf16[64,1792]{1,0:T(8,128)(2,1)S(1)}, bf16[64,1792]{1,0:T(8,128)(2,1)S(1)}, u32[]{:S(2)}, u32[]{:S(2)}) collective-permute-start(bf16[64,1792]{1,0:T(8,128)(2,1)S(1)} %get-tuple-element.78), channel_id=1, source_target_pairs={{0,9},{1,8},{8,17},{9,16},{16,25},{17,24},{24,1},{25,0},{2,11},{3,... | collective-permute-start | bytes 688136 | tf_op jit(solution)/shard_map/ppermute | solution.py:32

commit v4 on v3

v4 whole, which is shorter than its diff:
```python
import functools

import jax
import jax.numpy as jnp
from jax import lax
from jax.experimental import pallas as pl
from jax.experimental.pallas import tpu as pltpu
from jax.sharding import PartitionSpec as P

FF = 1024
TOP = 2
TILE = 256
VMEM_LIMIT = 20 * 1024 * 1024
META = 16
COST = 10**7
F32 = jnp.float32
BF16 = jnp.bfloat16


def exchange(value, axis, mask):
    count = lax.axis_size(axis)
    return lax.ppermute(value, axis, [(source, source ^ mask) for source in range(count)])


def section_shift(value, flip):
    sections, cores = lax.axis_size("section"), lax.axis_size("dp")
    pairs = []
    for section in range(sections):
        for core in range(cores):
            target = ((section + 1) % sections) * cores + (core ^ flip)
            pairs.append((section * cores + core, target))
    return lax.ppermute(value, ("section", "dp"), pairs)


def dot(left, right, left_dim, right_dim):
    return lax.dot_general(
        left, right, (((left_dim,), (right_dim,)), ((), ())), preferred_element_type=F32
    )


VMEM = pl.BlockSpec(memory_space=pltpu.VMEM)
HBM = pl.BlockSpec(memory_space=pltpu.HBM)
AFTER = pl.BlockSpec(memory_space=pl.ANY)


def call(kernel, out_shape, in_specs, out_specs, scratch, grid=(), weight=1, aliases={}):
    return pl.pallas_call(
        kernel,
        out_shape=out_shape,
        grid=grid,
        in_specs=in_specs,
        out_specs=out_specs,
        scratch_shapes=scratch,
        input_output_aliases=aliases,
        compiler_params=pltpu.CompilerParams(vmem_limit_bytes=VMEM_LIMIT),
        cost_estimate=pl.CostEstimate(
            flops=weight * COST, bytes_accessed=1, transcendentals=0
        ),
    )


def array(*shape):
    return jax.ShapeDtypeStruct(shape, BF16)


def in_vmem(value):
    return pltpu.with_memory_space_constraint(value, pltpu.VMEM)


def in_hbm(value):
    return pltpu.with_memory_space_constraint(value, pltpu.HBM)


def halves(value_ref, own_ref, other_ref, sems, first):
    tokens, width = value_ref.shape[0], value_ref.shape[1] // 2
    core = lax.axis_index("dp")
    copies = []
    for place, (half, target) in enumerate(((core, own_ref), (1 - core, other_ref))):
        columns = pl.ds(pl.multiple_of(half * width, 128), width)
        copies.append(
            pltpu.make_async_copy(
                value_ref.at[:, columns], target.at[0:tokens], sems.at[first + place]
            )
        )
    for copy in copies:
        copy.start()
    return copies


def pack_kernel(f_ref, x_ref, dy_ref, *refs):
    sources, outs, (packed, sems), held = refs[:4], refs[4:9], refs[9:11], refs[11:]
    own_f, other_f, own_x, own_dy, other_rest = outs
    tokens = f_ref.shape[0]
    copies = halves(f_ref, own_f, other_f, sems, 0)
    small = [
        pltpu.make_async_copy(source, target, sems.at[6 + place])
        for place, (source, target) in enumerate(zip(sources, held))
    ]
    for copy in small:
        copy.start()
    copies += halves(x_ref, own_x, other_rest.at[0:tokens], sems, 2)
    copies += halves(dy_ref, own_dy, other_rest.at[tokens : 2 * tokens], sems, 4)
    packed[...] = jnp.zeros_like(packed)
    for copy in small:
        copy.wait()
    for start, ids, route in ((0, *held[:2]), (META // 2, *held[2:])):
        packed[start : start + 2, 0:tokens] = ids[...].astype(F32)
        rest = route[...]
        for piece in range(3):
            top = rest.astype(BF16).astype(F32)
            row = start + 2 + 2 * piece
            packed[row : row + 2, 0:tokens] = top
            rest = rest - top
    mine = packed[...]
    lanes = packed.shape[1]
    own_f[tokens : tokens + META, 0:lanes] = mine.astype(BF16)
    other_f[tokens : tokens + META, 0:lanes] = pltpu.roll(mine, tokens, 1).astype(BF16)
    for copy in copies:
        copy.wait()


def pack(f, x, dy, *small):
    tokens, width = f.shape[0], f.shape[1] // 2
    return call(
        pack_kernel,
        [array(tokens + META, width)] * 2 + [array(tokens, width)] * 2 + [array(2 * tokens, width)],
        [HBM] * 7,
        [VMEM] * 5,
        [pltpu.VMEM((META, 2 * tokens), F32), pltpu.SemaphoreType.DMA((10,))]
        + [pltpu.VMEM(value.shape, value.dtype) for value in small],
    )(f, x, dy, *small)


def load_kernel(*refs, count):
    sources, targets, sems = refs[:count], refs[-count - 1 : -1], refs[-1]
    copies = [
        pltpu.make_async_copy(source, target, sems.at[place])
        for place, (source, target) in enumerate(zip(sources, targets))
    ]
    for copy in copies:
        copy.start()
    for copy in copies:
        copy.wait()


def load(weights, after):
    return call(
        functools.partial(load_kernel, count=len(weights)),
        [array(*weight.shape) for weight in weights],
        [HBM] * len(weights) + [AFTER] * len(after),
        [VMEM] * len(weights),
        [pltpu.SemaphoreType.DMA((len(weights),))],
    )(*weights, *after)


class Plan:
    def __init__(self, blocks, part, group, tokens, relative):
        self.blocks, self.part, self.group = blocks, part, group
        self.tokens, self.relative = tokens, relative


def slot_rows(own_meta, other_meta, plan, first_row):
    lanes = 2 * plan.tokens
    padded = max(8, plan.blocks)
    me = lax.axis_index("expert") if plan.relative else 0
    meta = own_meta[plan.tokens : plan.tokens + META, 0:lanes].astype(F32)
    meta = meta + other_meta[plan.tokens : plan.tokens + META, 0:lanes].astype(F32)
    meta = meta[first_row : first_row + META // 2]
    first, second = meta[0:1], meta[1:2]
    route = meta[2:4] + meta[4:6] + meta[6:8]
    row = lax.broadcasted_iota(jnp.int32, (padded, lanes), 0)
    expert = ((row ^ me) // plan.group).astype(F32)
    is_first, is_second = expert == first, expert == second
    named = jnp.where(is_first | is_second, 1.0, 0.0)
    before = lax.broadcasted_iota(jnp.int32, (lanes, lanes), 0)
    after = lax.broadcasted_iota(jnp.int32, (lanes, lanes), 1)
    earlier = (before < after) & ((before < plan.tokens) == (after < plan.tokens))
    position = dot(named.astype(BF16), jnp.where(earlier, 1.0, 0.0).astype(BF16), 1, 0)
    lane = lax.broadcasted_iota(jnp.int32, (padded, lanes), 1)
    slot = position + jnp.where(lane < plan.tokens, 0, plan.part).astype(F32)
    slot = jnp.where(named > 0.5, slot, -1.0)
    return slot, jnp.where(is_first, route[0:1], route[1:2])


def slot_table(slot, block, first, rows):
    index = lax.broadcasted_iota(jnp.int32, (rows, slot.shape[1]), 0) + first
    index = index.astype(F32)
    return jnp.where(index == slot[block : block + 1, :], 1.0, 0.0)


def dispatch_kernel(
    own_meta, other_meta, own_ref, other_ref, *refs, plan, first_row, other_row, weighted, passed
):
    outs = refs[len(refs) - plan.blocks - passed : len(refs) - passed]
    width, tokens = outs[0].shape[1], plan.tokens
    slot, route = slot_rows(own_meta, other_meta, plan, first_row)
    values = jnp.concatenate([own_ref[0:tokens, :], other_ref[other_row : other_row + tokens, :]], axis=0)
    for block in range(plan.blocks):
        table = slot_table(slot, block, 0, 2 * plan.part)
        if weighted:
            scale = jnp.sum(table * route[block : block + 1, :], axis=1, keepdims=True)
        table = table.astype(BF16)
        for start in range(0, width, TILE):
            picked = dot(table, values[:, start : start + TILE], 1, 0)
            if weighted:
                picked = picked * scale
            outs[block][:, start : start + TILE] = picked.astype(BF16)


def dispatch(metas, own, other, plan, first_row, other_row, weighted, after=(), passing=()):
    width = own.shape[1]
    return call(
        functools.partial(
            dispatch_kernel,
            plan=plan,
            first_row=first_row,
            other_row=other_row,
            weighted=weighted,
            passed=len(passing),
        ),
        [array(2 * plan.part, width)] * plan.blocks + [array(*value.shape) for value in passing],
        [VMEM] * (4 + len(passing)) + [AFTER] * len(after),
        [VMEM] * (plan.blocks + len(passing)),
        [],
        aliases={4 + place: plan.blocks + place for place in range(len(passing))},
    )(*metas, own, other, *passing, *after)


def combine_kernel(own_meta, other_meta, *refs, plan, first_row, weighted, other):
    returned, out = refs[: plan.blocks], refs[-1]
    width, tokens = out.shape[1], plan.tokens
    slot, route = slot_rows(own_meta, other_meta, plan, first_row)
    table = []
    for block in range(plan.blocks):
        table.append(slot_table(slot, block, plan.part if other else 0, plan.part))
        if weighted:
            table[block] = table[block] * route[block : block + 1, :]
    table = jnp.concatenate(table, axis=0)
    high = table.astype(BF16)
    low = (table - high.astype(F32)).astype(BF16)
    for start in range(0, width, TILE):
        part = slice(start, start + TILE)
        values = jnp.concatenate([ref[:, part].astype(F32) for ref in returned], axis=0)
        values = values.astype(BF16)
        total = dot(high, values, 0, 0)
        if weighted:
            total += dot(low, values, 0, 0)
        out[:, part] = total[tokens if other else 0 :][:tokens].astype(BF16)


def combine(metas, returned, plan, first_row, weighted, other, after=(), weight=1):
    return call(
        functools.partial(
            combine_kernel, plan=plan, first_row=first_row, weighted=weighted, other=other
        ),
        array(plan.tokens, returned[0].shape[1]),
        [VMEM] * (2 + plan.blocks) + [AFTER] * len(after),
        VMEM,
        [],
        weight=weight,
    )(*metas, *returned, *after)


def joined(refs):
    return jnp.concatenate([ref[...] for ref in refs], axis=0)


def gate_up_kernel(*refs, blocks):
    gate_w, up_w = refs[blocks : blocks + 2]
    out, rows = refs[-2:]
    rows[...] = joined(refs[:blocks])
    for start in range(0, out.shape[2], TILE):
        part = slice(start, start + TILE)
        out[0, :, part] = dot(rows[...], gate_w[:, part], 1, 0).astype(BF16)
        out[1, :, part] = dot(rows[...], up_w[:, part], 1, 0).astype(BF16)


def gate_up(inputs, gate_w, up_w, after=(), weight=1):
    blocks, (rows, width) = len(inputs), inputs[0].shape
    units, total = gate_w.shape[1], blocks * rows
    return call(
        functools.partial(gate_up_kernel, blocks=blocks),
        array(2, total, units),
        [VMEM] * (blocks + 2) + [AFTER] * len(after),
        VMEM,
        [pltpu.VMEM((total, width), BF16)],
        weight=weight,
    )(*inputs, gate_w, up_w, *after)


def d_hidden_kernel(*refs, blocks):
    down_w = refs[blocks]
    out, rows = refs[-2:]
    rows[...] = joined(refs[:blocks])
    for start in range(0, out.shape[1], TILE):
        part = slice(start, start + TILE)
        out[:, part] = dot(rows[...], down_w[part, :], 1, 1).astype(BF16)


def d_hidden(inputs, down_w, after=(), weight=1):
    blocks, (rows, width) = len(inputs), inputs[0].shape
    units, total = down_w.shape[0], blocks * rows
    return call(
        functools.partial(d_hidden_kernel, blocks=blocks),
        array(total, units),
        [VMEM] * (blocks + 1) + [AFTER] * len(after),
        VMEM,
        [pltpu.VMEM((total, width), BF16)],
        weight=weight,
    )(*inputs, down_w, *after)


def scatter_tile(value, outs, columns):
    blocks, part = len(outs) // 2, outs[0].shape[0]
    for place, out in enumerate(outs):
        first = (2 * (place % blocks) + place // blocks) * part
        out[:, columns] = value[first : first + part].astype(BF16)


def total_of(own, other, part):
    own, other = own.astype(F32), other.astype(F32)
    rows = own.shape[0]
    turned = []
    for first in range(0, rows, 2 * part):
        turned += [other[first + part : first + 2 * part], other[first : first + part]]
    return own + jnp.concatenate(turned, axis=0)


def down_kernel(own_ref, other_ref, down_w, *refs, blocks):
    outs, hidden = refs[-1 - 2 * blocks : -1], refs[-1]
    part = outs[0].shape[0]
    for start in range(0, hidden.shape[1], TILE):
        columns = slice(start, start + TILE)
        gate = total_of(own_ref[0, :, columns], other_ref[0, :, columns], part)
        up = total_of(own_ref[1, :, columns], other_ref[1, :, columns], part)
        hidden[:, columns] = (gate * jax.nn.sigmoid(gate) * up).astype(BF16)
    for start in range(0, outs[0].shape[1], TILE):
        columns = slice(start, start + TILE)
        scatter_tile(dot(hidden[...], down_w[:, columns], 1, 0), outs, columns)


def down(own, other, down_w, plan, after=()):
    _, total, units = own.shape
    return call(
        functools.partial(down_kernel, blocks=plan.blocks),
        [array(plan.part, down_w.shape[1])] * (2 * plan.blocks),
        [VMEM] * 3 + [AFTER] * len(after),
        [VMEM] * (2 * plan.blocks),
        [pltpu.VMEM((total, units), BF16)],
    )(own, other, down_w, *after)


def back_kernel(
    own_ref, other_ref, own_d, other_d, gate_w, up_w, hidden, d_gate, d_up, *outs
):
    part = outs[0].shape[0]
    for start in range(0, hidden.shape[1], TILE):
        columns = slice(start, start + TILE)
        gate = total_of(own_ref[0, :, columns], other_ref[0, :, columns], part)
        up = total_of(own_ref[1, :, columns], other_ref[1, :, columns], part)
        d_hid = total_of(own_d[:, columns], other_d[:, columns], part)
        sigmoid = jax.nn.sigmoid(gate)
        activated = gate * sigmoid
        hidden[:, columns] = (activated * up).astype(BF16)
        d_up[:, columns] = (d_hid * activated).astype(BF16)
        d_gate[:, columns] = (
            d_hid * up * sigmoid * (1.0 + gate * (1.0 - sigmoid))
        ).astype(BF16)
    for start in range(0, outs[0].shape[1], TILE):
        columns = slice(start, start + TILE)
        total = dot(d_gate[...], gate_w[columns, :], 1, 1)
        total += dot(d_up[...], up_w[columns, :], 1, 1)
        scatter_tile(total, outs, columns)


def back(own, other, own_d, other_d, gate_w, up_w, plan):
    _, total, units = own.shape
    return call(
        back_kernel,
        [array(total, units)] * 3 + [array(plan.part, gate_w.shape[0])] * (2 * plan.blocks),
        [VMEM] * 6,
        [VMEM] * (3 + 2 * plan.blocks),
        [],
    )(own, other, own_d, other_d, gate_w, up_w)


def grad_in_kernel(d_gate, d_up, *refs, blocks):
    inputs, (grad_gate, grad_up, turned) = refs[:blocks], refs[-3:]

    @pl.when(pl.program_id(0) == 0)
    def _():
        for start in range(0, turned.shape[0], TILE):
            part = slice(start, start + TILE)
            piece = jnp.concatenate([ref[:, part] for ref in inputs], axis=0)
            turned[part, :] = piece.T

    part = pl.ds(pl.multiple_of(pl.program_id(0) * TILE, TILE), TILE)
    grad_gate[...] = dot(turned[...], d_gate[:, part], 1, 0).astype(BF16)
    grad_up[...] = dot(turned[...], d_up[:, part], 1, 0).astype(BF16)


def grad_in(d_gate, d_up, inputs, after=(), weight=1):
    blocks, (rows, width) = len(inputs), inputs[0].shape
    total, units = d_gate.shape
    return call(
        functools.partial(grad_in_kernel, blocks=blocks),
        [pltpu.HBM((width, units), BF16)] * 2,
        [VMEM] * (2 + blocks) + [AFTER] * len(after),
        [pl.BlockSpec((width, TILE), lambda i: (0, i))] * 2,
        [pltpu.VMEM((width, total), BF16)],
        grid=(units // TILE,),
        weight=weight,
    )(d_gate, d_up, *inputs, *after)


def grad_down_kernel(hidden, *refs, blocks):
    cots, (grad, cot_all) = refs[:blocks], refs[-2:]

    @pl.when(pl.program_id(0) == 0)
    def _():
        cot_all[...] = joined(cots)

    part = pl.ds(pl.multiple_of(pl.program_id(0) * TILE, TILE), TILE)
    grad[...] = dot(hidden[:, part], cot_all[...], 0, 0).astype(BF16)


def grad_down(hidden, cots, after=()):
    blocks, (rows, width) = len(cots), cots[0].shape
    total, units = hidden.shape
    return call(
        functools.partial(grad_down_kernel, blocks=blocks),
        pltpu.HBM((units, width), BF16),
        [VMEM] * (1 + blocks) + [AFTER] * len(after),
        pl.BlockSpec((TILE, width), lambda i: (i, 0)),
        [pltpu.VMEM((total, width), BF16)],
        grid=(units // TILE,),
    )(hidden, *cots, *after)


def to_experts(blocks, relative):
    if not relative:
        stacked = lax.all_to_all(jnp.stack(blocks), "expert", split_axis=0, concat_axis=0)
        return [stacked[block] for block in range(len(blocks))]
    return [blocks[0]] + [
        exchange(block, "expert", mask) for mask, block in enumerate(blocks) if mask > 0
    ]


def finish_kernel(mine_ref, rest_ref, out_ref, sems):
    width = mine_ref.shape[1]
    core = lax.axis_index("dp")
    copies = []
    for place, (half, source) in enumerate(((core, mine_ref), (1 - core, rest_ref))):
        columns = pl.ds(pl.multiple_of(half * width, 128), width)
        copies.append(
            pltpu.make_async_copy(source, out_ref.at[:, columns], sems.at[place])
        )
    for copy in copies:
        copy.start()
    for copy in copies:
        copy.wait()


def finish(mine, rest):
    tokens, width = mine.shape
    return call(
        finish_kernel,
        pltpu.HBM((tokens, 2 * width), BF16),
        [VMEM, VMEM],
        HBM,
        [pltpu.SemaphoreType.DMA((2,))],
    )(mine, rest)


def local(x_fwd, ids_fwd, route_fwd, x_bwd, ids_bwd, route_bwd, dy_bwd, w_gate, w_up, w_down):
    n_expert = lax.axis_size("expert")
    slab_width = w_gate.shape[-1]
    group = FF // slab_width
    experts = n_expert // group
    tokens = x_fwd.shape[1]
    spread = 4 * experts * group
    capacity = group * ((5 * tokens * TOP + spread - 1) // spread)
    relative = n_expert <= 8
    plan = Plan(n_expert, (capacity + 7) // 8 * 8, group, tokens, relative)
    row_b, row_f = 0, META // 2

    own_f, send_f, own_x, own_dy, send_rest = pack(
        *[in_hbm(value[0]) for value in (x_fwd, x_bwd, dy_bwd)],
        *[in_hbm(value[0].T) for value in (ids_bwd, route_bwd, ids_fwd, route_fwd)],
    )
    other_f = exchange(send_f, "dp", 1)
    metas = (own_f, other_f)
    *sent_f, send_rest = dispatch(
        metas, own_f, other_f, plan, row_f, 0, False, passing=(send_rest,)
    )
    rows_f = to_experts(sent_f, relative)
    other_rest = exchange(send_rest, "dp", 1)
    sent_x = dispatch(metas, own_x, other_rest, plan, row_b, 0, False)
    rows_b = to_experts(sent_x, relative)
    gate_w, up_w, down_w = load(
        [in_hbm(weight[0, 0]) for weight in (w_gate, w_up, w_down)], after=sent_x[:1]
    )
    sent_dy = dispatch(
        metas, own_dy, other_rest, plan, row_b, tokens, True, after=(in_vmem(down_w),)
    )
    cots_b = to_experts(sent_dy, relative)

    part_f = gate_up(rows_f, gate_w, up_w, after=sent_dy[:1])
    part_f_other = exchange(part_f, "dp", 1)
    part_b = gate_up(rows_b, gate_w, up_w, after=(part_f,), weight=1000)
    part_b_other = exchange(part_b, "dp", 1)
    down_blocks = down(part_f, part_f_other, down_w, plan, after=(part_b,))
    part_d = d_hidden(cots_b, down_w, after=(down_blocks[0], in_vmem(part_b_other)), weight=1000)
    part_d_other = exchange(part_d, "dp", 1)
    own_back_f = to_experts(down_blocks[:n_expert], relative)
    other_back_f = to_experts(down_blocks[n_expert:], relative)
    hidden, d_gate, d_up, *back_blocks = back(
        part_b, part_b_other, part_d, part_d_other, gate_w, up_w, plan
    )
    own_back_b = to_experts(back_blocks[:n_expert], relative)
    other_back_b = to_experts(back_blocks[n_expert:], relative)

    own_sum = combine(
        metas, own_back_f, plan, row_f, True, False, after=back_blocks[:1]
    )
    y_mine = section_shift(own_sum, 0)
    grad_d = grad_down(hidden, cots_b, after=(own_sum,))
    other_sum = combine(
        metas, other_back_f, plan, row_f, True, True, after=(in_hbm(grad_d),), weight=150
    )
    y_rest = section_shift(other_sum, 1)
    own_sum = combine(
        metas, own_back_b, plan, row_b, False, False, after=(other_sum, in_vmem(y_mine)), weight=150
    )
    dx_mine = section_shift(own_sum, 0)
    y_next = finish(y_mine, y_rest)
    grad_g, grad_u = grad_in(d_gate, d_up, rows_b, after=(own_sum, in_hbm(y_next)))
    other_sum = combine(
        metas,
        other_back_b,
        plan,
        row_b,
        False,
        True,
        after=(in_hbm(grad_g),),
    )
    dx_rest = section_shift(other_sum, 1)
    dx_next = finish(dx_mine, dx_rest)
    return (
        y_next[None],
        dx_next[None],
        grad_g[None, None],
        grad_u[None, None],
        grad_d[None, None],
    )


def solution(mesh):
    rows = P("section", ("expert", "dp"), None)
    by_feature = P("section", "expert", "dp", None)
    down_spec = P("section", "expert", None, "dp")
    return jax.shard_map(
        local,
        mesh=mesh,
        in_specs=(rows,) * 7 + (by_feature, by_feature, down_spec),
        out_specs=(rows, rows, by_feature, by_feature, down_spec),
        check_vma=False,
    )
```

time: 94.9 us -> 104 us (1.096)
  starting transfers between devices: 28.7 us -> 33.1 us
  Pallas kernels: 29.8 us -> 32.8 us
  waiting for transfers between devices: 35.3 us -> 37.3 us
    ppermute x20 -> x26, starting transfers between devices: 24.5 us -> 29.6 us  [exchange(): lax.ppermute(value, axis, [(source, source ^ mask) for source in range(co...]
    ppermute x20 -> x26, waiting for transfers between devices: 24.4 us -> 27.4 us  [exchange(): lax.ppermute(value, axis, [(source, source ^ mask) for source in range(co...]
    pallas_call x5 -> x6, Pallas kernels: 14.3 us -> 16.6 us  [the longest x1 6.27 us: grad_in(): call(functools.partial(grad_in_kernel, blocks=blocks), [pltpu.HBM((width,...]
  transfers between devices with their start and end apart: 24 -> 30, of which waited for: 13 -> 13; matrix products, arithmetic and copies ran while one was open for 0% -> 0% of each run, Pallas kernels for 29% -> 27%
where the time goes in v4:
time: 104 us
  waiting for transfers between devices  37.3 us (36%)
  starting transfers between devices  33.1 us (32%)
  Pallas kernels  32.8 us (32%)
    ppermute x26, starting transfers between devices, exchange(): lax.ppermute(value, axis, [(source, source ^ mask) for source in range(co...  29.6 us
    ppermute x26, waiting for transfers between devices, exchange(): lax.ppermute(value, axis, [(source, source ^ mask) for source in range(co...  27.4 us
    ppermute x4, waiting for transfers between devices, section_shift(): return lax.ppermute(value, ('section', 'dp'), pairs)  9.92 us
    pallas_call x1, Pallas kernels, grad_in(): call(functools.partial(grad_in_kernel, blocks=blocks), [pltpu.HBM((width,...  6.27 us
    pallas_call x2, Pallas kernels, gate_up(): call(functools.partial(gate_up_kernel, blocks=blocks), array(2, total, un...  5.21 us
    pallas_call x1, Pallas kernels, load(): call(functools.partial(load_kernel, count=len(weights)), [array(*weight.s...  4.23 us
    pallas_call x1, Pallas kernels, grad_down(): call(functools.partial(grad_down_kernel, blocks=blocks), pltpu.HBM((units...  3.98 us
    ppermute x4, starting transfers between devices, section_shift(): return lax.ppermute(value, ('section', 'dp'), pairs)  3.54 us
  transfers between devices with their start and end apart: 30, of which 13 were waited for; matrix products, arithmetic and copies ran while one was open for 0% of the time, Pallas kernels for 27%

profile of v4, /device:TPU:0, one launch (start us, length us, event | category | flops | bytes accessed | tf_op | source)
XLA Modules:
  0.0 104.2 jit_solution(12553808434268241948)
XLA Ops:
  0.6 1.6 %shard_map.137 = (bf16[80,1792]{1,0:T(8,128)(2,1)S(1)}, bf16[80,1792]{1,0:T(8,128)(2,1)S(1)}, bf16[64,1792]{1,0:T(8,128)(2,1)S(1)}, bf16[64,1792]{1,0:T(8,128)(2,1)S(1)}, bf16[128,1792]{1,0:T(8,128)(2,1)S(1)}) custom-call(bf16[64,3584]{1,0:T(8,128)(2,1)} %bitcast.30, bf16[64,3584]{1,0:T(8,128)(2,1)} %bitcast.31, bf16[64,3584]{1,0:T(8,128)(2,1)} %bitcast.32, ...), custom_call_target="tpu_custom_call" | custom-call | flops 10000000 | bytes 1 | tf_op jit(solution)/shard_map/pallas_call | solution.py:124
  5.0 2.6 %collective-permute-start.1 = (bf16[80,1792]{1,0:T(8,128)(2,1)S(1)}, bf16[80,1792]{1,0:T(8,128)(2,1)S(1)}, u32[]{:S(2)}, u32[]{:S(2)}) collective-permute-start(bf16[80,1792]{1,0:T(8,128)(2,1)S(1)} %get-tuple-element.51), channel_id=1, source_target_pairs={{0,2},{2,0},{4,6},{6,4},{1,3},{3,1},{5,7},{7,5},{8,10},{10,8},{12,... | collective-permute-start | bytes 860168 | tf_op jit(solution)/shard_map/ppermute | solution.py:22
  7.6 1.5 %collective-permute-start.2 = (bf16[80,1792]{1,0:T(8,128)(2,1)S(1)}, bf16[80,1792]{1,0:T(8,128)(2,1)S(1)}, u32[]{:S(2)}, u32[]{:S(2)}) collective-permute-start(bf16[80,1792]{1,0:T(8,128)(2,1)S(1)} %get-tuple-element.52), channel_id=1, source_target_pairs={{0,4},{2,6},{4,0},{6,2},{1,5},{3,7},{5,1},{7,3},{8,12},{10,14},{12... | collective-permute-start | bytes 860168 | tf_op jit(solution)/shard_map/ppermute | solution.py:22
  9.7 2.0 %collective-permute-start.6 = (bf16[80,1792]{1,0:T(8,128)(2,1)S(1)}, bf16[80,1792]{1,0:T(8,128)(2,1)S(1)}, u32[]{:S(2)}, u32[]{:S(2)}) collective-permute-start(bf16[80,1792]{1,0:T(8,128)(2,1)S(1)} %get-tuple-element.62), channel_id=1, source_target_pairs={{0,2},{2,0},{4,6},{6,4},{1,3},{3,1},{5,7},{7,5},{8,10},{10,8},{12,... | collective-permute-start | bytes 860168 | tf_op jit(solution)/shard_map/ppermute | solution.py:22
  11.7 1.5 %collective-permute-start.7 = (bf16[80,1792]{1,0:T(8,128)(2,1)S(1)}, bf16[80,1792]{1,0:T(8,128)(2,1)S(1)}, u32[]{:S(2)}, u32[]{:S(2)}) collective-permute-start(bf16[80,1792]{1,0:T(8,128)(2,1)S(1)} %get-tuple-element.63), channel_id=1, source_target_pairs={{0,4},{2,6},{4,0},{6,2},{1,5},{3,7},{5,1},{7,3},{8,12},{10,14},{12... | collective-permute-start | bytes 860168 | tf_op jit(solution)/shard_map/ppermute | solution.py:22
  13.3 2.0 %collective-permute-done.1.refs_1_ = bf16[80,1792]{1,0:T(8,128)(2,1)S(1)} collective-permute-done((bf16[80,1792]{1,0:T(8,128)(2,1)S(1)}, bf16[80,1792]{1,0:T(8,128)(2,1)S(1)}, u32[]{:S(2)}, u32[]{:S(2)}) %collective-permute-start.1) | collective-permute-done | bytes 286752 | tf_op jit(solution)/shard_map/ppermute | solution.py:22
  15.3 2.9 %collective-permute-start.8 = (bf16[80,1792]{1,0:T(8,128)(2,1)S(1)}, bf16[80,1792]{1,0:T(8,128)(2,1)S(1)}, u32[]{:S(2)}, u32[]{:S(2)}) collective-permute-start(bf16[80,1792]{1,0:T(8,128)(2,1)S(1)} %get-tuple-element.64), channel_id=1, source_target_pairs={{0,6},{2,4},{4,2},{6,0},{1,7},{3,5},{5,3},{7,1},{8,14},{10,12},{12... | collective-permute-start | bytes 860168 | tf_op jit(solution)/shard_map/ppermute | solution.py:22
  18.2 4.2 %shard_map.140 = (bf16[1792,1024]{1,0:T(8,128)(2,1)S(1)}, bf16[1792,1024]{1,0:T(8,128)(2,1)S(1)}, bf16[1024,1792]{1,0:T(8,128)(2,1)S(1)}) custom-call(bf16[1792,1024]{1,0:T(8,128)(2,1)} %bitcast.24, bf16[1792,1024]{1,0:T(8,128)(2,1)} %bitcast.25, bf16[1024,1792]{1,0:T(8,128)(2,1)} %bitcast.26, bf16[80,1792]{1,0:T(8,128)(2,1)S(1)} %get-tuple-element.56.refs_3_.refs_0_), custom_call_target="tpu_custom_call" | custom-call | flops 10000000 | bytes 1 | tf_op jit(solution)/shard_map/pallas_call | solution.py:147
  23.4 2.6 %shard_map.142.refs_6_.own_ref = bf16[2,320,1024]{2,1,0:T(8,128)(2,1)S(1)} custom-call(bf16[80,1792]{1,0:T(8,128)(2,1)S(1)} %get-tuple-element.50.refs_0_, bf16[80,1792]{1,0:T(8,128)(2,1)S(1)} %collective-permute-done.1.refs_1_, bf16[80,1792]{1,0:T(8,128)(2,1)S(1)} %collective-permute-done.2.refs_2_, bf16[80,1792]{1,0:T(8,128)(2,1)S(1)} %collective-permute-done.3.refs_3_, ...), custom_call_target="tpu_custom_call" | custom-call | flops 10000000 | bytes 1 | tf_op jit(solution)/shard_map/pallas_call | solution.py:281
  27.6 7.2 %collective-permute-done.7.refs_2_ = bf16[80,1792]{1,0:T(8,128)(2,1)S(1)} collective-permute-done((bf16[80,1792]{1,0:T(8,128)(2,1)S(1)}, bf16[80,1792]{1,0:T(8,128)(2,1)S(1)}, u32[]{:S(2)}, u32[]{:S(2)}) %collective-permute-start.7) | collective-permute-done | bytes 286752 | tf_op jit(solution)/shard_map/ppermute | solution.py:22
  34.9 2.6 %shard_map.143.refs_0_.own_ref = bf16[2,320,1024]{2,1,0:T(8,128)(2,1)S(1)} custom-call(bf16[80,1792]{1,0:T(8,128)(2,1)S(1)} %get-tuple-element.56.refs_3_.refs_0_, bf16[80,1792]{1,0:T(8,128)(2,1)S(1)} %collective-permute-done.6.refs_1_, bf16[80,1792]{1,0:T(8,128)(2,1)S(1)} %collective-permute-done.7.refs_2_, ...), custom_call_target="tpu_custom_call" | custom-call | flops 10000000000 | bytes 1 | tf_op jit(solution)/shard_map/pallas_call | solution.py:281
  41.1 1.6 %shard_map.144 = (bf16[40,1792]{1,0:T(8,128)(2,1)S(1)}, bf16[40,1792]{1,0:T(8,128)(2,1)S(1)}, bf16[40,1792]{1,0:T(8,128)(2,1)S(1)}, bf16[40,1792]{1,0:T(8,128)(2...) custom-call(bf16[2,320,1024]{2,1,0:T(8,128)(2,1)S(1)} %shard_map.142, ...), custom_call_target="tpu_custom_call" | custom-call | flops 10000000 | bytes 1 | tf_op jit(solution)/shard_map/pallas_call | solution.py:344
  42.7 4.5 %collective-permute-done.13.refs_1_ = bf16[80,1792]{1,0:T(8,128)(2,1)S(1)} collective-permute-done((bf16[80,1792]{1,0:T(8,128)(2,1)S(1)}, bf16[80,1792]{1,0:T(8,128)(2,1)S(1)}, u32[]{:S(2)}, u32[]{:S(2)}) %collective-permute-start.13) | collective-permute-done | bytes 286752 | tf_op jit(solution)/shard_map/ppermute | solution.py:22
  47.3 5.0 %collective-permute-done.14.refs_2_ = bf16[80,1792]{1,0:T(8,128)(2,1)S(1)} collective-permute-done((bf16[80,1792]{1,0:T(8,128)(2,1)S(1)}, bf16[80,1792]{1,0:T(8,128)(2,1)S(1)}, u32[]{:S(2)}, u32[]{:S(2)}) %collective-permute-start.14) | collective-permute-done | bytes 286752 | tf_op jit(solution)/shard_map/ppermute | solution.py:22
  52.3 1.7 %collective-permute-done.15.refs_3_ = bf16[80,1792]{1,0:T(8,128)(2,1)S(1)} collective-permute-done((bf16[80,1792]{1,0:T(8,128)(2,1)S(1)}, bf16[80,1792]{1,0:T(8,128)(2,1)S(1)}, u32[]{:S(2)}, u32[]{:S(2)}) %collective-permute-start.15) | collective-permute-done | bytes 286752 | tf_op jit(solution)/shard_map/ppermute | solution.py:22
  56.2 1.5 %collective-permute-start.10 = (bf16[40,1792]{1,0:T(8,128)(2,1)S(1)}, bf16[40,1792]{1,0:T(8,128)(2,1)S(1)}, u32[]{:S(2)}, u32[]{:S(2)}) collective-permute-start(bf16[40,1792]{1,0:T(8,128)(2,1)S(1)} %get-tuple-element.67), channel_id=1, source_target_pairs={{0,4},{2,6},{4,0},{6,2},{1,5},{3,7},{5,1},{7,3},{8,12},{10,14},{12... | collective-permute-start | bytes 430088 | tf_op jit(solution)/shard_map/ppermute | solution.py:22
  59.7 2.3 %collective-permute-done.9.refs_1_ = bf16[40,1792]{1,0:T(8,128)(2,1)S(1)} collective-permute-done((bf16[40,1792]{1,0:T(8,128)(2,1)S(1)}, bf16[40,1792]{1,0:T(8,128)(2,1)S(1)}, u32[]{:S(2)}, u32[]{:S(2)}) %collective-permute-start.9) | collective-permute-done | bytes 143392 | tf_op jit(solution)/shard_map/ppermute | solution.py:22
  64.3 3.2 %shard_map.146 = (bf16[320,1024]{1,0:T(8,128)(2,1)S(1)}, bf16[320,1024]{1,0:T(8,128)(2,1)S(1)}, bf16[320,1024]{1,0:T(8,128)(2,1)S(1)}, bf16[40,1792]{1,0:T(8,128...) custom-call(bf16[2,320,1024]{2,1,0:T(8,128)(2,1)S(1)} %shard_map.143, ...), custom_call_target="tpu_custom_call" | custom-call | flops 10000000 | bytes 1 | tf_op jit(solution)/shard_map/pallas_call | solution.py:378
  68.1 1.8 %collective-permute-start.17 = (bf16[64,1792]{1,0:T(8,128)(2,1)S(1)}, bf16[64,1792]{1,0:T(8,128)(2,1)S(1)}, u32[]{:S(2)}, u32[]{:S(2)}) collective-permute-start(bf16[64,1792]{1,0:T(8,128)(2,1)S(1)} %shard_map.147.refs_4_), channel_id=1, source_target_pairs={{0,8},{1,9},{8,16},{9,17},{16,24},{17,25},{24,0},{25,1},{2,10},{3,... | collective-permute-start | bytes 688136 | tf_op jit(solution)/shard_map/ppermute | solution.py:32
  71.1 4.0 %shard_map.148.refs_4_ = bf16[1024,1792]{1,0:T(8,128)(2,1)} custom-call(bf16[320,1024]{1,0:T(8,128)(2,1)S(1)} %get-tuple-element.77.hidden, bf16[80,1792]{1,0:T(8,128)(2,1)S(1)} %get-tuple-element.61.refs_6_.refs_0_, bf16[80,1792]{1,0:T(8,128)(2,1)S(1)} %collective-permute-done.13.refs_1_, bf16[80,1792]{1,0:T(8,128)(2,1)S(1)} %collective-permute-done.14.refs_2_, ...), custom_call_target="tpu_custom_call" | custom-call | flops 10000000 | bytes 1 | tf_op jit(solution)/shard_map/pallas_call | solution.py:430
  82.0 1.7 %collective-permute-start.28 = (bf16[40,1792]{1,0:T(8,128)(2,1)S(1)}, bf16[40,1792]{1,0:T(8,128)(2,1)S(1)}, u32[]{:S(2)}, u32[]{:S(2)}) collective-permute-start(bf16[40,1792]{1,0:T(8,128)(2,1)S(1)} %get-tuple-element.84), channel_id=1, source_target_pairs={{0,6},{2,4},{4,2},{6,0},{1,7},{3,5},{5,3},{7,1},{8,14},{10,12},{12... | collective-permute-start | bytes 430088 | tf_op jit(solution)/shard_map/ppermute | solution.py:22
  84.1 1.6 %collective-permute-start.25 = (bf16[64,1792]{1,0:T(8,128)(2,1)S(1)}, bf16[64,1792]{1,0:T(8,128)(2,1)S(1)}, u32[]{:S(2)}, u32[]{:S(2)}) collective-permute-start(bf16[64,1792]{1,0:T(8,128)(2,1)S(1)} %shard_map.151.refs_4_), channel_id=1, source_target_pairs={{0,8},{1,9},{8,16},{9,17},{16,24},{17,25},{24,0},{25,1},{2,10},{3,... | collective-permute-start | bytes 688136 | tf_op jit(solution)/shard_map/ppermute | solution.py:32
  87.5 6.3 %shard_map.152 = (bf16[1792,1024]{1,0:T(8,128)(2,1)}, bf16[1792,1024]{1,0:T(8,128)(2,1)}) custom-call(bf16[320,1024]{1,0:T(8,128)(2,1)S(1)} %get-tuple-element.85.d_gate, bf16[320,1024]{1,0:T(8,128)(2,1)S(1)} %get-tuple-element.86.d_up, bf16[80,1792]{1,0:T(8,128)(2,1)S(1)} %get-tuple-element.56.refs_3_.refs_0_, ...), custom_call_target="tpu_custom_call" | custom-call | flops 10000000 | bytes 1 | tf_op jit(solution)/shard_map/pallas_call | solution.py:405
  94.3 9.0 %collective-permute-done.29.rest_ref = bf16[64,1792]{1,0:T(8,128)(2,1)S(1)} collective-permute-done((bf16[64,1792]{1,0:T(8,128)(2,1)S(1)}, bf16[64,1792]{1,0:T(8,128)(2,1)S(1)}, u32[]{:S(2)}, u32[]{:S(2)}) %collective-permute-start.29) | collective-permute-done | bytes 229408 | tf_op jit(solution)/shard_map/ppermute | solution.py:32
  (54 shorter events, 28.1 us)
Async XLA Ops:
  5.0 10.3 %collective-permute-start.1 = (bf16[80,1792]{1,0:T(8,128)(2,1)S(1)}, bf16[80,1792]{1,0:T(8,128)(2,1)S(1)}, u32[]{:S(2)}, u32[]{:S(2)}) collective-permute-start(bf16[80,1792]{1,0:T(8,128)(2,1)S(1)} %get-tuple-element.51), channel_id=1, source_target_pairs={{0,2},{2,0},{4,6},{6,4},{1,3},{3,1},{5,7},{7,5},{8,10},{10,8},{12,... | collective-permute-start | bytes 860168 | tf_op jit(solution)/shard_map/ppermute | solution.py:22
  7.6 15.8 %collective-permute-start.2 = (bf16[80,1792]{1,0:T(8,128)(2,1)S(1)}, bf16[80,1792]{1,0:T(8,128)(2,1)S(1)}, u32[]{:S(2)}, u32[]{:S(2)}) collective-permute-start(bf16[80,1792]{1,0:T(8,128)(2,1)S(1)} %get-tuple-element.52), channel_id=1, source_target_pairs={{0,4},{2,6},{4,0},{6,2},{1,5},{3,7},{5,1},{7,3},{8,12},{10,14},{12... | collective-permute-start | bytes 860168 | tf_op jit(solution)/shard_map/ppermute | solution.py:22
  9.1 14.3 %collective-permute-start.3 = (bf16[80,1792]{1,0:T(8,128)(2,1)S(1)}, bf16[80,1792]{1,0:T(8,128)(2,1)S(1)}, u32[]{:S(2)}, u32[]{:S(2)}) collective-permute-start(bf16[80,1792]{1,0:T(8,128)(2,1)S(1)} %get-tuple-element.53), channel_id=1, source_target_pairs={{0,6},{2,4},{4,2},{6,0},{1,7},{3,5},{5,3},{7,1},{8,14},{10,12},{12... | collective-permute-start | bytes 860168 | tf_op jit(solution)/shard_map/ppermute | solution.py:22
  9.7 17.9 %collective-permute-start.6 = (bf16[80,1792]{1,0:T(8,128)(2,1)S(1)}, bf16[80,1792]{1,0:T(8,128)(2,1)S(1)}, u32[]{:S(2)}, u32[]{:S(2)}) collective-permute-start(bf16[80,1792]{1,0:T(8,128)(2,1)S(1)} %get-tuple-element.62), channel_id=1, source_target_pairs={{0,2},{2,0},{4,6},{6,4},{1,3},{3,1},{5,7},{7,5},{8,10},{10,8},{12,... | collective-permute-start | bytes 860168 | tf_op jit(solution)/shard_map/ppermute | solution.py:22
  11.7 23.1 %collective-permute-start.7 = (bf16[80,1792]{1,0:T(8,128)(2,1)S(1)}, bf16[80,1792]{1,0:T(8,128)(2,1)S(1)}, u32[]{:S(2)}, u32[]{:S(2)}) collective-permute-start(bf16[80,1792]{1,0:T(8,128)(2,1)S(1)} %get-tuple-element.63), channel_id=1, source_target_pairs={{0,4},{2,6},{4,0},{6,2},{1,5},{3,7},{5,1},{7,3},{8,12},{10,14},{12... | collective-permute-start | bytes 860168 | tf_op jit(solution)/shard_map/ppermute | solution.py:22
  15.3 19.6 %collective-permute-start.8 = (bf16[80,1792]{1,0:T(8,128)(2,1)S(1)}, bf16[80,1792]{1,0:T(8,128)(2,1)S(1)}, u32[]{:S(2)}, u32[]{:S(2)}) collective-permute-start(bf16[80,1792]{1,0:T(8,128)(2,1)S(1)} %get-tuple-element.64), channel_id=1, source_target_pairs={{0,6},{2,4},{4,2},{6,0},{1,7},{3,5},{5,3},{7,1},{8,14},{10,12},{12... | collective-permute-start | bytes 860168 | tf_op jit(solution)/shard_map/ppermute | solution.py:22
  26.0 15.1 %collective-permute-start.5 = (bf16[2,320,1024]{2,1,0:T(8,128)(2,1)S(1)}, bf16[2,320,1024]{2,1,0:T(8,128)(2,1)S(1)}, u32[]{:S(2)}, u32[]{:S(2)}) collective-permute-start(bf16[2,320,1024]{2,1,0:T(8,128)(2,1)S(1)} %shard_map.142.refs_6_.own_ref), channel_id=1, source_target_pairs={{0,1},{1,0},{2,3},{3,2},{4,5},{5,4},{6,7},{7,6},{8,9},{9,8},{10,11... | collective-permute-start | bytes 3932168 | tf_op jit(solution)/shard_map/ppermute | solution.py:22
  37.5 16.5 %collective-permute-start.12 = (bf16[2,320,1024]{2,1,0:T(8,128)(2,1)S(1)}, bf16[2,320,1024]{2,1,0:T(8,128)(2,1)S(1)}, u32[]{:S(2)}, u32[]{:S(2)}) collective-permute-start(bf16[2,320,1024]{2,1,0:T(8,128)(2,1)S(1)} %shard_map.143.refs_0_.own_ref), channel_id=1, source_target_pairs={{0,1},{1,0},{2,3},{3,2},{4,5},{5,4},{6,7},{7,6},{8,9},{9,8},{10,11... | collective-permute-start | bytes 3932168 | tf_op jit(solution)/shard_map/ppermute | solution.py:22
  37.6 9.7 %collective-permute-start.13 = (bf16[80,1792]{1,0:T(8,128)(2,1)S(1)}, bf16[80,1792]{1,0:T(8,128)(2,1)S(1)}, u32[]{:S(2)}, u32[]{:S(2)}) collective-permute-start(bf16[80,1792]{1,0:T(8,128)(2,1)S(1)} %get-tuple-element.69), channel_id=1, source_target_pairs={{0,2},{2,0},{4,6},{6,4},{1,3},{3,1},{5,7},{7,5},{8,10},{10,8},{12,... | collective-permute-start | bytes 860168 | tf_op jit(solution)/shard_map/ppermute | solution.py:22
  38.9 13.4 %collective-permute-start.14 = (bf16[80,1792]{1,0:T(8,128)(2,1)S(1)}, bf16[80,1792]{1,0:T(8,128)(2,1)S(1)}, u32[]{:S(2)}, u32[]{:S(2)}) collective-permute-start(bf16[80,1792]{1,0:T(8,128)(2,1)S(1)} %get-tuple-element.70), channel_id=1, source_target_pairs={{0,4},{2,6},{4,0},{6,2},{1,5},{3,7},{5,1},{7,3},{8,12},{10,14},{12... | collective-permute-start | bytes 860168 | tf_op jit(solution)/shard_map/ppermute | solution.py:22
  39.7 14.3 %collective-permute-start.15 = (bf16[80,1792]{1,0:T(8,128)(2,1)S(1)}, bf16[80,1792]{1,0:T(8,128)(2,1)S(1)}, u32[]{:S(2)}, u32[]{:S(2)}) collective-permute-start(bf16[80,1792]{1,0:T(8,128)(2,1)S(1)} %get-tuple-element.71), channel_id=1, source_target_pairs={{0,6},{2,4},{4,2},{6,0},{1,7},{3,5},{5,3},{7,1},{8,14},{10,12},{12... | collective-permute-start | bytes 860168 | tf_op jit(solution)/shard_map/ppermute | solution.py:22
  56.2 11.2 %collective-permute-start.10 = (bf16[40,1792]{1,0:T(8,128)(2,1)S(1)}, bf16[40,1792]{1,0:T(8,128)(2,1)S(1)}, u32[]{:S(2)}, u32[]{:S(2)}) collective-permute-start(bf16[40,1792]{1,0:T(8,128)(2,1)S(1)} %get-tuple-element.67), channel_id=1, source_target_pairs={{0,4},{2,6},{4,0},{6,2},{1,5},{3,7},{5,1},{7,3},{8,12},{10,14},{12... | collective-permute-start | bytes 430088 | tf_op jit(solution)/shard_map/ppermute | solution.py:22
  57.8 9.7 %collective-permute-start.11 = (bf16[40,1792]{1,0:T(8,128)(2,1)S(1)}, bf16[40,1792]{1,0:T(8,128)(2,1)S(1)}, u32[]{:S(2)}, u32[]{:S(2)}) collective-permute-start(bf16[40,1792]{1,0:T(8,128)(2,1)S(1)} %get-tuple-element.68), channel_id=1, source_target_pairs={{0,6},{2,4},{4,2},{6,0},{1,7},{3,5},{5,3},{7,1},{8,14},{10,12},{12... | collective-permute-start | bytes 430088 | tf_op jit(solution)/shard_map/ppermute | solution.py:22
  59.0 16.2 %collective-permute-start.18 = (bf16[40,1792]{1,0:T(8,128)(2,1)S(1)}, bf16[40,1792]{1,0:T(8,128)(2,1)S(1)}, u32[]{:S(2)}, u32[]{:S(2)}) collective-permute-start(bf16[40,1792]{1,0:T(8,128)(2,1)S(1)} %get-tuple-element.74), channel_id=1, source_target_pairs={{0,2},{2,0},{4,6},{6,4},{1,3},{3,1},{5,7},{7,5},{8,10},{10,8},{12,... | collective-permute-start | bytes 430088 | tf_op jit(solution)/shard_map/ppermute | solution.py:22
  62.0 13.9 %collective-permute-start.19 = (bf16[40,1792]{1,0:T(8,128)(2,1)S(1)}, bf16[40,1792]{1,0:T(8,128)(2,1)S(1)}, u32[]{:S(2)}, u32[]{:S(2)}) collective-permute-start(bf16[40,1792]{1,0:T(8,128)(2,1)S(1)} %get-tuple-element.75), channel_id=1, source_target_pairs={{0,4},{2,6},{4,0},{6,2},{1,5},{3,7},{5,1},{7,3},{8,12},{10,14},{12... | collective-permute-start | bytes 430088 | tf_op jit(solution)/shard_map/ppermute | solution.py:22
  62.8 14.5 %collective-permute-start.20 = (bf16[40,1792]{1,0:T(8,128)(2,1)S(1)}, bf16[40,1792]{1,0:T(8,128)(2,1)S(1)}, u32[]{:S(2)}, u32[]{:S(2)}) collective-permute-start(bf16[40,1792]{1,0:T(8,128)(2,1)S(1)} %get-tuple-element.76), channel_id=1, source_target_pairs={{0,6},{2,4},{4,2},{6,0},{1,7},{3,5},{5,3},{7,1},{8,14},{10,12},{12... | collective-permute-start | bytes 430088 | tf_op jit(solution)/shard_map/ppermute | solution.py:22
  68.1 15.6 %collective-permute-start.17 = (bf16[64,1792]{1,0:T(8,128)(2,1)S(1)}, bf16[64,1792]{1,0:T(8,128)(2,1)S(1)}, u32[]{:S(2)}, u32[]{:S(2)}) collective-permute-start(bf16[64,1792]{1,0:T(8,128)(2,1)S(1)} %shard_map.147.refs_4_), channel_id=1, source_target_pairs={{0,8},{1,9},{8,16},{9,17},{16,24},{17,25},{24,0},{25,1},{2,10},{3,... | collective-permute-start | bytes 688136 | tf_op jit(solution)/shard_map/ppermute | solution.py:32
  69.9 8.1 %collective-permute-start.22 = (bf16[40,1792]{1,0:T(8,128)(2,1)S(1)}, bf16[40,1792]{1,0:T(8,128)(2,1)S(1)}, u32[]{:S(2)}, u32[]{:S(2)}) collective-permute-start(bf16[40,1792]{1,0:T(8,128)(2,1)S(1)} %get-tuple-element.78), channel_id=1, source_target_pairs={{0,2},{2,0},{4,6},{6,4},{1,3},{3,1},{5,7},{7,5},{8,10},{10,8},{12,... | collective-permute-start | bytes 430088 | tf_op jit(solution)/shard_map/ppermute | solution.py:22
  77.9 8.8 %collective-permute-start.21 = (bf16[64,1792]{1,0:T(8,128)(2,1)S(1)}, bf16[64,1792]{1,0:T(8,128)(2,1)S(1)}, u32[]{:S(2)}, u32[]{:S(2)}) collective-permute-start(bf16[64,1792]{1,0:T(8,128)(2,1)S(1)} %shard_map.149.refs_4_), channel_id=1, source_target_pairs={{0,9},{1,8},{8,17},{9,16},{16,25},{17,24},{24,1},{25,0},{2,11},{3,... | collective-permute-start | bytes 688136 | tf_op jit(solution)/shard_map/ppermute | solution.py:32
  78.0 15.8 %collective-permute-start.26 = (bf16[40,1792]{1,0:T(8,128)(2,1)S(1)}, bf16[40,1792]{1,0:T(8,128)(2,1)S(1)}, u32[]{:S(2)}, u32[]{:S(2)}) collective-permute-start(bf16[40,1792]{1,0:T(8,128)(2,1)S(1)} %get-tuple-element.82), channel_id=1, source_target_pairs={{0,2},{2,0},{4,6},{6,4},{1,3},{3,1},{5,7},{7,5},{8,10},{10,8},{12,... | collective-permute-start | bytes 430088 | tf_op jit(solution)/shard_map/ppermute | solution.py:22
  80.4 13.3 %collective-permute-start.27 = (bf16[40,1792]{1,0:T(8,128)(2,1)S(1)}, bf16[40,1792]{1,0:T(8,128)(2,1)S(1)}, u32[]{:S(2)}, u32[]{:S(2)}) collective-permute-start(bf16[40,1792]{1,0:T(8,128)(2,1)S(1)} %get-tuple-element.83), channel_id=1, source_target_pairs={{0,4},{2,6},{4,0},{6,2},{1,5},{3,7},{5,1},{7,3},{8,12},{10,14},{12... | collective-permute-start | bytes 430088 | tf_op jit(solution)/shard_map/ppermute | solution.py:22
  82.0 11.8 %collective-permute-start.28 = (bf16[40,1792]{1,0:T(8,128)(2,1)S(1)}, bf16[40,1792]{1,0:T(8,128)(2,1)S(1)}, u32[]{:S(2)}, u32[]{:S(2)}) collective-permute-start(bf16[40,1792]{1,0:T(8,128)(2,1)S(1)} %get-tuple-element.84), channel_id=1, source_target_pairs={{0,6},{2,4},{4,2},{6,0},{1,7},{3,5},{5,3},{7,1},{8,14},{10,12},{12... | collective-permute-start | bytes 430088 | tf_op jit(solution)/shard_map/ppermute | solution.py:22
  84.1 10.2 %collective-permute-start.25 = (bf16[64,1792]{1,0:T(8,128)(2,1)S(1)}, bf16[64,1792]{1,0:T(8,128)(2,1)S(1)}, u32[]{:S(2)}, u32[]{:S(2)}) collective-permute-start(bf16[64,1792]{1,0:T(8,128)(2,1)S(1)} %shard_map.151.refs_4_), channel_id=1, source_target_pairs={{0,8},{1,9},{8,16},{9,17},{16,24},{17,25},{24,0},{25,1},{2,10},{3,... | collective-permute-start | bytes 688136 | tf_op jit(solution)/shard_map/ppermute | solution.py:32
  94.2 9.1 %collective-permute-start.29 = (bf16[64,1792]{1,0:T(8,128)(2,1)S(1)}, bf16[64,1792]{1,0:T(8,128)(2,1)S(1)}, u32[]{:S(2)}, u32[]{:S(2)}) collective-permute-start(bf16[64,1792]{1,0:T(8,128)(2,1)S(1)} %shard_map.153), channel_id=1, source_target_pairs={{0,9},{1,8},{8,17},{9,16},{16,25},{17,24},{24,1},{25,0},{2,11},{3,... | collective-permute-start | bytes 688136 | tf_op jit(solution)/shard_map/ppermute | solution.py:32
  (6 other events, 31.8 us)

commit v5 on v4

--- a/solution.py
+++ b/solution.py
@@ -350,9 +350,8 @@
     )(own, other, down_w, *after)
 
 
-def back_kernel(
-    own_ref, other_ref, own_d, other_d, gate_w, up_w, hidden, d_gate, d_up, *outs
-):
+def back_kernel(own_ref, other_ref, own_d, other_d, gate_w, up_w, *refs, blocks):
+    hidden, d_gate, d_up, *outs = refs[-3 - 2 * blocks :]
     part = outs[0].shape[0]
     for start in range(0, hidden.shape[1], TILE):
         columns = slice(start, start + TILE)
@@ -373,15 +372,15 @@
         scatter_tile(total, outs, columns)
 
 
-def back(own, other, own_d, other_d, gate_w, up_w, plan):
+def back(own, other, own_d, other_d, gate_w, up_w, plan, after=()):
     _, total, units = own.shape
     return call(
-        back_kernel,
+        functools.partial(back_kernel, blocks=plan.blocks),
         [array(total, units)] * 3 + [array(plan.part, gate_w.shape[0])] * (2 * plan.blocks),
-        [VMEM] * 6,
+        [VMEM] * 6 + [AFTER] * len(after),
         [VMEM] * (3 + 2 * plan.blocks),
         [],
-    )(own, other, own_d, other_d, gate_w, up_w)
+    )(own, other, own_d, other_d, gate_w, up_w, *after)
 
 
 def grad_in_kernel(d_gate, d_up, *refs, blocks):
@@ -424,7 +423,7 @@
     grad[...] = dot(hidden[:, part], cot_all[...], 0, 0).astype(BF16)
 
 
-def grad_down(hidden, cots, after=()):
+def grad_down(hidden, cots, after=(), weight=1):
     blocks, (rows, width) = len(cots), cots[0].shape
     total, units = hidden.shape
     return call(
@@ -434,6 +433,7 @@
         pl.BlockSpec((TILE, width), lambda i: (i, 0)),
         [pltpu.VMEM((total, width), BF16)],
         grid=(units // TILE,),
+        weight=weight,
     )(hidden, *cots, *after)
 
 
@@ -446,7 +446,8 @@
     ]
 
 
-def finish_kernel(mine_ref, rest_ref, out_ref, sems):
+def finish_kernel(mine_ref, rest_ref, *refs):
+    out_ref, sems = refs[-2:]
     width = mine_ref.shape[1]
     core = lax.axis_index("dp")
     copies = []
@@ -461,15 +462,15 @@
         copy.wait()
 
 
-def finish(mine, rest):
+def finish(mine, rest, after=()):
     tokens, width = mine.shape
     return call(
         finish_kernel,
         pltpu.HBM((tokens, 2 * width), BF16),
-        [VMEM, VMEM],
+        [VMEM, VMEM] + [AFTER] * len(after),
         HBM,
         [pltpu.SemaphoreType.DMA((2,))],
-    )(mine, rest)
+    )(mine, rest, *after)
 
 
 def local(x_fwd, ids_fwd, route_fwd, x_bwd, ids_bwd, route_bwd, dy_bwd, w_gate, w_up, w_down):
@@ -507,34 +508,39 @@
 
     part_f = gate_up(rows_f, gate_w, up_w, after=sent_dy[:1])
     part_f_other = exchange(part_f, "dp", 1)
-    part_b = gate_up(rows_b, gate_w, up_w, after=(part_f,), weight=1000)
+    part_b = gate_up(rows_b, gate_w, up_w, after=(part_f,), weight=3000)
     part_b_other = exchange(part_b, "dp", 1)
     down_blocks = down(part_f, part_f_other, down_w, plan, after=(part_b,))
-    part_d = d_hidden(cots_b, down_w, after=(down_blocks[0], in_vmem(part_b_other)), weight=1000)
+    part_d = d_hidden(cots_b, down_w, after=down_blocks[:1], weight=1000)
     part_d_other = exchange(part_d, "dp", 1)
     own_back_f = to_experts(down_blocks[:n_expert], relative)
     other_back_f = to_experts(down_blocks[n_expert:], relative)
+    own_sum = combine(
+        metas, own_back_f, plan, row_f, True, False, after=(part_d,), weight=1000
+    )
+    y_mine = section_shift(own_sum, 0)
     hidden, d_gate, d_up, *back_blocks = back(
-        part_b, part_b_other, part_d, part_d_other, gate_w, up_w, plan
+        part_b, part_b_other, part_d, part_d_other, gate_w, up_w, plan, after=(own_sum,)
     )
     own_back_b = to_experts(back_blocks[:n_expert], relative)
     other_back_b = to_experts(back_blocks[n_expert:], relative)
-
-    own_sum = combine(
-        metas, own_back_f, plan, row_f, True, False, after=back_blocks[:1]
-    )
-    y_mine = section_shift(own_sum, 0)
-    grad_d = grad_down(hidden, cots_b, after=(own_sum,))
     other_sum = combine(
-        metas, other_back_f, plan, row_f, True, True, after=(in_hbm(grad_d),), weight=150
+        metas, other_back_f, plan, row_f, True, True, after=back_blocks[:1], weight=150
     )
     y_rest = section_shift(other_sum, 1)
     own_sum = combine(
-        metas, own_back_b, plan, row_b, False, False, after=(other_sum, in_vmem(y_mine)), weight=150
+        metas,
+        own_back_b,
+        plan,
+        row_b,
+        False,
+        False,
+        after=(other_sum, in_vmem(y_mine)),
+        weight=150,
     )
     dx_mine = section_shift(own_sum, 0)
+    grad_g, grad_u = grad_in(d_gate, d_up, rows_b, after=(own_sum,))
     y_next = finish(y_mine, y_rest)
-    grad_g, grad_u = grad_in(d_gate, d_up, rows_b, after=(own_sum, in_hbm(y_next)))
     other_sum = combine(
         metas,
         other_back_b,
@@ -542,10 +548,11 @@
         row_b,
         False,
         True,
-        after=(in_hbm(grad_g),),
+        after=(in_hbm(grad_g), in_hbm(y_next)),
     )
     dx_rest = section_shift(other_sum, 1)
-    dx_next = finish(dx_mine, dx_rest)
+    grad_d = grad_down(hidden, cots_b, after=(other_sum, in_vmem(dx_mine)), weight=100)
+    dx_next = finish(dx_mine, dx_rest, after=(in_hbm(grad_d),))
     return (
         y_next[None],
         dx_next[None],

time: 104 us -> 92.4 us (0.89)
  waiting for transfers between devices: 37.3 us -> 24.2 us
  starting transfers between devices: 33.1 us -> 34.3 us
    ppermute x26, waiting for transfers between devices: 27.4 us -> 19.5 us  [exchange(): lax.ppermute(value, axis, [(source, source ^ mask) for source in range(co...]
    ppermute x4, waiting for transfers between devices: 9.92 us -> 4.68 us  [section_shift(): return lax.ppermute(value, ('section', 'dp'), pairs)]
    ppermute x26, starting transfers between devices: 29.6 us -> 30.8 us  [exchange(): lax.ppermute(value, axis, [(source, source ^ mask) for source in range(co...]
  transfers between devices with their start and end apart: 30 -> 30, of which waited for: 13 -> 10; matrix products, arithmetic and copies ran while one was open for 0% -> 0% of each run, Pallas kernels for 27% -> 32%
where the time goes in v5:
time: 92.4 us; the launch traced here: 92.2 us
  starting transfers between devices  34.3 us (37%)
  Pallas kernels  32.8 us (35%)
  waiting for transfers between devices  24.2 us (26%)
  between operations  1.02 us (1%)
    ppermute x26, starting transfers between devices, exchange(): lax.ppermute(value, axis, [(source, source ^ mask) for source in range(co...  30.8 us
    ppermute x26, waiting for transfers between devices, exchange(): lax.ppermute(value, axis, [(source, source ^ mask) for source in range(co...  19.5 us
    pallas_call x1, Pallas kernels, grad_in(): call(functools.partial(grad_in_kernel, blocks=blocks), [pltpu.HBM((width,...  6.25 us
    pallas_call x2, Pallas kernels, gate_up(): call(functools.partial(gate_up_kernel, blocks=blocks), array(2, total, un...  5.15 us
    ppermute x4, waiting for transfers between devices, section_shift(): return lax.ppermute(value, ('section', 'dp'), pairs)  4.68 us
    pallas_call x1, Pallas kernels, load(): call(functools.partial(load_kernel, count=len(weights)), [array(*weight.s...  4.23 us
    pallas_call x1, Pallas kernels, grad_down(): call(functools.partial(grad_down_kernel, blocks=blocks), pltpu.HBM((units...  4.01 us
    ppermute x4, starting transfers between devices, section_shift(): return lax.ppermute(value, ('section', 'dp'), pairs)  3.54 us
  transfers between devices with their start and end apart: 30, of which 10 were waited for; matrix products, arithmetic and copies ran while one was open for 0% of the time, Pallas kernels for 32%

profile of v5, /device:TPU:0, one launch (start us, length us, event | category | flops | bytes accessed | tf_op | source)
XLA Modules:
  0.0 92.2 jit_solution(9095944568266900824)
XLA Ops:
  0.6 1.6 %shard_map.137 = (bf16[80,1792]{1,0:T(8,128)(2,1)S(1)}, bf16[80,1792]{1,0:T(8,128)(2,1)S(1)}, bf16[64,1792]{1,0:T(8,128)(2,1)S(1)}, bf16[64,1792]{1,0:T(8,128)(2,1)S(1)}, bf16[128,1792]{1,0:T(8,128)(2,1)S(1)}) custom-call(bf16[64,3584]{1,0:T(8,128)(2,1)} %bitcast.30, bf16[64,3584]{1,0:T(8,128)(2,1)} %bitcast.31, bf16[64,3584]{1,0:T(8,128)(2,1)} %bitcast.32, ...), custom_call_target="tpu_custom_call" | custom-call | flops 10000000 | bytes 1 | tf_op jit(solution)/shard_map/pallas_call | solution.py:124
  5.0 2.6 %collective-permute-start.1 = (bf16[80,1792]{1,0:T(8,128)(2,1)S(1)}, bf16[80,1792]{1,0:T(8,128)(2,1)S(1)}, u32[]{:S(2)}, u32[]{:S(2)}) collective-permute-start(bf16[80,1792]{1,0:T(8,128)(2,1)S(1)} %get-tuple-element.51), channel_id=1, source_target_pairs={{0,2},{2,0},{4,6},{6,4},{1,3},{3,1},{5,7},{7,5},{8,10},{10,8},{12,... | collective-permute-start | bytes 860168 | tf_op jit(solution)/shard_map/ppermute | solution.py:22
  9.7 2.0 %collective-permute-start.6 = (bf16[80,1792]{1,0:T(8,128)(2,1)S(1)}, bf16[80,1792]{1,0:T(8,128)(2,1)S(1)}, u32[]{:S(2)}, u32[]{:S(2)}) collective-permute-start(bf16[80,1792]{1,0:T(8,128)(2,1)S(1)} %get-tuple-element.62), channel_id=1, source_target_pairs={{0,2},{2,0},{4,6},{6,4},{1,3},{3,1},{5,7},{7,5},{8,10},{10,8},{12,... | collective-permute-start | bytes 860168 | tf_op jit(solution)/shard_map/ppermute | solution.py:22
  13.3 2.0 %collective-permute-done.1.refs_1_ = bf16[80,1792]{1,0:T(8,128)(2,1)S(1)} collective-permute-done((bf16[80,1792]{1,0:T(8,128)(2,1)S(1)}, bf16[80,1792]{1,0:T(8,128)(2,1)S(1)}, u32[]{:S(2)}, u32[]{:S(2)}) %collective-permute-start.1) | collective-permute-done | bytes 286752 | tf_op jit(solution)/shard_map/ppermute | solution.py:22
  15.3 2.9 %collective-permute-start.8 = (bf16[80,1792]{1,0:T(8,128)(2,1)S(1)}, bf16[80,1792]{1,0:T(8,128)(2,1)S(1)}, u32[]{:S(2)}, u32[]{:S(2)}) collective-permute-start(bf16[80,1792]{1,0:T(8,128)(2,1)S(1)} %get-tuple-element.64), channel_id=1, source_target_pairs={{0,6},{2,4},{4,2},{6,0},{1,7},{3,5},{5,3},{7,1},{8,14},{10,12},{12... | collective-permute-start | bytes 860168 | tf_op jit(solution)/shard_map/ppermute | solution.py:22
  18.2 4.2 %shard_map.140 = (bf16[1792,1024]{1,0:T(8,128)(2,1)S(1)}, bf16[1792,1024]{1,0:T(8,128)(2,1)S(1)}, bf16[1024,1792]{1,0:T(8,128)(2,1)S(1)}) custom-call(bf16[1792,1024]{1,0:T(8,128)(2,1)} %bitcast.24, bf16[1792,1024]{1,0:T(8,128)(2,1)} %bitcast.25, bf16[1024,1792]{1,0:T(8,128)(2,1)} %bitcast.26, bf16[80,1792]{1,0:T(8,128)(2,1)S(1)} %get-tuple-element.56.refs_3_.refs_0_), custom_call_target="tpu_custom_call" | custom-call | flops 10000000 | bytes 1 | tf_op jit(solution)/shard_map/pallas_call | solution.py:147
  23.4 2.6 %shard_map.142.refs_6_.own_ref = bf16[2,320,1024]{2,1,0:T(8,128)(2,1)S(1)} custom-call(bf16[80,1792]{1,0:T(8,128)(2,1)S(1)} %get-tuple-element.50.refs_0_, bf16[80,1792]{1,0:T(8,128)(2,1)S(1)} %collective-permute-done.1.refs_1_, bf16[80,1792]{1,0:T(8,128)(2,1)S(1)} %collective-permute-done.2.refs_2_, bf16[80,1792]{1,0:T(8,128)(2,1)S(1)} %collective-permute-done.3.refs_3_, ...), custom_call_target="tpu_custom_call" | custom-call | flops 10000000 | bytes 1 | tf_op jit(solution)/shard_map/pallas_call | solution.py:281
  27.6 2.0 %collective-permute-start.13 = (bf16[80,1792]{1,0:T(8,128)(2,1)S(1)}, bf16[80,1792]{1,0:T(8,128)(2,1)S(1)}, u32[]{:S(2)}, u32[]{:S(2)}) collective-permute-start(bf16[80,1792]{1,0:T(8,128)(2,1)S(1)} %get-tuple-element.70), channel_id=1, source_target_pairs={{0,4},{2,6},{4,0},{6,2},{1,5},{3,7},{5,1},{7,3},{8,12},{10,14},{12... | collective-permute-start | bytes 860168 | tf_op jit(solution)/shard_map/ppermute | solution.py:22
  29.6 5.1 %collective-permute-done.7.refs_2_ = bf16[80,1792]{1,0:T(8,128)(2,1)S(1)} collective-permute-done((bf16[80,1792]{1,0:T(8,128)(2,1)S(1)}, bf16[80,1792]{1,0:T(8,128)(2,1)S(1)}, u32[]{:S(2)}, u32[]{:S(2)}) %collective-permute-start.7) | collective-permute-done | bytes 286752 | tf_op jit(solution)/shard_map/ppermute | solution.py:22
  36.2 2.6 %shard_map.143.refs_0_.own_ref = bf16[2,320,1024]{2,1,0:T(8,128)(2,1)S(1)} custom-call(bf16[80,1792]{1,0:T(8,128)(2,1)S(1)} %get-tuple-element.56.refs_3_.refs_0_, bf16[80,1792]{1,0:T(8,128)(2,1)S(1)} %collective-permute-done.6.refs_1_, bf16[80,1792]{1,0:T(8,128)(2,1)S(1)} %collective-permute-done.7.refs_2_, ...), custom_call_target="tpu_custom_call" | custom-call | flops 30000001024 | bytes 1 | tf_op jit(solution)/shard_map/pallas_call | solution.py:281
  38.9 1.6 %shard_map.144 = (bf16[40,1792]{1,0:T(8,128)(2,1)S(1)}, bf16[40,1792]{1,0:T(8,128)(2,1)S(1)}, bf16[40,1792]{1,0:T(8,128)(2,1)S(1)}, bf16[40,1792]{1,0:T(8,128)(2...) custom-call(bf16[2,320,1024]{2,1,0:T(8,128)(2,1)S(1)} %shard_map.142, ...), custom_call_target="tpu_custom_call" | custom-call | flops 10000000 | bytes 1 | tf_op jit(solution)/shard_map/pallas_call | solution.py:344
  41.6 2.9 %collective-permute-start.11 = (bf16[40,1792]{1,0:T(8,128)(2,1)S(1)}, bf16[40,1792]{1,0:T(8,128)(2,1)S(1)}, u32[]{:S(2)}, u32[]{:S(2)}) collective-permute-start(bf16[40,1792]{1,0:T(8,128)(2,1)S(1)} %get-tuple-element.68), channel_id=1, source_target_pairs={{0,6},{2,4},{4,2},{6,0},{1,7},{3,5},{5,3},{7,1},{8,14},{10,12},{12... | collective-permute-start | bytes 430088 | tf_op jit(solution)/shard_map/ppermute | solution.py:22
  44.5 5.7 %collective-permute-done.13.refs_2_ = bf16[80,1792]{1,0:T(8,128)(2,1)S(1)} collective-permute-done((bf16[80,1792]{1,0:T(8,128)(2,1)S(1)}, bf16[80,1792]{1,0:T(8,128)(2,1)S(1)}, u32[]{:S(2)}, u32[]{:S(2)}) %collective-permute-start.13) | collective-permute-done | bytes 286752 | tf_op jit(solution)/shard_map/ppermute | solution.py:22
  51.7 1.5 %collective-permute-done.10.refs_2_ = bf16[40,1792]{1,0:T(8,128)(2,1)S(1)} collective-permute-done((bf16[40,1792]{1,0:T(8,128)(2,1)S(1)}, bf16[40,1792]{1,0:T(8,128)(2,1)S(1)}, u32[]{:S(2)}, u32[]{:S(2)}) %collective-permute-start.10) | collective-permute-done | bytes 143392 | tf_op jit(solution)/shard_map/ppermute | solution.py:22
  54.6 1.6 %collective-permute-start.17 = (bf16[40,1792]{1,0:T(8,128)(2,1)S(1)}, bf16[40,1792]{1,0:T(8,128)(2,1)S(1)}, u32[]{:S(2)}, u32[]{:S(2)}) collective-permute-start(bf16[40,1792]{1,0:T(8,128)(2,1)S(1)} %get-tuple-element.74), channel_id=1, source_target_pairs={{0,4},{2,6},{4,0},{6,2},{1,5},{3,7},{5,1},{7,3},{8,12},{10,14},{12... | collective-permute-start | bytes 430088 | tf_op jit(solution)/shard_map/ppermute | solution.py:22
  58.0 1.8 %collective-permute-start.15 = (bf16[64,1792]{1,0:T(8,128)(2,1)S(1)}, bf16[64,1792]{1,0:T(8,128)(2,1)S(1)}, u32[]{:S(2)}, u32[]{:S(2)}) collective-permute-start(bf16[64,1792]{1,0:T(8,128)(2,1)S(1)} %shard_map.146.refs_0_), channel_id=1, source_target_pairs={{0,8},{1,9},{8,16},{9,17},{16,24},{17,25},{24,0},{25,1},{2,10},{3,... | collective-permute-start | bytes 688136 | tf_op jit(solution)/shard_map/ppermute | solution.py:32
  59.8 3.2 %shard_map.147 = (bf16[320,1024]{1,0:T(8,128)(2,1)S(1)}, bf16[320,1024]{1,0:T(8,128)(2,1)S(1)}, bf16[320,1024]{1,0:T(8,128)(2,1)S(1)}, bf16[40,1792]{1,0:T(8,128...) custom-call(bf16[2,320,1024]{2,1,0:T(8,128)(2,1)S(1)} %shard_map.143, ...), custom_call_target="tpu_custom_call" | custom-call | flops 10000000 | bytes 1 | tf_op jit(solution)/shard_map/pallas_call | solution.py:377
  63.0 2.1 %collective-permute-start.22 = (bf16[40,1792]{1,0:T(8,128)(2,1)S(1)}, bf16[40,1792]{1,0:T(8,128)(2,1)S(1)}, u32[]{:S(2)}, u32[]{:S(2)}) collective-permute-start(bf16[40,1792]{1,0:T(8,128)(2,1)S(1)} %get-tuple-element.77), channel_id=1, source_target_pairs={{0,2},{2,0},{4,6},{6,4},{1,3},{3,1},{5,7},{7,5},{8,10},{10,8},{12,... | collective-permute-start | bytes 430088 | tf_op jit(solution)/shard_map/ppermute | solution.py:22
  67.3 2.0 %collective-permute-start.26 = (bf16[40,1792]{1,0:T(8,128)(2,1)S(1)}, bf16[40,1792]{1,0:T(8,128)(2,1)S(1)}, u32[]{:S(2)}, u32[]{:S(2)}) collective-permute-start(bf16[40,1792]{1,0:T(8,128)(2,1)S(1)} %get-tuple-element.81), channel_id=1, source_target_pairs={{0,2},{2,0},{4,6},{6,4},{1,3},{3,1},{5,7},{7,5},{8,10},{10,8},{12,... | collective-permute-start | bytes 430088 | tf_op jit(solution)/shard_map/ppermute | solution.py:22
  70.0 2.7 %collective-permute-done.23.refs_2_ = bf16[40,1792]{1,0:T(8,128)(2,1)S(1)} collective-permute-done((bf16[40,1792]{1,0:T(8,128)(2,1)S(1)}, bf16[40,1792]{1,0:T(8,128)(2,1)S(1)}, u32[]{:S(2)}, u32[]{:S(2)}) %collective-permute-start.23) | collective-permute-done | bytes 143392 | tf_op jit(solution)/shard_map/ppermute | solution.py:22
  73.4 1.6 %collective-permute-start.25 = (bf16[64,1792]{1,0:T(8,128)(2,1)S(1)}, bf16[64,1792]{1,0:T(8,128)(2,1)S(1)}, u32[]{:S(2)}, u32[]{:S(2)}) collective-permute-start(bf16[64,1792]{1,0:T(8,128)(2,1)S(1)} %shard_map.150.refs_4_), channel_id=1, source_target_pairs={{0,8},{1,9},{8,16},{9,17},{16,24},{17,25},{24,0},{25,1},{2,10},{3,... | collective-permute-start | bytes 688136 | tf_op jit(solution)/shard_map/ppermute | solution.py:32
  75.0 6.2 %shard_map.151 = (bf16[1792,1024]{1,0:T(8,128)(2,1)}, bf16[1792,1024]{1,0:T(8,128)(2,1)}) custom-call(bf16[320,1024]{1,0:T(8,128)(2,1)S(1)} %get-tuple-element.84.d_gate, bf16[320,1024]{1,0:T(8,128)(2,1)S(1)} %get-tuple-element.85.d_up, bf16[80,1792]{1,0:T(8,128)(2,1)S(1)} %get-tuple-element.56.refs_3_.refs_0_, ...), custom_call_target="tpu_custom_call" | custom-call | flops 10000000 | bytes 1 | tf_op jit(solution)/shard_map/pallas_call | solution.py:404
  82.6 4.0 %shard_map.153.refs_0_ = bf16[1024,1792]{1,0:T(8,128)(2,1)} custom-call(bf16[320,1024]{1,0:T(8,128)(2,1)S(1)} %get-tuple-element.87.hidden, bf16[80,1792]{1,0:T(8,128)(2,1)S(1)} %get-tuple-element.61.refs_6_.refs_0_, bf16[80,1792]{1,0:T(8,128)(2,1)S(1)} %collective-permute-done.12.refs_1_, bf16[80,1792]{1,0:T(8,128)(2,1)S(1)} %collective-permute-done.13.refs_2_, ...), custom_call_target="tpu_custom_call" | custom-call | flops 1000000000 | bytes 1 | tf_op jit(solution)/shard_map/pallas_call | solution.py:429
  86.6 4.7 %collective-permute-done.29.rest_ref = bf16[64,1792]{1,0:T(8,128)(2,1)S(1)} collective-permute-done((bf16[64,1792]{1,0:T(8,128)(2,1)S(1)}, bf16[64,1792]{1,0:T(8,128)(2,1)S(1)}, u32[]{:S(2)}, u32[]{:S(2)}) %collective-permute-start.29) | collective-permute-done | bytes 229408 | tf_op jit(solution)/shard_map/ppermute | solution.py:32
  (54 shorter events, 21.8 us)
Async XLA Ops:
  5.0 10.3 %collective-permute-start.1 = (bf16[80,1792]{1,0:T(8,128)(2,1)S(1)}, bf16[80,1792]{1,0:T(8,128)(2,1)S(1)}, u32[]{:S(2)}, u32[]{:S(2)}) collective-permute-start(bf16[80,1792]{1,0:T(8,128)(2,1)S(1)} %get-tuple-element.51), channel_id=1, source_target_pairs={{0,2},{2,0},{4,6},{6,4},{1,3},{3,1},{5,7},{7,5},{8,10},{10,8},{12,... | collective-permute-start | bytes 860168 | tf_op jit(solution)/shard_map/ppermute | solution.py:22
  7.6 15.8 %collective-permute-start.2 = (bf16[80,1792]{1,0:T(8,128)(2,1)S(1)}, bf16[80,1792]{1,0:T(8,128)(2,1)S(1)}, u32[]{:S(2)}, u32[]{:S(2)}) collective-permute-start(bf16[80,1792]{1,0:T(8,128)(2,1)S(1)} %get-tuple-element.52), channel_id=1, source_target_pairs={{0,4},{2,6},{4,0},{6,2},{1,5},{3,7},{5,1},{7,3},{8,12},{10,14},{12... | collective-permute-start | bytes 860168 | tf_op jit(solution)/shard_map/ppermute | solution.py:22
  9.1 14.3 %collective-permute-start.3 = (bf16[80,1792]{1,0:T(8,128)(2,1)S(1)}, bf16[80,1792]{1,0:T(8,128)(2,1)S(1)}, u32[]{:S(2)}, u32[]{:S(2)}) collective-permute-start(bf16[80,1792]{1,0:T(8,128)(2,1)S(1)} %get-tuple-element.53), channel_id=1, source_target_pairs={{0,6},{2,4},{4,2},{6,0},{1,7},{3,5},{5,3},{7,1},{8,14},{10,12},{12... | collective-permute-start | bytes 860168 | tf_op jit(solution)/shard_map/ppermute | solution.py:22
  9.7 17.9 %collective-permute-start.6 = (bf16[80,1792]{1,0:T(8,128)(2,1)S(1)}, bf16[80,1792]{1,0:T(8,128)(2,1)S(1)}, u32[]{:S(2)}, u32[]{:S(2)}) collective-permute-start(bf16[80,1792]{1,0:T(8,128)(2,1)S(1)} %get-tuple-element.62), channel_id=1, source_target_pairs={{0,2},{2,0},{4,6},{6,4},{1,3},{3,1},{5,7},{7,5},{8,10},{10,8},{12,... | collective-permute-start | bytes 860168 | tf_op jit(solution)/shard_map/ppermute | solution.py:22
  11.7 23.0 %collective-permute-start.7 = (bf16[80,1792]{1,0:T(8,128)(2,1)S(1)}, bf16[80,1792]{1,0:T(8,128)(2,1)S(1)}, u32[]{:S(2)}, u32[]{:S(2)}) collective-permute-start(bf16[80,1792]{1,0:T(8,128)(2,1)S(1)} %get-tuple-element.63), channel_id=1, source_target_pairs={{0,4},{2,6},{4,0},{6,2},{1,5},{3,7},{5,1},{7,3},{8,12},{10,14},{12... | collective-permute-start | bytes 860168 | tf_op jit(solution)/shard_map/ppermute | solution.py:22
  15.3 20.9 %collective-permute-start.8 = (bf16[80,1792]{1,0:T(8,128)(2,1)S(1)}, bf16[80,1792]{1,0:T(8,128)(2,1)S(1)}, u32[]{:S(2)}, u32[]{:S(2)}) collective-permute-start(bf16[80,1792]{1,0:T(8,128)(2,1)S(1)} %get-tuple-element.64), channel_id=1, source_target_pairs={{0,6},{2,4},{4,2},{6,0},{1,7},{3,5},{5,3},{7,1},{8,14},{10,12},{12... | collective-permute-start | bytes 860168 | tf_op jit(solution)/shard_map/ppermute | solution.py:22
  26.0 12.8 %collective-permute-start.5 = (bf16[2,320,1024]{2,1,0:T(8,128)(2,1)S(1)}, bf16[2,320,1024]{2,1,0:T(8,128)(2,1)S(1)}, u32[]{:S(2)}, u32[]{:S(2)}) collective-permute-start(bf16[2,320,1024]{2,1,0:T(8,128)(2,1)S(1)} %shard_map.142.refs_6_.own_ref), channel_id=1, source_target_pairs={{0,1},{1,0},{2,3},{3,2},{4,5},{5,4},{6,7},{7,6},{8,9},{9,8},{10,11... | collective-permute-start | bytes 3932168 | tf_op jit(solution)/shard_map/ppermute | solution.py:22
  26.1 15.5 %collective-permute-start.12 = (bf16[80,1792]{1,0:T(8,128)(2,1)S(1)}, bf16[80,1792]{1,0:T(8,128)(2,1)S(1)}, u32[]{:S(2)}, u32[]{:S(2)}) collective-permute-start(bf16[80,1792]{1,0:T(8,128)(2,1)S(1)} %get-tuple-element.69), channel_id=1, source_target_pairs={{0,2},{2,0},{4,6},{6,4},{1,3},{3,1},{5,7},{7,5},{8,10},{10,8},{12,... | collective-permute-start | bytes 860168 | tf_op jit(solution)/shard_map/ppermute | solution.py:22
  27.6 22.7 %collective-permute-start.13 = (bf16[80,1792]{1,0:T(8,128)(2,1)S(1)}, bf16[80,1792]{1,0:T(8,128)(2,1)S(1)}, u32[]{:S(2)}, u32[]{:S(2)}) collective-permute-start(bf16[80,1792]{1,0:T(8,128)(2,1)S(1)} %get-tuple-element.70), channel_id=1, source_target_pairs={{0,4},{2,6},{4,0},{6,2},{1,5},{3,7},{5,1},{7,3},{8,12},{10,14},{12... | collective-permute-start | bytes 860168 | tf_op jit(solution)/shard_map/ppermute | solution.py:22
  34.8 15.5 %collective-permute-start.14 = (bf16[80,1792]{1,0:T(8,128)(2,1)S(1)}, bf16[80,1792]{1,0:T(8,128)(2,1)S(1)}, u32[]{:S(2)}, u32[]{:S(2)}) collective-permute-start(bf16[80,1792]{1,0:T(8,128)(2,1)S(1)} %get-tuple-element.71), channel_id=1, source_target_pairs={{0,6},{2,4},{4,2},{6,0},{1,7},{3,5},{5,3},{7,1},{8,14},{10,12},{12... | collective-permute-start | bytes 860168 | tf_op jit(solution)/shard_map/ppermute | solution.py:22
  38.8 19.2 %collective-permute-start.19 = (bf16[2,320,1024]{2,1,0:T(8,128)(2,1)S(1)}, bf16[2,320,1024]{2,1,0:T(8,128)(2,1)S(1)}, u32[]{:S(2)}, u32[]{:S(2)}) collective-permute-start(bf16[2,320,1024]{2,1,0:T(8,128)(2,1)S(1)} %shard_map.143.refs_0_.own_ref), channel_id=1, source_target_pairs={{0,1},{1,0},{2,3},{3,2},{4,5},{5,4},{6,7},{7,6},{8,9},{9,8},{10,11... | collective-permute-start | bytes 3932168 | tf_op jit(solution)/shard_map/ppermute | solution.py:22
  40.5 12.8 %collective-permute-start.10 = (bf16[40,1792]{1,0:T(8,128)(2,1)S(1)}, bf16[40,1792]{1,0:T(8,128)(2,1)S(1)}, u32[]{:S(2)}, u32[]{:S(2)}) collective-permute-start(bf16[40,1792]{1,0:T(8,128)(2,1)S(1)} %get-tuple-element.67), channel_id=1, source_target_pairs={{0,4},{2,6},{4,0},{6,2},{1,5},{3,7},{5,1},{7,3},{8,12},{10,14},{12... | collective-permute-start | bytes 430088 | tf_op jit(solution)/shard_map/ppermute | solution.py:22
  41.6 13.0 %collective-permute-start.11 = (bf16[40,1792]{1,0:T(8,128)(2,1)S(1)}, bf16[40,1792]{1,0:T(8,128)(2,1)S(1)}, u32[]{:S(2)}, u32[]{:S(2)}) collective-permute-start(bf16[40,1792]{1,0:T(8,128)(2,1)S(1)} %get-tuple-element.68), channel_id=1, source_target_pairs={{0,6},{2,4},{4,2},{6,0},{1,7},{3,5},{5,3},{7,1},{8,14},{10,12},{12... | collective-permute-start | bytes 430088 | tf_op jit(solution)/shard_map/ppermute | solution.py:22
  51.6 8.1 %collective-permute-start.20 = (bf16[320,1024]{1,0:T(8,128)(2,1)S(1)}, bf16[320,1024]{1,0:T(8,128)(2,1)S(1)}, u32[]{:S(2)}, u32[]{:S(2)}) collective-permute-start(bf16[320,1024]{1,0:T(8,128)(2,1)S(1)} %shard_map.145.refs_4_.own_d), channel_id=1, source_target_pairs={{0,1},{1,0},{2,3},{3,2},{4,5},{5,4},{6,7},{7,6},{8,9},{9,8},{10,11... | collective-permute-start | bytes 1966088 | tf_op jit(solution)/shard_map/ppermute | solution.py:22
  53.3 11.8 %collective-permute-start.16 = (bf16[40,1792]{1,0:T(8,128)(2,1)S(1)}, bf16[40,1792]{1,0:T(8,128)(2,1)S(1)}, u32[]{:S(2)}, u32[]{:S(2)}) collective-permute-start(bf16[40,1792]{1,0:T(8,128)(2,1)S(1)} %get-tuple-element.73), channel_id=1, source_target_pairs={{0,2},{2,0},{4,6},{6,4},{1,3},{3,1},{5,7},{7,5},{8,10},{10,8},{12,... | collective-permute-start | bytes 430088 | tf_op jit(solution)/shard_map/ppermute | solution.py:22
  54.6 10.7 %collective-permute-start.17 = (bf16[40,1792]{1,0:T(8,128)(2,1)S(1)}, bf16[40,1792]{1,0:T(8,128)(2,1)S(1)}, u32[]{:S(2)}, u32[]{:S(2)}) collective-permute-start(bf16[40,1792]{1,0:T(8,128)(2,1)S(1)} %get-tuple-element.74), channel_id=1, source_target_pairs={{0,4},{2,6},{4,0},{6,2},{1,5},{3,7},{5,1},{7,3},{8,12},{10,14},{12... | collective-permute-start | bytes 430088 | tf_op jit(solution)/shard_map/ppermute | solution.py:22
  56.2 10.4 %collective-permute-start.18 = (bf16[40,1792]{1,0:T(8,128)(2,1)S(1)}, bf16[40,1792]{1,0:T(8,128)(2,1)S(1)}, u32[]{:S(2)}, u32[]{:S(2)}) collective-permute-start(bf16[40,1792]{1,0:T(8,128)(2,1)S(1)} %get-tuple-element.75), channel_id=1, source_target_pairs={{0,6},{2,4},{4,2},{6,0},{1,7},{3,5},{5,3},{7,1},{8,14},{10,12},{12... | collective-permute-start | bytes 430088 | tf_op jit(solution)/shard_map/ppermute | solution.py:22
  58.0 9.3 %collective-permute-start.15 = (bf16[64,1792]{1,0:T(8,128)(2,1)S(1)}, bf16[64,1792]{1,0:T(8,128)(2,1)S(1)}, u32[]{:S(2)}, u32[]{:S(2)}) collective-permute-start(bf16[64,1792]{1,0:T(8,128)(2,1)S(1)} %shard_map.146.refs_0_), channel_id=1, source_target_pairs={{0,8},{1,9},{8,16},{9,17},{16,24},{17,25},{24,0},{25,1},{2,10},{3,... | collective-permute-start | bytes 688136 | tf_op jit(solution)/shard_map/ppermute | solution.py:32
  67.2 14.1 %collective-permute-start.21 = (bf16[64,1792]{1,0:T(8,128)(2,1)S(1)}, bf16[64,1792]{1,0:T(8,128)(2,1)S(1)}, u32[]{:S(2)}, u32[]{:S(2)}) collective-permute-start(bf16[64,1792]{1,0:T(8,128)(2,1)S(1)} %shard_map.148.refs_4_), channel_id=1, source_target_pairs={{0,9},{1,8},{8,17},{9,16},{16,25},{17,24},{24,1},{25,0},{2,11},{3,... | collective-permute-start | bytes 688136 | tf_op jit(solution)/shard_map/ppermute | solution.py:32
  67.3 14.8 %collective-permute-start.26 = (bf16[40,1792]{1,0:T(8,128)(2,1)S(1)}, bf16[40,1792]{1,0:T(8,128)(2,1)S(1)}, u32[]{:S(2)}, u32[]{:S(2)}) collective-permute-start(bf16[40,1792]{1,0:T(8,128)(2,1)S(1)} %get-tuple-element.81), channel_id=1, source_target_pairs={{0,2},{2,0},{4,6},{6,4},{1,3},{3,1},{5,7},{7,5},{8,10},{10,8},{12,... | collective-permute-start | bytes 430088 | tf_op jit(solution)/shard_map/ppermute | solution.py:22
  69.6 12.5 %collective-permute-start.27 = (bf16[40,1792]{1,0:T(8,128)(2,1)S(1)}, bf16[40,1792]{1,0:T(8,128)(2,1)S(1)}, u32[]{:S(2)}, u32[]{:S(2)}) collective-permute-start(bf16[40,1792]{1,0:T(8,128)(2,1)S(1)} %get-tuple-element.82), channel_id=1, source_target_pairs={{0,4},{2,6},{4,0},{6,2},{1,5},{3,7},{5,1},{7,3},{8,12},{10,14},{12... | collective-permute-start | bytes 430088 | tf_op jit(solution)/shard_map/ppermute | solution.py:22
  72.7 9.4 %collective-permute-start.28 = (bf16[40,1792]{1,0:T(8,128)(2,1)S(1)}, bf16[40,1792]{1,0:T(8,128)(2,1)S(1)}, u32[]{:S(2)}, u32[]{:S(2)}) collective-permute-start(bf16[40,1792]{1,0:T(8,128)(2,1)S(1)} %get-tuple-element.83), channel_id=1, source_target_pairs={{0,6},{2,4},{4,2},{6,0},{1,7},{3,5},{5,3},{7,1},{8,14},{10,12},{12... | collective-permute-start | bytes 430088 | tf_op jit(solution)/shard_map/ppermute | solution.py:22
  73.4 9.2 %collective-permute-start.25 = (bf16[64,1792]{1,0:T(8,128)(2,1)S(1)}, bf16[64,1792]{1,0:T(8,128)(2,1)S(1)}, u32[]{:S(2)}, u32[]{:S(2)}) collective-permute-start(bf16[64,1792]{1,0:T(8,128)(2,1)S(1)} %shard_map.150.refs_4_), channel_id=1, source_target_pairs={{0,8},{1,9},{8,16},{9,17},{16,24},{17,25},{24,0},{25,1},{2,10},{3,... | collective-permute-start | bytes 688136 | tf_op jit(solution)/shard_map/ppermute | solution.py:32
  82.5 8.8 %collective-permute-start.29 = (bf16[64,1792]{1,0:T(8,128)(2,1)S(1)}, bf16[64,1792]{1,0:T(8,128)(2,1)S(1)}, u32[]{:S(2)}, u32[]{:S(2)}) collective-permute-start(bf16[64,1792]{1,0:T(8,128)(2,1)S(1)} %shard_map.152.refs_4_), channel_id=1, source_target_pairs={{0,9},{1,8},{8,17},{9,16},{16,25},{17,24},{24,1},{25,0},{2,11},{3,... | collective-permute-start | bytes 688136 | tf_op jit(solution)/shard_map/ppermute | solution.py:32
  (6 other events, 34.0 us)

commit v6 on v5

--- a/solution.py
+++ b/solution.py
@@ -275,12 +275,12 @@
         out[1, :, part] = dot(rows[...], up_w[:, part], 1, 0).astype(BF16)
 
 
-def gate_up(inputs, gate_w, up_w, after=(), weight=1):
+def gate_up(inputs, gate_w, up_w, planes=2, after=(), weight=1):
     blocks, (rows, width) = len(inputs), inputs[0].shape
     units, total = gate_w.shape[1], blocks * rows
     return call(
         functools.partial(gate_up_kernel, blocks=blocks),
-        array(2, total, units),
+        array(planes, total, units),
         [VMEM] * (blocks + 2) + [AFTER] * len(after),
         VMEM,
         [pltpu.VMEM((total, width), BF16)],
@@ -292,22 +292,22 @@
     down_w = refs[blocks]
     out, rows = refs[-2:]
     rows[...] = joined(refs[:blocks])
-    for start in range(0, out.shape[1], TILE):
+    for start in range(0, out.shape[2], TILE):
         part = slice(start, start + TILE)
-        out[:, part] = dot(rows[...], down_w[part, :], 1, 1).astype(BF16)
-
-
-def d_hidden(inputs, down_w, after=(), weight=1):
+        out[2, :, part] = dot(rows[...], down_w[part, :], 1, 1).astype(BF16)
+
+
+def d_hidden(inputs, down_w, partial, after=(), weight=1):
     blocks, (rows, width) = len(inputs), inputs[0].shape
-    units, total = down_w.shape[0], blocks * rows
     return call(
         functools.partial(d_hidden_kernel, blocks=blocks),
-        array(total, units),
-        [VMEM] * (blocks + 1) + [AFTER] * len(after),
+        array(*partial.shape),
+        [VMEM] * (blocks + 2) + [AFTER] * len(after),
         VMEM,
-        [pltpu.VMEM((total, width), BF16)],
+        [pltpu.VMEM((blocks * rows, width), BF16)],
         weight=weight,
-    )(*inputs, down_w, *after)
+        aliases={blocks + 1: 0},
+    )(*inputs, down_w, partial, *after)
 
 
 def scatter_tile(value, outs, columns):
@@ -350,14 +350,14 @@
     )(own, other, down_w, *after)
 
 
-def back_kernel(own_ref, other_ref, own_d, other_d, gate_w, up_w, *refs, blocks):
+def back_kernel(own_ref, other_ref, gate_w, up_w, *refs, blocks):
     hidden, d_gate, d_up, *outs = refs[-3 - 2 * blocks :]
     part = outs[0].shape[0]
     for start in range(0, hidden.shape[1], TILE):
         columns = slice(start, start + TILE)
         gate = total_of(own_ref[0, :, columns], other_ref[0, :, columns], part)
         up = total_of(own_ref[1, :, columns], other_ref[1, :, columns], part)
-        d_hid = total_of(own_d[:, columns], other_d[:, columns], part)
+        d_hid = total_of(own_ref[2, :, columns], other_ref[2, :, columns], part)
         sigmoid = jax.nn.sigmoid(gate)
         activated = gate * sigmoid
         hidden[:, columns] = (activated * up).astype(BF16)
@@ -372,44 +372,53 @@
         scatter_tile(total, outs, columns)
 
 
-def back(own, other, own_d, other_d, gate_w, up_w, plan, after=()):
+def back(own, other, gate_w, up_w, plan, after=()):
     _, total, units = own.shape
     return call(
         functools.partial(back_kernel, blocks=plan.blocks),
         [array(total, units)] * 3 + [array(plan.part, gate_w.shape[0])] * (2 * plan.blocks),
-        [VMEM] * 6 + [AFTER] * len(after),
+        [VMEM] * 4 + [AFTER] * len(after),
         [VMEM] * (3 + 2 * plan.blocks),
         [],
-    )(own, other, own_d, other_d, gate_w, up_w, *after)
-
-
-def grad_in_kernel(d_gate, d_up, *refs, blocks):
-    inputs, (grad_gate, grad_up, turned) = refs[:blocks], refs[-3:]
-
-    @pl.when(pl.program_id(0) == 0)
-    def _():
-        for start in range(0, turned.shape[0], TILE):
-            part = slice(start, start + TILE)
-            piece = jnp.concatenate([ref[:, part] for ref in inputs], axis=0)
-            turned[part, :] = piece.T
-
+    )(own, other, gate_w, up_w, *after)
+
+
+def turn_kernel(*refs, blocks):
+    inputs, turned = refs[:blocks], refs[-1]
+    for start in range(0, turned.shape[0], TILE):
+        part = slice(start, start + TILE)
+        turned[part, :] = jnp.concatenate([ref[:, part] for ref in inputs], axis=0).T
+
+
+def turn(inputs, after=()):
+    blocks, (rows, width) = len(inputs), inputs[0].shape
+    return call(
+        functools.partial(turn_kernel, blocks=blocks),
+        array(width, blocks * rows),
+        [VMEM] * blocks + [AFTER] * len(after),
+        VMEM,
+        [],
+    )(*inputs, *after)
+
+
+def grad_in_kernel(d_gate, d_up, turned, *refs):
+    grad_gate, grad_up = refs[-2:]
     part = pl.ds(pl.multiple_of(pl.program_id(0) * TILE, TILE), TILE)
     grad_gate[...] = dot(turned[...], d_gate[:, part], 1, 0).astype(BF16)
     grad_up[...] = dot(turned[...], d_up[:, part], 1, 0).astype(BF16)
 
 
-def grad_in(d_gate, d_up, inputs, after=(), weight=1):
-    blocks, (rows, width) = len(inputs), inputs[0].shape
-    total, units = d_gate.shape
-    return call(
-        functools.partial(grad_in_kernel, blocks=blocks),
+def grad_in(d_gate, d_up, turned, after=(), weight=1):
+    width, units = turned.shape[0], d_gate.shape[1]
+    return call(
+        grad_in_kernel,
         [pltpu.HBM((width, units), BF16)] * 2,
-        [VMEM] * (2 + blocks) + [AFTER] * len(after),
+        [VMEM] * 3 + [AFTER] * len(after),
         [pl.BlockSpec((width, TILE), lambda i: (0, i))] * 2,
-        [pltpu.VMEM((width, total), BF16)],
+        [],
         grid=(units // TILE,),
         weight=weight,
-    )(d_gate, d_up, *inputs, *after)
+    )(d_gate, d_up, turned, *after)
 
 
 def grad_down_kernel(hidden, *refs, blocks):
@@ -508,19 +517,19 @@
 
     part_f = gate_up(rows_f, gate_w, up_w, after=sent_dy[:1])
     part_f_other = exchange(part_f, "dp", 1)
-    part_b = gate_up(rows_b, gate_w, up_w, after=(part_f,), weight=3000)
-    part_b_other = exchange(part_b, "dp", 1)
-    down_blocks = down(part_f, part_f_other, down_w, plan, after=(part_b,))
-    part_d = d_hidden(cots_b, down_w, after=down_blocks[:1], weight=1000)
-    part_d_other = exchange(part_d, "dp", 1)
+    part_b = gate_up(rows_b, gate_w, up_w, planes=3, after=(part_f,), weight=3000)
+    down_blocks = down(part_f, part_f_other, down_w, plan, after=(in_vmem(part_b),))
     own_back_f = to_experts(down_blocks[:n_expert], relative)
     other_back_f = to_experts(down_blocks[n_expert:], relative)
+    turned = turn(rows_b, after=down_blocks[:1])
+    part_b = d_hidden(cots_b, down_w, part_b, after=(in_vmem(turned),), weight=1000)
+    part_b_other = exchange(part_b, "dp", 1)
     own_sum = combine(
-        metas, own_back_f, plan, row_f, True, False, after=(part_d,), weight=1000
+        metas, own_back_f, plan, row_f, True, False, after=(in_vmem(part_b),), weight=2000
     )
     y_mine = section_shift(own_sum, 0)
     hidden, d_gate, d_up, *back_blocks = back(
-        part_b, part_b_other, part_d, part_d_other, gate_w, up_w, plan, after=(own_sum,)
+        part_b, part_b_other, gate_w, up_w, plan, after=(own_sum,)
     )
     own_back_b = to_experts(back_blocks[:n_expert], relative)
     other_back_b = to_experts(back_blocks[n_expert:], relative)
@@ -539,8 +548,7 @@
         weight=150,
     )
     dx_mine = section_shift(own_sum, 0)
-    grad_g, grad_u = grad_in(d_gate, d_up, rows_b, after=(own_sum,))
-    y_next = finish(y_mine, y_rest)
+    grad_d = grad_down(hidden, cots_b, after=(own_sum, in_vmem(y_rest)), weight=100)
     other_sum = combine(
         metas,
         other_back_b,
@@ -548,11 +556,14 @@
         row_b,
         False,
         True,
-        after=(in_hbm(grad_g), in_hbm(y_next)),
+        after=(in_hbm(grad_d),),
     )
     dx_rest = section_shift(other_sum, 1)
-    grad_d = grad_down(hidden, cots_b, after=(other_sum, in_vmem(dx_mine)), weight=100)
-    dx_next = finish(dx_mine, dx_rest, after=(in_hbm(grad_d),))
+    y_next = finish(y_mine, y_rest, after=(other_sum,))
+    grad_g, grad_u = grad_in(
+        d_gate, d_up, turned, after=(in_hbm(y_next), in_vmem(dx_mine)), weight=100
+    )
+    dx_next = finish(dx_mine, dx_rest, after=(in_hbm(grad_g),))
     return (
         y_next[None],
         dx_next[None],

time: 92.4 us -> 88.4 us (0.957)
  waiting for transfers between devices: 24.2 us -> 21.1 us
    ppermute x26 -> x25, waiting for transfers between devices: 19.5 us -> 17.7 us  [exchange(): lax.ppermute(value, axis, [(source, source ^ mask) for source in range(co...]
    ppermute x26 -> x25, starting transfers between devices: 30.8 us -> 29.2 us  [exchange(): lax.ppermute(value, axis, [(source, source ^ mask) for source in range(co...]
    ppermute x4, waiting for transfers between devices: 4.68 us -> 3.33 us  [section_shift(): return lax.ppermute(value, ('section', 'dp'), pairs)]
    pallas_call x4 -> x5, Pallas kernels: 12.8 us -> 12.8 us  [the longest x1 5.84 us: grad_in(): call(grad_in_kernel, [pltpu.HBM((width, units), BF16)] * 2, [VMEM] * 3 +...]
  transfers between devices with their start and end apart: 30 -> 29, of which waited for: 10 -> 12; matrix products, arithmetic and copies ran while one was open for 0% -> 0% of each run, Pallas kernels for 32% -> 34%
where the time goes in v6:
time: 88.4 us; the launch traced here: 88.3 us
  starting transfers between devices  33.4 us (38%)
  Pallas kernels  32.8 us (37%)
  waiting for transfers between devices  21.1 us (24%)
  between operations  0.99 us (1%)
    ppermute x25, starting transfers between devices, exchange(): lax.ppermute(value, axis, [(source, source ^ mask) for source in range(co...  29.2 us
    ppermute x25, waiting for transfers between devices, exchange(): lax.ppermute(value, axis, [(source, source ^ mask) for source in range(co...  17.7 us
    pallas_call x1, Pallas kernels, grad_in(): call(grad_in_kernel, [pltpu.HBM((width, units), BF16)] * 2, [VMEM] * 3 +...  5.84 us
    pallas_call x2, Pallas kernels, gate_up(): call(functools.partial(gate_up_kernel, blocks=blocks), array(planes, tota...  5.18 us
    pallas_call x1, Pallas kernels, load(): call(functools.partial(load_kernel, count=len(weights)), [array(*weight.s...  4.23 us
    ppermute x4, starting transfers between devices, section_shift(): return lax.ppermute(value, ('section', 'dp'), pairs)  4.15 us
    pallas_call x1, Pallas kernels, grad_down(): call(functools.partial(grad_down_kernel, blocks=blocks), pltpu.HBM((units...  3.98 us
    ppermute x4, waiting for transfers between devices, section_shift(): return lax.ppermute(value, ('section', 'dp'), pairs)  3.33 us
  transfers between devices with their start and end apart: 29, of which 12 were waited for; matrix products, arithmetic and copies ran while one was open for 0% of the time, Pallas kernels for 34%

profile of v6, /device:TPU:0, one launch (start us, length us, event | category | flops | bytes accessed | tf_op | source)
XLA Modules:
  0.0 88.3 jit_solution(18095679785752714213)
XLA Ops:
  0.6 1.6 %shard_map.137 = (bf16[80,1792]{1,0:T(8,128)(2,1)S(1)}, bf16[80,1792]{1,0:T(8,128)(2,1)S(1)}, bf16[64,1792]{1,0:T(8,128)(2,1)S(1)}, bf16[64,1792]{1,0:T(8,128)(2,1)S(1)}, bf16[128,1792]{1,0:T(8,128)(2,1)S(1)}) custom-call(bf16[64,3584]{1,0:T(8,128)(2,1)} %bitcast.30, bf16[64,3584]{1,0:T(8,128)(2,1)} %bitcast.31, bf16[64,3584]{1,0:T(8,128)(2,1)} %bitcast.32, ...), custom_call_target="tpu_custom_call" | custom-call | flops 10000000 | bytes 1 | tf_op jit(solution)/shard_map/pallas_call | solution.py:124
  5.0 2.6 %collective-permute-start.1 = (bf16[80,1792]{1,0:T(8,128)(2,1)S(1)}, bf16[80,1792]{1,0:T(8,128)(2,1)S(1)}, u32[]{:S(2)}, u32[]{:S(2)}) collective-permute-start(bf16[80,1792]{1,0:T(8,128)(2,1)S(1)} %get-tuple-element.51), channel_id=1, source_target_pairs={{0,2},{2,0},{4,6},{6,4},{1,3},{3,1},{5,7},{7,5},{8,10},{10,8},{12,... | collective-permute-start | bytes 860168 | tf_op jit(solution)/shard_map/ppermute | solution.py:22
  9.7 2.0 %collective-permute-start.6 = (bf16[80,1792]{1,0:T(8,128)(2,1)S(1)}, bf16[80,1792]{1,0:T(8,128)(2,1)S(1)}, u32[]{:S(2)}, u32[]{:S(2)}) collective-permute-start(bf16[80,1792]{1,0:T(8,128)(2,1)S(1)} %get-tuple-element.62), channel_id=1, source_target_pairs={{0,2},{2,0},{4,6},{6,4},{1,3},{3,1},{5,7},{7,5},{8,10},{10,8},{12,... | collective-permute-start | bytes 860168 | tf_op jit(solution)/shard_map/ppermute | solution.py:22
  13.3 2.0 %collective-permute-done.1.refs_1_ = bf16[80,1792]{1,0:T(8,128)(2,1)S(1)} collective-permute-done((bf16[80,1792]{1,0:T(8,128)(2,1)S(1)}, bf16[80,1792]{1,0:T(8,128)(2,1)S(1)}, u32[]{:S(2)}, u32[]{:S(2)}) %collective-permute-start.1) | collective-permute-done | bytes 286752 | tf_op jit(solution)/shard_map/ppermute | solution.py:22
  15.3 2.9 %collective-permute-start.8 = (bf16[80,1792]{1,0:T(8,128)(2,1)S(1)}, bf16[80,1792]{1,0:T(8,128)(2,1)S(1)}, u32[]{:S(2)}, u32[]{:S(2)}) collective-permute-start(bf16[80,1792]{1,0:T(8,128)(2,1)S(1)} %get-tuple-element.64), channel_id=1, source_target_pairs={{0,6},{2,4},{4,2},{6,0},{1,7},{3,5},{5,3},{7,1},{8,14},{10,12},{12... | collective-permute-start | bytes 860168 | tf_op jit(solution)/shard_map/ppermute | solution.py:22
  18.2 4.2 %shard_map.140 = (bf16[1792,1024]{1,0:T(8,128)(2,1)S(1)}, bf16[1792,1024]{1,0:T(8,128)(2,1)S(1)}, bf16[1024,1792]{1,0:T(8,128)(2,1)S(1)}) custom-call(bf16[1792,1024]{1,0:T(8,128)(2,1)} %bitcast.24, bf16[1792,1024]{1,0:T(8,128)(2,1)} %bitcast.25, bf16[1024,1792]{1,0:T(8,128)(2,1)} %bitcast.26, bf16[80,1792]{1,0:T(8,128)(2,1)S(1)} %get-tuple-element.56.refs_3_.refs_0_), custom_call_target="tpu_custom_call" | custom-call | flops 10000000 | bytes 1 | tf_op jit(solution)/shard_map/pallas_call | solution.py:147
  23.6 1.8 %collective-permute-start.13 = (bf16[80,1792]{1,0:T(8,128)(2,1)S(1)}, bf16[80,1792]{1,0:T(8,128)(2,1)S(1)}, u32[]{:S(2)}, u32[]{:S(2)}) collective-permute-start(bf16[80,1792]{1,0:T(8,128)(2,1)S(1)} %get-tuple-element.70), channel_id=1, source_target_pairs={{0,4},{2,6},{4,0},{6,2},{1,5},{3,7},{5,1},{7,3},{8,12},{10,14},{12... | collective-permute-start | bytes 860168 | tf_op jit(solution)/shard_map/ppermute | solution.py:22
  25.5 2.6 %shard_map.142.refs_6_.own_ref = bf16[2,320,1024]{2,1,0:T(8,128)(2,1)S(1)} custom-call(bf16[80,1792]{1,0:T(8,128)(2,1)S(1)} %get-tuple-element.50.refs_0_, bf16[80,1792]{1,0:T(8,128)(2,1)S(1)} %collective-permute-done.1.refs_1_, bf16[80,1792]{1,0:T(8,128)(2,1)S(1)} %collective-permute-done.2.refs_2_, bf16[80,1792]{1,0:T(8,128)(2,1)S(1)} %collective-permute-done.3.refs_3_, ...), custom_call_target="tpu_custom_call" | custom-call | flops 10000000 | bytes 1 | tf_op jit(solution)/shard_map/pallas_call | solution.py:281
  28.1 2.5 %collective-permute-start.14 = (bf16[80,1792]{1,0:T(8,128)(2,1)S(1)}, bf16[80,1792]{1,0:T(8,128)(2,1)S(1)}, u32[]{:S(2)}, u32[]{:S(2)}) collective-permute-start(bf16[80,1792]{1,0:T(8,128)(2,1)S(1)} %get-tuple-element.71), channel_id=1, source_target_pairs={{0,6},{2,4},{4,2},{6,0},{1,7},{3,5},{5,3},{7,1},{8,14},{10,12},{12... | collective-permute-start | bytes 860168 | tf_op jit(solution)/shard_map/ppermute | solution.py:22
  30.5 5.2 %collective-permute-done.7.refs_2_ = bf16[80,1792]{1,0:T(8,128)(2,1)S(1)} collective-permute-done((bf16[80,1792]{1,0:T(8,128)(2,1)S(1)}, bf16[80,1792]{1,0:T(8,128)(2,1)S(1)}, u32[]{:S(2)}, u32[]{:S(2)}) %collective-permute-start.7) | collective-permute-done | bytes 286752 | tf_op jit(solution)/shard_map/ppermute | solution.py:22
  35.7 2.6 %shard_map.143.refs_0_.refs_5_ = bf16[3,320,1024]{2,1,0:T(8,128)(2,1)S(1)} custom-call(bf16[80,1792]{1,0:T(8,128)(2,1)S(1)} %get-tuple-element.56.refs_3_.refs_0_, bf16[80,1792]{1,0:T(8,128)(2,1)S(1)} %collective-permute-done.6.refs_1_, bf16[80,1792]{1,0:T(8,128)(2,1)S(1)} %collective-permute-done.7.refs_2_, ...), custom_call_target="tpu_custom_call" | custom-call | flops 30000001024 | bytes 1 | tf_op jit(solution)/shard_map/pallas_call | solution.py:281
  38.8 1.7 %shard_map.144 = (bf16[40,1792]{1,0:T(8,128)(2,1)S(1)}, bf16[40,1792]{1,0:T(8,128)(2,1)S(1)}, bf16[40,1792]{1,0:T(8,128)(2,1)S(1)}, bf16[40,1792]{1,0:T(8,128)(2...) custom-call(bf16[2,320,1024]{2,1,0:T(8,128)(2,1)S(1)} %shard_map.142, ...), custom_call_target="tpu_custom_call" | custom-call | flops 10000000 | bytes 1 | tf_op jit(solution)/shard_map/pallas_call | solution.py:344
  44.5 2.6 %collective-permute-done.13.refs_2_ = bf16[80,1792]{1,0:T(8,128)(2,1)S(1)} collective-permute-done((bf16[80,1792]{1,0:T(8,128)(2,1)S(1)}, bf16[80,1792]{1,0:T(8,128)(2,1)S(1)}, u32[]{:S(2)}, u32[]{:S(2)}) %collective-permute-start.13) | collective-permute-done | bytes 286752 | tf_op jit(solution)/shard_map/ppermute | solution.py:22
  49.0 1.6 %collective-permute-start.16 = (bf16[40,1792]{1,0:T(8,128)(2,1)S(1)}, bf16[40,1792]{1,0:T(8,128)(2,1)S(1)}, u32[]{:S(2)}, u32[]{:S(2)}) collective-permute-start(bf16[40,1792]{1,0:T(8,128)(2,1)S(1)} %get-tuple-element.73), channel_id=1, source_target_pairs={{0,2},{2,0},{4,6},{6,4},{1,3},{3,1},{5,7},{7,5},{8,10},{10,8},{12,... | collective-permute-start | bytes 430088 | tf_op jit(solution)/shard_map/ppermute | solution.py:22
  51.2 2.1 %collective-permute-done.10.refs_2_ = bf16[40,1792]{1,0:T(8,128)(2,1)S(1)} collective-permute-done((bf16[40,1792]{1,0:T(8,128)(2,1)S(1)}, bf16[40,1792]{1,0:T(8,128)(2,1)S(1)}, u32[]{:S(2)}, u32[]{:S(2)}) %collective-permute-start.10) | collective-permute-done | bytes 143392 | tf_op jit(solution)/shard_map/ppermute | solution.py:22
  55.4 1.8 %collective-permute-start.15 = (bf16[64,1792]{1,0:T(8,128)(2,1)S(1)}, bf16[64,1792]{1,0:T(8,128)(2,1)S(1)}, u32[]{:S(2)}, u32[]{:S(2)}) collective-permute-start(bf16[64,1792]{1,0:T(8,128)(2,1)S(1)} %shard_map.147.refs_0_), channel_id=1, source_target_pairs={{0,8},{1,9},{8,16},{9,17},{16,24},{17,25},{24,0},{25,1},{2,10},{3,... | collective-permute-start | bytes 688136 | tf_op jit(solution)/shard_map/ppermute | solution.py:32
  57.2 3.2 %shard_map.148 = (bf16[320,1024]{1,0:T(8,128)(2,1)S(1)}, bf16[320,1024]{1,0:T(8,128)(2,1)S(1)}, bf16[320,1024]{1,0:T(8,128)(2,1)S(1)}, bf16[40,1792]{1,0:T(8,128...) custom-call(bf16[3,320,1024]{2,1,0:T(8,128)(2,1)S(1)} %shard_map.146, ...), custom_call_target="tpu_custom_call" | custom-call | flops 10000000 | bytes 1 | tf_op jit(solution)/shard_map/pallas_call | solution.py:377
  60.4 2.2 %collective-permute-start.24 = (bf16[40,1792]{1,0:T(8,128)(2,1)S(1)}, bf16[40,1792]{1,0:T(8,128)(2,1)S(1)}, u32[]{:S(2)}, u32[]{:S(2)}) collective-permute-start(bf16[40,1792]{1,0:T(8,128)(2,1)S(1)} %get-tuple-element.82), channel_id=1, source_target_pairs={{0,2},{2,0},{4,6},{6,4},{1,3},{3,1},{5,7},{7,5},{8,10},{10,8},{12,... | collective-permute-start | bytes 430088 | tf_op jit(solution)/shard_map/ppermute | solution.py:22
  64.8 2.0 %collective-permute-start.21 = (bf16[40,1792]{1,0:T(8,128)(2,1)S(1)}, bf16[40,1792]{1,0:T(8,128)(2,1)S(1)}, u32[]{:S(2)}, u32[]{:S(2)}) collective-permute-start(bf16[40,1792]{1,0:T(8,128)(2,1)S(1)} %get-tuple-element.78), channel_id=1, source_target_pairs={{0,2},{2,0},{4,6},{6,4},{1,3},{3,1},{5,7},{7,5},{8,10},{10,8},{12,... | collective-permute-start | bytes 430088 | tf_op jit(solution)/shard_map/ppermute | solution.py:22
  67.2 2.9 %collective-permute-done.25.refs_2_ = bf16[40,1792]{1,0:T(8,128)(2,1)S(1)} collective-permute-done((bf16[40,1792]{1,0:T(8,128)(2,1)S(1)}, bf16[40,1792]{1,0:T(8,128)(2,1)S(1)}, u32[]{:S(2)}, u32[]{:S(2)}) %collective-permute-start.25) | collective-permute-done | bytes 143392 | tf_op jit(solution)/shard_map/ppermute | solution.py:22
  70.6 1.6 %collective-permute-start.27 = (bf16[64,1792]{1,0:T(8,128)(2,1)S(1)}, bf16[64,1792]{1,0:T(8,128)(2,1)S(1)}, u32[]{:S(2)}, u32[]{:S(2)}) collective-permute-start(bf16[64,1792]{1,0:T(8,128)(2,1)S(1)} %shard_map.150.refs_4_), channel_id=1, source_target_pairs={{0,8},{1,9},{8,16},{9,17},{16,24},{17,25},{24,0},{25,1},{2,10},{3,... | collective-permute-start | bytes 688136 | tf_op jit(solution)/shard_map/ppermute | solution.py:32
  73.5 4.0 %shard_map.151.refs_4_ = bf16[1024,1792]{1,0:T(8,128)(2,1)} custom-call(bf16[320,1024]{1,0:T(8,128)(2,1)S(1)} %get-tuple-element.81.hidden, bf16[80,1792]{1,0:T(8,128)(2,1)S(1)} %get-tuple-element.61.refs_6_.refs_0_, bf16[80,1792]{1,0:T(8,128)(2,1)S(1)} %collective-permute-done.12.refs_1_, bf16[80,1792]{1,0:T(8,128)(2,1)S(1)} %collective-permute-done.13.refs_2_, ...), custom_call_target="tpu_custom_call" | custom-call | flops 1000000000 | bytes 1 | tf_op jit(solution)/shard_map/pallas_call | solution.py:438
  79.4 5.8 %shard_map.154 = (bf16[1792,1024]{1,0:T(8,128)(2,1)}, bf16[1792,1024]{1,0:T(8,128)(2,1)}) custom-call(bf16[320,1024]{1,0:T(8,128)(2,1)S(1)} %get-tuple-element.85.d_gate, bf16[320,1024]{1,0:T(8,128)(2,1)S(1)} %get-tuple-element.86.d_up, bf16[1792,320]{1,0:T(8,128)(2,1)S(1)} %shard_map.145.refs_6_.turned, bf16[64,3584]{1,0:T(8,128)(2,1)} %shard_map.153.refs_0_, ...), custom_call_target="tpu_custom_call" | custom-call | flops 1000000000 | bytes 1 | tf_op jit(solution)/shard_map/pallas_call | solution.py:413
  85.3 2.1 %collective-permute-done.28.rest_ref = bf16[64,1792]{1,0:T(8,128)(2,1)S(1)} collective-permute-done((bf16[64,1792]{1,0:T(8,128)(2,1)S(1)}, bf16[64,1792]{1,0:T(8,128)(2,1)S(1)}, u32[]{:S(2)}, u32[]{:S(2)}) %collective-permute-start.28) | collective-permute-done | bytes 229408 | tf_op jit(solution)/shard_map/ppermute | solution.py:32
  (53 shorter events, 23.7 us)
Async XLA Ops:
  5.0 10.3 %collective-permute-start.1 = (bf16[80,1792]{1,0:T(8,128)(2,1)S(1)}, bf16[80,1792]{1,0:T(8,128)(2,1)S(1)}, u32[]{:S(2)}, u32[]{:S(2)}) collective-permute-start(bf16[80,1792]{1,0:T(8,128)(2,1)S(1)} %get-tuple-element.51), channel_id=1, source_target_pairs={{0,2},{2,0},{4,6},{6,4},{1,3},{3,1},{5,7},{7,5},{8,10},{10,8},{12,... | collective-permute-start | bytes 860168 | tf_op jit(solution)/shard_map/ppermute | solution.py:22
  7.6 15.8 %collective-permute-start.2 = (bf16[80,1792]{1,0:T(8,128)(2,1)S(1)}, bf16[80,1792]{1,0:T(8,128)(2,1)S(1)}, u32[]{:S(2)}, u32[]{:S(2)}) collective-permute-start(bf16[80,1792]{1,0:T(8,128)(2,1)S(1)} %get-tuple-element.52), channel_id=1, source_target_pairs={{0,4},{2,6},{4,0},{6,2},{1,5},{3,7},{5,1},{7,3},{8,12},{10,14},{12... | collective-permute-start | bytes 860168 | tf_op jit(solution)/shard_map/ppermute | solution.py:22
  9.1 14.5 %collective-permute-start.3 = (bf16[80,1792]{1,0:T(8,128)(2,1)S(1)}, bf16[80,1792]{1,0:T(8,128)(2,1)S(1)}, u32[]{:S(2)}, u32[]{:S(2)}) collective-permute-start(bf16[80,1792]{1,0:T(8,128)(2,1)S(1)} %get-tuple-element.53), channel_id=1, source_target_pairs={{0,6},{2,4},{4,2},{6,0},{1,7},{3,5},{5,3},{7,1},{8,14},{10,12},{12... | collective-permute-start | bytes 860168 | tf_op jit(solution)/shard_map/ppermute | solution.py:22
  9.7 18.4 %collective-permute-start.6 = (bf16[80,1792]{1,0:T(8,128)(2,1)S(1)}, bf16[80,1792]{1,0:T(8,128)(2,1)S(1)}, u32[]{:S(2)}, u32[]{:S(2)}) collective-permute-start(bf16[80,1792]{1,0:T(8,128)(2,1)S(1)} %get-tuple-element.62), channel_id=1, source_target_pairs={{0,2},{2,0},{4,6},{6,4},{1,3},{3,1},{5,7},{7,5},{8,10},{10,8},{12,... | collective-permute-start | bytes 860168 | tf_op jit(solution)/shard_map/ppermute | solution.py:22
  11.7 24.0 %collective-permute-start.7 = (bf16[80,1792]{1,0:T(8,128)(2,1)S(1)}, bf16[80,1792]{1,0:T(8,128)(2,1)S(1)}, u32[]{:S(2)}, u32[]{:S(2)}) collective-permute-start(bf16[80,1792]{1,0:T(8,128)(2,1)S(1)} %get-tuple-element.63), channel_id=1, source_target_pairs={{0,4},{2,6},{4,0},{6,2},{1,5},{3,7},{5,1},{7,3},{8,12},{10,14},{12... | collective-permute-start | bytes 860168 | tf_op jit(solution)/shard_map/ppermute | solution.py:22
  15.3 20.5 %collective-permute-start.8 = (bf16[80,1792]{1,0:T(8,128)(2,1)S(1)}, bf16[80,1792]{1,0:T(8,128)(2,1)S(1)}, u32[]{:S(2)}, u32[]{:S(2)}) collective-permute-start(bf16[80,1792]{1,0:T(8,128)(2,1)S(1)} %get-tuple-element.64), channel_id=1, source_target_pairs={{0,6},{2,4},{4,2},{6,0},{1,7},{3,5},{5,3},{7,1},{8,14},{10,12},{12... | collective-permute-start | bytes 860168 | tf_op jit(solution)/shard_map/ppermute | solution.py:22
  23.4 19.5 %collective-permute-start.12 = (bf16[80,1792]{1,0:T(8,128)(2,1)S(1)}, bf16[80,1792]{1,0:T(8,128)(2,1)S(1)}, u32[]{:S(2)}, u32[]{:S(2)}) collective-permute-start(bf16[80,1792]{1,0:T(8,128)(2,1)S(1)} %get-tuple-element.69), channel_id=1, source_target_pairs={{0,2},{2,0},{4,6},{6,4},{1,3},{3,1},{5,7},{7,5},{8,10},{10,8},{12,... | collective-permute-start | bytes 860168 | tf_op jit(solution)/shard_map/ppermute | solution.py:22
  23.6 23.4 %collective-permute-start.13 = (bf16[80,1792]{1,0:T(8,128)(2,1)S(1)}, bf16[80,1792]{1,0:T(8,128)(2,1)S(1)}, u32[]{:S(2)}, u32[]{:S(2)}) collective-permute-start(bf16[80,1792]{1,0:T(8,128)(2,1)S(1)} %get-tuple-element.70), channel_id=1, source_target_pairs={{0,4},{2,6},{4,0},{6,2},{1,5},{3,7},{5,1},{7,3},{8,12},{10,14},{12... | collective-permute-start | bytes 860168 | tf_op jit(solution)/shard_map/ppermute | solution.py:22
  28.1 19.5 %collective-permute-start.14 = (bf16[80,1792]{1,0:T(8,128)(2,1)S(1)}, bf16[80,1792]{1,0:T(8,128)(2,1)S(1)}, u32[]{:S(2)}, u32[]{:S(2)}) collective-permute-start(bf16[80,1792]{1,0:T(8,128)(2,1)S(1)} %get-tuple-element.71), channel_id=1, source_target_pairs={{0,6},{2,4},{4,2},{6,0},{1,7},{3,5},{5,3},{7,1},{8,14},{10,12},{12... | collective-permute-start | bytes 860168 | tf_op jit(solution)/shard_map/ppermute | solution.py:22
  40.4 10.2 %collective-permute-start.9 = (bf16[40,1792]{1,0:T(8,128)(2,1)S(1)}, bf16[40,1792]{1,0:T(8,128)(2,1)S(1)}, u32[]{:S(2)}, u32[]{:S(2)}) collective-permute-start(bf16[40,1792]{1,0:T(8,128)(2,1)S(1)} %get-tuple-element.66), channel_id=1, source_target_pairs={{0,2},{2,0},{4,6},{6,4},{1,3},{3,1},{5,7},{7,5},{8,10},{10,8},{12,... | collective-permute-start | bytes 430088 | tf_op jit(solution)/shard_map/ppermute | solution.py:22
  41.1 12.2 %collective-permute-start.10 = (bf16[40,1792]{1,0:T(8,128)(2,1)S(1)}, bf16[40,1792]{1,0:T(8,128)(2,1)S(1)}, u32[]{:S(2)}, u32[]{:S(2)}) collective-permute-start(bf16[40,1792]{1,0:T(8,128)(2,1)S(1)} %get-tuple-element.67), channel_id=1, source_target_pairs={{0,4},{2,6},{4,0},{6,2},{1,5},{3,7},{5,1},{7,3},{8,12},{10,14},{12... | collective-permute-start | bytes 430088 | tf_op jit(solution)/shard_map/ppermute | solution.py:22
  43.0 11.8 %collective-permute-start.11 = (bf16[40,1792]{1,0:T(8,128)(2,1)S(1)}, bf16[40,1792]{1,0:T(8,128)(2,1)S(1)}, u32[]{:S(2)}, u32[]{:S(2)}) collective-permute-start(bf16[40,1792]{1,0:T(8,128)(2,1)S(1)} %get-tuple-element.68), channel_id=1, source_target_pairs={{0,6},{2,4},{4,2},{6,0},{1,7},{3,5},{5,3},{7,1},{8,14},{10,12},{12... | collective-permute-start | bytes 430088 | tf_op jit(solution)/shard_map/ppermute | solution.py:22
  49.0 8.2 %collective-permute-start.19 = (bf16[3,320,1024]{2,1,0:T(8,128)(2,1)S(1)}, bf16[3,320,1024]{2,1,0:T(8,128)(2,1)S(1)}, u32[]{:S(2)}, u32[]{:S(2)}) collective-permute-start(bf16[3,320,1024]{2,1,0:T(8,128)(2,1)S(1)} %shard_map.146.refs_4_.own_ref), channel_id=1, source_target_pairs={{0,1},{1,0},{2,3},{3,2},{4,5},{5,4},{6,7},{7,6},{8,9},{9,8},{10,11... | collective-permute-start | bytes 5898248 | tf_op jit(solution)/shard_map/ppermute | solution.py:22
  49.0 13.5 %collective-permute-start.16 = (bf16[40,1792]{1,0:T(8,128)(2,1)S(1)}, bf16[40,1792]{1,0:T(8,128)(2,1)S(1)}, u32[]{:S(2)}, u32[]{:S(2)}) collective-permute-start(bf16[40,1792]{1,0:T(8,128)(2,1)S(1)} %get-tuple-element.73), channel_id=1, source_target_pairs={{0,2},{2,0},{4,6},{6,4},{1,3},{3,1},{5,7},{7,5},{8,10},{10,8},{12,... | collective-permute-start | bytes 430088 | tf_op jit(solution)/shard_map/ppermute | solution.py:22
  50.6 12.0 %collective-permute-start.17 = (bf16[40,1792]{1,0:T(8,128)(2,1)S(1)}, bf16[40,1792]{1,0:T(8,128)(2,1)S(1)}, u32[]{:S(2)}, u32[]{:S(2)}) collective-permute-start(bf16[40,1792]{1,0:T(8,128)(2,1)S(1)} %get-tuple-element.74), channel_id=1, source_target_pairs={{0,4},{2,6},{4,0},{6,2},{1,5},{3,7},{5,1},{7,3},{8,12},{10,14},{12... | collective-permute-start | bytes 430088 | tf_op jit(solution)/shard_map/ppermute | solution.py:22
  53.3 10.8 %collective-permute-start.18 = (bf16[40,1792]{1,0:T(8,128)(2,1)S(1)}, bf16[40,1792]{1,0:T(8,128)(2,1)S(1)}, u32[]{:S(2)}, u32[]{:S(2)}) collective-permute-start(bf16[40,1792]{1,0:T(8,128)(2,1)S(1)} %get-tuple-element.75), channel_id=1, source_target_pairs={{0,6},{2,4},{4,2},{6,0},{1,7},{3,5},{5,3},{7,1},{8,14},{10,12},{12... | collective-permute-start | bytes 430088 | tf_op jit(solution)/shard_map/ppermute | solution.py:22
  55.4 9.4 %collective-permute-start.15 = (bf16[64,1792]{1,0:T(8,128)(2,1)S(1)}, bf16[64,1792]{1,0:T(8,128)(2,1)S(1)}, u32[]{:S(2)}, u32[]{:S(2)}) collective-permute-start(bf16[64,1792]{1,0:T(8,128)(2,1)S(1)} %shard_map.147.refs_0_), channel_id=1, source_target_pairs={{0,8},{1,9},{8,16},{9,17},{16,24},{17,25},{24,0},{25,1},{2,10},{3,... | collective-permute-start | bytes 688136 | tf_op jit(solution)/shard_map/ppermute | solution.py:32
  62.6 7.6 %collective-permute-start.25 = (bf16[40,1792]{1,0:T(8,128)(2,1)S(1)}, bf16[40,1792]{1,0:T(8,128)(2,1)S(1)}, u32[]{:S(2)}, u32[]{:S(2)}) collective-permute-start(bf16[40,1792]{1,0:T(8,128)(2,1)S(1)} %get-tuple-element.83), channel_id=1, source_target_pairs={{0,4},{2,6},{4,0},{6,2},{1,5},{3,7},{5,1},{7,3},{8,12},{10,14},{12... | collective-permute-start | bytes 430088 | tf_op jit(solution)/shard_map/ppermute | solution.py:22
  62.6 7.6 %collective-permute-start.26 = (bf16[40,1792]{1,0:T(8,128)(2,1)S(1)}, bf16[40,1792]{1,0:T(8,128)(2,1)S(1)}, u32[]{:S(2)}, u32[]{:S(2)}) collective-permute-start(bf16[40,1792]{1,0:T(8,128)(2,1)S(1)} %get-tuple-element.84), channel_id=1, source_target_pairs={{0,6},{2,4},{4,2},{6,0},{1,7},{3,5},{5,3},{7,1},{8,14},{10,12},{12... | collective-permute-start | bytes 430088 | tf_op jit(solution)/shard_map/ppermute | solution.py:22
  64.7 8.8 %collective-permute-start.20 = (bf16[64,1792]{1,0:T(8,128)(2,1)S(1)}, bf16[64,1792]{1,0:T(8,128)(2,1)S(1)}, u32[]{:S(2)}, u32[]{:S(2)}) collective-permute-start(bf16[64,1792]{1,0:T(8,128)(2,1)S(1)} %shard_map.149.refs_4_), channel_id=1, source_target_pairs={{0,9},{1,8},{8,17},{9,16},{16,25},{17,24},{24,1},{25,0},{2,11},{3,... | collective-permute-start | bytes 688136 | tf_op jit(solution)/shard_map/ppermute | solution.py:32
  64.8 12.7 %collective-permute-start.21 = (bf16[40,1792]{1,0:T(8,128)(2,1)S(1)}, bf16[40,1792]{1,0:T(8,128)(2,1)S(1)}, u32[]{:S(2)}, u32[]{:S(2)}) collective-permute-start(bf16[40,1792]{1,0:T(8,128)(2,1)S(1)} %get-tuple-element.78), channel_id=1, source_target_pairs={{0,2},{2,0},{4,6},{6,4},{1,3},{3,1},{5,7},{7,5},{8,10},{10,8},{12,... | collective-permute-start | bytes 430088 | tf_op jit(solution)/shard_map/ppermute | solution.py:22
  67.2 10.3 %collective-permute-start.22 = (bf16[40,1792]{1,0:T(8,128)(2,1)S(1)}, bf16[40,1792]{1,0:T(8,128)(2,1)S(1)}, u32[]{:S(2)}, u32[]{:S(2)}) collective-permute-start(bf16[40,1792]{1,0:T(8,128)(2,1)S(1)} %get-tuple-element.79), channel_id=1, source_target_pairs={{0,4},{2,6},{4,0},{6,2},{1,5},{3,7},{5,1},{7,3},{8,12},{10,14},{12... | collective-permute-start | bytes 430088 | tf_op jit(solution)/shard_map/ppermute | solution.py:22
  70.6 8.8 %collective-permute-start.27 = (bf16[64,1792]{1,0:T(8,128)(2,1)S(1)}, bf16[64,1792]{1,0:T(8,128)(2,1)S(1)}, u32[]{:S(2)}, u32[]{:S(2)}) collective-permute-start(bf16[64,1792]{1,0:T(8,128)(2,1)S(1)} %shard_map.150.refs_4_), channel_id=1, source_target_pairs={{0,8},{1,9},{8,16},{9,17},{16,24},{17,25},{24,0},{25,1},{2,10},{3,... | collective-permute-start | bytes 688136 | tf_op jit(solution)/shard_map/ppermute | solution.py:32
  77.9 9.4 %collective-permute-start.28 = (bf16[64,1792]{1,0:T(8,128)(2,1)S(1)}, bf16[64,1792]{1,0:T(8,128)(2,1)S(1)}, u32[]{:S(2)}, u32[]{:S(2)}) collective-permute-start(bf16[64,1792]{1,0:T(8,128)(2,1)S(1)} %shard_map.152.refs_0_), channel_id=1, source_target_pairs={{0,9},{1,8},{8,17},{9,16},{16,25},{17,24},{24,1},{25,0},{2,11},{3,... | collective-permute-start | bytes 688136 | tf_op jit(solution)/shard_map/ppermute | solution.py:32
  (5 other events, 23.5 us)

commit v7 on v6

--- a/solution.py
+++ b/solution.py
@@ -87,19 +87,16 @@
     return copies
 
 
-def pack_kernel(f_ref, x_ref, dy_ref, *refs):
-    sources, outs, (packed, sems), held = refs[:4], refs[4:9], refs[9:11], refs[11:]
-    own_f, other_f, own_x, own_dy, other_rest = outs
+def pack_kernel(f_ref, *refs):
+    sources, (own, other, packed, sems), held = refs[:4], refs[4:8], refs[8:]
     tokens = f_ref.shape[0]
-    copies = halves(f_ref, own_f, other_f, sems, 0)
     small = [
-        pltpu.make_async_copy(source, target, sems.at[6 + place])
+        pltpu.make_async_copy(source, target, sems.at[2 + place])
         for place, (source, target) in enumerate(zip(sources, held))
     ]
     for copy in small:
         copy.start()
-    copies += halves(x_ref, own_x, other_rest.at[0:tokens], sems, 2)
-    copies += halves(dy_ref, own_dy, other_rest.at[tokens : 2 * tokens], sems, 4)
+    copies = halves(f_ref, own, other, sems, 0)
     packed[...] = jnp.zeros_like(packed)
     for copy in small:
         copy.wait()
@@ -113,22 +110,42 @@
             rest = rest - top
     mine = packed[...]
     lanes = packed.shape[1]
-    own_f[tokens : tokens + META, 0:lanes] = mine.astype(BF16)
-    other_f[tokens : tokens + META, 0:lanes] = pltpu.roll(mine, tokens, 1).astype(BF16)
+    own[tokens : tokens + META, 0:lanes] = mine.astype(BF16)
+    other[tokens : tokens + META, 0:lanes] = pltpu.roll(mine, tokens, 1).astype(BF16)
     for copy in copies:
         copy.wait()
 
 
-def pack(f, x, dy, *small):
+def pack(f, *small):
     tokens, width = f.shape[0], f.shape[1] // 2
     return call(
         pack_kernel,
-        [array(tokens + META, width)] * 2 + [array(tokens, width)] * 2 + [array(2 * tokens, width)],
-        [HBM] * 7,
-        [VMEM] * 5,
-        [pltpu.VMEM((META, 2 * tokens), F32), pltpu.SemaphoreType.DMA((10,))]
+        [array(tokens + META, width)] * 2,
+        [HBM] * 5,
+        [VMEM] * 2,
+        [pltpu.VMEM((META, 2 * tokens), F32), pltpu.SemaphoreType.DMA((6,))]
         + [pltpu.VMEM(value.shape, value.dtype) for value in small],
-    )(f, x, dy, *small)
+    )(f, *small)
+
+
+def cut_kernel(x_ref, dy_ref, *refs):
+    own_x, own_dy, other, sems = refs[-4:]
+    tokens = x_ref.shape[0]
+    copies = halves(x_ref, own_x, other.at[0:tokens], sems, 0)
+    copies += halves(dy_ref, own_dy, other.at[tokens : 2 * tokens], sems, 2)
+    for copy in copies:
+        copy.wait()
+
+
+def cut(x, dy, after):
+    tokens, width = x.shape[0], x.shape[1] // 2
+    return call(
+        cut_kernel,
+        [array(tokens, width)] * 2 + [array(2 * tokens, width)],
+        [HBM] * 2 + [AFTER] * len(after),
+        [VMEM] * 3,
+        [pltpu.SemaphoreType.DMA((4,))],
+    )(x, dy, *after)
 
 
 def load_kernel(*refs, count):
@@ -290,7 +307,7 @@
 
 def d_hidden_kernel(*refs, blocks):
     down_w = refs[blocks]
-    out, rows = refs[-2:]
+    rows, out = refs[-2:]
     rows[...] = joined(refs[:blocks])
     for start in range(0, out.shape[2], TILE):
         part = slice(start, start + TILE)
@@ -301,12 +318,12 @@
     blocks, (rows, width) = len(inputs), inputs[0].shape
     return call(
         functools.partial(d_hidden_kernel, blocks=blocks),
-        array(*partial.shape),
+        [array(blocks * rows, width), array(*partial.shape)],
         [VMEM] * (blocks + 2) + [AFTER] * len(after),
-        VMEM,
-        [pltpu.VMEM((blocks * rows, width), BF16)],
+        [VMEM] * 2,
+        [],
         weight=weight,
-        aliases={blocks + 1: 0},
+        aliases={blocks + 1: 1},
     )(*inputs, down_w, partial, *after)
 
 
@@ -401,49 +418,26 @@
     )(*inputs, *after)
 
 
-def grad_in_kernel(d_gate, d_up, turned, *refs):
-    grad_gate, grad_up = refs[-2:]
+def grad_kernel(hidden, d_gate, d_up, turned, cots, *refs):
+    grad_gate, grad_up, grad_down = refs[-3:]
     part = pl.ds(pl.multiple_of(pl.program_id(0) * TILE, TILE), TILE)
     grad_gate[...] = dot(turned[...], d_gate[:, part], 1, 0).astype(BF16)
     grad_up[...] = dot(turned[...], d_up[:, part], 1, 0).astype(BF16)
-
-
-def grad_in(d_gate, d_up, turned, after=(), weight=1):
+    grad_down[...] = dot(hidden[:, part], cots[...], 0, 0).astype(BF16)
+
+
+def grads(hidden, d_gate, d_up, turned, cots, after=(), weight=1):
     width, units = turned.shape[0], d_gate.shape[1]
-    return call(
-        grad_in_kernel,
-        [pltpu.HBM((width, units), BF16)] * 2,
-        [VMEM] * 3 + [AFTER] * len(after),
-        [pl.BlockSpec((width, TILE), lambda i: (0, i))] * 2,
+    by_column = pl.BlockSpec((width, TILE), lambda i: (0, i))
+    return call(
+        grad_kernel,
+        [pltpu.HBM((width, units), BF16)] * 2 + [pltpu.HBM((units, width), BF16)],
+        [VMEM] * 5 + [AFTER] * len(after),
+        [by_column, by_column, pl.BlockSpec((TILE, width), lambda i: (i, 0))],
         [],
         grid=(units // TILE,),
         weight=weight,
-    )(d_gate, d_up, turned, *after)
-
-
-def grad_down_kernel(hidden, *refs, blocks):
-    cots, (grad, cot_all) = refs[:blocks], refs[-2:]
-
-    @pl.when(pl.program_id(0) == 0)
-    def _():
-        cot_all[...] = joined(cots)
-
-    part = pl.ds(pl.multiple_of(pl.program_id(0) * TILE, TILE), TILE)
-    grad[...] = dot(hidden[:, part], cot_all[...], 0, 0).astype(BF16)
-
-
-def grad_down(hidden, cots, after=(), weight=1):
-    blocks, (rows, width) = len(cots), cots[0].shape
-    total, units = hidden.shape
-    return call(
-        functools.partial(grad_down_kernel, blocks=blocks),
-        pltpu.HBM((units, width), BF16),
-        [VMEM] * (1 + blocks) + [AFTER] * len(after),
-        pl.BlockSpec((TILE, width), lambda i: (i, 0)),
-        [pltpu.VMEM((total, width), BF16)],
-        grid=(units // TILE,),
-        weight=weight,
-    )(hidden, *cots, *after)
+    )(hidden, d_gate, d_up, turned, cots, *after)
 
 
 def to_experts(blocks, relative):
@@ -455,15 +449,16 @@
     ]
 
 
-def finish_kernel(mine_ref, rest_ref, *refs):
-    out_ref, sems = refs[-2:]
-    width = mine_ref.shape[1]
+def finish_kernel(*refs):
+    sources, outs, sems = refs[:4], refs[-3:-1], refs[-1]
+    width = sources[0].shape[1]
     core = lax.axis_index("dp")
     copies = []
-    for place, (half, source) in enumerate(((core, mine_ref), (1 - core, rest_ref))):
+    for place, source in enumerate(sources):
+        half = core if place % 2 == 0 else 1 - core
         columns = pl.ds(pl.multiple_of(half * width, 128), width)
         copies.append(
-            pltpu.make_async_copy(source, out_ref.at[:, columns], sems.at[place])
+            pltpu.make_async_copy(source, outs[place // 2].at[:, columns], sems.at[place])
         )
     for copy in copies:
         copy.start()
@@ -471,15 +466,15 @@
         copy.wait()
 
 
-def finish(mine, rest, after=()):
-    tokens, width = mine.shape
+def finish(y_mine, y_rest, dx_mine, dx_rest, after):
+    tokens, width = y_mine.shape
     return call(
         finish_kernel,
-        pltpu.HBM((tokens, 2 * width), BF16),
-        [VMEM, VMEM] + [AFTER] * len(after),
-        HBM,
-        [pltpu.SemaphoreType.DMA((2,))],
-    )(mine, rest, *after)
+        [pltpu.HBM((tokens, 2 * width), BF16)] * 2,
+        [VMEM] * 4 + [AFTER] * len(after),
+        [HBM] * 2,
+        [pltpu.SemaphoreType.DMA((4,))],
+    )(y_mine, y_rest, dx_mine, dx_rest, *after)
 
 
 def local(x_fwd, ids_fwd, route_fwd, x_bwd, ids_bwd, route_bwd, dy_bwd, w_gate, w_up, w_down):
@@ -494,11 +489,12 @@
     plan = Plan(n_expert, (capacity + 7) // 8 * 8, group, tokens, relative)
     row_b, row_f = 0, META // 2
 
-    own_f, send_f, own_x, own_dy, send_rest = pack(
-        *[in_hbm(value[0]) for value in (x_fwd, x_bwd, dy_bwd)],
+    own_f, send_f = pack(
+        in_hbm(x_fwd[0]),
         *[in_hbm(value[0].T) for value in (ids_bwd, route_bwd, ids_fwd, route_fwd)],
     )
     other_f = exchange(send_f, "dp", 1)
+    own_x, own_dy, send_rest = cut(in_hbm(x_bwd[0]), in_hbm(dy_bwd[0]), after=(own_f,))
     metas = (own_f, other_f)
     *sent_f, send_rest = dispatch(
         metas, own_f, other_f, plan, row_f, 0, False, passing=(send_rest,)
@@ -522,7 +518,7 @@
     own_back_f = to_experts(down_blocks[:n_expert], relative)
     other_back_f = to_experts(down_blocks[n_expert:], relative)
     turned = turn(rows_b, after=down_blocks[:1])
-    part_b = d_hidden(cots_b, down_w, part_b, after=(in_vmem(turned),), weight=1000)
+    cots, part_b = d_hidden(cots_b, down_w, part_b, after=(in_vmem(turned),), weight=1000)
     part_b_other = exchange(part_b, "dp", 1)
     own_sum = combine(
         metas, own_back_f, plan, row_f, True, False, after=(in_vmem(part_b),), weight=2000
@@ -548,7 +544,6 @@
         weight=150,
     )
     dx_mine = section_shift(own_sum, 0)
-    grad_d = grad_down(hidden, cots_b, after=(own_sum, in_vmem(y_rest)), weight=100)
     other_sum = combine(
         metas,
         other_back_b,
@@ -556,14 +551,14 @@
         row_b,
         False,
         True,
-        after=(in_hbm(grad_d),),
+        after=(own_sum, in_vmem(y_rest)),
+        weight=100,
     )
     dx_rest = section_shift(other_sum, 1)
-    y_next = finish(y_mine, y_rest, after=(other_sum,))
-    grad_g, grad_u = grad_in(
-        d_gate, d_up, turned, after=(in_hbm(y_next), in_vmem(dx_mine)), weight=100
-    )
-    dx_next = finish(dx_mine, dx_rest, after=(in_hbm(grad_g),))
+    grad_g, grad_u, grad_d = grads(
+        hidden, d_gate, d_up, turned, cots, after=(other_sum, in_vmem(dx_mine)), weight=100
+    )
+    y_next, dx_next = finish(y_mine, y_rest, dx_mine, dx_rest, after=(in_hbm(grad_g),))
     return (
         y_next[None],
         dx_next[None],

time: 88.4 us -> 87.7 us (level)
  Pallas kernels: 32.8 us -> 30.7 us
  waiting for transfers between devices: 21.1 us -> 22 us
    ppermute x25, waiting for transfers between devices: 17.7 us -> 21 us  [exchange(): lax.ppermute(value, axis, [(source, source ^ mask) for source in range(co...]
    ppermute x4, waiting for transfers between devices: 3.33 us -> 1.04 us  [section_shift(): return lax.ppermute(value, ('section', 'dp'), pairs)]
    pallas_call x6 -> x5, Pallas kernels: 14.3 us -> 12.2 us  [the longest x1 7.37 us: grads(): call(grad_kernel, [pltpu.HBM((width, units), BF16)] * 2 + [pltpu.HBM((uni...]
  transfers between devices with their start and end apart: 29 -> 29, of which waited for: 12 -> 13; matrix products, arithmetic and copies ran while one was open for 0% -> 0% of each run, Pallas kernels for 34% -> 32%
where the time goes in v7:
time: 87.7 us; the launch traced here: 87.5 us
  starting transfers between devices  33.8 us (39%)
  Pallas kernels  30.7 us (35%)
  waiting for transfers between devices  22 us (25%)
  between operations  0.98 us (1%)
    ppermute x25, starting transfers between devices, exchange(): lax.ppermute(value, axis, [(source, source ^ mask) for source in range(co...  29 us
    ppermute x25, waiting for transfers between devices, exchange(): lax.ppermute(value, axis, [(source, source ^ mask) for source in range(co...  21 us
    pallas_call x1, Pallas kernels, grads(): call(grad_kernel, [pltpu.HBM((width, units), BF16)] * 2 + [pltpu.HBM((uni...  7.37 us
    pallas_call x2, Pallas kernels, gate_up(): call(functools.partial(gate_up_kernel, blocks=blocks), array(planes, tota...  5.22 us
    ppermute x4, starting transfers between devices, section_shift(): return lax.ppermute(value, ('section', 'dp'), pairs)  4.73 us
    pallas_call x1, Pallas kernels, load(): call(functools.partial(load_kernel, count=len(weights)), [array(*weight.s...  4.23 us
    pallas_call x1, Pallas kernels, back(): call(functools.partial(back_kernel, blocks=plan.blocks), [array(total, un...  3.23 us
    pallas_call x4, Pallas kernels, combine(): call(functools.partial(combine_kernel, plan=plan, first_row=first_row, we...  2.05 us
  transfers between devices with their start and end apart: 29, of which 13 were waited for; matrix products, arithmetic and copies ran while one was open for 0% of the time, Pallas kernels for 32%

profile of v7, /device:TPU:0, one launch (start us, length us, event | category | flops | bytes accessed | tf_op | source)
XLA Modules:
  0.0 87.5 jit_solution(16403199821831781029)
XLA Ops:
  4.5 2.8 %collective-permute-start.1 = (bf16[80,1792]{1,0:T(8,128)(2,1)S(1)}, bf16[80,1792]{1,0:T(8,128)(2,1)S(1)}, u32[]{:S(2)}, u32[]{:S(2)}) collective-permute-start(bf16[80,1792]{1,0:T(8,128)(2,1)S(1)} %get-tuple-element.56), channel_id=1, source_target_pairs={{0,2},{2,0},{4,6},{6,4},{1,3},{3,1},{5,7},{7,5},{8,10},{10,8},{12,... | collective-permute-start | bytes 860168 | tf_op jit(solution)/shard_map/ppermute | solution.py:22
  7.3 1.5 %collective-permute-start.2 = (bf16[80,1792]{1,0:T(8,128)(2,1)S(1)}, bf16[80,1792]{1,0:T(8,128)(2,1)S(1)}, u32[]{:S(2)}, u32[]{:S(2)}) collective-permute-start(bf16[80,1792]{1,0:T(8,128)(2,1)S(1)} %get-tuple-element.57), channel_id=1, source_target_pairs={{0,4},{2,6},{4,0},{6,2},{1,5},{3,7},{5,1},{7,3},{8,12},{10,14},{12... | collective-permute-start | bytes 860168 | tf_op jit(solution)/shard_map/ppermute | solution.py:22
  9.4 2.0 %collective-permute-start.6 = (bf16[80,1792]{1,0:T(8,128)(2,1)S(1)}, bf16[80,1792]{1,0:T(8,128)(2,1)S(1)}, u32[]{:S(2)}, u32[]{:S(2)}) collective-permute-start(bf16[80,1792]{1,0:T(8,128)(2,1)S(1)} %get-tuple-element.67), channel_id=1, source_target_pairs={{0,2},{2,0},{4,6},{6,4},{1,3},{3,1},{5,7},{7,5},{8,10},{10,8},{12,... | collective-permute-start | bytes 860168 | tf_op jit(solution)/shard_map/ppermute | solution.py:22
  13.0 1.9 %collective-permute-done.1.refs_1_ = bf16[80,1792]{1,0:T(8,128)(2,1)S(1)} collective-permute-done((bf16[80,1792]{1,0:T(8,128)(2,1)S(1)}, bf16[80,1792]{1,0:T(8,128)(2,1)S(1)}, u32[]{:S(2)}, u32[]{:S(2)}) %collective-permute-start.1) | collective-permute-done | bytes 286752 | tf_op jit(solution)/shard_map/ppermute | solution.py:22
  14.9 3.0 %collective-permute-start.8 = (bf16[80,1792]{1,0:T(8,128)(2,1)S(1)}, bf16[80,1792]{1,0:T(8,128)(2,1)S(1)}, u32[]{:S(2)}, u32[]{:S(2)}) collective-permute-start(bf16[80,1792]{1,0:T(8,128)(2,1)S(1)} %get-tuple-element.69), channel_id=1, source_target_pairs={{0,6},{2,4},{4,2},{6,0},{1,7},{3,5},{5,3},{7,1},{8,14},{10,12},{12... | collective-permute-start | bytes 860168 | tf_op jit(solution)/shard_map/ppermute | solution.py:22
  17.9 4.2 %shard_map.141 = (bf16[1792,1024]{1,0:T(8,128)(2,1)S(1)}, bf16[1792,1024]{1,0:T(8,128)(2,1)S(1)}, bf16[1024,1792]{1,0:T(8,128)(2,1)S(1)}) custom-call(bf16[1792,1024]{1,0:T(8,128)(2,1)} %bitcast.23, bf16[1792,1024]{1,0:T(8,128)(2,1)} %bitcast.24, bf16[1024,1792]{1,0:T(8,128)(2,1)} %bitcast.25, bf16[80,1792]{1,0:T(8,128)(2,1)S(1)} %get-tuple-element.61.refs_3_.refs_0_), custom_call_target="tpu_custom_call" | custom-call | flops 10000000 | bytes 1 | tf_op jit(solution)/shard_map/pallas_call | solution.py:164
  23.4 1.8 %collective-permute-start.13 = (bf16[80,1792]{1,0:T(8,128)(2,1)S(1)}, bf16[80,1792]{1,0:T(8,128)(2,1)S(1)}, u32[]{:S(2)}, u32[]{:S(2)}) collective-permute-start(bf16[80,1792]{1,0:T(8,128)(2,1)S(1)} %get-tuple-element.75), channel_id=1, source_target_pairs={{0,4},{2,6},{4,0},{6,2},{1,5},{3,7},{5,1},{7,3},{8,12},{10,14},{12... | collective-permute-start | bytes 860168 | tf_op jit(solution)/shard_map/ppermute | solution.py:22
  25.2 2.6 %shard_map.143.refs_6_.own_ref = bf16[2,320,1024]{2,1,0:T(8,128)(2,1)S(1)} custom-call(bf16[80,1792]{1,0:T(8,128)(2,1)S(1)} %get-tuple-element.55.refs_0_, bf16[80,1792]{1,0:T(8,128)(2,1)S(1)} %collective-permute-done.1.refs_1_, bf16[80,1792]{1,0:T(8,128)(2,1)S(1)} %collective-permute-done.2.refs_2_, bf16[80,1792]{1,0:T(8,128)(2,1)S(1)} %collective-permute-done.3.refs_3_, ...), custom_call_target="tpu_custom_call" | custom-call | flops 10000000 | bytes 1 | tf_op jit(solution)/shard_map/pallas_call | solution.py:298
  27.8 2.4 %collective-permute-start.14 = (bf16[80,1792]{1,0:T(8,128)(2,1)S(1)}, bf16[80,1792]{1,0:T(8,128)(2,1)S(1)}, u32[]{:S(2)}, u32[]{:S(2)}) collective-permute-start(bf16[80,1792]{1,0:T(8,128)(2,1)S(1)} %get-tuple-element.76), channel_id=1, source_target_pairs={{0,6},{2,4},{4,2},{6,0},{1,7},{3,5},{5,3},{7,1},{8,14},{10,12},{12... | collective-permute-start | bytes 860168 | tf_op jit(solution)/shard_map/ppermute | solution.py:22
  30.3 5.2 %collective-permute-done.7.refs_2_ = bf16[80,1792]{1,0:T(8,128)(2,1)S(1)} collective-permute-done((bf16[80,1792]{1,0:T(8,128)(2,1)S(1)}, bf16[80,1792]{1,0:T(8,128)(2,1)S(1)}, u32[]{:S(2)}, u32[]{:S(2)}) %collective-permute-start.7) | collective-permute-done | bytes 286752 | tf_op jit(solution)/shard_map/ppermute | solution.py:22
  35.4 2.6 %shard_map.144.refs_0_.refs_5_ = bf16[3,320,1024]{2,1,0:T(8,128)(2,1)S(1)} custom-call(bf16[80,1792]{1,0:T(8,128)(2,1)S(1)} %get-tuple-element.61.refs_3_.refs_0_, bf16[80,1792]{1,0:T(8,128)(2,1)S(1)} %collective-permute-done.6.refs_1_, bf16[80,1792]{1,0:T(8,128)(2,1)S(1)} %collective-permute-done.7.refs_2_, ...), custom_call_target="tpu_custom_call" | custom-call | flops 30000001024 | bytes 1 | tf_op jit(solution)/shard_map/pallas_call | solution.py:298
  38.5 1.7 %shard_map.145 = (bf16[40,1792]{1,0:T(8,128)(2,1)S(1)}, bf16[40,1792]{1,0:T(8,128)(2,1)S(1)}, bf16[40,1792]{1,0:T(8,128)(2,1)S(1)}, bf16[40,1792]{1,0:T(8,128)(2...) custom-call(bf16[2,320,1024]{2,1,0:T(8,128)(2,1)S(1)} %shard_map.143, ...), custom_call_target="tpu_custom_call" | custom-call | flops 10000000 | bytes 1 | tf_op jit(solution)/shard_map/pallas_call | solution.py:361
  44.2 2.6 %collective-permute-done.13.refs_2_ = bf16[80,1792]{1,0:T(8,128)(2,1)S(1)} collective-permute-done((bf16[80,1792]{1,0:T(8,128)(2,1)S(1)}, bf16[80,1792]{1,0:T(8,128)(2,1)S(1)}, u32[]{:S(2)}, u32[]{:S(2)}) %collective-permute-start.13) | collective-permute-done | bytes 286752 | tf_op jit(solution)/shard_map/ppermute | solution.py:22
  48.8 1.6 %collective-permute-start.16 = (bf16[40,1792]{1,0:T(8,128)(2,1)S(1)}, bf16[40,1792]{1,0:T(8,128)(2,1)S(1)}, u32[]{:S(2)}, u32[]{:S(2)}) collective-permute-start(bf16[40,1792]{1,0:T(8,128)(2,1)S(1)} %get-tuple-element.79), channel_id=1, source_target_pairs={{0,2},{2,0},{4,6},{6,4},{1,3},{3,1},{5,7},{7,5},{8,10},{10,8},{12,... | collective-permute-start | bytes 430088 | tf_op jit(solution)/shard_map/ppermute | solution.py:22
  50.9 1.9 %collective-permute-done.10.refs_2_ = bf16[40,1792]{1,0:T(8,128)(2,1)S(1)} collective-permute-done((bf16[40,1792]{1,0:T(8,128)(2,1)S(1)}, bf16[40,1792]{1,0:T(8,128)(2,1)S(1)}, u32[]{:S(2)}, u32[]{:S(2)}) %collective-permute-start.10) | collective-permute-done | bytes 143392 | tf_op jit(solution)/shard_map/ppermute | solution.py:22
  54.9 1.8 %collective-permute-start.15 = (bf16[64,1792]{1,0:T(8,128)(2,1)S(1)}, bf16[64,1792]{1,0:T(8,128)(2,1)S(1)}, u32[]{:S(2)}, u32[]{:S(2)}) collective-permute-start(bf16[64,1792]{1,0:T(8,128)(2,1)S(1)} %shard_map.148.refs_0_), channel_id=1, source_target_pairs={{0,8},{1,9},{8,16},{9,17},{16,24},{17,25},{24,0},{25,1},{2,10},{3,... | collective-permute-start | bytes 688136 | tf_op jit(solution)/shard_map/ppermute | solution.py:32
  56.8 3.2 %shard_map.149 = (bf16[320,1024]{1,0:T(8,128)(2,1)S(1)}, bf16[320,1024]{1,0:T(8,128)(2,1)S(1)}, bf16[320,1024]{1,0:T(8,128)(2,1)S(1)}, bf16[40,1792]{1,0:T(8,128...) custom-call(bf16[3,320,1024]{2,1,0:T(8,128)(2,1)S(1)} %get-tuple-ele, ...), custom_call_target="tpu_custom_call" | custom-call | flops 10000000 | bytes 1 | tf_op jit(solution)/shard_map/pallas_call | solution.py:394
  60.0 2.1 %collective-permute-start.21 = (bf16[40,1792]{1,0:T(8,128)(2,1)S(1)}, bf16[40,1792]{1,0:T(8,128)(2,1)S(1)}, u32[]{:S(2)}, u32[]{:S(2)}) collective-permute-start(bf16[40,1792]{1,0:T(8,128)(2,1)S(1)} %get-tuple-element.83), channel_id=1, source_target_pairs={{0,2},{2,0},{4,6},{6,4},{1,3},{3,1},{5,7},{7,5},{8,10},{10,8},{12,... | collective-permute-start | bytes 430088 | tf_op jit(solution)/shard_map/ppermute | solution.py:22
  62.1 1.5 %collective-permute-start.23 = (bf16[40,1792]{1,0:T(8,128)(2,1)S(1)}, bf16[40,1792]{1,0:T(8,128)(2,1)S(1)}, u32[]{:S(2)}, u32[]{:S(2)}) collective-permute-start(bf16[40,1792]{1,0:T(8,128)(2,1)S(1)} %get-tuple-element.85), channel_id=1, source_target_pairs={{0,6},{2,4},{4,2},{6,0},{1,7},{3,5},{5,3},{7,1},{8,14},{10,12},{12... | collective-permute-start | bytes 430088 | tf_op jit(solution)/shard_map/ppermute | solution.py:22
  64.3 1.9 %collective-permute-start.25 = (bf16[40,1792]{1,0:T(8,128)(2,1)S(1)}, bf16[40,1792]{1,0:T(8,128)(2,1)S(1)}, u32[]{:S(2)}, u32[]{:S(2)}) collective-permute-start(bf16[40,1792]{1,0:T(8,128)(2,1)S(1)} %get-tuple-element.87), channel_id=1, source_target_pairs={{0,2},{2,0},{4,6},{6,4},{1,3},{3,1},{5,7},{7,5},{8,10},{10,8},{12,... | collective-permute-start | bytes 430088 | tf_op jit(solution)/shard_map/ppermute | solution.py:22
  66.7 2.9 %collective-permute-done.22.refs_2_ = bf16[40,1792]{1,0:T(8,128)(2,1)S(1)} collective-permute-done((bf16[40,1792]{1,0:T(8,128)(2,1)S(1)}, bf16[40,1792]{1,0:T(8,128)(2,1)S(1)}, u32[]{:S(2)}, u32[]{:S(2)}) %collective-permute-start.22) | collective-permute-done | bytes 143392 | tf_op jit(solution)/shard_map/ppermute | solution.py:22
  70.1 1.6 %collective-permute-start.24 = (bf16[64,1792]{1,0:T(8,128)(2,1)S(1)}, bf16[64,1792]{1,0:T(8,128)(2,1)S(1)}, u32[]{:S(2)}, u32[]{:S(2)}) collective-permute-start(bf16[64,1792]{1,0:T(8,128)(2,1)S(1)} %shard_map.151.refs_4_), channel_id=1, source_target_pairs={{0,8},{1,9},{8,16},{9,17},{16,24},{17,25},{24,0},{25,1},{2,10},{3,... | collective-permute-start | bytes 688136 | tf_op jit(solution)/shard_map/ppermute | solution.py:32
  71.8 4.6 %collective-permute-done.26.refs_2_ = bf16[40,1792]{1,0:T(8,128)(2,1)S(1)} collective-permute-done((bf16[40,1792]{1,0:T(8,128)(2,1)S(1)}, bf16[40,1792]{1,0:T(8,128)(2,1)S(1)}, u32[]{:S(2)}, u32[]{:S(2)}) %collective-permute-start.26) | collective-permute-done | bytes 143392 | tf_op jit(solution)/shard_map/ppermute | solution.py:22
  78.7 7.4 %shard_map.153 = (bf16[1792,1024]{1,0:T(8,128)(2,1)}, bf16[1792,1024]{1,0:T(8,128)(2,1)}, bf16[1024,1792]{1,0:T(8,128)(2,1)}) custom-call(bf16[320,1024]{1,0:T(8,128)(2,1)S(1)} %get-tuple-element.90.hidden, bf16[320,1024]{1,0:T(8,128)(2,1)S(1)} %get-tuple-element.91.d_gate, bf16[320,1024]{1,0:T(8,128)(2,1)S(1)} %get-tuple-element.92.d_up, ...), custom_call_target="tpu_custom_call" | custom-call | flops 1000000000 | bytes 1 | tf_op jit(solution)/shard_map/pallas_call | solution.py:432
  (52 shorter events, 21.6 us)
Async XLA Ops:
  4.5 10.4 %collective-permute-start.1 = (bf16[80,1792]{1,0:T(8,128)(2,1)S(1)}, bf16[80,1792]{1,0:T(8,128)(2,1)S(1)}, u32[]{:S(2)}, u32[]{:S(2)}) collective-permute-start(bf16[80,1792]{1,0:T(8,128)(2,1)S(1)} %get-tuple-element.56), channel_id=1, source_target_pairs={{0,2},{2,0},{4,6},{6,4},{1,3},{3,1},{5,7},{7,5},{8,10},{10,8},{12,... | collective-permute-start | bytes 860168 | tf_op jit(solution)/shard_map/ppermute | solution.py:22
  7.3 15.8 %collective-permute-start.2 = (bf16[80,1792]{1,0:T(8,128)(2,1)S(1)}, bf16[80,1792]{1,0:T(8,128)(2,1)S(1)}, u32[]{:S(2)}, u32[]{:S(2)}) collective-permute-start(bf16[80,1792]{1,0:T(8,128)(2,1)S(1)} %get-tuple-element.57), channel_id=1, source_target_pairs={{0,4},{2,6},{4,0},{6,2},{1,5},{3,7},{5,1},{7,3},{8,12},{10,14},{12... | collective-permute-start | bytes 860168 | tf_op jit(solution)/shard_map/ppermute | solution.py:22
  8.8 14.5 %collective-permute-start.3 = (bf16[80,1792]{1,0:T(8,128)(2,1)S(1)}, bf16[80,1792]{1,0:T(8,128)(2,1)S(1)}, u32[]{:S(2)}, u32[]{:S(2)}) collective-permute-start(bf16[80,1792]{1,0:T(8,128)(2,1)S(1)} %get-tuple-element.58), channel_id=1, source_target_pairs={{0,6},{2,4},{4,2},{6,0},{1,7},{3,5},{5,3},{7,1},{8,14},{10,12},{12... | collective-permute-start | bytes 860168 | tf_op jit(solution)/shard_map/ppermute | solution.py:22
  9.4 18.4 %collective-permute-start.6 = (bf16[80,1792]{1,0:T(8,128)(2,1)S(1)}, bf16[80,1792]{1,0:T(8,128)(2,1)S(1)}, u32[]{:S(2)}, u32[]{:S(2)}) collective-permute-start(bf16[80,1792]{1,0:T(8,128)(2,1)S(1)} %get-tuple-element.67), channel_id=1, source_target_pairs={{0,2},{2,0},{4,6},{6,4},{1,3},{3,1},{5,7},{7,5},{8,10},{10,8},{12,... | collective-permute-start | bytes 860168 | tf_op jit(solution)/shard_map/ppermute | solution.py:22
  11.5 24.0 %collective-permute-start.7 = (bf16[80,1792]{1,0:T(8,128)(2,1)S(1)}, bf16[80,1792]{1,0:T(8,128)(2,1)S(1)}, u32[]{:S(2)}, u32[]{:S(2)}) collective-permute-start(bf16[80,1792]{1,0:T(8,128)(2,1)S(1)} %get-tuple-element.68), channel_id=1, source_target_pairs={{0,4},{2,6},{4,0},{6,2},{1,5},{3,7},{5,1},{7,3},{8,12},{10,14},{12... | collective-permute-start | bytes 860168 | tf_op jit(solution)/shard_map/ppermute | solution.py:22
  14.9 20.5 %collective-permute-start.8 = (bf16[80,1792]{1,0:T(8,128)(2,1)S(1)}, bf16[80,1792]{1,0:T(8,128)(2,1)S(1)}, u32[]{:S(2)}, u32[]{:S(2)}) collective-permute-start(bf16[80,1792]{1,0:T(8,128)(2,1)S(1)} %get-tuple-element.69), channel_id=1, source_target_pairs={{0,6},{2,4},{4,2},{6,0},{1,7},{3,5},{5,3},{7,1},{8,14},{10,12},{12... | collective-permute-start | bytes 860168 | tf_op jit(solution)/shard_map/ppermute | solution.py:22
  23.2 19.5 %collective-permute-start.12 = (bf16[80,1792]{1,0:T(8,128)(2,1)S(1)}, bf16[80,1792]{1,0:T(8,128)(2,1)S(1)}, u32[]{:S(2)}, u32[]{:S(2)}) collective-permute-start(bf16[80,1792]{1,0:T(8,128)(2,1)S(1)} %get-tuple-element.74), channel_id=1, source_target_pairs={{0,2},{2,0},{4,6},{6,4},{1,3},{3,1},{5,7},{7,5},{8,10},{10,8},{12,... | collective-permute-start | bytes 860168 | tf_op jit(solution)/shard_map/ppermute | solution.py:22
  23.4 23.4 %collective-permute-start.13 = (bf16[80,1792]{1,0:T(8,128)(2,1)S(1)}, bf16[80,1792]{1,0:T(8,128)(2,1)S(1)}, u32[]{:S(2)}, u32[]{:S(2)}) collective-permute-start(bf16[80,1792]{1,0:T(8,128)(2,1)S(1)} %get-tuple-element.75), channel_id=1, source_target_pairs={{0,4},{2,6},{4,0},{6,2},{1,5},{3,7},{5,1},{7,3},{8,12},{10,14},{12... | collective-permute-start | bytes 860168 | tf_op jit(solution)/shard_map/ppermute | solution.py:22
  27.8 19.5 %collective-permute-start.14 = (bf16[80,1792]{1,0:T(8,128)(2,1)S(1)}, bf16[80,1792]{1,0:T(8,128)(2,1)S(1)}, u32[]{:S(2)}, u32[]{:S(2)}) collective-permute-start(bf16[80,1792]{1,0:T(8,128)(2,1)S(1)} %get-tuple-element.76), channel_id=1, source_target_pairs={{0,6},{2,4},{4,2},{6,0},{1,7},{3,5},{5,3},{7,1},{8,14},{10,12},{12... | collective-permute-start | bytes 860168 | tf_op jit(solution)/shard_map/ppermute | solution.py:22
  40.1 10.2 %collective-permute-start.9 = (bf16[40,1792]{1,0:T(8,128)(2,1)S(1)}, bf16[40,1792]{1,0:T(8,128)(2,1)S(1)}, u32[]{:S(2)}, u32[]{:S(2)}) collective-permute-start(bf16[40,1792]{1,0:T(8,128)(2,1)S(1)} %get-tuple-element.71), channel_id=1, source_target_pairs={{0,2},{2,0},{4,6},{6,4},{1,3},{3,1},{5,7},{7,5},{8,10},{10,8},{12,... | collective-permute-start | bytes 430088 | tf_op jit(solution)/shard_map/ppermute | solution.py:22
  40.8 12.1 %collective-permute-start.10 = (bf16[40,1792]{1,0:T(8,128)(2,1)S(1)}, bf16[40,1792]{1,0:T(8,128)(2,1)S(1)}, u32[]{:S(2)}, u32[]{:S(2)}) collective-permute-start(bf16[40,1792]{1,0:T(8,128)(2,1)S(1)} %get-tuple-element.72), channel_id=1, source_target_pairs={{0,4},{2,6},{4,0},{6,2},{1,5},{3,7},{5,1},{7,3},{8,12},{10,14},{12... | collective-permute-start | bytes 430088 | tf_op jit(solution)/shard_map/ppermute | solution.py:22
  42.7 11.7 %collective-permute-start.11 = (bf16[40,1792]{1,0:T(8,128)(2,1)S(1)}, bf16[40,1792]{1,0:T(8,128)(2,1)S(1)}, u32[]{:S(2)}, u32[]{:S(2)}) collective-permute-start(bf16[40,1792]{1,0:T(8,128)(2,1)S(1)} %get-tuple-element.73), channel_id=1, source_target_pairs={{0,6},{2,4},{4,2},{6,0},{1,7},{3,5},{5,3},{7,1},{8,14},{10,12},{12... | collective-permute-start | bytes 430088 | tf_op jit(solution)/shard_map/ppermute | solution.py:22
  48.7 8.1 %collective-permute-start.19 = (bf16[3,320,1024]{2,1,0:T(8,128)(2,1)S(1)}, bf16[3,320,1024]{2,1,0:T(8,128)(2,1)S(1)}, u32[]{:S(2)}, u32[]{:S(2)}) collective-permute-start(bf16[3,320,1024]{2,1,0:T(8,128)(2,1)S(1)} %get-tuple-element.77.refs_4_.own_ref), channel_id=1, source_target_pairs={{0,1},{1,0},{2,3},{3,2},{4,5},{5,4},{6,7},{7,6},{8,9},{9,8},{10,11... | collective-permute-start | bytes 5898248 | tf_op jit(solution)/shard_map/ppermute | solution.py:22
  48.8 13.3 %collective-permute-start.16 = (bf16[40,1792]{1,0:T(8,128)(2,1)S(1)}, bf16[40,1792]{1,0:T(8,128)(2,1)S(1)}, u32[]{:S(2)}, u32[]{:S(2)}) collective-permute-start(bf16[40,1792]{1,0:T(8,128)(2,1)S(1)} %get-tuple-element.79), channel_id=1, source_target_pairs={{0,2},{2,0},{4,6},{6,4},{1,3},{3,1},{5,7},{7,5},{8,10},{10,8},{12,... | collective-permute-start | bytes 430088 | tf_op jit(solution)/shard_map/ppermute | solution.py:22
  50.3 11.7 %collective-permute-start.17 = (bf16[40,1792]{1,0:T(8,128)(2,1)S(1)}, bf16[40,1792]{1,0:T(8,128)(2,1)S(1)}, u32[]{:S(2)}, u32[]{:S(2)}) collective-permute-start(bf16[40,1792]{1,0:T(8,128)(2,1)S(1)} %get-tuple-element.80), channel_id=1, source_target_pairs={{0,4},{2,6},{4,0},{6,2},{1,5},{3,7},{5,1},{7,3},{8,12},{10,14},{12... | collective-permute-start | bytes 430088 | tf_op jit(solution)/shard_map/ppermute | solution.py:22
  52.9 10.7 %collective-permute-start.18 = (bf16[40,1792]{1,0:T(8,128)(2,1)S(1)}, bf16[40,1792]{1,0:T(8,128)(2,1)S(1)}, u32[]{:S(2)}, u32[]{:S(2)}) collective-permute-start(bf16[40,1792]{1,0:T(8,128)(2,1)S(1)} %get-tuple-element.81), channel_id=1, source_target_pairs={{0,6},{2,4},{4,2},{6,0},{1,7},{3,5},{5,3},{7,1},{8,14},{10,12},{12... | collective-permute-start | bytes 430088 | tf_op jit(solution)/shard_map/ppermute | solution.py:22
  54.9 9.4 %collective-permute-start.15 = (bf16[64,1792]{1,0:T(8,128)(2,1)S(1)}, bf16[64,1792]{1,0:T(8,128)(2,1)S(1)}, u32[]{:S(2)}, u32[]{:S(2)}) collective-permute-start(bf16[64,1792]{1,0:T(8,128)(2,1)S(1)} %shard_map.148.refs_0_), channel_id=1, source_target_pairs={{0,8},{1,9},{8,16},{9,17},{16,24},{17,25},{24,0},{25,1},{2,10},{3,... | collective-permute-start | bytes 688136 | tf_op jit(solution)/shard_map/ppermute | solution.py:32
  62.0 7.6 %collective-permute-start.22 = (bf16[40,1792]{1,0:T(8,128)(2,1)S(1)}, bf16[40,1792]{1,0:T(8,128)(2,1)S(1)}, u32[]{:S(2)}, u32[]{:S(2)}) collective-permute-start(bf16[40,1792]{1,0:T(8,128)(2,1)S(1)} %get-tuple-element.84), channel_id=1, source_target_pairs={{0,4},{2,6},{4,0},{6,2},{1,5},{3,7},{5,1},{7,3},{8,12},{10,14},{12... | collective-permute-start | bytes 430088 | tf_op jit(solution)/shard_map/ppermute | solution.py:22
  62.1 7.6 %collective-permute-start.23 = (bf16[40,1792]{1,0:T(8,128)(2,1)S(1)}, bf16[40,1792]{1,0:T(8,128)(2,1)S(1)}, u32[]{:S(2)}, u32[]{:S(2)}) collective-permute-start(bf16[40,1792]{1,0:T(8,128)(2,1)S(1)} %get-tuple-element.85), channel_id=1, source_target_pairs={{0,6},{2,4},{4,2},{6,0},{1,7},{3,5},{5,3},{7,1},{8,14},{10,12},{12... | collective-permute-start | bytes 430088 | tf_op jit(solution)/shard_map/ppermute | solution.py:22
  64.2 12.2 %collective-permute-start.20 = (bf16[64,1792]{1,0:T(8,128)(2,1)S(1)}, bf16[64,1792]{1,0:T(8,128)(2,1)S(1)}, u32[]{:S(2)}, u32[]{:S(2)}) collective-permute-start(bf16[64,1792]{1,0:T(8,128)(2,1)S(1)} %shard_map.150.refs_4_), channel_id=1, source_target_pairs={{0,9},{1,8},{8,17},{9,16},{16,25},{17,24},{24,1},{25,0},{2,11},{3,... | collective-permute-start | bytes 688136 | tf_op jit(solution)/shard_map/ppermute | solution.py:32
  64.3 7.5 %collective-permute-start.25 = (bf16[40,1792]{1,0:T(8,128)(2,1)S(1)}, bf16[40,1792]{1,0:T(8,128)(2,1)S(1)}, u32[]{:S(2)}, u32[]{:S(2)}) collective-permute-start(bf16[40,1792]{1,0:T(8,128)(2,1)S(1)} %get-tuple-element.87), channel_id=1, source_target_pairs={{0,2},{2,0},{4,6},{6,4},{1,3},{3,1},{5,7},{7,5},{8,10},{10,8},{12,... | collective-permute-start | bytes 430088 | tf_op jit(solution)/shard_map/ppermute | solution.py:22
  66.7 9.6 %collective-permute-start.26 = (bf16[40,1792]{1,0:T(8,128)(2,1)S(1)}, bf16[40,1792]{1,0:T(8,128)(2,1)S(1)}, u32[]{:S(2)}, u32[]{:S(2)}) collective-permute-start(bf16[40,1792]{1,0:T(8,128)(2,1)S(1)} %get-tuple-element.88), channel_id=1, source_target_pairs={{0,4},{2,6},{4,0},{6,2},{1,5},{3,7},{5,1},{7,3},{8,12},{10,14},{12... | collective-permute-start | bytes 430088 | tf_op jit(solution)/shard_map/ppermute | solution.py:22
  70.1 8.5 %collective-permute-start.24 = (bf16[64,1792]{1,0:T(8,128)(2,1)S(1)}, bf16[64,1792]{1,0:T(8,128)(2,1)S(1)}, u32[]{:S(2)}, u32[]{:S(2)}) collective-permute-start(bf16[64,1792]{1,0:T(8,128)(2,1)S(1)} %shard_map.151.refs_4_), channel_id=1, source_target_pairs={{0,8},{1,9},{8,16},{9,17},{16,24},{17,25},{24,0},{25,1},{2,10},{3,... | collective-permute-start | bytes 688136 | tf_op jit(solution)/shard_map/ppermute | solution.py:32
  76.8 9.6 %collective-permute-start.28 = (bf16[64,1792]{1,0:T(8,128)(2,1)S(1)}, bf16[64,1792]{1,0:T(8,128)(2,1)S(1)}, u32[]{:S(2)}, u32[]{:S(2)}) collective-permute-start(bf16[64,1792]{1,0:T(8,128)(2,1)S(1)} %shard_map.152.refs_0_), channel_id=1, source_target_pairs={{0,9},{1,8},{8,17},{9,16},{16,25},{17,24},{24,1},{25,0},{2,11},{3,... | collective-permute-start | bytes 688136 | tf_op jit(solution)/shard_map/ppermute | solution.py:32
  (5 other events, 22.9 us)

commit v8 on v7

--- a/solution.py
+++ b/solution.py
@@ -292,12 +292,12 @@
         out[1, :, part] = dot(rows[...], up_w[:, part], 1, 0).astype(BF16)
 
 
-def gate_up(inputs, gate_w, up_w, planes=2, after=(), weight=1):
+def gate_up(inputs, gate_w, up_w, after=(), weight=1):
     blocks, (rows, width) = len(inputs), inputs[0].shape
     units, total = gate_w.shape[1], blocks * rows
     return call(
         functools.partial(gate_up_kernel, blocks=blocks),
-        array(planes, total, units),
+        array(2, total, units),
         [VMEM] * (blocks + 2) + [AFTER] * len(after),
         VMEM,
         [pltpu.VMEM((total, width), BF16)],
@@ -309,22 +309,21 @@
     down_w = refs[blocks]
     rows, out = refs[-2:]
     rows[...] = joined(refs[:blocks])
-    for start in range(0, out.shape[2], TILE):
+    for start in range(0, out.shape[1], TILE):
         part = slice(start, start + TILE)
-        out[2, :, part] = dot(rows[...], down_w[part, :], 1, 1).astype(BF16)
-
-
-def d_hidden(inputs, down_w, partial, after=(), weight=1):
+        out[:, part] = dot(rows[...], down_w[part, :], 1, 1).astype(BF16)
+
+
+def d_hidden(inputs, down_w, after=(), weight=1):
     blocks, (rows, width) = len(inputs), inputs[0].shape
     return call(
         functools.partial(d_hidden_kernel, blocks=blocks),
-        [array(blocks * rows, width), array(*partial.shape)],
-        [VMEM] * (blocks + 2) + [AFTER] * len(after),
+        [array(blocks * rows, width), array(blocks * rows, down_w.shape[0])],
+        [VMEM] * (blocks + 1) + [AFTER] * len(after),
         [VMEM] * 2,
         [],
         weight=weight,
-        aliases={blocks + 1: 1},
-    )(*inputs, down_w, partial, *after)
+    )(*inputs, down_w, *after)
 
 
 def scatter_tile(value, outs, columns):
@@ -367,14 +366,14 @@
     )(own, other, down_w, *after)
 
 
-def back_kernel(own_ref, other_ref, gate_w, up_w, *refs, blocks):
+def back_kernel(own_ref, other_ref, own_d, other_d, gate_w, up_w, *refs, blocks):
     hidden, d_gate, d_up, *outs = refs[-3 - 2 * blocks :]
     part = outs[0].shape[0]
     for start in range(0, hidden.shape[1], TILE):
         columns = slice(start, start + TILE)
         gate = total_of(own_ref[0, :, columns], other_ref[0, :, columns], part)
         up = total_of(own_ref[1, :, columns], other_ref[1, :, columns], part)
-        d_hid = total_of(own_ref[2, :, columns], other_ref[2, :, columns], part)
+        d_hid = total_of(own_d[:, columns], other_d[:, columns], part)
         sigmoid = jax.nn.sigmoid(gate)
         activated = gate * sigmoid
         hidden[:, columns] = (activated * up).astype(BF16)
@@ -389,15 +388,15 @@
         scatter_tile(total, outs, columns)
 
 
-def back(own, other, gate_w, up_w, plan, after=()):
+def back(own, other, own_d, other_d, gate_w, up_w, plan, after=()):
     _, total, units = own.shape
     return call(
         functools.partial(back_kernel, blocks=plan.blocks),
         [array(total, units)] * 3 + [array(plan.part, gate_w.shape[0])] * (2 * plan.blocks),
-        [VMEM] * 4 + [AFTER] * len(after),
+        [VMEM] * 6 + [AFTER] * len(after),
         [VMEM] * (3 + 2 * plan.blocks),
         [],
-    )(own, other, gate_w, up_w, *after)
+    )(own, other, own_d, other_d, gate_w, up_w, *after)
 
 
 def turn_kernel(*refs, blocks):
@@ -513,20 +512,21 @@
 
     part_f = gate_up(rows_f, gate_w, up_w, after=sent_dy[:1])
     part_f_other = exchange(part_f, "dp", 1)
-    part_b = gate_up(rows_b, gate_w, up_w, planes=3, after=(part_f,), weight=3000)
+    part_b = gate_up(rows_b, gate_w, up_w, after=(part_f,), weight=3000)
+    part_b_other = exchange(part_b, "dp", 1)
     down_blocks = down(part_f, part_f_other, down_w, plan, after=(in_vmem(part_b),))
     own_back_f = to_experts(down_blocks[:n_expert], relative)
     other_back_f = to_experts(down_blocks[n_expert:], relative)
     turned = turn(rows_b, after=down_blocks[:1])
-    cots, part_b = d_hidden(cots_b, down_w, part_b, after=(in_vmem(turned),), weight=1000)
-    part_b_other = exchange(part_b, "dp", 1)
+    cots, part_d = d_hidden(cots_b, down_w, after=(in_vmem(turned),), weight=1000)
+    part_d_other = exchange(part_d, "dp", 1)
+    hidden, d_gate, d_up, *back_blocks = back(
+        part_b, part_b_other, part_d, part_d_other, gate_w, up_w, plan
+    )
     own_sum = combine(
-        metas, own_back_f, plan, row_f, True, False, after=(in_vmem(part_b),), weight=2000
+        metas, own_back_f, plan, row_f, True, False, after=(back_blocks[0],), weight=2000
     )
     y_mine = section_shift(own_sum, 0)
-    hidden, d_gate, d_up, *back_blocks = back(
-        part_b, part_b_other, gate_w, up_w, plan, after=(own_sum,)
-    )
     own_back_b = to_experts(back_blocks[:n_expert], relative)
     other_back_b = to_experts(back_blocks[n_expert:], relative)
     other_sum = combine(

time: 87.7 us -> 90.8 us (1.035)
  waiting for transfers between devices: 22 us -> 25.6 us
    ppermute x4, waiting for transfers between devices: 1.04 us -> 3.26 us  [section_shift(): return lax.ppermute(value, ('section', 'dp'), pairs)]
    ppermute x4, starting transfers between devices: 4.73 us -> 3.38 us  [section_shift(): return lax.ppermute(value, ('section', 'dp'), pairs)]
    ppermute x25 -> x26, waiting for transfers between devices: 21 us -> 22.3 us  [exchange(): lax.ppermute(value, axis, [(source, source ^ mask) for source in range(co...]
    ppermute x25 -> x26, starting transfers between devices: 29 us -> 29.8 us  [exchange(): lax.ppermute(value, axis, [(source, source ^ mask) for source in range(co...]
  transfers between devices with their start and end apart: 29 -> 30, of which waited for: 13 -> 13; matrix products, arithmetic and copies ran while one was open for 0% -> 0% of each run, Pallas kernels for 32% -> 31%
where the time goes in v8:
time: 90.8 us; the launch traced here: 90.6 us
  starting transfers between devices  33.2 us (37%)
  Pallas kernels  30.8 us (34%)
  waiting for transfers between devices  25.6 us (28%)
  between operations  1 us (1%)
    ppermute x26, starting transfers between devices, exchange(): lax.ppermute(value, axis, [(source, source ^ mask) for source in range(co...  29.8 us
    ppermute x26, waiting for transfers between devices, exchange(): lax.ppermute(value, axis, [(source, source ^ mask) for source in range(co...  22.3 us
    pallas_call x1, Pallas kernels, grads(): call(grad_kernel, [pltpu.HBM((width, units), BF16)] * 2 + [pltpu.HBM((uni...  7.37 us
    pallas_call x2, Pallas kernels, gate_up(): call(functools.partial(gate_up_kernel, blocks=blocks), array(2, total, un...  5.25 us
    pallas_call x1, Pallas kernels, load(): call(functools.partial(load_kernel, count=len(weights)), [array(*weight.s...  4.23 us
    ppermute x4, starting transfers between devices, section_shift(): return lax.ppermute(value, ('section', 'dp'), pairs)  3.38 us
    ppermute x4, waiting for transfers between devices, section_shift(): return lax.ppermute(value, ('section', 'dp'), pairs)  3.26 us
    pallas_call x1, Pallas kernels, back(): call(functools.partial(back_kernel, blocks=plan.blocks), [array(total, un...  3.19 us
  transfers between devices with their start and end apart: 30, of which 13 were waited for; matrix products, arithmetic and copies ran while one was open for 0% of the time, Pallas kernels for 31%

profile of v8, /device:TPU:0, one launch (start us, length us, event | category | flops | bytes accessed | tf_op | source)
XLA Modules:
  0.0 90.6 jit_solution(7217461961326682092)
XLA Ops:
  4.5 2.8 %collective-permute-start.1 = (bf16[80,1792]{1,0:T(8,128)(2,1)S(1)}, bf16[80,1792]{1,0:T(8,128)(2,1)S(1)}, u32[]{:S(2)}, u32[]{:S(2)}) collective-permute-start(bf16[80,1792]{1,0:T(8,128)(2,1)S(1)} %get-tuple-element.56), channel_id=1, source_target_pairs={{0,2},{2,0},{4,6},{6,4},{1,3},{3,1},{5,7},{7,5},{8,10},{10,8},{12,... | collective-permute-start | bytes 860168 | tf_op jit(solution)/shard_map/ppermute | solution.py:22
  7.3 1.5 %collective-permute-start.2 = (bf16[80,1792]{1,0:T(8,128)(2,1)S(1)}, bf16[80,1792]{1,0:T(8,128)(2,1)S(1)}, u32[]{:S(2)}, u32[]{:S(2)}) collective-permute-start(bf16[80,1792]{1,0:T(8,128)(2,1)S(1)} %get-tuple-element.57), channel_id=1, source_target_pairs={{0,4},{2,6},{4,0},{6,2},{1,5},{3,7},{5,1},{7,3},{8,12},{10,14},{12... | collective-permute-start | bytes 860168 | tf_op jit(solution)/shard_map/ppermute | solution.py:22
  9.4 2.0 %collective-permute-start.6 = (bf16[80,1792]{1,0:T(8,128)(2,1)S(1)}, bf16[80,1792]{1,0:T(8,128)(2,1)S(1)}, u32[]{:S(2)}, u32[]{:S(2)}) collective-permute-start(bf16[80,1792]{1,0:T(8,128)(2,1)S(1)} %get-tuple-element.67), channel_id=1, source_target_pairs={{0,2},{2,0},{4,6},{6,4},{1,3},{3,1},{5,7},{7,5},{8,10},{10,8},{12,... | collective-permute-start | bytes 860168 | tf_op jit(solution)/shard_map/ppermute | solution.py:22
  11.5 1.5 %collective-permute-start.7 = (bf16[80,1792]{1,0:T(8,128)(2,1)S(1)}, bf16[80,1792]{1,0:T(8,128)(2,1)S(1)}, u32[]{:S(2)}, u32[]{:S(2)}) collective-permute-start(bf16[80,1792]{1,0:T(8,128)(2,1)S(1)} %get-tuple-element.68), channel_id=1, source_target_pairs={{0,4},{2,6},{4,0},{6,2},{1,5},{3,7},{5,1},{7,3},{8,12},{10,14},{12... | collective-permute-start | bytes 860168 | tf_op jit(solution)/shard_map/ppermute | solution.py:22
  13.0 1.9 %collective-permute-done.1.refs_1_ = bf16[80,1792]{1,0:T(8,128)(2,1)S(1)} collective-permute-done((bf16[80,1792]{1,0:T(8,128)(2,1)S(1)}, bf16[80,1792]{1,0:T(8,128)(2,1)S(1)}, u32[]{:S(2)}, u32[]{:S(2)}) %collective-permute-start.1) | collective-permute-done | bytes 286752 | tf_op jit(solution)/shard_map/ppermute | solution.py:22
  14.9 3.0 %collective-permute-start.8 = (bf16[80,1792]{1,0:T(8,128)(2,1)S(1)}, bf16[80,1792]{1,0:T(8,128)(2,1)S(1)}, u32[]{:S(2)}, u32[]{:S(2)}) collective-permute-start(bf16[80,1792]{1,0:T(8,128)(2,1)S(1)} %get-tuple-element.69), channel_id=1, source_target_pairs={{0,6},{2,4},{4,2},{6,0},{1,7},{3,5},{5,3},{7,1},{8,14},{10,12},{12... | collective-permute-start | bytes 860168 | tf_op jit(solution)/shard_map/ppermute | solution.py:22
  17.9 4.2 %shard_map.141 = (bf16[1792,1024]{1,0:T(8,128)(2,1)S(1)}, bf16[1792,1024]{1,0:T(8,128)(2,1)S(1)}, bf16[1024,1792]{1,0:T(8,128)(2,1)S(1)}) custom-call(bf16[1792,1024]{1,0:T(8,128)(2,1)} %bitcast.23, bf16[1792,1024]{1,0:T(8,128)(2,1)} %bitcast.24, bf16[1024,1792]{1,0:T(8,128)(2,1)} %bitcast.25, bf16[80,1792]{1,0:T(8,128)(2,1)S(1)} %get-tuple-element.61.refs_3_.refs_0_), custom_call_target="tpu_custom_call" | custom-call | flops 10000000 | bytes 1 | tf_op jit(solution)/shard_map/pallas_call | solution.py:164
  23.2 2.6 %shard_map.143.refs_6_.own_ref = bf16[2,320,1024]{2,1,0:T(8,128)(2,1)S(1)} custom-call(bf16[80,1792]{1,0:T(8,128)(2,1)S(1)} %get-tuple-element.55.refs_0_, bf16[80,1792]{1,0:T(8,128)(2,1)S(1)} %collective-permute-done.1.refs_1_, bf16[80,1792]{1,0:T(8,128)(2,1)S(1)} %collective-permute-done.2.refs_2_, bf16[80,1792]{1,0:T(8,128)(2,1)S(1)} %collective-permute-done.3.refs_3_, ...), custom_call_target="tpu_custom_call" | custom-call | flops 10000000 | bytes 1 | tf_op jit(solution)/shard_map/pallas_call | solution.py:298
  27.2 2.1 %collective-permute-start.14 = (bf16[80,1792]{1,0:T(8,128)(2,1)S(1)}, bf16[80,1792]{1,0:T(8,128)(2,1)S(1)}, u32[]{:S(2)}, u32[]{:S(2)}) collective-permute-start(bf16[80,1792]{1,0:T(8,128)(2,1)S(1)} %get-tuple-element.75), channel_id=1, source_target_pairs={{0,4},{2,6},{4,0},{6,2},{1,5},{3,7},{5,1},{7,3},{8,12},{10,14},{12... | collective-permute-start | bytes 860168 | tf_op jit(solution)/shard_map/ppermute | solution.py:22
  29.3 5.1 %collective-permute-done.7.refs_2_ = bf16[80,1792]{1,0:T(8,128)(2,1)S(1)} collective-permute-done((bf16[80,1792]{1,0:T(8,128)(2,1)S(1)}, bf16[80,1792]{1,0:T(8,128)(2,1)S(1)}, u32[]{:S(2)}, u32[]{:S(2)}) %collective-permute-start.7) | collective-permute-done | bytes 286752 | tf_op jit(solution)/shard_map/ppermute | solution.py:22
  35.7 2.6 %shard_map.144.refs_0_.own_ref = bf16[2,320,1024]{2,1,0:T(8,128)(2,1)S(1)} custom-call(bf16[80,1792]{1,0:T(8,128)(2,1)S(1)} %get-tuple-element.61.refs_3_.refs_0_, bf16[80,1792]{1,0:T(8,128)(2,1)S(1)} %collective-permute-done.6.refs_1_, bf16[80,1792]{1,0:T(8,128)(2,1)S(1)} %collective-permute-done.7.refs_2_, ...), custom_call_target="tpu_custom_call" | custom-call | flops 30000001024 | bytes 1 | tf_op jit(solution)/shard_map/pallas_call | solution.py:298
  38.4 1.6 %shard_map.145 = (bf16[40,1792]{1,0:T(8,128)(2,1)S(1)}, bf16[40,1792]{1,0:T(8,128)(2,1)S(1)}, bf16[40,1792]{1,0:T(8,128)(2,1)S(1)}, bf16[40,1792]{1,0:T(8,128)(2...) custom-call(bf16[2,320,1024]{2,1,0:T(8,128)(2,1)S(1)} %shard_map.143, ...), custom_call_target="tpu_custom_call" | custom-call | flops 10000000 | bytes 1 | tf_op jit(solution)/shard_map/pallas_call | solution.py:360
  40.4 6.3 %collective-permute-done.14.refs_2_ = bf16[80,1792]{1,0:T(8,128)(2,1)S(1)} collective-permute-done((bf16[80,1792]{1,0:T(8,128)(2,1)S(1)}, bf16[80,1792]{1,0:T(8,128)(2,1)S(1)}, u32[]{:S(2)}, u32[]{:S(2)}) %collective-permute-start.14) | collective-permute-done | bytes 286752 | tf_op jit(solution)/shard_map/ppermute | solution.py:22
  48.2 1.5 %collective-permute-start.10 = (bf16[40,1792]{1,0:T(8,128)(2,1)S(1)}, bf16[40,1792]{1,0:T(8,128)(2,1)S(1)}, u32[]{:S(2)}, u32[]{:S(2)}) collective-permute-start(bf16[40,1792]{1,0:T(8,128)(2,1)S(1)} %get-tuple-element.72), channel_id=1, source_target_pairs={{0,4},{2,6},{4,0},{6,2},{1,5},{3,7},{5,1},{7,3},{8,12},{10,14},{12... | collective-permute-start | bytes 430088 | tf_op jit(solution)/shard_map/ppermute | solution.py:22
  53.8 3.2 %shard_map.148 = (bf16[320,1024]{1,0:T(8,128)(2,1)S(1)}, bf16[320,1024]{1,0:T(8,128)(2,1)S(1)}, bf16[320,1024]{1,0:T(8,128)(2,1)S(1)}, bf16[40,1792]{1,0:T(8,128...) custom-call(bf16[2,320,1024]{2,1,0:T(8,128)(2,1)S(1)} %shard_map.144, ...), custom_call_target="tpu_custom_call" | custom-call | flops 10000000 | bytes 1 | tf_op jit(solution)/shard_map/pallas_call | solution.py:393
  57.9 1.5 %collective-permute-start.20 = (bf16[40,1792]{1,0:T(8,128)(2,1)S(1)}, bf16[40,1792]{1,0:T(8,128)(2,1)S(1)}, u32[]{:S(2)}, u32[]{:S(2)}) collective-permute-start(bf16[40,1792]{1,0:T(8,128)(2,1)S(1)} %get-tuple-element.82), channel_id=1, source_target_pairs={{0,6},{2,4},{4,2},{6,0},{1,7},{3,5},{5,3},{7,1},{8,14},{10,12},{12... | collective-permute-start | bytes 430088 | tf_op jit(solution)/shard_map/ppermute | solution.py:22
  60.2 1.6 %collective-permute-start.17 = (bf16[64,1792]{1,0:T(8,128)(2,1)S(1)}, bf16[64,1792]{1,0:T(8,128)(2,1)S(1)}, u32[]{:S(2)}, u32[]{:S(2)}) collective-permute-start(bf16[64,1792]{1,0:T(8,128)(2,1)S(1)} %shard_map.149), channel_id=1, source_target_pairs={{0,8},{1,9},{8,16},{9,17},{16,24},{17,25},{24,0},{25,1},{2,10},{3,... | collective-permute-start | bytes 688136 | tf_op jit(solution)/shard_map/ppermute | solution.py:32
  61.8 1.4 %collective-permute-start.22 = (bf16[40,1792]{1,0:T(8,128)(2,1)S(1)}, bf16[40,1792]{1,0:T(8,128)(2,1)S(1)}, u32[]{:S(2)}, u32[]{:S(2)}) collective-permute-start(bf16[40,1792]{1,0:T(8,128)(2,1)S(1)} %get-tuple-element.83), channel_id=1, source_target_pairs={{0,2},{2,0},{4,6},{6,4},{1,3},{3,1},{5,7},{7,5},{8,10},{10,8},{12,... | collective-permute-start | bytes 430088 | tf_op jit(solution)/shard_map/ppermute | solution.py:22
  67.2 1.5 %collective-permute-done.22.refs_1_ = bf16[40,1792]{1,0:T(8,128)(2,1)S(1)} collective-permute-done((bf16[40,1792]{1,0:T(8,128)(2,1)S(1)}, bf16[40,1792]{1,0:T(8,128)(2,1)S(1)}, u32[]{:S(2)}, u32[]{:S(2)}) %collective-permute-start.22) | collective-permute-done | bytes 143392 | tf_op jit(solution)/shard_map/ppermute | solution.py:22
  70.7 1.6 %collective-permute-done.24.refs_3_ = bf16[40,1792]{1,0:T(8,128)(2,1)S(1)} collective-permute-done((bf16[40,1792]{1,0:T(8,128)(2,1)S(1)}, bf16[40,1792]{1,0:T(8,128)(2,1)S(1)}, u32[]{:S(2)}, u32[]{:S(2)}) %collective-permute-start.24) | collective-permute-done | bytes 143392 | tf_op jit(solution)/shard_map/ppermute | solution.py:22
  73.9 1.6 %collective-permute-start.25 = (bf16[64,1792]{1,0:T(8,128)(2,1)S(1)}, bf16[64,1792]{1,0:T(8,128)(2,1)S(1)}, u32[]{:S(2)}, u32[]{:S(2)}) collective-permute-start(bf16[64,1792]{1,0:T(8,128)(2,1)S(1)} %shard_map.151.refs_4_), channel_id=1, source_target_pairs={{0,8},{1,9},{8,16},{9,17},{16,24},{17,25},{24,0},{25,1},{2,10},{3,... | collective-permute-start | bytes 688136 | tf_op jit(solution)/shard_map/ppermute | solution.py:32
  76.7 1.7 %collective-permute-done.28.refs_3_ = bf16[40,1792]{1,0:T(8,128)(2,1)S(1)} collective-permute-done((bf16[40,1792]{1,0:T(8,128)(2,1)S(1)}, bf16[40,1792]{1,0:T(8,128)(2,1)S(1)}, u32[]{:S(2)}, u32[]{:S(2)}) %collective-permute-start.28) | collective-permute-done | bytes 143392 | tf_op jit(solution)/shard_map/ppermute | solution.py:22
  78.9 3.2 %collective-permute-done.25.refs_1_.refs_2_ = bf16[64,1792]{1,0:T(8,128)(2,1)S(1)} collective-permute-done((bf16[64,1792]{1,0:T(8,128)(2,1)S(1)}, bf16[64,1792]{1,0:T(8,128)(2,1)S(1)}, u32[]{:S(2)}, u32[]{:S(2)}) %collective-permute-start.25) | collective-permute-done | bytes 229408 | tf_op jit(solution)/shard_map/ppermute | solution.py:32
  82.1 7.4 %shard_map.153 = (bf16[1792,1024]{1,0:T(8,128)(2,1)}, bf16[1792,1024]{1,0:T(8,128)(2,1)}, bf16[1024,1792]{1,0:T(8,128)(2,1)}) custom-call(bf16[320,1024]{1,0:T(8,128)(2,1)S(1)} %get-tuple-element.90.hidden, bf16[320,1024]{1,0:T(8,128)(2,1)S(1)} %get-tuple-element.91.d_gate, bf16[320,1024]{1,0:T(8,128)(2,1)S(1)} %get-tuple-element.92.d_up, ...), custom_call_target="tpu_custom_call" | custom-call | flops 1000000000 | bytes 1 | tf_op jit(solution)/shard_map/pallas_call | solution.py:431
  (54 shorter events, 25.9 us)
Async XLA Ops:
  4.5 10.4 %collective-permute-start.1 = (bf16[80,1792]{1,0:T(8,128)(2,1)S(1)}, bf16[80,1792]{1,0:T(8,128)(2,1)S(1)}, u32[]{:S(2)}, u32[]{:S(2)}) collective-permute-start(bf16[80,1792]{1,0:T(8,128)(2,1)S(1)} %get-tuple-element.56), channel_id=1, source_target_pairs={{0,2},{2,0},{4,6},{6,4},{1,3},{3,1},{5,7},{7,5},{8,10},{10,8},{12,... | collective-permute-start | bytes 860168 | tf_op jit(solution)/shard_map/ppermute | solution.py:22
  7.3 15.8 %collective-permute-start.2 = (bf16[80,1792]{1,0:T(8,128)(2,1)S(1)}, bf16[80,1792]{1,0:T(8,128)(2,1)S(1)}, u32[]{:S(2)}, u32[]{:S(2)}) collective-permute-start(bf16[80,1792]{1,0:T(8,128)(2,1)S(1)} %get-tuple-element.57), channel_id=1, source_target_pairs={{0,4},{2,6},{4,0},{6,2},{1,5},{3,7},{5,1},{7,3},{8,12},{10,14},{12... | collective-permute-start | bytes 860168 | tf_op jit(solution)/shard_map/ppermute | solution.py:22
  8.8 14.3 %collective-permute-start.3 = (bf16[80,1792]{1,0:T(8,128)(2,1)S(1)}, bf16[80,1792]{1,0:T(8,128)(2,1)S(1)}, u32[]{:S(2)}, u32[]{:S(2)}) collective-permute-start(bf16[80,1792]{1,0:T(8,128)(2,1)S(1)} %get-tuple-element.58), channel_id=1, source_target_pairs={{0,6},{2,4},{4,2},{6,0},{1,7},{3,5},{5,3},{7,1},{8,14},{10,12},{12... | collective-permute-start | bytes 860168 | tf_op jit(solution)/shard_map/ppermute | solution.py:22
  9.4 17.8 %collective-permute-start.6 = (bf16[80,1792]{1,0:T(8,128)(2,1)S(1)}, bf16[80,1792]{1,0:T(8,128)(2,1)S(1)}, u32[]{:S(2)}, u32[]{:S(2)}) collective-permute-start(bf16[80,1792]{1,0:T(8,128)(2,1)S(1)} %get-tuple-element.67), channel_id=1, source_target_pairs={{0,2},{2,0},{4,6},{6,4},{1,3},{3,1},{5,7},{7,5},{8,10},{10,8},{12,... | collective-permute-start | bytes 860168 | tf_op jit(solution)/shard_map/ppermute | solution.py:22
  11.5 23.0 %collective-permute-start.7 = (bf16[80,1792]{1,0:T(8,128)(2,1)S(1)}, bf16[80,1792]{1,0:T(8,128)(2,1)S(1)}, u32[]{:S(2)}, u32[]{:S(2)}) collective-permute-start(bf16[80,1792]{1,0:T(8,128)(2,1)S(1)} %get-tuple-element.68), channel_id=1, source_target_pairs={{0,4},{2,6},{4,0},{6,2},{1,5},{3,7},{5,1},{7,3},{8,12},{10,14},{12... | collective-permute-start | bytes 860168 | tf_op jit(solution)/shard_map/ppermute | solution.py:22
  14.9 20.7 %collective-permute-start.8 = (bf16[80,1792]{1,0:T(8,128)(2,1)S(1)}, bf16[80,1792]{1,0:T(8,128)(2,1)S(1)}, u32[]{:S(2)}, u32[]{:S(2)}) collective-permute-start(bf16[80,1792]{1,0:T(8,128)(2,1)S(1)} %get-tuple-element.69), channel_id=1, source_target_pairs={{0,6},{2,4},{4,2},{6,0},{1,7},{3,5},{5,3},{7,1},{8,14},{10,12},{12... | collective-permute-start | bytes 860168 | tf_op jit(solution)/shard_map/ppermute | solution.py:22
  25.8 12.6 %collective-permute-start.5 = (bf16[2,320,1024]{2,1,0:T(8,128)(2,1)S(1)}, bf16[2,320,1024]{2,1,0:T(8,128)(2,1)S(1)}, u32[]{:S(2)}, u32[]{:S(2)}) collective-permute-start(bf16[2,320,1024]{2,1,0:T(8,128)(2,1)S(1)} %shard_map.143.refs_6_.own_ref), channel_id=1, source_target_pairs={{0,1},{1,0},{2,3},{3,2},{4,5},{5,4},{6,7},{7,6},{8,9},{9,8},{10,11... | collective-permute-start | bytes 3932168 | tf_op jit(solution)/shard_map/ppermute | solution.py:22
  25.9 14.6 %collective-permute-start.13 = (bf16[80,1792]{1,0:T(8,128)(2,1)S(1)}, bf16[80,1792]{1,0:T(8,128)(2,1)S(1)}, u32[]{:S(2)}, u32[]{:S(2)}) collective-permute-start(bf16[80,1792]{1,0:T(8,128)(2,1)S(1)} %get-tuple-element.74), channel_id=1, source_target_pairs={{0,2},{2,0},{4,6},{6,4},{1,3},{3,1},{5,7},{7,5},{8,10},{10,8},{12,... | collective-permute-start | bytes 860168 | tf_op jit(solution)/shard_map/ppermute | solution.py:22
  27.2 19.5 %collective-permute-start.14 = (bf16[80,1792]{1,0:T(8,128)(2,1)S(1)}, bf16[80,1792]{1,0:T(8,128)(2,1)S(1)}, u32[]{:S(2)}, u32[]{:S(2)}) collective-permute-start(bf16[80,1792]{1,0:T(8,128)(2,1)S(1)} %get-tuple-element.75), channel_id=1, source_target_pairs={{0,4},{2,6},{4,0},{6,2},{1,5},{3,7},{5,1},{7,3},{8,12},{10,14},{12... | collective-permute-start | bytes 860168 | tf_op jit(solution)/shard_map/ppermute | solution.py:22
  34.5 12.2 %collective-permute-start.15 = (bf16[80,1792]{1,0:T(8,128)(2,1)S(1)}, bf16[80,1792]{1,0:T(8,128)(2,1)S(1)}, u32[]{:S(2)}, u32[]{:S(2)}) collective-permute-start(bf16[80,1792]{1,0:T(8,128)(2,1)S(1)} %get-tuple-element.76), channel_id=1, source_target_pairs={{0,6},{2,4},{4,2},{6,0},{1,7},{3,5},{5,3},{7,1},{8,14},{10,12},{12... | collective-permute-start | bytes 860168 | tf_op jit(solution)/shard_map/ppermute | solution.py:22
  38.3 13.5 %collective-permute-start.12 = (bf16[2,320,1024]{2,1,0:T(8,128)(2,1)S(1)}, bf16[2,320,1024]{2,1,0:T(8,128)(2,1)S(1)}, u32[]{:S(2)}, u32[]{:S(2)}) collective-permute-start(bf16[2,320,1024]{2,1,0:T(8,128)(2,1)S(1)} %shard_map.144.refs_0_.own_ref), channel_id=1, source_target_pairs={{0,1},{1,0},{2,3},{3,2},{4,5},{5,4},{6,7},{7,6},{8,9},{9,8},{10,11... | collective-permute-start | bytes 3932168 | tf_op jit(solution)/shard_map/ppermute | solution.py:22
  48.2 9.7 %collective-permute-start.10 = (bf16[40,1792]{1,0:T(8,128)(2,1)S(1)}, bf16[40,1792]{1,0:T(8,128)(2,1)S(1)}, u32[]{:S(2)}, u32[]{:S(2)}) collective-permute-start(bf16[40,1792]{1,0:T(8,128)(2,1)S(1)} %get-tuple-element.72), channel_id=1, source_target_pairs={{0,4},{2,6},{4,0},{6,2},{1,5},{3,7},{5,1},{7,3},{8,12},{10,14},{12... | collective-permute-start | bytes 430088 | tf_op jit(solution)/shard_map/ppermute | solution.py:22
  49.8 9.6 %collective-permute-start.11 = (bf16[40,1792]{1,0:T(8,128)(2,1)S(1)}, bf16[40,1792]{1,0:T(8,128)(2,1)S(1)}, u32[]{:S(2)}, u32[]{:S(2)}) collective-permute-start(bf16[40,1792]{1,0:T(8,128)(2,1)S(1)} %get-tuple-element.73), channel_id=1, source_target_pairs={{0,6},{2,4},{4,2},{6,0},{1,7},{3,5},{5,3},{7,1},{8,14},{10,12},{12... | collective-permute-start | bytes 430088 | tf_op jit(solution)/shard_map/ppermute | solution.py:22
  51.0 8.4 %collective-permute-start.9 = (bf16[40,1792]{1,0:T(8,128)(2,1)S(1)}, bf16[40,1792]{1,0:T(8,128)(2,1)S(1)}, u32[]{:S(2)}, u32[]{:S(2)}) collective-permute-start(bf16[40,1792]{1,0:T(8,128)(2,1)S(1)} %get-tuple-element.71), channel_id=1, source_target_pairs={{0,2},{2,0},{4,6},{6,4},{1,3},{3,1},{5,7},{7,5},{8,10},{10,8},{12,... | collective-permute-start | bytes 430088 | tf_op jit(solution)/shard_map/ppermute | solution.py:22
  51.8 11.5 %collective-permute-start.18 = (bf16[40,1792]{1,0:T(8,128)(2,1)S(1)}, bf16[40,1792]{1,0:T(8,128)(2,1)S(1)}, u32[]{:S(2)}, u32[]{:S(2)}) collective-permute-start(bf16[40,1792]{1,0:T(8,128)(2,1)S(1)} %get-tuple-element.80), channel_id=1, source_target_pairs={{0,2},{2,0},{4,6},{6,4},{1,3},{3,1},{5,7},{7,5},{8,10},{10,8},{12,... | collective-permute-start | bytes 430088 | tf_op jit(solution)/shard_map/ppermute | solution.py:22
  53.1 11.0 %collective-permute-start.19 = (bf16[40,1792]{1,0:T(8,128)(2,1)S(1)}, bf16[40,1792]{1,0:T(8,128)(2,1)S(1)}, u32[]{:S(2)}, u32[]{:S(2)}) collective-permute-start(bf16[40,1792]{1,0:T(8,128)(2,1)S(1)} %get-tuple-element.81), channel_id=1, source_target_pairs={{0,4},{2,6},{4,0},{6,2},{1,5},{3,7},{5,1},{7,3},{8,12},{10,14},{12... | collective-permute-start | bytes 430088 | tf_op jit(solution)/shard_map/ppermute | solution.py:22
  57.9 8.7 %collective-permute-start.20 = (bf16[40,1792]{1,0:T(8,128)(2,1)S(1)}, bf16[40,1792]{1,0:T(8,128)(2,1)S(1)}, u32[]{:S(2)}, u32[]{:S(2)}) collective-permute-start(bf16[40,1792]{1,0:T(8,128)(2,1)S(1)} %get-tuple-element.82), channel_id=1, source_target_pairs={{0,6},{2,4},{4,2},{6,0},{1,7},{3,5},{5,3},{7,1},{8,14},{10,12},{12... | collective-permute-start | bytes 430088 | tf_op jit(solution)/shard_map/ppermute | solution.py:22
  60.2 13.2 %collective-permute-start.17 = (bf16[64,1792]{1,0:T(8,128)(2,1)S(1)}, bf16[64,1792]{1,0:T(8,128)(2,1)S(1)}, u32[]{:S(2)}, u32[]{:S(2)}) collective-permute-start(bf16[64,1792]{1,0:T(8,128)(2,1)S(1)} %shard_map.149), channel_id=1, source_target_pairs={{0,8},{1,9},{8,16},{9,17},{16,24},{17,25},{24,0},{25,1},{2,10},{3,... | collective-permute-start | bytes 688136 | tf_op jit(solution)/shard_map/ppermute | solution.py:32
  61.8 6.8 %collective-permute-start.22 = (bf16[40,1792]{1,0:T(8,128)(2,1)S(1)}, bf16[40,1792]{1,0:T(8,128)(2,1)S(1)}, u32[]{:S(2)}, u32[]{:S(2)}) collective-permute-start(bf16[40,1792]{1,0:T(8,128)(2,1)S(1)} %get-tuple-element.83), channel_id=1, source_target_pairs={{0,2},{2,0},{4,6},{6,4},{1,3},{3,1},{5,7},{7,5},{8,10},{10,8},{12,... | collective-permute-start | bytes 430088 | tf_op jit(solution)/shard_map/ppermute | solution.py:22
  64.0 8.3 %collective-permute-start.24 = (bf16[40,1792]{1,0:T(8,128)(2,1)S(1)}, bf16[40,1792]{1,0:T(8,128)(2,1)S(1)}, u32[]{:S(2)}, u32[]{:S(2)}) collective-permute-start(bf16[40,1792]{1,0:T(8,128)(2,1)S(1)} %get-tuple-element.85), channel_id=1, source_target_pairs={{0,6},{2,4},{4,2},{6,0},{1,7},{3,5},{5,3},{7,1},{8,14},{10,12},{12... | collective-permute-start | bytes 430088 | tf_op jit(solution)/shard_map/ppermute | solution.py:22
  67.1 11.2 %collective-permute-start.21 = (bf16[64,1792]{1,0:T(8,128)(2,1)S(1)}, bf16[64,1792]{1,0:T(8,128)(2,1)S(1)}, u32[]{:S(2)}, u32[]{:S(2)}) collective-permute-start(bf16[64,1792]{1,0:T(8,128)(2,1)S(1)} %shard_map.150.refs_4_), channel_id=1, source_target_pairs={{0,9},{1,8},{8,17},{9,16},{16,25},{17,24},{24,1},{25,0},{2,11},{3,... | collective-permute-start | bytes 688136 | tf_op jit(solution)/shard_map/ppermute | solution.py:32
  68.7 6.8 %collective-permute-start.26 = (bf16[40,1792]{1,0:T(8,128)(2,1)S(1)}, bf16[40,1792]{1,0:T(8,128)(2,1)S(1)}, u32[]{:S(2)}, u32[]{:S(2)}) collective-permute-start(bf16[40,1792]{1,0:T(8,128)(2,1)S(1)} %get-tuple-element.87), channel_id=1, source_target_pairs={{0,2},{2,0},{4,6},{6,4},{1,3},{3,1},{5,7},{7,5},{8,10},{10,8},{12,... | collective-permute-start | bytes 430088 | tf_op jit(solution)/shard_map/ppermute | solution.py:22
  73.9 8.3 %collective-permute-start.25 = (bf16[64,1792]{1,0:T(8,128)(2,1)S(1)}, bf16[64,1792]{1,0:T(8,128)(2,1)S(1)}, u32[]{:S(2)}, u32[]{:S(2)}) collective-permute-start(bf16[64,1792]{1,0:T(8,128)(2,1)S(1)} %shard_map.151.refs_4_), channel_id=1, source_target_pairs={{0,8},{1,9},{8,16},{9,17},{16,24},{17,25},{24,0},{25,1},{2,10},{3,... | collective-permute-start | bytes 688136 | tf_op jit(solution)/shard_map/ppermute | solution.py:32
  78.8 10.7 %collective-permute-start.29 = (bf16[64,1792]{1,0:T(8,128)(2,1)S(1)}, bf16[64,1792]{1,0:T(8,128)(2,1)S(1)}, u32[]{:S(2)}, u32[]{:S(2)}) collective-permute-start(bf16[64,1792]{1,0:T(8,128)(2,1)S(1)} %shard_map.152.refs_0_), channel_id=1, source_target_pairs={{0,9},{1,8},{8,17},{9,16},{16,25},{17,24},{24,1},{25,0},{2,11},{3,... | collective-permute-start | bytes 688136 | tf_op jit(solution)/shard_map/ppermute | solution.py:32
  (6 other events, 30.7 us)

commit v9 on v8

--- a/solution.py
+++ b/solution.py
@@ -520,13 +520,13 @@
     turned = turn(rows_b, after=down_blocks[:1])
     cots, part_d = d_hidden(cots_b, down_w, after=(in_vmem(turned),), weight=1000)
     part_d_other = exchange(part_d, "dp", 1)
+    own_sum = combine(
+        metas, own_back_f, plan, row_f, True, False, after=(part_d,), weight=2000
+    )
+    y_mine = section_shift(own_sum, 0)
     hidden, d_gate, d_up, *back_blocks = back(
-        part_b, part_b_other, part_d, part_d_other, gate_w, up_w, plan
-    )
-    own_sum = combine(
-        metas, own_back_f, plan, row_f, True, False, after=(back_blocks[0],), weight=2000
-    )
-    y_mine = section_shift(own_sum, 0)
+        part_b, part_b_other, part_d, part_d_other, gate_w, up_w, plan, after=(own_sum,)
+    )
     own_back_b = to_experts(back_blocks[:n_expert], relative)
     other_back_b = to_experts(back_blocks[n_expert:], relative)
     other_sum = combine(
@@ -540,8 +540,8 @@
         row_b,
         False,
         False,
-        after=(other_sum, in_vmem(y_mine)),
-        weight=150,
+        after=(other_sum,),
+        weight=300,
     )
     dx_mine = section_shift(own_sum, 0)
     other_sum = combine(
@@ -551,7 +551,7 @@
         row_b,
         False,
         True,
-        after=(own_sum, in_vmem(y_rest)),
+        after=(own_sum, in_vmem(y_rest), in_vmem(y_mine)),
         weight=100,
     )
     dx_rest = section_shift(other_sum, 1)

time: 90.8 us -> 91 us (level)
  starting transfers between devices: 33.2 us -> 34.9 us
  waiting for transfers between devices: 25.6 us -> 24 us
    ppermute x26, starting transfers between devices: 29.8 us -> 31.6 us  [exchange(): lax.ppermute(value, axis, [(source, source ^ mask) for source in range(co...]
    ppermute x26, waiting for transfers between devices: 22.3 us -> 21.2 us  [exchange(): lax.ppermute(value, axis, [(source, source ^ mask) for source in range(co...]
  transfers between devices with their start and end apart: 30 -> 30, of which waited for: 13 -> 10; matrix products, arithmetic and copies ran while one was open for 0% -> 0% of each run, Pallas kernels for 31% -> 31%
where the time goes in v9:
time: 91 us; the launch traced here: 90.8 us
  starting transfers between devices  34.9 us (38%)
  Pallas kernels  30.8 us (34%)
  waiting for transfers between devices  24 us (26%)
  between operations  1.02 us (1%)
    ppermute x26, starting transfers between devices, exchange(): lax.ppermute(value, axis, [(source, source ^ mask) for source in range(co...  31.6 us
    ppermute x26, waiting for transfers between devices, exchange(): lax.ppermute(value, axis, [(source, source ^ mask) for source in range(co...  21.2 us
    pallas_call x1, Pallas kernels, grads(): call(grad_kernel, [pltpu.HBM((width, units), BF16)] * 2 + [pltpu.HBM((uni...  7.37 us
    pallas_call x2, Pallas kernels, gate_up(): call(functools.partial(gate_up_kernel, blocks=blocks), array(2, total, un...  5.25 us
    pallas_call x1, Pallas kernels, load(): call(functools.partial(load_kernel, count=len(weights)), [array(*weight.s...  4.23 us
    pallas_call x1, Pallas kernels, back(): call(functools.partial(back_kernel, blocks=plan.blocks), [array(total, un...  3.34 us
    ppermute x4, starting transfers between devices, section_shift(): return lax.ppermute(value, ('section', 'dp'), pairs)  3.32 us
    ppermute x4, waiting for transfers between devices, section_shift(): return lax.ppermute(value, ('section', 'dp'), pairs)  2.81 us
  transfers between devices with their start and end apart: 30, of which 10 were waited for; matrix products, arithmetic and copies ran while one was open for 0% of the time, Pallas kernels for 31%

profile of v9, /device:TPU:0, one launch (start us, length us, event | category | flops | bytes accessed | tf_op | source)
XLA Modules:
  0.0 90.8 jit_solution(15711097956406340383)
XLA Ops:
  4.5 2.8 %collective-permute-start.1 = (bf16[80,1792]{1,0:T(8,128)(2,1)S(1)}, bf16[80,1792]{1,0:T(8,128)(2,1)S(1)}, u32[]{:S(2)}, u32[]{:S(2)}) collective-permute-start(bf16[80,1792]{1,0:T(8,128)(2,1)S(1)} %get-tuple-element.56), channel_id=1, source_target_pairs={{0,2},{2,0},{4,6},{6,4},{1,3},{3,1},{5,7},{7,5},{8,10},{10,8},{12,... | collective-permute-start | bytes 860168 | tf_op jit(solution)/shard_map/ppermute | solution.py:22
  7.3 1.5 %collective-permute-start.2 = (bf16[80,1792]{1,0:T(8,128)(2,1)S(1)}, bf16[80,1792]{1,0:T(8,128)(2,1)S(1)}, u32[]{:S(2)}, u32[]{:S(2)}) collective-permute-start(bf16[80,1792]{1,0:T(8,128)(2,1)S(1)} %get-tuple-element.57), channel_id=1, source_target_pairs={{0,4},{2,6},{4,0},{6,2},{1,5},{3,7},{5,1},{7,3},{8,12},{10,14},{12... | collective-permute-start | bytes 860168 | tf_op jit(solution)/shard_map/ppermute | solution.py:22
  9.4 2.0 %collective-permute-start.6 = (bf16[80,1792]{1,0:T(8,128)(2,1)S(1)}, bf16[80,1792]{1,0:T(8,128)(2,1)S(1)}, u32[]{:S(2)}, u32[]{:S(2)}) collective-permute-start(bf16[80,1792]{1,0:T(8,128)(2,1)S(1)} %get-tuple-element.67), channel_id=1, source_target_pairs={{0,2},{2,0},{4,6},{6,4},{1,3},{3,1},{5,7},{7,5},{8,10},{10,8},{12,... | collective-permute-start | bytes 860168 | tf_op jit(solution)/shard_map/ppermute | solution.py:22
  11.5 1.5 %collective-permute-start.7 = (bf16[80,1792]{1,0:T(8,128)(2,1)S(1)}, bf16[80,1792]{1,0:T(8,128)(2,1)S(1)}, u32[]{:S(2)}, u32[]{:S(2)}) collective-permute-start(bf16[80,1792]{1,0:T(8,128)(2,1)S(1)} %get-tuple-element.68), channel_id=1, source_target_pairs={{0,4},{2,6},{4,0},{6,2},{1,5},{3,7},{5,1},{7,3},{8,12},{10,14},{12... | collective-permute-start | bytes 860168 | tf_op jit(solution)/shard_map/ppermute | solution.py:22
  13.0 1.9 %collective-permute-done.1.refs_1_ = bf16[80,1792]{1,0:T(8,128)(2,1)S(1)} collective-permute-done((bf16[80,1792]{1,0:T(8,128)(2,1)S(1)}, bf16[80,1792]{1,0:T(8,128)(2,1)S(1)}, u32[]{:S(2)}, u32[]{:S(2)}) %collective-permute-start.1) | collective-permute-done | bytes 286752 | tf_op jit(solution)/shard_map/ppermute | solution.py:22
  14.9 3.0 %collective-permute-start.8 = (bf16[80,1792]{1,0:T(8,128)(2,1)S(1)}, bf16[80,1792]{1,0:T(8,128)(2,1)S(1)}, u32[]{:S(2)}, u32[]{:S(2)}) collective-permute-start(bf16[80,1792]{1,0:T(8,128)(2,1)S(1)} %get-tuple-element.69), channel_id=1, source_target_pairs={{0,6},{2,4},{4,2},{6,0},{1,7},{3,5},{5,3},{7,1},{8,14},{10,12},{12... | collective-permute-start | bytes 860168 | tf_op jit(solution)/shard_map/ppermute | solution.py:22
  17.9 4.2 %shard_map.141 = (bf16[1792,1024]{1,0:T(8,128)(2,1)S(1)}, bf16[1792,1024]{1,0:T(8,128)(2,1)S(1)}, bf16[1024,1792]{1,0:T(8,128)(2,1)S(1)}) custom-call(bf16[1792,1024]{1,0:T(8,128)(2,1)} %bitcast.23, bf16[1792,1024]{1,0:T(8,128)(2,1)} %bitcast.24, bf16[1024,1792]{1,0:T(8,128)(2,1)} %bitcast.25, bf16[80,1792]{1,0:T(8,128)(2,1)S(1)} %get-tuple-element.61.refs_3_.refs_0_), custom_call_target="tpu_custom_call" | custom-call | flops 10000000 | bytes 1 | tf_op jit(solution)/shard_map/pallas_call | solution.py:164
  23.2 2.6 %shard_map.143.refs_6_.own_ref = bf16[2,320,1024]{2,1,0:T(8,128)(2,1)S(1)} custom-call(bf16[80,1792]{1,0:T(8,128)(2,1)S(1)} %get-tuple-element.55.refs_0_, bf16[80,1792]{1,0:T(8,128)(2,1)S(1)} %collective-permute-done.1.refs_1_, bf16[80,1792]{1,0:T(8,128)(2,1)S(1)} %collective-permute-done.2.refs_2_, bf16[80,1792]{1,0:T(8,128)(2,1)S(1)} %collective-permute-done.3.refs_3_, ...), custom_call_target="tpu_custom_call" | custom-call | flops 10000000 | bytes 1 | tf_op jit(solution)/shard_map/pallas_call | solution.py:298
  27.2 2.1 %collective-permute-start.13 = (bf16[80,1792]{1,0:T(8,128)(2,1)S(1)}, bf16[80,1792]{1,0:T(8,128)(2,1)S(1)}, u32[]{:S(2)}, u32[]{:S(2)}) collective-permute-start(bf16[80,1792]{1,0:T(8,128)(2,1)S(1)} %get-tuple-element.75), channel_id=1, source_target_pairs={{0,4},{2,6},{4,0},{6,2},{1,5},{3,7},{5,1},{7,3},{8,12},{10,14},{12... | collective-permute-start | bytes 860168 | tf_op jit(solution)/shard_map/ppermute | solution.py:22
  29.3 5.1 %collective-permute-done.7.refs_2_ = bf16[80,1792]{1,0:T(8,128)(2,1)S(1)} collective-permute-done((bf16[80,1792]{1,0:T(8,128)(2,1)S(1)}, bf16[80,1792]{1,0:T(8,128)(2,1)S(1)}, u32[]{:S(2)}, u32[]{:S(2)}) %collective-permute-start.7) | collective-permute-done | bytes 286752 | tf_op jit(solution)/shard_map/ppermute | solution.py:22
  35.7 2.6 %shard_map.144.refs_0_.own_ref = bf16[2,320,1024]{2,1,0:T(8,128)(2,1)S(1)} custom-call(bf16[80,1792]{1,0:T(8,128)(2,1)S(1)} %get-tuple-element.61.refs_3_.refs_0_, bf16[80,1792]{1,0:T(8,128)(2,1)S(1)} %collective-permute-done.6.refs_1_, bf16[80,1792]{1,0:T(8,128)(2,1)S(1)} %collective-permute-done.7.refs_2_, ...), custom_call_target="tpu_custom_call" | custom-call | flops 30000001024 | bytes 1 | tf_op jit(solution)/shard_map/pallas_call | solution.py:298
  38.4 1.6 %shard_map.145 = (bf16[40,1792]{1,0:T(8,128)(2,1)S(1)}, bf16[40,1792]{1,0:T(8,128)(2,1)S(1)}, bf16[40,1792]{1,0:T(8,128)(2,1)S(1)}, bf16[40,1792]{1,0:T(8,128)(2...) custom-call(bf16[2,320,1024]{2,1,0:T(8,128)(2,1)S(1)} %shard_map.143, ...), custom_call_target="tpu_custom_call" | custom-call | flops 10000000 | bytes 1 | tf_op jit(solution)/shard_map/pallas_call | solution.py:360
  41.8 3.0 %collective-permute-start.11 = (bf16[40,1792]{1,0:T(8,128)(2,1)S(1)}, bf16[40,1792]{1,0:T(8,128)(2,1)S(1)}, u32[]{:S(2)}, u32[]{:S(2)}) collective-permute-start(bf16[40,1792]{1,0:T(8,128)(2,1)S(1)} %get-tuple-element.73), channel_id=1, source_target_pairs={{0,6},{2,4},{4,2},{6,0},{1,7},{3,5},{5,3},{7,1},{8,14},{10,12},{12... | collective-permute-start | bytes 430088 | tf_op jit(solution)/shard_map/ppermute | solution.py:22
  44.8 5.0 %collective-permute-done.13.refs_2_ = bf16[80,1792]{1,0:T(8,128)(2,1)S(1)} collective-permute-done((bf16[80,1792]{1,0:T(8,128)(2,1)S(1)}, bf16[80,1792]{1,0:T(8,128)(2,1)S(1)}, u32[]{:S(2)}, u32[]{:S(2)}) %collective-permute-start.13) | collective-permute-done | bytes 286752 | tf_op jit(solution)/shard_map/ppermute | solution.py:22
  51.3 1.5 %collective-permute-done.10.refs_2_ = bf16[40,1792]{1,0:T(8,128)(2,1)S(1)} collective-permute-done((bf16[40,1792]{1,0:T(8,128)(2,1)S(1)}, bf16[40,1792]{1,0:T(8,128)(2,1)S(1)}, u32[]{:S(2)}, u32[]{:S(2)}) %collective-permute-start.10) | collective-permute-done | bytes 143392 | tf_op jit(solution)/shard_map/ppermute | solution.py:22
  54.2 1.7 %collective-permute-start.17 = (bf16[40,1792]{1,0:T(8,128)(2,1)S(1)}, bf16[40,1792]{1,0:T(8,128)(2,1)S(1)}, u32[]{:S(2)}, u32[]{:S(2)}) collective-permute-start(bf16[40,1792]{1,0:T(8,128)(2,1)S(1)} %get-tuple-element.80), channel_id=1, source_target_pairs={{0,4},{2,6},{4,0},{6,2},{1,5},{3,7},{5,1},{7,3},{8,12},{10,14},{12... | collective-permute-start | bytes 430088 | tf_op jit(solution)/shard_map/ppermute | solution.py:22
  57.5 3.3 %shard_map.149 = (bf16[320,1024]{1,0:T(8,128)(2,1)S(1)}, bf16[320,1024]{1,0:T(8,128)(2,1)S(1)}, bf16[320,1024]{1,0:T(8,128)(2,1)S(1)}, bf16[40,1792]{1,0:T(8,128...) custom-call(bf16[2,320,1024]{2,1,0:T(8,128)(2,1)S(1)} %shard_map.144, ...), custom_call_target="tpu_custom_call" | custom-call | flops 10000000 | bytes 1 | tf_op jit(solution)/shard_map/pallas_call | solution.py:393
  60.8 2.3 %collective-permute-start.22 = (bf16[40,1792]{1,0:T(8,128)(2,1)S(1)}, bf16[40,1792]{1,0:T(8,128)(2,1)S(1)}, u32[]{:S(2)}, u32[]{:S(2)}) collective-permute-start(bf16[40,1792]{1,0:T(8,128)(2,1)S(1)} %get-tuple-element.83), channel_id=1, source_target_pairs={{0,2},{2,0},{4,6},{6,4},{1,3},{3,1},{5,7},{7,5},{8,10},{10,8},{12,... | collective-permute-start | bytes 430088 | tf_op jit(solution)/shard_map/ppermute | solution.py:22
  64.7 1.6 %collective-permute-start.15 = (bf16[64,1792]{1,0:T(8,128)(2,1)S(1)}, bf16[64,1792]{1,0:T(8,128)(2,1)S(1)}, u32[]{:S(2)}, u32[]{:S(2)}) collective-permute-start(bf16[64,1792]{1,0:T(8,128)(2,1)S(1)} %shard_map.148.refs_0_), channel_id=1, source_target_pairs={{0,8},{1,9},{8,16},{9,17},{16,24},{17,25},{24,0},{25,1},{2,10},{3,... | collective-permute-start | bytes 688136 | tf_op jit(solution)/shard_map/ppermute | solution.py:32
  68.9 2.0 %collective-permute-done.23.refs_2_ = bf16[40,1792]{1,0:T(8,128)(2,1)S(1)} collective-permute-done((bf16[40,1792]{1,0:T(8,128)(2,1)S(1)}, bf16[40,1792]{1,0:T(8,128)(2,1)S(1)}, u32[]{:S(2)}, u32[]{:S(2)}) %collective-permute-start.23) | collective-permute-done | bytes 143392 | tf_op jit(solution)/shard_map/ppermute | solution.py:22
  73.2 1.6 %collective-permute-start.25 = (bf16[64,1792]{1,0:T(8,128)(2,1)S(1)}, bf16[64,1792]{1,0:T(8,128)(2,1)S(1)}, u32[]{:S(2)}, u32[]{:S(2)}) collective-permute-start(bf16[64,1792]{1,0:T(8,128)(2,1)S(1)} %shard_map.151.refs_4_), channel_id=1, source_target_pairs={{0,8},{1,9},{8,16},{9,17},{16,24},{17,25},{24,0},{25,1},{2,10},{3,... | collective-permute-start | bytes 688136 | tf_op jit(solution)/shard_map/ppermute | solution.py:32
  74.9 4.1 %collective-permute-done.27.refs_2_ = bf16[40,1792]{1,0:T(8,128)(2,1)S(1)} collective-permute-done((bf16[40,1792]{1,0:T(8,128)(2,1)S(1)}, bf16[40,1792]{1,0:T(8,128)(2,1)S(1)}, u32[]{:S(2)}, u32[]{:S(2)}) %collective-permute-start.27) | collective-permute-done | bytes 143392 | tf_op jit(solution)/shard_map/ppermute | solution.py:22
  79.5 2.8 %collective-permute-done.25.refs_1_.refs_2_ = bf16[64,1792]{1,0:T(8,128)(2,1)S(1)} collective-permute-done((bf16[64,1792]{1,0:T(8,128)(2,1)S(1)}, bf16[64,1792]{1,0:T(8,128)(2,1)S(1)}, u32[]{:S(2)}, u32[]{:S(2)}) %collective-permute-start.25) | collective-permute-done | bytes 229408 | tf_op jit(solution)/shard_map/ppermute | solution.py:32
  82.3 7.4 %shard_map.153 = (bf16[1792,1024]{1,0:T(8,128)(2,1)}, bf16[1792,1024]{1,0:T(8,128)(2,1)}, bf16[1024,1792]{1,0:T(8,128)(2,1)}) custom-call(bf16[320,1024]{1,0:T(8,128)(2,1)S(1)} %get-tuple-element.90.hidden, bf16[320,1024]{1,0:T(8,128)(2,1)S(1)} %get-tuple-element.91.d_gate, bf16[320,1024]{1,0:T(8,128)(2,1)S(1)} %get-tuple-element.92.d_up, ...), custom_call_target="tpu_custom_call" | custom-call | flops 1000000000 | bytes 1 | tf_op jit(solution)/shard_map/pallas_call | solution.py:431
  (54 shorter events, 22.3 us)
Async XLA Ops:
  4.5 10.4 %collective-permute-start.1 = (bf16[80,1792]{1,0:T(8,128)(2,1)S(1)}, bf16[80,1792]{1,0:T(8,128)(2,1)S(1)}, u32[]{:S(2)}, u32[]{:S(2)}) collective-permute-start(bf16[80,1792]{1,0:T(8,128)(2,1)S(1)} %get-tuple-element.56), channel_id=1, source_target_pairs={{0,2},{2,0},{4,6},{6,4},{1,3},{3,1},{5,7},{7,5},{8,10},{10,8},{12,... | collective-permute-start | bytes 860168 | tf_op jit(solution)/shard_map/ppermute | solution.py:22
  7.3 15.8 %collective-permute-start.2 = (bf16[80,1792]{1,0:T(8,128)(2,1)S(1)}, bf16[80,1792]{1,0:T(8,128)(2,1)S(1)}, u32[]{:S(2)}, u32[]{:S(2)}) collective-permute-start(bf16[80,1792]{1,0:T(8,128)(2,1)S(1)} %get-tuple-element.57), channel_id=1, source_target_pairs={{0,4},{2,6},{4,0},{6,2},{1,5},{3,7},{5,1},{7,3},{8,12},{10,14},{12... | collective-permute-start | bytes 860168 | tf_op jit(solution)/shard_map/ppermute | solution.py:22
  8.8 14.3 %collective-permute-start.3 = (bf16[80,1792]{1,0:T(8,128)(2,1)S(1)}, bf16[80,1792]{1,0:T(8,128)(2,1)S(1)}, u32[]{:S(2)}, u32[]{:S(2)}) collective-permute-start(bf16[80,1792]{1,0:T(8,128)(2,1)S(1)} %get-tuple-element.58), channel_id=1, source_target_pairs={{0,6},{2,4},{4,2},{6,0},{1,7},{3,5},{5,3},{7,1},{8,14},{10,12},{12... | collective-permute-start | bytes 860168 | tf_op jit(solution)/shard_map/ppermute | solution.py:22
  9.4 17.8 %collective-permute-start.6 = (bf16[80,1792]{1,0:T(8,128)(2,1)S(1)}, bf16[80,1792]{1,0:T(8,128)(2,1)S(1)}, u32[]{:S(2)}, u32[]{:S(2)}) collective-permute-start(bf16[80,1792]{1,0:T(8,128)(2,1)S(1)} %get-tuple-element.67), channel_id=1, source_target_pairs={{0,2},{2,0},{4,6},{6,4},{1,3},{3,1},{5,7},{7,5},{8,10},{10,8},{12,... | collective-permute-start | bytes 860168 | tf_op jit(solution)/shard_map/ppermute | solution.py:22
  11.5 23.0 %collective-permute-start.7 = (bf16[80,1792]{1,0:T(8,128)(2,1)S(1)}, bf16[80,1792]{1,0:T(8,128)(2,1)S(1)}, u32[]{:S(2)}, u32[]{:S(2)}) collective-permute-start(bf16[80,1792]{1,0:T(8,128)(2,1)S(1)} %get-tuple-element.68), channel_id=1, source_target_pairs={{0,4},{2,6},{4,0},{6,2},{1,5},{3,7},{5,1},{7,3},{8,12},{10,14},{12... | collective-permute-start | bytes 860168 | tf_op jit(solution)/shard_map/ppermute | solution.py:22
  14.9 20.7 %collective-permute-start.8 = (bf16[80,1792]{1,0:T(8,128)(2,1)S(1)}, bf16[80,1792]{1,0:T(8,128)(2,1)S(1)}, u32[]{:S(2)}, u32[]{:S(2)}) collective-permute-start(bf16[80,1792]{1,0:T(8,128)(2,1)S(1)} %get-tuple-element.69), channel_id=1, source_target_pairs={{0,6},{2,4},{4,2},{6,0},{1,7},{3,5},{5,3},{7,1},{8,14},{10,12},{12... | collective-permute-start | bytes 860168 | tf_op jit(solution)/shard_map/ppermute | solution.py:22
  25.8 12.6 %collective-permute-start.5 = (bf16[2,320,1024]{2,1,0:T(8,128)(2,1)S(1)}, bf16[2,320,1024]{2,1,0:T(8,128)(2,1)S(1)}, u32[]{:S(2)}, u32[]{:S(2)}) collective-permute-start(bf16[2,320,1024]{2,1,0:T(8,128)(2,1)S(1)} %shard_map.143.refs_6_.own_ref), channel_id=1, source_target_pairs={{0,1},{1,0},{2,3},{3,2},{4,5},{5,4},{6,7},{7,6},{8,9},{9,8},{10,11... | collective-permute-start | bytes 3932168 | tf_op jit(solution)/shard_map/ppermute | solution.py:22
  25.9 15.9 %collective-permute-start.12 = (bf16[80,1792]{1,0:T(8,128)(2,1)S(1)}, bf16[80,1792]{1,0:T(8,128)(2,1)S(1)}, u32[]{:S(2)}, u32[]{:S(2)}) collective-permute-start(bf16[80,1792]{1,0:T(8,128)(2,1)S(1)} %get-tuple-element.74), channel_id=1, source_target_pairs={{0,2},{2,0},{4,6},{6,4},{1,3},{3,1},{5,7},{7,5},{8,10},{10,8},{12,... | collective-permute-start | bytes 860168 | tf_op jit(solution)/shard_map/ppermute | solution.py:22
  27.2 22.6 %collective-permute-start.13 = (bf16[80,1792]{1,0:T(8,128)(2,1)S(1)}, bf16[80,1792]{1,0:T(8,128)(2,1)S(1)}, u32[]{:S(2)}, u32[]{:S(2)}) collective-permute-start(bf16[80,1792]{1,0:T(8,128)(2,1)S(1)} %get-tuple-element.75), channel_id=1, source_target_pairs={{0,4},{2,6},{4,0},{6,2},{1,5},{3,7},{5,1},{7,3},{8,12},{10,14},{12... | collective-permute-start | bytes 860168 | tf_op jit(solution)/shard_map/ppermute | solution.py:22
  34.5 15.4 %collective-permute-start.14 = (bf16[80,1792]{1,0:T(8,128)(2,1)S(1)}, bf16[80,1792]{1,0:T(8,128)(2,1)S(1)}, u32[]{:S(2)}, u32[]{:S(2)}) collective-permute-start(bf16[80,1792]{1,0:T(8,128)(2,1)S(1)} %get-tuple-element.76), channel_id=1, source_target_pairs={{0,6},{2,4},{4,2},{6,0},{1,7},{3,5},{5,3},{7,1},{8,14},{10,12},{12... | collective-permute-start | bytes 860168 | tf_op jit(solution)/shard_map/ppermute | solution.py:22
  38.3 19.1 %collective-permute-start.19 = (bf16[2,320,1024]{2,1,0:T(8,128)(2,1)S(1)}, bf16[2,320,1024]{2,1,0:T(8,128)(2,1)S(1)}, u32[]{:S(2)}, u32[]{:S(2)}) collective-permute-start(bf16[2,320,1024]{2,1,0:T(8,128)(2,1)S(1)} %shard_map.144.refs_0_.own_ref), channel_id=1, source_target_pairs={{0,1},{1,0},{2,3},{3,2},{4,5},{5,4},{6,7},{7,6},{8,9},{9,8},{10,11... | collective-permute-start | bytes 3932168 | tf_op jit(solution)/shard_map/ppermute | solution.py:22
  40.0 12.9 %collective-permute-start.10 = (bf16[40,1792]{1,0:T(8,128)(2,1)S(1)}, bf16[40,1792]{1,0:T(8,128)(2,1)S(1)}, u32[]{:S(2)}, u32[]{:S(2)}) collective-permute-start(bf16[40,1792]{1,0:T(8,128)(2,1)S(1)} %get-tuple-element.72), channel_id=1, source_target_pairs={{0,4},{2,6},{4,0},{6,2},{1,5},{3,7},{5,1},{7,3},{8,12},{10,14},{12... | collective-permute-start | bytes 430088 | tf_op jit(solution)/shard_map/ppermute | solution.py:22
  41.8 12.4 %collective-permute-start.11 = (bf16[40,1792]{1,0:T(8,128)(2,1)S(1)}, bf16[40,1792]{1,0:T(8,128)(2,1)S(1)}, u32[]{:S(2)}, u32[]{:S(2)}) collective-permute-start(bf16[40,1792]{1,0:T(8,128)(2,1)S(1)} %get-tuple-element.73), channel_id=1, source_target_pairs={{0,6},{2,4},{4,2},{6,0},{1,7},{3,5},{5,3},{7,1},{8,14},{10,12},{12... | collective-permute-start | bytes 430088 | tf_op jit(solution)/shard_map/ppermute | solution.py:22
  52.9 10.5 %collective-permute-start.16 = (bf16[40,1792]{1,0:T(8,128)(2,1)S(1)}, bf16[40,1792]{1,0:T(8,128)(2,1)S(1)}, u32[]{:S(2)}, u32[]{:S(2)}) collective-permute-start(bf16[40,1792]{1,0:T(8,128)(2,1)S(1)} %get-tuple-element.79), channel_id=1, source_target_pairs={{0,2},{2,0},{4,6},{6,4},{1,3},{3,1},{5,7},{7,5},{8,10},{10,8},{12,... | collective-permute-start | bytes 430088 | tf_op jit(solution)/shard_map/ppermute | solution.py:22
  54.2 10.4 %collective-permute-start.17 = (bf16[40,1792]{1,0:T(8,128)(2,1)S(1)}, bf16[40,1792]{1,0:T(8,128)(2,1)S(1)}, u32[]{:S(2)}, u32[]{:S(2)}) collective-permute-start(bf16[40,1792]{1,0:T(8,128)(2,1)S(1)} %get-tuple-element.80), channel_id=1, source_target_pairs={{0,4},{2,6},{4,0},{6,2},{1,5},{3,7},{5,1},{7,3},{8,12},{10,14},{12... | collective-permute-start | bytes 430088 | tf_op jit(solution)/shard_map/ppermute | solution.py:22
  55.9 10.3 %collective-permute-start.18 = (bf16[40,1792]{1,0:T(8,128)(2,1)S(1)}, bf16[40,1792]{1,0:T(8,128)(2,1)S(1)}, u32[]{:S(2)}, u32[]{:S(2)}) collective-permute-start(bf16[40,1792]{1,0:T(8,128)(2,1)S(1)} %get-tuple-element.81), channel_id=1, source_target_pairs={{0,6},{2,4},{4,2},{6,0},{1,7},{3,5},{5,3},{7,1},{8,14},{10,12},{12... | collective-permute-start | bytes 430088 | tf_op jit(solution)/shard_map/ppermute | solution.py:22
  63.1 7.8 %collective-permute-start.23 = (bf16[40,1792]{1,0:T(8,128)(2,1)S(1)}, bf16[40,1792]{1,0:T(8,128)(2,1)S(1)}, u32[]{:S(2)}, u32[]{:S(2)}) collective-permute-start(bf16[40,1792]{1,0:T(8,128)(2,1)S(1)} %get-tuple-element.84), channel_id=1, source_target_pairs={{0,4},{2,6},{4,0},{6,2},{1,5},{3,7},{5,1},{7,3},{8,12},{10,14},{12... | collective-permute-start | bytes 430088 | tf_op jit(solution)/shard_map/ppermute | solution.py:22
  63.4 8.1 %collective-permute-start.24 = (bf16[40,1792]{1,0:T(8,128)(2,1)S(1)}, bf16[40,1792]{1,0:T(8,128)(2,1)S(1)}, u32[]{:S(2)}, u32[]{:S(2)}) collective-permute-start(bf16[40,1792]{1,0:T(8,128)(2,1)S(1)} %get-tuple-element.85), channel_id=1, source_target_pairs={{0,6},{2,4},{4,2},{6,0},{1,7},{3,5},{5,3},{7,1},{8,14},{10,12},{12... | collective-permute-start | bytes 430088 | tf_op jit(solution)/shard_map/ppermute | solution.py:22
  64.7 8.6 %collective-permute-start.15 = (bf16[64,1792]{1,0:T(8,128)(2,1)S(1)}, bf16[64,1792]{1,0:T(8,128)(2,1)S(1)}, u32[]{:S(2)}, u32[]{:S(2)}) collective-permute-start(bf16[64,1792]{1,0:T(8,128)(2,1)S(1)} %shard_map.148.refs_0_), channel_id=1, source_target_pairs={{0,8},{1,9},{8,16},{9,17},{16,24},{17,25},{24,0},{25,1},{2,10},{3,... | collective-permute-start | bytes 688136 | tf_op jit(solution)/shard_map/ppermute | solution.py:32
  66.8 12.2 %collective-permute-start.21 = (bf16[64,1792]{1,0:T(8,128)(2,1)S(1)}, bf16[64,1792]{1,0:T(8,128)(2,1)S(1)}, u32[]{:S(2)}, u32[]{:S(2)}) collective-permute-start(bf16[64,1792]{1,0:T(8,128)(2,1)S(1)} %shard_map.150.refs_4_), channel_id=1, source_target_pairs={{0,9},{1,8},{8,17},{9,16},{16,25},{17,24},{24,1},{25,0},{2,11},{3,... | collective-permute-start | bytes 688136 | tf_op jit(solution)/shard_map/ppermute | solution.py:32
  70.9 8.1 %collective-permute-start.27 = (bf16[40,1792]{1,0:T(8,128)(2,1)S(1)}, bf16[40,1792]{1,0:T(8,128)(2,1)S(1)}, u32[]{:S(2)}, u32[]{:S(2)}) collective-permute-start(bf16[40,1792]{1,0:T(8,128)(2,1)S(1)} %get-tuple-element.88), channel_id=1, source_target_pairs={{0,4},{2,6},{4,0},{6,2},{1,5},{3,7},{5,1},{7,3},{8,12},{10,14},{12... | collective-permute-start | bytes 430088 | tf_op jit(solution)/shard_map/ppermute | solution.py:22
  71.5 7.5 %collective-permute-start.28 = (bf16[40,1792]{1,0:T(8,128)(2,1)S(1)}, bf16[40,1792]{1,0:T(8,128)(2,1)S(1)}, u32[]{:S(2)}, u32[]{:S(2)}) collective-permute-start(bf16[40,1792]{1,0:T(8,128)(2,1)S(1)} %get-tuple-element.89), channel_id=1, source_target_pairs={{0,6},{2,4},{4,2},{6,0},{1,7},{3,5},{5,3},{7,1},{8,14},{10,12},{12... | collective-permute-start | bytes 430088 | tf_op jit(solution)/shard_map/ppermute | solution.py:22
  73.2 9.1 %collective-permute-start.25 = (bf16[64,1792]{1,0:T(8,128)(2,1)S(1)}, bf16[64,1792]{1,0:T(8,128)(2,1)S(1)}, u32[]{:S(2)}, u32[]{:S(2)}) collective-permute-start(bf16[64,1792]{1,0:T(8,128)(2,1)S(1)} %shard_map.151.refs_4_), channel_id=1, source_target_pairs={{0,8},{1,9},{8,16},{9,17},{16,24},{17,25},{24,0},{25,1},{2,10},{3,... | collective-permute-start | bytes 688136 | tf_op jit(solution)/shard_map/ppermute | solution.py:32
  79.4 10.2 %collective-permute-start.29 = (bf16[64,1792]{1,0:T(8,128)(2,1)S(1)}, bf16[64,1792]{1,0:T(8,128)(2,1)S(1)}, u32[]{:S(2)}, u32[]{:S(2)}) collective-permute-start(bf16[64,1792]{1,0:T(8,128)(2,1)S(1)} %shard_map.152.refs_0_), channel_id=1, source_target_pairs={{0,9},{1,8},{8,17},{9,16},{16,25},{17,24},{24,1},{25,0},{2,11},{3,... | collective-permute-start | bytes 688136 | tf_op jit(solution)/shard_map/ppermute | solution.py:32
  (6 other events, 32.8 us)

commit v10 on v7

--- a/solution.py
+++ b/solution.py
@@ -243,13 +243,13 @@
     )(*metas, own, other, *passing, *after)
 
 
-def combine_kernel(own_meta, other_meta, *refs, plan, first_row, weighted, other):
-    returned, out = refs[: plan.blocks], refs[-1]
-    width, tokens = out.shape[1], plan.tokens
+def combine_kernel(own_meta, other_meta, *refs, plan, first_row, weighted, cores):
+    returned, outs = refs[: plan.blocks], refs[-len(cores) :]
+    width, tokens = outs[0].shape[1], plan.tokens
     slot, route = slot_rows(own_meta, other_meta, plan, first_row)
     table = []
     for block in range(plan.blocks):
-        table.append(slot_table(slot, block, plan.part if other else 0, plan.part))
+        table.append(slot_table(slot, block, plan.part * cores[0], plan.part * len(cores)))
         if weighted:
             table[block] = table[block] * route[block : block + 1, :]
     table = jnp.concatenate(table, axis=0)
@@ -262,17 +262,18 @@
         total = dot(high, values, 0, 0)
         if weighted:
             total += dot(low, values, 0, 0)
-        out[:, part] = total[tokens if other else 0 :][:tokens].astype(BF16)
-
-
-def combine(metas, returned, plan, first_row, weighted, other, after=(), weight=1):
+        for core, out in zip(cores, outs):
+            out[:, part] = total[core * tokens : (core + 1) * tokens].astype(BF16)
+
+
+def combine(metas, returned, plan, first_row, weighted, cores, after=(), weight=1):
     return call(
         functools.partial(
-            combine_kernel, plan=plan, first_row=first_row, weighted=weighted, other=other
+            combine_kernel, plan=plan, first_row=first_row, weighted=weighted, cores=cores
         ),
-        array(plan.tokens, returned[0].shape[1]),
+        [array(plan.tokens, returned[0].shape[1])] * len(cores),
         [VMEM] * (2 + plan.blocks) + [AFTER] * len(after),
-        VMEM,
+        [VMEM] * len(cores),
         [],
         weight=weight,
     )(*metas, *returned, *after)
@@ -327,11 +328,11 @@
     )(*inputs, down_w, partial, *after)
 
 
-def scatter_tile(value, outs, columns):
-    blocks, part = len(outs) // 2, outs[0].shape[0]
+def scatter_tile(value, outs, columns, blocks):
+    pieces, rows = len(outs) // blocks, outs[0].shape[0]
     for place, out in enumerate(outs):
-        first = (2 * (place % blocks) + place // blocks) * part
-        out[:, columns] = value[first : first + part].astype(BF16)
+        first = (pieces * (place % blocks) + place // blocks) * rows
+        out[:, columns] = value[first : first + rows].astype(BF16)
 
 
 def total_of(own, other, part):
@@ -344,8 +345,8 @@
 
 
 def down_kernel(own_ref, other_ref, down_w, *refs, blocks):
-    outs, hidden = refs[-1 - 2 * blocks : -1], refs[-1]
-    part = outs[0].shape[0]
+    outs, hidden = refs[-1 - blocks : -1], refs[-1]
+    part = outs[0].shape[0] // 2
     for start in range(0, hidden.shape[1], TILE):
         columns = slice(start, start + TILE)
         gate = total_of(own_ref[0, :, columns], other_ref[0, :, columns], part)
@@ -353,16 +354,16 @@
         hidden[:, columns] = (gate * jax.nn.sigmoid(gate) * up).astype(BF16)
     for start in range(0, outs[0].shape[1], TILE):
         columns = slice(start, start + TILE)
-        scatter_tile(dot(hidden[...], down_w[:, columns], 1, 0), outs, columns)
+        scatter_tile(dot(hidden[...], down_w[:, columns], 1, 0), outs, columns, blocks)
 
 
 def down(own, other, down_w, plan, after=()):
     _, total, units = own.shape
     return call(
         functools.partial(down_kernel, blocks=plan.blocks),
-        [array(plan.part, down_w.shape[1])] * (2 * plan.blocks),
+        [array(2 * plan.part, down_w.shape[1])] * plan.blocks,
         [VMEM] * 3 + [AFTER] * len(after),
-        [VMEM] * (2 * plan.blocks),
+        [VMEM] * plan.blocks,
         [pltpu.VMEM((total, units), BF16)],
     )(own, other, down_w, *after)
 
@@ -386,7 +387,7 @@
         columns = slice(start, start + TILE)
         total = dot(d_gate[...], gate_w[columns, :], 1, 1)
         total += dot(d_up[...], up_w[columns, :], 1, 1)
-        scatter_tile(total, outs, columns)
+        scatter_tile(total, outs, columns, blocks)
 
 
 def back(own, other, gate_w, up_w, plan, after=()):
@@ -438,6 +439,21 @@
         grid=(units // TILE,),
         weight=weight,
     )(hidden, d_gate, d_up, turned, cots, *after)
+
+
+def arrived_kernel(*refs):
+    refs[-1][...] = jnp.zeros_like(refs[-1])
+
+
+def arrived(values, after=(), weight=1):
+    return call(
+        arrived_kernel,
+        array(16, 128),
+        [AFTER] * (len(values) + len(after)),
+        VMEM,
+        [],
+        weight=weight,
+    )(*[in_vmem(value) for value in values], *after)
 
 
 def to_experts(blocks, relative):
@@ -515,48 +531,43 @@
     part_f_other = exchange(part_f, "dp", 1)
     part_b = gate_up(rows_b, gate_w, up_w, planes=3, after=(part_f,), weight=3000)
     down_blocks = down(part_f, part_f_other, down_w, plan, after=(in_vmem(part_b),))
-    own_back_f = to_experts(down_blocks[:n_expert], relative)
-    other_back_f = to_experts(down_blocks[n_expert:], relative)
+    back_f = to_experts(down_blocks, relative)
     turned = turn(rows_b, after=down_blocks[:1])
     cots, part_b = d_hidden(cots_b, down_w, part_b, after=(in_vmem(turned),), weight=1000)
     part_b_other = exchange(part_b, "dp", 1)
-    own_sum = combine(
-        metas, own_back_f, plan, row_f, True, False, after=(in_vmem(part_b),), weight=2000
-    )
-    y_mine = section_shift(own_sum, 0)
+    near = arrived(back_f[1:3], after=(in_vmem(part_b),), weight=2000)
     hidden, d_gate, d_up, *back_blocks = back(
-        part_b, part_b_other, gate_w, up_w, plan, after=(own_sum,)
+        part_b, part_b_other, gate_w, up_w, plan, after=(near,)
     )
     own_back_b = to_experts(back_blocks[:n_expert], relative)
     other_back_b = to_experts(back_blocks[n_expert:], relative)
-    other_sum = combine(
-        metas, other_back_f, plan, row_f, True, True, after=back_blocks[:1], weight=150
-    )
-    y_rest = section_shift(other_sum, 1)
-    own_sum = combine(
-        metas,
-        own_back_b,
-        plan,
-        row_b,
-        False,
-        False,
-        after=(other_sum, in_vmem(y_mine)),
-        weight=150,
+    own_sum, other_sum = combine(
+        metas, back_f, plan, row_f, True, (0, 1), after=back_blocks[:1], weight=150
+    )
+    y_mine, y_rest = section_shift(own_sum, 0), section_shift(other_sum, 1)
+    (own_sum,) = combine(
+        metas, own_back_b, plan, row_b, False, (0,), after=(other_sum,), weight=150
     )
     dx_mine = section_shift(own_sum, 0)
-    other_sum = combine(
+    (other_sum,) = combine(
         metas,
         other_back_b,
         plan,
         row_b,
         False,
-        True,
-        after=(own_sum, in_vmem(y_rest)),
+        (1,),
+        after=(own_sum, in_vmem(y_mine), in_vmem(y_rest)),
         weight=100,
     )
     dx_rest = section_shift(other_sum, 1)
     grad_g, grad_u, grad_d = grads(
-        hidden, d_gate, d_up, turned, cots, after=(other_sum, in_vmem(dx_mine)), weight=100
+        hidden,
+        d_gate,
+        d_up,
+        turned,
+        cots,
+        after=(other_sum, in_vmem(y_rest), in_vmem(dx_mine)),
+        weight=100,
     )
     y_next, dx_next = finish(y_mine, y_rest, dx_mine, dx_rest, after=(in_hbm(grad_g),))
     return (

time: 87.7 us -> 91.8 us (1.047)
  starting transfers between devices: 33.8 us -> 36.8 us
  waiting for transfers between devices: 22 us -> 23.3 us
    ppermute x25 -> x22, starting transfers between devices: 29 us -> 32 us  [exchange(): lax.ppermute(value, axis, [(source, source ^ mask) for source in range(co...]
    ppermute x4, waiting for transfers between devices: 1.04 us -> 2.61 us  [section_shift(): return lax.ppermute(value, ('section', 'dp'), pairs)]
    ppermute x25 -> x22, waiting for transfers between devices: 21 us -> 20.7 us  [exchange(): lax.ppermute(value, axis, [(source, source ^ mask) for source in range(co...]
    pallas_call x4 -> x3, Pallas kernels: 2.05 us -> 1.94 us  [combine(): call(functools.partial(combine_kernel, plan=plan, first_row=first_row, we...]
  transfers between devices with their start and end apart: 29 -> 26, of which waited for: 13 -> 11; matrix products, arithmetic and copies ran while one was open for 0% -> 0% of each run, Pallas kernels for 32% -> 30%
where the time goes in v10:
time: 91.8 us; the launch traced here: 91.6 us
  starting transfers between devices  36.8 us (40%)
  Pallas kernels  30.6 us (33%)
  waiting for transfers between devices  23.3 us (25%)
  between operations  0.97 us (1%)
    ppermute x22, starting transfers between devices, exchange(): lax.ppermute(value, axis, [(source, source ^ mask) for source in range(co...  32 us
    ppermute x22, waiting for transfers between devices, exchange(): lax.ppermute(value, axis, [(source, source ^ mask) for source in range(co...  20.7 us
    pallas_call x1, Pallas kernels, grads(): call(grad_kernel, [pltpu.HBM((width, units), BF16)] * 2 + [pltpu.HBM((uni...  7.37 us
    pallas_call x2, Pallas kernels, gate_up(): call(functools.partial(gate_up_kernel, blocks=blocks), array(planes, tota...  5.22 us
    ppermute x4, starting transfers between devices, section_shift(): return lax.ppermute(value, ('section', 'dp'), pairs)  4.78 us
    pallas_call x1, Pallas kernels, load(): call(functools.partial(load_kernel, count=len(weights)), [array(*weight.s...  4.23 us
    pallas_call x1, Pallas kernels, back(): call(functools.partial(back_kernel, blocks=plan.blocks), [array(total, un...  3.25 us
    ppermute x4, waiting for transfers between devices, section_shift(): return lax.ppermute(value, ('section', 'dp'), pairs)  2.61 us
  transfers between devices with their start and end apart: 26, of which 11 were waited for; matrix products, arithmetic and copies ran while one was open for 0% of the time, Pallas kernels for 30%

profile of v10, /device:TPU:0, one launch (start us, length us, event | category | flops | bytes accessed | tf_op | source)
XLA Modules:
  0.0 91.6 jit_solution(13910526302538316403)
XLA Ops:
  4.5 2.8 %collective-permute-start.1 = (bf16[80,1792]{1,0:T(8,128)(2,1)S(1)}, bf16[80,1792]{1,0:T(8,128)(2,1)S(1)}, u32[]{:S(2)}, u32[]{:S(2)}) collective-permute-start(bf16[80,1792]{1,0:T(8,128)(2,1)S(1)} %get-tuple-element.54), channel_id=1, source_target_pairs={{0,2},{2,0},{4,6},{6,4},{1,3},{3,1},{5,7},{7,5},{8,10},{10,8},{12,... | collective-permute-start | bytes 860168 | tf_op jit(solution)/shard_map/ppermute | solution.py:22
  7.3 1.5 %collective-permute-start.2 = (bf16[80,1792]{1,0:T(8,128)(2,1)S(1)}, bf16[80,1792]{1,0:T(8,128)(2,1)S(1)}, u32[]{:S(2)}, u32[]{:S(2)}) collective-permute-start(bf16[80,1792]{1,0:T(8,128)(2,1)S(1)} %get-tuple-element.55), channel_id=1, source_target_pairs={{0,4},{2,6},{4,0},{6,2},{1,5},{3,7},{5,1},{7,3},{8,12},{10,14},{12... | collective-permute-start | bytes 860168 | tf_op jit(solution)/shard_map/ppermute | solution.py:22
  9.4 2.0 %collective-permute-start.6 = (bf16[80,1792]{1,0:T(8,128)(2,1)S(1)}, bf16[80,1792]{1,0:T(8,128)(2,1)S(1)}, u32[]{:S(2)}, u32[]{:S(2)}) collective-permute-start(bf16[80,1792]{1,0:T(8,128)(2,1)S(1)} %get-tuple-element.65), channel_id=1, source_target_pairs={{0,2},{2,0},{4,6},{6,4},{1,3},{3,1},{5,7},{7,5},{8,10},{10,8},{12,... | collective-permute-start | bytes 860168 | tf_op jit(solution)/shard_map/ppermute | solution.py:22
  11.5 1.5 %collective-permute-start.7 = (bf16[80,1792]{1,0:T(8,128)(2,1)S(1)}, bf16[80,1792]{1,0:T(8,128)(2,1)S(1)}, u32[]{:S(2)}, u32[]{:S(2)}) collective-permute-start(bf16[80,1792]{1,0:T(8,128)(2,1)S(1)} %get-tuple-element.66), channel_id=1, source_target_pairs={{0,4},{2,6},{4,0},{6,2},{1,5},{3,7},{5,1},{7,3},{8,12},{10,14},{12... | collective-permute-start | bytes 860168 | tf_op jit(solution)/shard_map/ppermute | solution.py:22
  13.0 1.9 %collective-permute-done.1.refs_1_ = bf16[80,1792]{1,0:T(8,128)(2,1)S(1)} collective-permute-done((bf16[80,1792]{1,0:T(8,128)(2,1)S(1)}, bf16[80,1792]{1,0:T(8,128)(2,1)S(1)}, u32[]{:S(2)}, u32[]{:S(2)}) %collective-permute-start.1) | collective-permute-done | bytes 286752 | tf_op jit(solution)/shard_map/ppermute | solution.py:22
  14.9 3.0 %collective-permute-start.8 = (bf16[80,1792]{1,0:T(8,128)(2,1)S(1)}, bf16[80,1792]{1,0:T(8,128)(2,1)S(1)}, u32[]{:S(2)}, u32[]{:S(2)}) collective-permute-start(bf16[80,1792]{1,0:T(8,128)(2,1)S(1)} %get-tuple-element.67), channel_id=1, source_target_pairs={{0,6},{2,4},{4,2},{6,0},{1,7},{3,5},{5,3},{7,1},{8,14},{10,12},{12... | collective-permute-start | bytes 860168 | tf_op jit(solution)/shard_map/ppermute | solution.py:22
  17.9 4.2 %shard_map.141 = (bf16[1792,1024]{1,0:T(8,128)(2,1)S(1)}, bf16[1792,1024]{1,0:T(8,128)(2,1)S(1)}, bf16[1024,1792]{1,0:T(8,128)(2,1)S(1)}) custom-call(bf16[1792,1024]{1,0:T(8,128)(2,1)} %bitcast.23, bf16[1792,1024]{1,0:T(8,128)(2,1)} %bitcast.24, bf16[1024,1792]{1,0:T(8,128)(2,1)} %bitcast.25, bf16[80,1792]{1,0:T(8,128)(2,1)S(1)} %get-tuple-element.59.refs_3_.refs_0_), custom_call_target="tpu_custom_call" | custom-call | flops 10000000 | bytes 1 | tf_op jit(solution)/shard_map/pallas_call | solution.py:164
  23.4 1.8 %collective-permute-start.13 = (bf16[80,1792]{1,0:T(8,128)(2,1)S(1)}, bf16[80,1792]{1,0:T(8,128)(2,1)S(1)}, u32[]{:S(2)}, u32[]{:S(2)}) collective-permute-start(bf16[80,1792]{1,0:T(8,128)(2,1)S(1)} %get-tuple-element.73), channel_id=1, source_target_pairs={{0,4},{2,6},{4,0},{6,2},{1,5},{3,7},{5,1},{7,3},{8,12},{10,14},{12... | collective-permute-start | bytes 860168 | tf_op jit(solution)/shard_map/ppermute | solution.py:22
  25.2 2.6 %shard_map.143.refs_6_.own_ref = bf16[2,320,1024]{2,1,0:T(8,128)(2,1)S(1)} custom-call(bf16[80,1792]{1,0:T(8,128)(2,1)S(1)} %get-tuple-element.53.refs_0_, bf16[80,1792]{1,0:T(8,128)(2,1)S(1)} %collective-permute-done.1.refs_1_, bf16[80,1792]{1,0:T(8,128)(2,1)S(1)} %collective-permute-done.2.refs_2_, bf16[80,1792]{1,0:T(8,128)(2,1)S(1)} %collective-permute-done.3.refs_3_, ...), custom_call_target="tpu_custom_call" | custom-call | flops 10000000 | bytes 1 | tf_op jit(solution)/shard_map/pallas_call | solution.py:299
  27.8 2.4 %collective-permute-start.14 = (bf16[80,1792]{1,0:T(8,128)(2,1)S(1)}, bf16[80,1792]{1,0:T(8,128)(2,1)S(1)}, u32[]{:S(2)}, u32[]{:S(2)}) collective-permute-start(bf16[80,1792]{1,0:T(8,128)(2,1)S(1)} %get-tuple-element.74), channel_id=1, source_target_pairs={{0,6},{2,4},{4,2},{6,0},{1,7},{3,5},{5,3},{7,1},{8,14},{10,12},{12... | collective-permute-start | bytes 860168 | tf_op jit(solution)/shard_map/ppermute | solution.py:22
  30.3 5.2 %collective-permute-done.7.refs_2_ = bf16[80,1792]{1,0:T(8,128)(2,1)S(1)} collective-permute-done((bf16[80,1792]{1,0:T(8,128)(2,1)S(1)}, bf16[80,1792]{1,0:T(8,128)(2,1)S(1)}, u32[]{:S(2)}, u32[]{:S(2)}) %collective-permute-start.7) | collective-permute-done | bytes 286752 | tf_op jit(solution)/shard_map/ppermute | solution.py:22
  35.4 2.6 %shard_map.144.refs_0_.refs_5_ = bf16[3,320,1024]{2,1,0:T(8,128)(2,1)S(1)} custom-call(bf16[80,1792]{1,0:T(8,128)(2,1)S(1)} %get-tuple-element.59.refs_3_.refs_0_, bf16[80,1792]{1,0:T(8,128)(2,1)S(1)} %collective-permute-done.6.refs_1_, bf16[80,1792]{1,0:T(8,128)(2,1)S(1)} %collective-permute-done.7.refs_2_, ...), custom_call_target="tpu_custom_call" | custom-call | flops 30000001024 | bytes 1 | tf_op jit(solution)/shard_map/pallas_call | solution.py:299
  38.5 1.6 %shard_map.145 = (bf16[80,1792]{1,0:T(8,128)(2,1)S(1)}, bf16[80,1792]{1,0:T(8,128)(2,1)S(1)}, bf16[80,1792]{1,0:T(8,128)(2,1)S(1)}, bf16[80,1792]{1,0:T(8,128)(2,1)S(1)}) custom-call(bf16[2,320,1024]{2,1,0:T(8,128)(2,1)S(1)} %shard_map.143.refs_6_.own_ref, bf16[2,320,1024]{2,1,0:T(8,128)(2,1)S(1)} %collective-permute-done.5.other_ref, ...), custom_call_target="tpu_custom_call" | custom-call | flops 10000000 | bytes 1 | tf_op jit(solution)/shard_map/pallas_call | solution.py:362
  42.7 4.1 %collective-permute-done.13.refs_2_ = bf16[80,1792]{1,0:T(8,128)(2,1)S(1)} collective-permute-done((bf16[80,1792]{1,0:T(8,128)(2,1)S(1)}, bf16[80,1792]{1,0:T(8,128)(2,1)S(1)}, u32[]{:S(2)}, u32[]{:S(2)}) %collective-permute-start.13) | collective-permute-done | bytes 286752 | tf_op jit(solution)/shard_map/ppermute | solution.py:22
  52.9 3.2 %shard_map.149 = (bf16[320,1024]{1,0:T(8,128)(2,1)S(1)}, bf16[320,1024]{1,0:T(8,128)(2,1)S(1)}, bf16[320,1024]{1,0:T(8,128)(2,1)S(1)}, bf16[40,1792]{1,0:T(8,128...) custom-call(bf16[3,320,1024]{2,1,0:T(8,128)(2,1)S(1)} %get-tuple-ele, ...), custom_call_target="tpu_custom_call" | custom-call | flops 10000000 | bytes 1 | tf_op jit(solution)/shard_map/pallas_call | solution.py:395
  57.5 6.9 %collective-permute-start.19 = (bf16[40,1792]{1,0:T(8,128)(2,1)S(1)}, bf16[40,1792]{1,0:T(8,128)(2,1)S(1)}, u32[]{:S(2)}, u32[]{:S(2)}) collective-permute-start(bf16[40,1792]{1,0:T(8,128)(2,1)S(1)} %get-tuple-element.80), channel_id=1, source_target_pairs={{0,4},{2,6},{4,0},{6,2},{1,5},{3,7},{5,1},{7,3},{8,12},{10,14},{12... | collective-permute-start | bytes 430088 | tf_op jit(solution)/shard_map/ppermute | solution.py:22
  65.4 1.6 %collective-permute-start.16 = (bf16[64,1792]{1,0:T(8,128)(2,1)S(1)}, bf16[64,1792]{1,0:T(8,128)(2,1)S(1)}, u32[]{:S(2)}, u32[]{:S(2)}) collective-permute-start(bf16[64,1792]{1,0:T(8,128)(2,1)S(1)} %get-tuple-element.77), channel_id=1, source_target_pairs={{0,8},{1,9},{8,16},{9,17},{16,24},{17,25},{24,0},{25,1},{2,10},{3,... | collective-permute-start | bytes 688136 | tf_op jit(solution)/shard_map/ppermute | solution.py:32
  68.6 2.4 %collective-permute-start.23 = (bf16[40,1792]{1,0:T(8,128)(2,1)S(1)}, bf16[40,1792]{1,0:T(8,128)(2,1)S(1)}, u32[]{:S(2)}, u32[]{:S(2)}) collective-permute-start(bf16[40,1792]{1,0:T(8,128)(2,1)S(1)} %get-tuple-element.84), channel_id=1, source_target_pairs={{0,4},{2,6},{4,0},{6,2},{1,5},{3,7},{5,1},{7,3},{8,12},{10,14},{12... | collective-permute-start | bytes 430088 | tf_op jit(solution)/shard_map/ppermute | solution.py:22
  71.5 1.5 %collective-permute-done.22.refs_1_ = bf16[40,1792]{1,0:T(8,128)(2,1)S(1)} collective-permute-done((bf16[40,1792]{1,0:T(8,128)(2,1)S(1)}, bf16[40,1792]{1,0:T(8,128)(2,1)S(1)}, u32[]{:S(2)}, u32[]{:S(2)}) %collective-permute-start.22) | collective-permute-done | bytes 143392 | tf_op jit(solution)/shard_map/ppermute | solution.py:22
  73.0 1.6 %collective-permute-start.21 = (bf16[64,1792]{1,0:T(8,128)(2,1)S(1)}, bf16[64,1792]{1,0:T(8,128)(2,1)S(1)}, u32[]{:S(2)}, u32[]{:S(2)}) collective-permute-start(bf16[64,1792]{1,0:T(8,128)(2,1)S(1)} %shard_map.151.refs_4_), channel_id=1, source_target_pairs={{0,8},{1,9},{8,16},{9,17},{16,24},{17,25},{24,0},{25,1},{2,10},{3,... | collective-permute-start | bytes 688136 | tf_op jit(solution)/shard_map/ppermute | solution.py:32
  74.6 3.9 %collective-permute-done.23.refs_2_ = bf16[40,1792]{1,0:T(8,128)(2,1)S(1)} collective-permute-done((bf16[40,1792]{1,0:T(8,128)(2,1)S(1)}, bf16[40,1792]{1,0:T(8,128)(2,1)S(1)}, u32[]{:S(2)}, u32[]{:S(2)}) %collective-permute-start.23) | collective-permute-done | bytes 143392 | tf_op jit(solution)/shard_map/ppermute | solution.py:22
  78.9 1.6 %collective-permute-start.25 = (bf16[64,1792]{1,0:T(8,128)(2,1)S(1)}, bf16[64,1792]{1,0:T(8,128)(2,1)S(1)}, u32[]{:S(2)}, u32[]{:S(2)}) collective-permute-start(bf16[64,1792]{1,0:T(8,128)(2,1)S(1)} %shard_map.152.refs_0_), channel_id=1, source_target_pairs={{0,9},{1,8},{8,17},{9,16},{16,25},{17,24},{24,1},{25,0},{2,11},{3,... | collective-permute-start | bytes 688136 | tf_op jit(solution)/shard_map/ppermute | solution.py:32
  80.5 2.6 %collective-permute-done.21.refs_2_ = bf16[64,1792]{1,0:T(8,128)(2,1)S(1)} collective-permute-done((bf16[64,1792]{1,0:T(8,128)(2,1)S(1)}, bf16[64,1792]{1,0:T(8,128)(2,1)S(1)}, u32[]{:S(2)}, u32[]{:S(2)}) %collective-permute-start.21) | collective-permute-done | bytes 229408 | tf_op jit(solution)/shard_map/ppermute | solution.py:32
  83.1 7.4 %shard_map.153 = (bf16[1792,1024]{1,0:T(8,128)(2,1)}, bf16[1792,1024]{1,0:T(8,128)(2,1)}, bf16[1024,1792]{1,0:T(8,128)(2,1)}) custom-call(bf16[320,1024]{1,0:T(8,128)(2,1)S(1)} %get-tuple-element.86.hidden, bf16[320,1024]{1,0:T(8,128)(2,1)S(1)} %get-tuple-element.87.d_gate, bf16[320,1024]{1,0:T(8,128)(2,1)S(1)} %get-tuple-element.88.d_up, ...), custom_call_target="tpu_custom_call" | custom-call | flops 1000000000 | bytes 1 | tf_op jit(solution)/shard_map/pallas_call | solution.py:433
  (46 shorter events, 20.5 us)
Async XLA Ops:
  4.2 4.6 %collective-permute-start.4 = (bf16[128,1792]{1,0:T(8,128)(2,1)S(1)}, bf16[128,1792]{1,0:T(8,128)(2,1)S(1)}, u32[]{:S(2)}, u32[]{:S(2)}) collective-permute-start(bf16[128,1792]{1,0:T(8,128)(2,1)S(1)} %get-tuple-element.58), channel_id=1, source_target_pairs={{0,1},{1,0},{2,3},{3,2},{4,5},{5,4},{6,7},{7,6},{8,9},{9,8},{10,11... | collective-permute-start | bytes 1376264 | tf_op jit(solution)/shard_map/ppermute | solution.py:22
  4.5 10.4 %collective-permute-start.1 = (bf16[80,1792]{1,0:T(8,128)(2,1)S(1)}, bf16[80,1792]{1,0:T(8,128)(2,1)S(1)}, u32[]{:S(2)}, u32[]{:S(2)}) collective-permute-start(bf16[80,1792]{1,0:T(8,128)(2,1)S(1)} %get-tuple-element.54), channel_id=1, source_target_pairs={{0,2},{2,0},{4,6},{6,4},{1,3},{3,1},{5,7},{7,5},{8,10},{10,8},{12,... | collective-permute-start | bytes 860168 | tf_op jit(solution)/shard_map/ppermute | solution.py:22
  7.3 15.8 %collective-permute-start.2 = (bf16[80,1792]{1,0:T(8,128)(2,1)S(1)}, bf16[80,1792]{1,0:T(8,128)(2,1)S(1)}, u32[]{:S(2)}, u32[]{:S(2)}) collective-permute-start(bf16[80,1792]{1,0:T(8,128)(2,1)S(1)} %get-tuple-element.55), channel_id=1, source_target_pairs={{0,4},{2,6},{4,0},{6,2},{1,5},{3,7},{5,1},{7,3},{8,12},{10,14},{12... | collective-permute-start | bytes 860168 | tf_op jit(solution)/shard_map/ppermute | solution.py:22
  8.8 14.5 %collective-permute-start.3 = (bf16[80,1792]{1,0:T(8,128)(2,1)S(1)}, bf16[80,1792]{1,0:T(8,128)(2,1)S(1)}, u32[]{:S(2)}, u32[]{:S(2)}) collective-permute-start(bf16[80,1792]{1,0:T(8,128)(2,1)S(1)} %get-tuple-element.56), channel_id=1, source_target_pairs={{0,6},{2,4},{4,2},{6,0},{1,7},{3,5},{5,3},{7,1},{8,14},{10,12},{12... | collective-permute-start | bytes 860168 | tf_op jit(solution)/shard_map/ppermute | solution.py:22
  9.4 18.4 %collective-permute-start.6 = (bf16[80,1792]{1,0:T(8,128)(2,1)S(1)}, bf16[80,1792]{1,0:T(8,128)(2,1)S(1)}, u32[]{:S(2)}, u32[]{:S(2)}) collective-permute-start(bf16[80,1792]{1,0:T(8,128)(2,1)S(1)} %get-tuple-element.65), channel_id=1, source_target_pairs={{0,2},{2,0},{4,6},{6,4},{1,3},{3,1},{5,7},{7,5},{8,10},{10,8},{12,... | collective-permute-start | bytes 860168 | tf_op jit(solution)/shard_map/ppermute | solution.py:22
  11.5 24.0 %collective-permute-start.7 = (bf16[80,1792]{1,0:T(8,128)(2,1)S(1)}, bf16[80,1792]{1,0:T(8,128)(2,1)S(1)}, u32[]{:S(2)}, u32[]{:S(2)}) collective-permute-start(bf16[80,1792]{1,0:T(8,128)(2,1)S(1)} %get-tuple-element.66), channel_id=1, source_target_pairs={{0,4},{2,6},{4,0},{6,2},{1,5},{3,7},{5,1},{7,3},{8,12},{10,14},{12... | collective-permute-start | bytes 860168 | tf_op jit(solution)/shard_map/ppermute | solution.py:22
  14.9 20.5 %collective-permute-start.8 = (bf16[80,1792]{1,0:T(8,128)(2,1)S(1)}, bf16[80,1792]{1,0:T(8,128)(2,1)S(1)}, u32[]{:S(2)}, u32[]{:S(2)}) collective-permute-start(bf16[80,1792]{1,0:T(8,128)(2,1)S(1)} %get-tuple-element.67), channel_id=1, source_target_pairs={{0,6},{2,4},{4,2},{6,0},{1,7},{3,5},{5,3},{7,1},{8,14},{10,12},{12... | collective-permute-start | bytes 860168 | tf_op jit(solution)/shard_map/ppermute | solution.py:22
  23.2 19.5 %collective-permute-start.12 = (bf16[80,1792]{1,0:T(8,128)(2,1)S(1)}, bf16[80,1792]{1,0:T(8,128)(2,1)S(1)}, u32[]{:S(2)}, u32[]{:S(2)}) collective-permute-start(bf16[80,1792]{1,0:T(8,128)(2,1)S(1)} %get-tuple-element.72), channel_id=1, source_target_pairs={{0,2},{2,0},{4,6},{6,4},{1,3},{3,1},{5,7},{7,5},{8,10},{10,8},{12,... | collective-permute-start | bytes 860168 | tf_op jit(solution)/shard_map/ppermute | solution.py:22
  23.4 23.4 %collective-permute-start.13 = (bf16[80,1792]{1,0:T(8,128)(2,1)S(1)}, bf16[80,1792]{1,0:T(8,128)(2,1)S(1)}, u32[]{:S(2)}, u32[]{:S(2)}) collective-permute-start(bf16[80,1792]{1,0:T(8,128)(2,1)S(1)} %get-tuple-element.73), channel_id=1, source_target_pairs={{0,4},{2,6},{4,0},{6,2},{1,5},{3,7},{5,1},{7,3},{8,12},{10,14},{12... | collective-permute-start | bytes 860168 | tf_op jit(solution)/shard_map/ppermute | solution.py:22
  27.8 19.5 %collective-permute-start.14 = (bf16[80,1792]{1,0:T(8,128)(2,1)S(1)}, bf16[80,1792]{1,0:T(8,128)(2,1)S(1)}, u32[]{:S(2)}, u32[]{:S(2)}) collective-permute-start(bf16[80,1792]{1,0:T(8,128)(2,1)S(1)} %get-tuple-element.74), channel_id=1, source_target_pairs={{0,6},{2,4},{4,2},{6,0},{1,7},{3,5},{5,3},{7,1},{8,14},{10,12},{12... | collective-permute-start | bytes 860168 | tf_op jit(solution)/shard_map/ppermute | solution.py:22
  40.1 11.4 %collective-permute-start.9 = (bf16[80,1792]{1,0:T(8,128)(2,1)S(1)}, bf16[80,1792]{1,0:T(8,128)(2,1)S(1)}, u32[]{:S(2)}, u32[]{:S(2)}) collective-permute-start(bf16[80,1792]{1,0:T(8,128)(2,1)S(1)} %get-tuple-element.69), channel_id=1, source_target_pairs={{0,2},{2,0},{4,6},{6,4},{1,3},{3,1},{5,7},{7,5},{8,10},{10,8},{12,... | collective-permute-start | bytes 860168 | tf_op jit(solution)/shard_map/ppermute | solution.py:22
  40.8 12.1 %collective-permute-start.10 = (bf16[80,1792]{1,0:T(8,128)(2,1)S(1)}, bf16[80,1792]{1,0:T(8,128)(2,1)S(1)}, u32[]{:S(2)}, u32[]{:S(2)}) collective-permute-start(bf16[80,1792]{1,0:T(8,128)(2,1)S(1)} %get-tuple-element.70), channel_id=1, source_target_pairs={{0,4},{2,6},{4,0},{6,2},{1,5},{3,7},{5,1},{7,3},{8,12},{10,14},{12... | collective-permute-start | bytes 860168 | tf_op jit(solution)/shard_map/ppermute | solution.py:22
  48.7 4.2 %collective-permute-start.15 = (bf16[3,320,1024]{2,1,0:T(8,128)(2,1)S(1)}, bf16[3,320,1024]{2,1,0:T(8,128)(2,1)S(1)}, u32[]{:S(2)}, u32[]{:S(2)}) collective-permute-start(bf16[3,320,1024]{2,1,0:T(8,128)(2,1)S(1)} %get-tuple-element.75.refs_2_.own_ref), channel_id=1, source_target_pairs={{0,1},{1,0},{2,3},{3,2},{4,5},{5,4},{6,7},{7,6},{8,9},{9,8},{10,11... | collective-permute-start | bytes 5898248 | tf_op jit(solution)/shard_map/ppermute | solution.py:22
  48.8 15.6 %collective-permute-start.11 = (bf16[80,1792]{1,0:T(8,128)(2,1)S(1)}, bf16[80,1792]{1,0:T(8,128)(2,1)S(1)}, u32[]{:S(2)}, u32[]{:S(2)}) collective-permute-start(bf16[80,1792]{1,0:T(8,128)(2,1)S(1)} %get-tuple-element.71), channel_id=1, source_target_pairs={{0,6},{2,4},{4,2},{6,0},{1,7},{3,5},{5,3},{7,1},{8,14},{10,12},{12... | collective-permute-start | bytes 860168 | tf_op jit(solution)/shard_map/ppermute | solution.py:22
  56.1 10.9 %collective-permute-start.18 = (bf16[40,1792]{1,0:T(8,128)(2,1)S(1)}, bf16[40,1792]{1,0:T(8,128)(2,1)S(1)}, u32[]{:S(2)}, u32[]{:S(2)}) collective-permute-start(bf16[40,1792]{1,0:T(8,128)(2,1)S(1)} %get-tuple-element.79), channel_id=1, source_target_pairs={{0,2},{2,0},{4,6},{6,4},{1,3},{3,1},{5,7},{7,5},{8,10},{10,8},{12,... | collective-permute-start | bytes 430088 | tf_op jit(solution)/shard_map/ppermute | solution.py:22
  57.5 11.1 %collective-permute-start.19 = (bf16[40,1792]{1,0:T(8,128)(2,1)S(1)}, bf16[40,1792]{1,0:T(8,128)(2,1)S(1)}, u32[]{:S(2)}, u32[]{:S(2)}) collective-permute-start(bf16[40,1792]{1,0:T(8,128)(2,1)S(1)} %get-tuple-element.80), channel_id=1, source_target_pairs={{0,4},{2,6},{4,0},{6,2},{1,5},{3,7},{5,1},{7,3},{8,12},{10,14},{12... | collective-permute-start | bytes 430088 | tf_op jit(solution)/shard_map/ppermute | solution.py:22
  64.4 6.6 %collective-permute-start.20 = (bf16[40,1792]{1,0:T(8,128)(2,1)S(1)}, bf16[40,1792]{1,0:T(8,128)(2,1)S(1)}, u32[]{:S(2)}, u32[]{:S(2)}) collective-permute-start(bf16[40,1792]{1,0:T(8,128)(2,1)S(1)} %get-tuple-element.81), channel_id=1, source_target_pairs={{0,6},{2,4},{4,2},{6,0},{1,7},{3,5},{5,3},{7,1},{8,14},{10,12},{12... | collective-permute-start | bytes 430088 | tf_op jit(solution)/shard_map/ppermute | solution.py:22
  65.4 13.0 %collective-permute-start.16 = (bf16[64,1792]{1,0:T(8,128)(2,1)S(1)}, bf16[64,1792]{1,0:T(8,128)(2,1)S(1)}, u32[]{:S(2)}, u32[]{:S(2)}) collective-permute-start(bf16[64,1792]{1,0:T(8,128)(2,1)S(1)} %get-tuple-element.77), channel_id=1, source_target_pairs={{0,8},{1,9},{8,16},{9,17},{16,24},{17,25},{24,0},{25,1},{2,10},{3,... | collective-permute-start | bytes 688136 | tf_op jit(solution)/shard_map/ppermute | solution.py:32
  67.1 11.4 %collective-permute-start.17 = (bf16[64,1792]{1,0:T(8,128)(2,1)S(1)}, bf16[64,1792]{1,0:T(8,128)(2,1)S(1)}, u32[]{:S(2)}, u32[]{:S(2)}) collective-permute-start(bf16[64,1792]{1,0:T(8,128)(2,1)S(1)} %get-tuple-element.78.refs_4_), channel_id=1, source_target_pairs={{0,9},{1,8},{8,17},{9,16},{16,25},{17,24},{24,1},{25,0},{2,11},{3,... | collective-permute-start | bytes 688136 | tf_op jit(solution)/shard_map/ppermute | solution.py:32
  67.1 6.0 %collective-permute-start.22 = (bf16[40,1792]{1,0:T(8,128)(2,1)S(1)}, bf16[40,1792]{1,0:T(8,128)(2,1)S(1)}, u32[]{:S(2)}, u32[]{:S(2)}) collective-permute-start(bf16[40,1792]{1,0:T(8,128)(2,1)S(1)} %get-tuple-element.83), channel_id=1, source_target_pairs={{0,2},{2,0},{4,6},{6,4},{1,3},{3,1},{5,7},{7,5},{8,10},{10,8},{12,... | collective-permute-start | bytes 430088 | tf_op jit(solution)/shard_map/ppermute | solution.py:22
  68.6 9.9 %collective-permute-start.23 = (bf16[40,1792]{1,0:T(8,128)(2,1)S(1)}, bf16[40,1792]{1,0:T(8,128)(2,1)S(1)}, u32[]{:S(2)}, u32[]{:S(2)}) collective-permute-start(bf16[40,1792]{1,0:T(8,128)(2,1)S(1)} %get-tuple-element.84), channel_id=1, source_target_pairs={{0,4},{2,6},{4,0},{6,2},{1,5},{3,7},{5,1},{7,3},{8,12},{10,14},{12... | collective-permute-start | bytes 430088 | tf_op jit(solution)/shard_map/ppermute | solution.py:22
  71.0 7.4 %collective-permute-start.24 = (bf16[40,1792]{1,0:T(8,128)(2,1)S(1)}, bf16[40,1792]{1,0:T(8,128)(2,1)S(1)}, u32[]{:S(2)}, u32[]{:S(2)}) collective-permute-start(bf16[40,1792]{1,0:T(8,128)(2,1)S(1)} %get-tuple-element.85), channel_id=1, source_target_pairs={{0,6},{2,4},{4,2},{6,0},{1,7},{3,5},{5,3},{7,1},{8,14},{10,12},{12... | collective-permute-start | bytes 430088 | tf_op jit(solution)/shard_map/ppermute | solution.py:22
  73.0 10.1 %collective-permute-start.21 = (bf16[64,1792]{1,0:T(8,128)(2,1)S(1)}, bf16[64,1792]{1,0:T(8,128)(2,1)S(1)}, u32[]{:S(2)}, u32[]{:S(2)}) collective-permute-start(bf16[64,1792]{1,0:T(8,128)(2,1)S(1)} %shard_map.151.refs_4_), channel_id=1, source_target_pairs={{0,8},{1,9},{8,16},{9,17},{16,24},{17,25},{24,0},{25,1},{2,10},{3,... | collective-permute-start | bytes 688136 | tf_op jit(solution)/shard_map/ppermute | solution.py:32
  78.9 11.6 %collective-permute-start.25 = (bf16[64,1792]{1,0:T(8,128)(2,1)S(1)}, bf16[64,1792]{1,0:T(8,128)(2,1)S(1)}, u32[]{:S(2)}, u32[]{:S(2)}) collective-permute-start(bf16[64,1792]{1,0:T(8,128)(2,1)S(1)} %shard_map.152.refs_0_), channel_id=1, source_target_pairs={{0,9},{1,8},{8,17},{9,16},{16,25},{17,24},{24,1},{25,0},{2,11},{3,... | collective-permute-start | bytes 688136 | tf_op jit(solution)/shard_map/ppermute | solution.py:32
  (2 other events, 4.9 us)

commit v11 on v7

--- a/solution.py
+++ b/solution.py
@@ -418,26 +418,42 @@
     )(*inputs, *after)
 
 
-def grad_kernel(hidden, d_gate, d_up, turned, cots, *refs):
-    grad_gate, grad_up, grad_down = refs[-3:]
+def grad_in_kernel(d_gate, d_up, turned, *refs):
+    grad_gate, grad_up = refs[-2:]
     part = pl.ds(pl.multiple_of(pl.program_id(0) * TILE, TILE), TILE)
     grad_gate[...] = dot(turned[...], d_gate[:, part], 1, 0).astype(BF16)
     grad_up[...] = dot(turned[...], d_up[:, part], 1, 0).astype(BF16)
-    grad_down[...] = dot(hidden[:, part], cots[...], 0, 0).astype(BF16)
-
-
-def grads(hidden, d_gate, d_up, turned, cots, after=(), weight=1):
+
+
+def grad_in(d_gate, d_up, turned, after=(), weight=1):
     width, units = turned.shape[0], d_gate.shape[1]
-    by_column = pl.BlockSpec((width, TILE), lambda i: (0, i))
-    return call(
-        grad_kernel,
-        [pltpu.HBM((width, units), BF16)] * 2 + [pltpu.HBM((units, width), BF16)],
-        [VMEM] * 5 + [AFTER] * len(after),
-        [by_column, by_column, pl.BlockSpec((TILE, width), lambda i: (i, 0))],
+    return call(
+        grad_in_kernel,
+        [pltpu.HBM((width, units), BF16)] * 2,
+        [VMEM] * 3 + [AFTER] * len(after),
+        [pl.BlockSpec((width, TILE), lambda i: (0, i))] * 2,
         [],
         grid=(units // TILE,),
         weight=weight,
-    )(hidden, d_gate, d_up, turned, cots, *after)
+    )(d_gate, d_up, turned, *after)
+
+
+def grad_down_kernel(hidden, cots, *refs):
+    part = pl.ds(pl.multiple_of(pl.program_id(0) * TILE, TILE), TILE)
+    refs[-1][...] = dot(hidden[:, part], cots[...], 0, 0).astype(BF16)
+
+
+def grad_down(hidden, cots, after=(), weight=1):
+    units, width = hidden.shape[1], cots.shape[1]
+    return call(
+        grad_down_kernel,
+        pltpu.HBM((units, width), BF16),
+        [VMEM] * 2 + [AFTER] * len(after),
+        pl.BlockSpec((TILE, width), lambda i: (i, 0)),
+        [],
+        grid=(units // TILE,),
+        weight=weight,
+    )(hidden, cots, *after)
 
 
 def to_experts(blocks, relative):
@@ -544,6 +560,7 @@
         weight=150,
     )
     dx_mine = section_shift(own_sum, 0)
+    grad_d = grad_down(hidden, cots, after=(own_sum,))
     other_sum = combine(
         metas,
         other_back_b,
@@ -551,12 +568,12 @@
         row_b,
         False,
         True,
-        after=(own_sum, in_vmem(y_rest)),
+        after=(in_hbm(grad_d), in_vmem(y_rest)),
         weight=100,
     )
     dx_rest = section_shift(other_sum, 1)
-    grad_g, grad_u, grad_d = grads(
-        hidden, d_gate, d_up, turned, cots, after=(other_sum, in_vmem(dx_mine)), weight=100
+    grad_g, grad_u = grad_in(
+        d_gate, d_up, turned, after=(other_sum, in_vmem(dx_mine)), weight=100
     )
     y_next, dx_next = finish(y_mine, y_rest, dx_mine, dx_rest, after=(in_hbm(grad_g),))
     return (

time: 87.7 us -> 87.6 us (level)
  Pallas kernels: 30.7 us -> 33 us
  waiting for transfers between devices: 22 us -> 19.7 us
    ppermute x25, waiting for transfers between devices: 21 us -> 17.1 us  [exchange(): lax.ppermute(value, axis, [(source, source ^ mask) for source in range(co...]
    pallas_call x1 -> x2, Pallas kernels: 7.37 us -> 9.72 us  [the longest x1 5.82 us: grad_in(): call(grad_in_kernel, [pltpu.HBM((width, units), BF16)] * 2, [VMEM] * 3 +...]
    ppermute x4, waiting for transfers between devices: 1.04 us -> 2.67 us  [section_shift(): return lax.ppermute(value, ('section', 'dp'), pairs)]
  transfers between devices with their start and end apart: 29 -> 29, of which waited for: 13 -> 13; matrix products, arithmetic and copies ran while one was open for 0% -> 0% of each run, Pallas kernels for 32% -> 35%
where the time goes in v11:
time: 87.6 us; the launch traced here: 87.5 us
  starting transfers between devices  33.7 us (38%)
  Pallas kernels  33 us (38%)
  waiting for transfers between devices  19.7 us (22%)
  between operations  0.98 us (1%)
    ppermute x25, starting transfers between devices, exchange(): lax.ppermute(value, axis, [(source, source ^ mask) for source in range(co...  29 us
    ppermute x25, waiting for transfers between devices, exchange(): lax.ppermute(value, axis, [(source, source ^ mask) for source in range(co...  17.1 us
    pallas_call x1, Pallas kernels, grad_in(): call(grad_in_kernel, [pltpu.HBM((width, units), BF16)] * 2, [VMEM] * 3 +...  5.82 us
    pallas_call x2, Pallas kernels, gate_up(): call(functools.partial(gate_up_kernel, blocks=blocks), array(planes, tota...  5.22 us
    ppermute x4, starting transfers between devices, section_shift(): return lax.ppermute(value, ('section', 'dp'), pairs)  4.72 us
    pallas_call x1, Pallas kernels, load(): call(functools.partial(load_kernel, count=len(weights)), [array(*weight.s...  4.23 us
    pallas_call x1, Pallas kernels, grad_down(): call(grad_down_kernel, pltpu.HBM((units, width), BF16), [VMEM] * 2 + [AFT...  3.9 us
    pallas_call x1, Pallas kernels, back(): call(functools.partial(back_kernel, blocks=plan.blocks), [array(total, un...  3.2 us
  transfers between devices with their start and end apart: 29, of which 13 were waited for; matrix products, arithmetic and copies ran while one was open for 0% of the time, Pallas kernels for 35%

profile of v11, /device:TPU:0, one launch (start us, length us, event | category | flops | bytes accessed | tf_op | source)
XLA Modules:
  0.0 87.5 jit_solution(3809681960347051421)
XLA Ops:
  4.5 2.8 %collective-permute-start.1 = (bf16[80,1792]{1,0:T(8,128)(2,1)S(1)}, bf16[80,1792]{1,0:T(8,128)(2,1)S(1)}, u32[]{:S(2)}, u32[]{:S(2)}) collective-permute-start(bf16[80,1792]{1,0:T(8,128)(2,1)S(1)} %get-tuple-element.55), channel_id=1, source_target_pairs={{0,2},{2,0},{4,6},{6,4},{1,3},{3,1},{5,7},{7,5},{8,10},{10,8},{12,... | collective-permute-start | bytes 860168 | tf_op jit(solution)/shard_map/ppermute | solution.py:22
  9.4 2.0 %collective-permute-start.6 = (bf16[80,1792]{1,0:T(8,128)(2,1)S(1)}, bf16[80,1792]{1,0:T(8,128)(2,1)S(1)}, u32[]{:S(2)}, u32[]{:S(2)}) collective-permute-start(bf16[80,1792]{1,0:T(8,128)(2,1)S(1)} %get-tuple-element.66), channel_id=1, source_target_pairs={{0,2},{2,0},{4,6},{6,4},{1,3},{3,1},{5,7},{7,5},{8,10},{10,8},{12,... | collective-permute-start | bytes 860168 | tf_op jit(solution)/shard_map/ppermute | solution.py:22
  13.0 1.9 %collective-permute-done.1.refs_1_ = bf16[80,1792]{1,0:T(8,128)(2,1)S(1)} collective-permute-done((bf16[80,1792]{1,0:T(8,128)(2,1)S(1)}, bf16[80,1792]{1,0:T(8,128)(2,1)S(1)}, u32[]{:S(2)}, u32[]{:S(2)}) %collective-permute-start.1) | collective-permute-done | bytes 286752 | tf_op jit(solution)/shard_map/ppermute | solution.py:22
  14.9 3.0 %collective-permute-start.8 = (bf16[80,1792]{1,0:T(8,128)(2,1)S(1)}, bf16[80,1792]{1,0:T(8,128)(2,1)S(1)}, u32[]{:S(2)}, u32[]{:S(2)}) collective-permute-start(bf16[80,1792]{1,0:T(8,128)(2,1)S(1)} %get-tuple-element.68), channel_id=1, source_target_pairs={{0,6},{2,4},{4,2},{6,0},{1,7},{3,5},{5,3},{7,1},{8,14},{10,12},{12... | collective-permute-start | bytes 860168 | tf_op jit(solution)/shard_map/ppermute | solution.py:22
  17.9 4.2 %shard_map.141 = (bf16[1792,1024]{1,0:T(8,128)(2,1)S(1)}, bf16[1792,1024]{1,0:T(8,128)(2,1)S(1)}, bf16[1024,1792]{1,0:T(8,128)(2,1)S(1)}) custom-call(bf16[1792,1024]{1,0:T(8,128)(2,1)} %bitcast.24, bf16[1792,1024]{1,0:T(8,128)(2,1)} %bitcast.25, bf16[1024,1792]{1,0:T(8,128)(2,1)} %bitcast.26, bf16[80,1792]{1,0:T(8,128)(2,1)S(1)} %get-tuple-element.60.refs_3_.refs_0_), custom_call_target="tpu_custom_call" | custom-call | flops 10000000 | bytes 1 | tf_op jit(solution)/shard_map/pallas_call | solution.py:164
  23.4 1.8 %collective-permute-start.13 = (bf16[80,1792]{1,0:T(8,128)(2,1)S(1)}, bf16[80,1792]{1,0:T(8,128)(2,1)S(1)}, u32[]{:S(2)}, u32[]{:S(2)}) collective-permute-start(bf16[80,1792]{1,0:T(8,128)(2,1)S(1)} %get-tuple-element.74), channel_id=1, source_target_pairs={{0,4},{2,6},{4,0},{6,2},{1,5},{3,7},{5,1},{7,3},{8,12},{10,14},{12... | collective-permute-start | bytes 860168 | tf_op jit(solution)/shard_map/ppermute | solution.py:22
  25.2 2.6 %shard_map.143.refs_6_.own_ref = bf16[2,320,1024]{2,1,0:T(8,128)(2,1)S(1)} custom-call(bf16[80,1792]{1,0:T(8,128)(2,1)S(1)} %get-tuple-element.54.refs_0_, bf16[80,1792]{1,0:T(8,128)(2,1)S(1)} %collective-permute-done.1.refs_1_, bf16[80,1792]{1,0:T(8,128)(2,1)S(1)} %collective-permute-done.2.refs_2_, bf16[80,1792]{1,0:T(8,128)(2,1)S(1)} %collective-permute-done.3.refs_3_, ...), custom_call_target="tpu_custom_call" | custom-call | flops 10000000 | bytes 1 | tf_op jit(solution)/shard_map/pallas_call | solution.py:298
  27.8 2.4 %collective-permute-start.14 = (bf16[80,1792]{1,0:T(8,128)(2,1)S(1)}, bf16[80,1792]{1,0:T(8,128)(2,1)S(1)}, u32[]{:S(2)}, u32[]{:S(2)}) collective-permute-start(bf16[80,1792]{1,0:T(8,128)(2,1)S(1)} %get-tuple-element.75), channel_id=1, source_target_pairs={{0,6},{2,4},{4,2},{6,0},{1,7},{3,5},{5,3},{7,1},{8,14},{10,12},{12... | collective-permute-start | bytes 860168 | tf_op jit(solution)/shard_map/ppermute | solution.py:22
  30.3 5.2 %collective-permute-done.7.refs_2_ = bf16[80,1792]{1,0:T(8,128)(2,1)S(1)} collective-permute-done((bf16[80,1792]{1,0:T(8,128)(2,1)S(1)}, bf16[80,1792]{1,0:T(8,128)(2,1)S(1)}, u32[]{:S(2)}, u32[]{:S(2)}) %collective-permute-start.7) | collective-permute-done | bytes 286752 | tf_op jit(solution)/shard_map/ppermute | solution.py:22
  35.4 2.6 %shard_map.144.refs_0_.refs_5_ = bf16[3,320,1024]{2,1,0:T(8,128)(2,1)S(1)} custom-call(bf16[80,1792]{1,0:T(8,128)(2,1)S(1)} %get-tuple-element.60.refs_3_.refs_0_, bf16[80,1792]{1,0:T(8,128)(2,1)S(1)} %collective-permute-done.6.refs_1_, bf16[80,1792]{1,0:T(8,128)(2,1)S(1)} %collective-permute-done.7.refs_2_, ...), custom_call_target="tpu_custom_call" | custom-call | flops 30000001024 | bytes 1 | tf_op jit(solution)/shard_map/pallas_call | solution.py:298
  38.5 1.7 %shard_map.145 = (bf16[40,1792]{1,0:T(8,128)(2,1)S(1)}, bf16[40,1792]{1,0:T(8,128)(2,1)S(1)}, bf16[40,1792]{1,0:T(8,128)(2,1)S(1)}, bf16[40,1792]{1,0:T(8,128)(2...) custom-call(bf16[2,320,1024]{2,1,0:T(8,128)(2,1)S(1)} %shard_map.143, ...), custom_call_target="tpu_custom_call" | custom-call | flops 10000000 | bytes 1 | tf_op jit(solution)/shard_map/pallas_call | solution.py:361
  44.2 2.6 %collective-permute-done.13.refs_2_ = bf16[80,1792]{1,0:T(8,128)(2,1)S(1)} collective-permute-done((bf16[80,1792]{1,0:T(8,128)(2,1)S(1)}, bf16[80,1792]{1,0:T(8,128)(2,1)S(1)}, u32[]{:S(2)}, u32[]{:S(2)}) %collective-permute-start.13) | collective-permute-done | bytes 286752 | tf_op jit(solution)/shard_map/ppermute | solution.py:22
  48.8 1.6 %collective-permute-start.16 = (bf16[40,1792]{1,0:T(8,128)(2,1)S(1)}, bf16[40,1792]{1,0:T(8,128)(2,1)S(1)}, u32[]{:S(2)}, u32[]{:S(2)}) collective-permute-start(bf16[40,1792]{1,0:T(8,128)(2,1)S(1)} %get-tuple-element.78), channel_id=1, source_target_pairs={{0,2},{2,0},{4,6},{6,4},{1,3},{3,1},{5,7},{7,5},{8,10},{10,8},{12,... | collective-permute-start | bytes 430088 | tf_op jit(solution)/shard_map/ppermute | solution.py:22
  50.9 1.9 %collective-permute-done.10.refs_2_ = bf16[40,1792]{1,0:T(8,128)(2,1)S(1)} collective-permute-done((bf16[40,1792]{1,0:T(8,128)(2,1)S(1)}, bf16[40,1792]{1,0:T(8,128)(2,1)S(1)}, u32[]{:S(2)}, u32[]{:S(2)}) %collective-permute-start.10) | collective-permute-done | bytes 143392 | tf_op jit(solution)/shard_map/ppermute | solution.py:22
  54.9 1.8 %collective-permute-start.15 = (bf16[64,1792]{1,0:T(8,128)(2,1)S(1)}, bf16[64,1792]{1,0:T(8,128)(2,1)S(1)}, u32[]{:S(2)}, u32[]{:S(2)}) collective-permute-start(bf16[64,1792]{1,0:T(8,128)(2,1)S(1)} %shard_map.148.refs_0_), channel_id=1, source_target_pairs={{0,8},{1,9},{8,16},{9,17},{16,24},{17,25},{24,0},{25,1},{2,10},{3,... | collective-permute-start | bytes 688136 | tf_op jit(solution)/shard_map/ppermute | solution.py:32
  56.7 3.2 %shard_map.149 = (bf16[320,1024]{1,0:T(8,128)(2,1)S(1)}, bf16[320,1024]{1,0:T(8,128)(2,1)S(1)}, bf16[320,1024]{1,0:T(8,128)(2,1)S(1)}, bf16[40,1792]{1,0:T(8,128...) custom-call(bf16[3,320,1024]{2,1,0:T(8,128)(2,1)S(1)} %get-tuple-ele, ...), custom_call_target="tpu_custom_call" | custom-call | flops 10000000 | bytes 1 | tf_op jit(solution)/shard_map/pallas_call | solution.py:394
  60.0 2.0 %collective-permute-start.21 = (bf16[40,1792]{1,0:T(8,128)(2,1)S(1)}, bf16[40,1792]{1,0:T(8,128)(2,1)S(1)}, u32[]{:S(2)}, u32[]{:S(2)}) collective-permute-start(bf16[40,1792]{1,0:T(8,128)(2,1)S(1)} %get-tuple-element.82), channel_id=1, source_target_pairs={{0,2},{2,0},{4,6},{6,4},{1,3},{3,1},{5,7},{7,5},{8,10},{10,8},{12,... | collective-permute-start | bytes 430088 | tf_op jit(solution)/shard_map/ppermute | solution.py:22
  62.0 1.5 %collective-permute-start.23 = (bf16[40,1792]{1,0:T(8,128)(2,1)S(1)}, bf16[40,1792]{1,0:T(8,128)(2,1)S(1)}, u32[]{:S(2)}, u32[]{:S(2)}) collective-permute-start(bf16[40,1792]{1,0:T(8,128)(2,1)S(1)} %get-tuple-element.84), channel_id=1, source_target_pairs={{0,6},{2,4},{4,2},{6,0},{1,7},{3,5},{5,3},{7,1},{8,14},{10,12},{12... | collective-permute-start | bytes 430088 | tf_op jit(solution)/shard_map/ppermute | solution.py:22
  64.3 1.9 %collective-permute-start.25 = (bf16[40,1792]{1,0:T(8,128)(2,1)S(1)}, bf16[40,1792]{1,0:T(8,128)(2,1)S(1)}, u32[]{:S(2)}, u32[]{:S(2)}) collective-permute-start(bf16[40,1792]{1,0:T(8,128)(2,1)S(1)} %get-tuple-element.86), channel_id=1, source_target_pairs={{0,2},{2,0},{4,6},{6,4},{1,3},{3,1},{5,7},{7,5},{8,10},{10,8},{12,... | collective-permute-start | bytes 430088 | tf_op jit(solution)/shard_map/ppermute | solution.py:22
  66.7 2.9 %collective-permute-done.22.refs_2_ = bf16[40,1792]{1,0:T(8,128)(2,1)S(1)} collective-permute-done((bf16[40,1792]{1,0:T(8,128)(2,1)S(1)}, bf16[40,1792]{1,0:T(8,128)(2,1)S(1)}, u32[]{:S(2)}, u32[]{:S(2)}) %collective-permute-start.22) | collective-permute-done | bytes 143392 | tf_op jit(solution)/shard_map/ppermute | solution.py:22
  70.1 1.6 %collective-permute-start.24 = (bf16[64,1792]{1,0:T(8,128)(2,1)S(1)}, bf16[64,1792]{1,0:T(8,128)(2,1)S(1)}, u32[]{:S(2)}, u32[]{:S(2)}) collective-permute-start(bf16[64,1792]{1,0:T(8,128)(2,1)S(1)} %shard_map.151.refs_0_), channel_id=1, source_target_pairs={{0,8},{1,9},{8,16},{9,17},{16,24},{17,25},{24,0},{25,1},{2,10},{3,... | collective-permute-start | bytes 688136 | tf_op jit(solution)/shard_map/ppermute | solution.py:32
  71.8 3.9 %shard_map.152.refs_4_ = bf16[1024,1792]{1,0:T(8,128)(2,1)} custom-call(bf16[320,1024]{1,0:T(8,128)(2,1)S(1)} %get-tuple-element.89.hidden, bf16[320,1792]{1,0:T(8,128)(2,1)S(1)} %get-tuple-element.90.cots, bf16[64,1792]{1,0:T(8,128)(2,1)S(1)} %shard_map.151.refs_0_), custom_call_target="tpu_custom_call" | custom-call | flops 10000000 | bytes 1 | tf_op jit(solution)/shard_map/pallas_call | solution.py:448
  78.6 5.8 %shard_map.154 = (bf16[1792,1024]{1,0:T(8,128)(2,1)}, bf16[1792,1024]{1,0:T(8,128)(2,1)}) custom-call(bf16[320,1024]{1,0:T(8,128)(2,1)S(1)} %get-tuple-element.91.d_gate, bf16[320,1024]{1,0:T(8,128)(2,1)S(1)} %get-tuple-element.92.d_up, bf16[1792,320]{1,0:T(8,128)(2,1)S(1)} %shard_map.146.refs_6_.turned, bf16[64,1792]{1,0:T(8,128)(2,1)S(1)} %shard_map.153.refs_0_, ...), custom_call_target="tpu_custom_call" | custom-call | flops 1000000000 | bytes 1 | tf_op jit(solution)/shard_map/pallas_call | solution.py:430
  84.4 1.9 %collective-permute-done.28.refs_3_ = bf16[64,1792]{1,0:T(8,128)(2,1)S(1)} collective-permute-done((bf16[64,1792]{1,0:T(8,128)(2,1)S(1)}, bf16[64,1792]{1,0:T(8,128)(2,1)S(1)}, u32[]{:S(2)}, u32[]{:S(2)}) %collective-permute-start.28) | collective-permute-done | bytes 229408 | tf_op jit(solution)/shard_map/ppermute | solution.py:32
  (53 shorter events, 23.4 us)
Async XLA Ops:
  4.5 10.4 %collective-permute-start.1 = (bf16[80,1792]{1,0:T(8,128)(2,1)S(1)}, bf16[80,1792]{1,0:T(8,128)(2,1)S(1)}, u32[]{:S(2)}, u32[]{:S(2)}) collective-permute-start(bf16[80,1792]{1,0:T(8,128)(2,1)S(1)} %get-tuple-element.55), channel_id=1, source_target_pairs={{0,2},{2,0},{4,6},{6,4},{1,3},{3,1},{5,7},{7,5},{8,10},{10,8},{12,... | collective-permute-start | bytes 860168 | tf_op jit(solution)/shard_map/ppermute | solution.py:22
  7.3 15.8 %collective-permute-start.2 = (bf16[80,1792]{1,0:T(8,128)(2,1)S(1)}, bf16[80,1792]{1,0:T(8,128)(2,1)S(1)}, u32[]{:S(2)}, u32[]{:S(2)}) collective-permute-start(bf16[80,1792]{1,0:T(8,128)(2,1)S(1)} %get-tuple-element.56), channel_id=1, source_target_pairs={{0,4},{2,6},{4,0},{6,2},{1,5},{3,7},{5,1},{7,3},{8,12},{10,14},{12... | collective-permute-start | bytes 860168 | tf_op jit(solution)/shard_map/ppermute | solution.py:22
  8.8 14.5 %collective-permute-start.3 = (bf16[80,1792]{1,0:T(8,128)(2,1)S(1)}, bf16[80,1792]{1,0:T(8,128)(2,1)S(1)}, u32[]{:S(2)}, u32[]{:S(2)}) collective-permute-start(bf16[80,1792]{1,0:T(8,128)(2,1)S(1)} %get-tuple-element.57), channel_id=1, source_target_pairs={{0,6},{2,4},{4,2},{6,0},{1,7},{3,5},{5,3},{7,1},{8,14},{10,12},{12... | collective-permute-start | bytes 860168 | tf_op jit(solution)/shard_map/ppermute | solution.py:22
  9.4 18.4 %collective-permute-start.6 = (bf16[80,1792]{1,0:T(8,128)(2,1)S(1)}, bf16[80,1792]{1,0:T(8,128)(2,1)S(1)}, u32[]{:S(2)}, u32[]{:S(2)}) collective-permute-start(bf16[80,1792]{1,0:T(8,128)(2,1)S(1)} %get-tuple-element.66), channel_id=1, source_target_pairs={{0,2},{2,0},{4,6},{6,4},{1,3},{3,1},{5,7},{7,5},{8,10},{10,8},{12,... | collective-permute-start | bytes 860168 | tf_op jit(solution)/shard_map/ppermute | solution.py:22
  11.5 24.0 %collective-permute-start.7 = (bf16[80,1792]{1,0:T(8,128)(2,1)S(1)}, bf16[80,1792]{1,0:T(8,128)(2,1)S(1)}, u32[]{:S(2)}, u32[]{:S(2)}) collective-permute-start(bf16[80,1792]{1,0:T(8,128)(2,1)S(1)} %get-tuple-element.67), channel_id=1, source_target_pairs={{0,4},{2,6},{4,0},{6,2},{1,5},{3,7},{5,1},{7,3},{8,12},{10,14},{12... | collective-permute-start | bytes 860168 | tf_op jit(solution)/shard_map/ppermute | solution.py:22
  14.9 20.5 %collective-permute-start.8 = (bf16[80,1792]{1,0:T(8,128)(2,1)S(1)}, bf16[80,1792]{1,0:T(8,128)(2,1)S(1)}, u32[]{:S(2)}, u32[]{:S(2)}) collective-permute-start(bf16[80,1792]{1,0:T(8,128)(2,1)S(1)} %get-tuple-element.68), channel_id=1, source_target_pairs={{0,6},{2,4},{4,2},{6,0},{1,7},{3,5},{5,3},{7,1},{8,14},{10,12},{12... | collective-permute-start | bytes 860168 | tf_op jit(solution)/shard_map/ppermute | solution.py:22
  23.2 19.5 %collective-permute-start.12 = (bf16[80,1792]{1,0:T(8,128)(2,1)S(1)}, bf16[80,1792]{1,0:T(8,128)(2,1)S(1)}, u32[]{:S(2)}, u32[]{:S(2)}) collective-permute-start(bf16[80,1792]{1,0:T(8,128)(2,1)S(1)} %get-tuple-element.73), channel_id=1, source_target_pairs={{0,2},{2,0},{4,6},{6,4},{1,3},{3,1},{5,7},{7,5},{8,10},{10,8},{12,... | collective-permute-start | bytes 860168 | tf_op jit(solution)/shard_map/ppermute | solution.py:22
  23.4 23.4 %collective-permute-start.13 = (bf16[80,1792]{1,0:T(8,128)(2,1)S(1)}, bf16[80,1792]{1,0:T(8,128)(2,1)S(1)}, u32[]{:S(2)}, u32[]{:S(2)}) collective-permute-start(bf16[80,1792]{1,0:T(8,128)(2,1)S(1)} %get-tuple-element.74), channel_id=1, source_target_pairs={{0,4},{2,6},{4,0},{6,2},{1,5},{3,7},{5,1},{7,3},{8,12},{10,14},{12... | collective-permute-start | bytes 860168 | tf_op jit(solution)/shard_map/ppermute | solution.py:22
  27.8 19.5 %collective-permute-start.14 = (bf16[80,1792]{1,0:T(8,128)(2,1)S(1)}, bf16[80,1792]{1,0:T(8,128)(2,1)S(1)}, u32[]{:S(2)}, u32[]{:S(2)}) collective-permute-start(bf16[80,1792]{1,0:T(8,128)(2,1)S(1)} %get-tuple-element.75), channel_id=1, source_target_pairs={{0,6},{2,4},{4,2},{6,0},{1,7},{3,5},{5,3},{7,1},{8,14},{10,12},{12... | collective-permute-start | bytes 860168 | tf_op jit(solution)/shard_map/ppermute | solution.py:22
  40.1 10.2 %collective-permute-start.9 = (bf16[40,1792]{1,0:T(8,128)(2,1)S(1)}, bf16[40,1792]{1,0:T(8,128)(2,1)S(1)}, u32[]{:S(2)}, u32[]{:S(2)}) collective-permute-start(bf16[40,1792]{1,0:T(8,128)(2,1)S(1)} %get-tuple-element.70), channel_id=1, source_target_pairs={{0,2},{2,0},{4,6},{6,4},{1,3},{3,1},{5,7},{7,5},{8,10},{10,8},{12,... | collective-permute-start | bytes 430088 | tf_op jit(solution)/shard_map/ppermute | solution.py:22
  40.8 12.1 %collective-permute-start.10 = (bf16[40,1792]{1,0:T(8,128)(2,1)S(1)}, bf16[40,1792]{1,0:T(8,128)(2,1)S(1)}, u32[]{:S(2)}, u32[]{:S(2)}) collective-permute-start(bf16[40,1792]{1,0:T(8,128)(2,1)S(1)} %get-tuple-element.71), channel_id=1, source_target_pairs={{0,4},{2,6},{4,0},{6,2},{1,5},{3,7},{5,1},{7,3},{8,12},{10,14},{12... | collective-permute-start | bytes 430088 | tf_op jit(solution)/shard_map/ppermute | solution.py:22
  42.7 11.7 %collective-permute-start.11 = (bf16[40,1792]{1,0:T(8,128)(2,1)S(1)}, bf16[40,1792]{1,0:T(8,128)(2,1)S(1)}, u32[]{:S(2)}, u32[]{:S(2)}) collective-permute-start(bf16[40,1792]{1,0:T(8,128)(2,1)S(1)} %get-tuple-element.72), channel_id=1, source_target_pairs={{0,6},{2,4},{4,2},{6,0},{1,7},{3,5},{5,3},{7,1},{8,14},{10,12},{12... | collective-permute-start | bytes 430088 | tf_op jit(solution)/shard_map/ppermute | solution.py:22
  48.7 8.1 %collective-permute-start.19 = (bf16[3,320,1024]{2,1,0:T(8,128)(2,1)S(1)}, bf16[3,320,1024]{2,1,0:T(8,128)(2,1)S(1)}, u32[]{:S(2)}, u32[]{:S(2)}) collective-permute-start(bf16[3,320,1024]{2,1,0:T(8,128)(2,1)S(1)} %get-tuple-element.76.refs_4_.own_ref), channel_id=1, source_target_pairs={{0,1},{1,0},{2,3},{3,2},{4,5},{5,4},{6,7},{7,6},{8,9},{9,8},{10,11... | collective-permute-start | bytes 5898248 | tf_op jit(solution)/shard_map/ppermute | solution.py:22
  48.8 13.2 %collective-permute-start.16 = (bf16[40,1792]{1,0:T(8,128)(2,1)S(1)}, bf16[40,1792]{1,0:T(8,128)(2,1)S(1)}, u32[]{:S(2)}, u32[]{:S(2)}) collective-permute-start(bf16[40,1792]{1,0:T(8,128)(2,1)S(1)} %get-tuple-element.78), channel_id=1, source_target_pairs={{0,2},{2,0},{4,6},{6,4},{1,3},{3,1},{5,7},{7,5},{8,10},{10,8},{12,... | collective-permute-start | bytes 430088 | tf_op jit(solution)/shard_map/ppermute | solution.py:22
  50.3 11.7 %collective-permute-start.17 = (bf16[40,1792]{1,0:T(8,128)(2,1)S(1)}, bf16[40,1792]{1,0:T(8,128)(2,1)S(1)}, u32[]{:S(2)}, u32[]{:S(2)}) collective-permute-start(bf16[40,1792]{1,0:T(8,128)(2,1)S(1)} %get-tuple-element.79), channel_id=1, source_target_pairs={{0,4},{2,6},{4,0},{6,2},{1,5},{3,7},{5,1},{7,3},{8,12},{10,14},{12... | collective-permute-start | bytes 430088 | tf_op jit(solution)/shard_map/ppermute | solution.py:22
  52.9 10.7 %collective-permute-start.18 = (bf16[40,1792]{1,0:T(8,128)(2,1)S(1)}, bf16[40,1792]{1,0:T(8,128)(2,1)S(1)}, u32[]{:S(2)}, u32[]{:S(2)}) collective-permute-start(bf16[40,1792]{1,0:T(8,128)(2,1)S(1)} %get-tuple-element.80), channel_id=1, source_target_pairs={{0,6},{2,4},{4,2},{6,0},{1,7},{3,5},{5,3},{7,1},{8,14},{10,12},{12... | collective-permute-start | bytes 430088 | tf_op jit(solution)/shard_map/ppermute | solution.py:22
  54.9 9.4 %collective-permute-start.15 = (bf16[64,1792]{1,0:T(8,128)(2,1)S(1)}, bf16[64,1792]{1,0:T(8,128)(2,1)S(1)}, u32[]{:S(2)}, u32[]{:S(2)}) collective-permute-start(bf16[64,1792]{1,0:T(8,128)(2,1)S(1)} %shard_map.148.refs_0_), channel_id=1, source_target_pairs={{0,8},{1,9},{8,16},{9,17},{16,24},{17,25},{24,0},{25,1},{2,10},{3,... | collective-permute-start | bytes 688136 | tf_op jit(solution)/shard_map/ppermute | solution.py:32
  62.0 7.6 %collective-permute-start.22 = (bf16[40,1792]{1,0:T(8,128)(2,1)S(1)}, bf16[40,1792]{1,0:T(8,128)(2,1)S(1)}, u32[]{:S(2)}, u32[]{:S(2)}) collective-permute-start(bf16[40,1792]{1,0:T(8,128)(2,1)S(1)} %get-tuple-element.83), channel_id=1, source_target_pairs={{0,4},{2,6},{4,0},{6,2},{1,5},{3,7},{5,1},{7,3},{8,12},{10,14},{12... | collective-permute-start | bytes 430088 | tf_op jit(solution)/shard_map/ppermute | solution.py:22
  62.0 7.6 %collective-permute-start.23 = (bf16[40,1792]{1,0:T(8,128)(2,1)S(1)}, bf16[40,1792]{1,0:T(8,128)(2,1)S(1)}, u32[]{:S(2)}, u32[]{:S(2)}) collective-permute-start(bf16[40,1792]{1,0:T(8,128)(2,1)S(1)} %get-tuple-element.84), channel_id=1, source_target_pairs={{0,6},{2,4},{4,2},{6,0},{1,7},{3,5},{5,3},{7,1},{8,14},{10,12},{12... | collective-permute-start | bytes 430088 | tf_op jit(solution)/shard_map/ppermute | solution.py:22
  64.1 12.2 %collective-permute-start.20 = (bf16[64,1792]{1,0:T(8,128)(2,1)S(1)}, bf16[64,1792]{1,0:T(8,128)(2,1)S(1)}, u32[]{:S(2)}, u32[]{:S(2)}) collective-permute-start(bf16[64,1792]{1,0:T(8,128)(2,1)S(1)} %shard_map.150.refs_4_), channel_id=1, source_target_pairs={{0,9},{1,8},{8,17},{9,16},{16,25},{17,24},{24,1},{25,0},{2,11},{3,... | collective-permute-start | bytes 688136 | tf_op jit(solution)/shard_map/ppermute | solution.py:32
  64.3 11.3 %collective-permute-start.25 = (bf16[40,1792]{1,0:T(8,128)(2,1)S(1)}, bf16[40,1792]{1,0:T(8,128)(2,1)S(1)}, u32[]{:S(2)}, u32[]{:S(2)}) collective-permute-start(bf16[40,1792]{1,0:T(8,128)(2,1)S(1)} %get-tuple-element.86), channel_id=1, source_target_pairs={{0,2},{2,0},{4,6},{6,4},{1,3},{3,1},{5,7},{7,5},{8,10},{10,8},{12,... | collective-permute-start | bytes 430088 | tf_op jit(solution)/shard_map/ppermute | solution.py:22
  66.7 9.6 %collective-permute-start.26 = (bf16[40,1792]{1,0:T(8,128)(2,1)S(1)}, bf16[40,1792]{1,0:T(8,128)(2,1)S(1)}, u32[]{:S(2)}, u32[]{:S(2)}) collective-permute-start(bf16[40,1792]{1,0:T(8,128)(2,1)S(1)} %get-tuple-element.87), channel_id=1, source_target_pairs={{0,4},{2,6},{4,0},{6,2},{1,5},{3,7},{5,1},{7,3},{8,12},{10,14},{12... | collective-permute-start | bytes 430088 | tf_op jit(solution)/shard_map/ppermute | solution.py:22
  70.1 8.5 %collective-permute-start.24 = (bf16[64,1792]{1,0:T(8,128)(2,1)S(1)}, bf16[64,1792]{1,0:T(8,128)(2,1)S(1)}, u32[]{:S(2)}, u32[]{:S(2)}) collective-permute-start(bf16[64,1792]{1,0:T(8,128)(2,1)S(1)} %shard_map.151.refs_0_), channel_id=1, source_target_pairs={{0,8},{1,9},{8,16},{9,17},{16,24},{17,25},{24,0},{25,1},{2,10},{3,... | collective-permute-start | bytes 688136 | tf_op jit(solution)/shard_map/ppermute | solution.py:32
  76.8 9.6 %collective-permute-start.28 = (bf16[64,1792]{1,0:T(8,128)(2,1)S(1)}, bf16[64,1792]{1,0:T(8,128)(2,1)S(1)}, u32[]{:S(2)}, u32[]{:S(2)}) collective-permute-start(bf16[64,1792]{1,0:T(8,128)(2,1)S(1)} %shard_map.153.refs_0_), channel_id=1, source_target_pairs={{0,9},{1,8},{8,17},{9,16},{16,25},{17,24},{24,1},{25,0},{2,11},{3,... | collective-permute-start | bytes 688136 | tf_op jit(solution)/shard_map/ppermute | solution.py:32
  (5 other events, 22.9 us)

commit v12 on v7

--- a/solution.py
+++ b/solution.py
@@ -540,8 +540,8 @@
         row_b,
         False,
         False,
-        after=(other_sum, in_vmem(y_mine)),
-        weight=150,
+        after=(other_sum,),
+        weight=300,
     )
     dx_mine = section_shift(own_sum, 0)
     other_sum = combine(
@@ -551,7 +551,7 @@
         row_b,
         False,
         True,
-        after=(own_sum, in_vmem(y_rest)),
+        after=(own_sum, in_vmem(y_rest), in_vmem(y_mine)),
         weight=100,
     )
     dx_rest = section_shift(other_sum, 1)

time: 87.7 us -> 93.9 us (1.071)
  waiting for transfers between devices: 22 us -> 29.5 us
  starting transfers between devices: 33.8 us -> 32.4 us
    ppermute x4, waiting for transfers between devices: 1.04 us -> 8.1 us  [section_shift(): return lax.ppermute(value, ('section', 'dp'), pairs)]
    ppermute x4, starting transfers between devices: 4.73 us -> 3.28 us  [section_shift(): return lax.ppermute(value, ('section', 'dp'), pairs)]
  transfers between devices with their start and end apart: 29 -> 29, of which waited for: 13 -> 12; matrix products, arithmetic and copies ran while one was open for 0% -> 0% of each run, Pallas kernels for 32% -> 30%
where the time goes in v12:
time: 93.9 us; the launch traced here: 93.7 us
  starting transfers between devices  32.4 us (35%)
  Pallas kernels  30.9 us (33%)
  waiting for transfers between devices  29.5 us (31%)
  between operations  1.01 us (1%)
    ppermute x25, starting transfers between devices, exchange(): lax.ppermute(value, axis, [(source, source ^ mask) for source in range(co...  29.1 us
    ppermute x25, waiting for transfers between devices, exchange(): lax.ppermute(value, axis, [(source, source ^ mask) for source in range(co...  21.4 us
    ppermute x4, waiting for transfers between devices, section_shift(): return lax.ppermute(value, ('section', 'dp'), pairs)  8.1 us
    pallas_call x1, Pallas kernels, grads(): call(grad_kernel, [pltpu.HBM((width, units), BF16)] * 2 + [pltpu.HBM((uni...  7.37 us
    pallas_call x2, Pallas kernels, gate_up(): call(functools.partial(gate_up_kernel, blocks=blocks), array(planes, tota...  5.22 us
    pallas_call x1, Pallas kernels, load(): call(functools.partial(load_kernel, count=len(weights)), [array(*weight.s...  4.23 us
    pallas_call x1, Pallas kernels, back(): call(functools.partial(back_kernel, blocks=plan.blocks), [array(total, un...  3.41 us
    ppermute x4, starting transfers between devices, section_shift(): return lax.ppermute(value, ('section', 'dp'), pairs)  3.28 us
  transfers between devices with their start and end apart: 29, of which 12 were waited for; matrix products, arithmetic and copies ran while one was open for 0% of the time, Pallas kernels for 30%

profile of v12, /device:TPU:0, one launch (start us, length us, event | category | flops | bytes accessed | tf_op | source)
XLA Modules:
  0.0 93.7 jit_solution(3941903611406897268)
XLA Ops:
  4.5 2.8 %collective-permute-start.1 = (bf16[80,1792]{1,0:T(8,128)(2,1)S(1)}, bf16[80,1792]{1,0:T(8,128)(2,1)S(1)}, u32[]{:S(2)}, u32[]{:S(2)}) collective-permute-start(bf16[80,1792]{1,0:T(8,128)(2,1)S(1)} %get-tuple-element.56), channel_id=1, source_target_pairs={{0,2},{2,0},{4,6},{6,4},{1,3},{3,1},{5,7},{7,5},{8,10},{10,8},{12,... | collective-permute-start | bytes 860168 | tf_op jit(solution)/shard_map/ppermute | solution.py:22
  9.4 2.0 %collective-permute-start.6 = (bf16[80,1792]{1,0:T(8,128)(2,1)S(1)}, bf16[80,1792]{1,0:T(8,128)(2,1)S(1)}, u32[]{:S(2)}, u32[]{:S(2)}) collective-permute-start(bf16[80,1792]{1,0:T(8,128)(2,1)S(1)} %get-tuple-element.67), channel_id=1, source_target_pairs={{0,2},{2,0},{4,6},{6,4},{1,3},{3,1},{5,7},{7,5},{8,10},{10,8},{12,... | collective-permute-start | bytes 860168 | tf_op jit(solution)/shard_map/ppermute | solution.py:22
  13.0 1.9 %collective-permute-done.1.refs_1_ = bf16[80,1792]{1,0:T(8,128)(2,1)S(1)} collective-permute-done((bf16[80,1792]{1,0:T(8,128)(2,1)S(1)}, bf16[80,1792]{1,0:T(8,128)(2,1)S(1)}, u32[]{:S(2)}, u32[]{:S(2)}) %collective-permute-start.1) | collective-permute-done | bytes 286752 | tf_op jit(solution)/shard_map/ppermute | solution.py:22
  14.9 3.0 %collective-permute-start.8 = (bf16[80,1792]{1,0:T(8,128)(2,1)S(1)}, bf16[80,1792]{1,0:T(8,128)(2,1)S(1)}, u32[]{:S(2)}, u32[]{:S(2)}) collective-permute-start(bf16[80,1792]{1,0:T(8,128)(2,1)S(1)} %get-tuple-element.69), channel_id=1, source_target_pairs={{0,6},{2,4},{4,2},{6,0},{1,7},{3,5},{5,3},{7,1},{8,14},{10,12},{12... | collective-permute-start | bytes 860168 | tf_op jit(solution)/shard_map/ppermute | solution.py:22
  17.9 4.2 %shard_map.141 = (bf16[1792,1024]{1,0:T(8,128)(2,1)S(1)}, bf16[1792,1024]{1,0:T(8,128)(2,1)S(1)}, bf16[1024,1792]{1,0:T(8,128)(2,1)S(1)}) custom-call(bf16[1792,1024]{1,0:T(8,128)(2,1)} %bitcast.23, bf16[1792,1024]{1,0:T(8,128)(2,1)} %bitcast.24, bf16[1024,1792]{1,0:T(8,128)(2,1)} %bitcast.25, bf16[80,1792]{1,0:T(8,128)(2,1)S(1)} %get-tuple-element.61.refs_3_.refs_0_), custom_call_target="tpu_custom_call" | custom-call | flops 10000000 | bytes 1 | tf_op jit(solution)/shard_map/pallas_call | solution.py:164
  23.4 1.8 %collective-permute-start.13 = (bf16[80,1792]{1,0:T(8,128)(2,1)S(1)}, bf16[80,1792]{1,0:T(8,128)(2,1)S(1)}, u32[]{:S(2)}, u32[]{:S(2)}) collective-permute-start(bf16[80,1792]{1,0:T(8,128)(2,1)S(1)} %get-tuple-element.75), channel_id=1, source_target_pairs={{0,4},{2,6},{4,0},{6,2},{1,5},{3,7},{5,1},{7,3},{8,12},{10,14},{12... | collective-permute-start | bytes 860168 | tf_op jit(solution)/shard_map/ppermute | solution.py:22
  25.2 2.6 %shard_map.143.refs_6_.own_ref = bf16[2,320,1024]{2,1,0:T(8,128)(2,1)S(1)} custom-call(bf16[80,1792]{1,0:T(8,128)(2,1)S(1)} %get-tuple-element.55.refs_0_, bf16[80,1792]{1,0:T(8,128)(2,1)S(1)} %collective-permute-done.1.refs_1_, bf16[80,1792]{1,0:T(8,128)(2,1)S(1)} %collective-permute-done.2.refs_2_, bf16[80,1792]{1,0:T(8,128)(2,1)S(1)} %collective-permute-done.3.refs_3_, ...), custom_call_target="tpu_custom_call" | custom-call | flops 10000000 | bytes 1 | tf_op jit(solution)/shard_map/pallas_call | solution.py:298
  27.8 2.4 %collective-permute-start.14 = (bf16[80,1792]{1,0:T(8,128)(2,1)S(1)}, bf16[80,1792]{1,0:T(8,128)(2,1)S(1)}, u32[]{:S(2)}, u32[]{:S(2)}) collective-permute-start(bf16[80,1792]{1,0:T(8,128)(2,1)S(1)} %get-tuple-element.76), channel_id=1, source_target_pairs={{0,6},{2,4},{4,2},{6,0},{1,7},{3,5},{5,3},{7,1},{8,14},{10,12},{12... | collective-permute-start | bytes 860168 | tf_op jit(solution)/shard_map/ppermute | solution.py:22
  30.3 5.2 %collective-permute-done.7.refs_2_ = bf16[80,1792]{1,0:T(8,128)(2,1)S(1)} collective-permute-done((bf16[80,1792]{1,0:T(8,128)(2,1)S(1)}, bf16[80,1792]{1,0:T(8,128)(2,1)S(1)}, u32[]{:S(2)}, u32[]{:S(2)}) %collective-permute-start.7) | collective-permute-done | bytes 286752 | tf_op jit(solution)/shard_map/ppermute | solution.py:22
  35.4 2.6 %shard_map.144.refs_0_.refs_5_ = bf16[3,320,1024]{2,1,0:T(8,128)(2,1)S(1)} custom-call(bf16[80,1792]{1,0:T(8,128)(2,1)S(1)} %get-tuple-element.61.refs_3_.refs_0_, bf16[80,1792]{1,0:T(8,128)(2,1)S(1)} %collective-permute-done.6.refs_1_, bf16[80,1792]{1,0:T(8,128)(2,1)S(1)} %collective-permute-done.7.refs_2_, ...), custom_call_target="tpu_custom_call" | custom-call | flops 30000001024 | bytes 1 | tf_op jit(solution)/shard_map/pallas_call | solution.py:298
  38.5 1.7 %shard_map.145 = (bf16[40,1792]{1,0:T(8,128)(2,1)S(1)}, bf16[40,1792]{1,0:T(8,128)(2,1)S(1)}, bf16[40,1792]{1,0:T(8,128)(2,1)S(1)}, bf16[40,1792]{1,0:T(8,128)(2...) custom-call(bf16[2,320,1024]{2,1,0:T(8,128)(2,1)S(1)} %shard_map.143, ...), custom_call_target="tpu_custom_call" | custom-call | flops 10000000 | bytes 1 | tf_op jit(solution)/shard_map/pallas_call | solution.py:361
  44.2 2.6 %collective-permute-done.13.refs_2_ = bf16[80,1792]{1,0:T(8,128)(2,1)S(1)} collective-permute-done((bf16[80,1792]{1,0:T(8,128)(2,1)S(1)}, bf16[80,1792]{1,0:T(8,128)(2,1)S(1)}, u32[]{:S(2)}, u32[]{:S(2)}) %collective-permute-start.13) | collective-permute-done | bytes 286752 | tf_op jit(solution)/shard_map/ppermute | solution.py:22
  48.8 1.6 %collective-permute-start.16 = (bf16[40,1792]{1,0:T(8,128)(2,1)S(1)}, bf16[40,1792]{1,0:T(8,128)(2,1)S(1)}, u32[]{:S(2)}, u32[]{:S(2)}) collective-permute-start(bf16[40,1792]{1,0:T(8,128)(2,1)S(1)} %get-tuple-element.79), channel_id=1, source_target_pairs={{0,2},{2,0},{4,6},{6,4},{1,3},{3,1},{5,7},{7,5},{8,10},{10,8},{12,... | collective-permute-start | bytes 430088 | tf_op jit(solution)/shard_map/ppermute | solution.py:22
  50.9 1.9 %collective-permute-done.10.refs_2_ = bf16[40,1792]{1,0:T(8,128)(2,1)S(1)} collective-permute-done((bf16[40,1792]{1,0:T(8,128)(2,1)S(1)}, bf16[40,1792]{1,0:T(8,128)(2,1)S(1)}, u32[]{:S(2)}, u32[]{:S(2)}) %collective-permute-start.10) | collective-permute-done | bytes 143392 | tf_op jit(solution)/shard_map/ppermute | solution.py:22
  54.9 3.4 %shard_map.149 = (bf16[320,1024]{1,0:T(8,128)(2,1)S(1)}, bf16[320,1024]{1,0:T(8,128)(2,1)S(1)}, bf16[320,1024]{1,0:T(8,128)(2,1)S(1)}, bf16[40,1792]{1,0:T(8,128...) custom-call(bf16[3,320,1024]{2,1,0:T(8,128)(2,1)S(1)} %get-tuple-ele, ...), custom_call_target="tpu_custom_call" | custom-call | flops 10000000 | bytes 1 | tf_op jit(solution)/shard_map/pallas_call | solution.py:394
  58.4 2.1 %collective-permute-start.21 = (bf16[40,1792]{1,0:T(8,128)(2,1)S(1)}, bf16[40,1792]{1,0:T(8,128)(2,1)S(1)}, u32[]{:S(2)}, u32[]{:S(2)}) collective-permute-start(bf16[40,1792]{1,0:T(8,128)(2,1)S(1)} %get-tuple-element.83), channel_id=1, source_target_pairs={{0,2},{2,0},{4,6},{6,4},{1,3},{3,1},{5,7},{7,5},{8,10},{10,8},{12,... | collective-permute-start | bytes 430088 | tf_op jit(solution)/shard_map/ppermute | solution.py:22
  62.0 1.6 %collective-permute-start.15 = (bf16[64,1792]{1,0:T(8,128)(2,1)S(1)}, bf16[64,1792]{1,0:T(8,128)(2,1)S(1)}, u32[]{:S(2)}, u32[]{:S(2)}) collective-permute-start(bf16[64,1792]{1,0:T(8,128)(2,1)S(1)} %shard_map.148.refs_0_), channel_id=1, source_target_pairs={{0,8},{1,9},{8,16},{9,17},{16,24},{17,25},{24,0},{25,1},{2,10},{3,... | collective-permute-start | bytes 688136 | tf_op jit(solution)/shard_map/ppermute | solution.py:32
  63.5 1.9 %collective-permute-start.25 = (bf16[40,1792]{1,0:T(8,128)(2,1)S(1)}, bf16[40,1792]{1,0:T(8,128)(2,1)S(1)}, u32[]{:S(2)}, u32[]{:S(2)}) collective-permute-start(bf16[40,1792]{1,0:T(8,128)(2,1)S(1)} %get-tuple-element.87), channel_id=1, source_target_pairs={{0,2},{2,0},{4,6},{6,4},{1,3},{3,1},{5,7},{7,5},{8,10},{10,8},{12,... | collective-permute-start | bytes 430088 | tf_op jit(solution)/shard_map/ppermute | solution.py:22
  66.2 4.5 %collective-permute-done.22.refs_2_ = bf16[40,1792]{1,0:T(8,128)(2,1)S(1)} collective-permute-done((bf16[40,1792]{1,0:T(8,128)(2,1)S(1)}, bf16[40,1792]{1,0:T(8,128)(2,1)S(1)}, u32[]{:S(2)}, u32[]{:S(2)}) %collective-permute-start.22) | collective-permute-done | bytes 143392 | tf_op jit(solution)/shard_map/ppermute | solution.py:22
  71.1 1.6 %collective-permute-start.24 = (bf16[64,1792]{1,0:T(8,128)(2,1)S(1)}, bf16[64,1792]{1,0:T(8,128)(2,1)S(1)}, u32[]{:S(2)}, u32[]{:S(2)}) collective-permute-start(bf16[64,1792]{1,0:T(8,128)(2,1)S(1)} %shard_map.151.refs_4_), channel_id=1, source_target_pairs={{0,8},{1,9},{8,16},{9,17},{16,24},{17,25},{24,0},{25,1},{2,10},{3,... | collective-permute-start | bytes 688136 | tf_op jit(solution)/shard_map/ppermute | solution.py:32
  72.8 3.8 %collective-permute-done.27.refs_3_ = bf16[40,1792]{1,0:T(8,128)(2,1)S(1)} collective-permute-done((bf16[40,1792]{1,0:T(8,128)(2,1)S(1)}, bf16[40,1792]{1,0:T(8,128)(2,1)S(1)}, u32[]{:S(2)}, u32[]{:S(2)}) %collective-permute-start.27) | collective-permute-done | bytes 143392 | tf_op jit(solution)/shard_map/ppermute | solution.py:22
  76.6 3.2 %collective-permute-done.20.refs_5_.refs_1_ = bf16[64,1792]{1,0:T(8,128)(2,1)S(1)} collective-permute-done((bf16[64,1792]{1,0:T(8,128)(2,1)S(1)}, bf16[64,1792]{1,0:T(8,128)(2,1)S(1)}, u32[]{:S(2)}, u32[]{:S(2)}) %collective-permute-start.20) | collective-permute-done | bytes 229408 | tf_op jit(solution)/shard_map/ppermute | solution.py:32
  80.4 4.9 %collective-permute-done.24.refs_1_.refs_2_ = bf16[64,1792]{1,0:T(8,128)(2,1)S(1)} collective-permute-done((bf16[64,1792]{1,0:T(8,128)(2,1)S(1)}, bf16[64,1792]{1,0:T(8,128)(2,1)S(1)}, u32[]{:S(2)}, u32[]{:S(2)}) %collective-permute-start.24) | collective-permute-done | bytes 229408 | tf_op jit(solution)/shard_map/ppermute | solution.py:32
  85.3 7.4 %shard_map.153 = (bf16[1792,1024]{1,0:T(8,128)(2,1)}, bf16[1792,1024]{1,0:T(8,128)(2,1)}, bf16[1024,1792]{1,0:T(8,128)(2,1)}) custom-call(bf16[320,1024]{1,0:T(8,128)(2,1)S(1)} %get-tuple-element.90.hidden, bf16[320,1024]{1,0:T(8,128)(2,1)S(1)} %get-tuple-element.91.d_gate, bf16[320,1024]{1,0:T(8,128)(2,1)S(1)} %get-tuple-element.92.d_up, ...), custom_call_target="tpu_custom_call" | custom-call | flops 1000000000 | bytes 1 | tf_op jit(solution)/shard_map/pallas_call | solution.py:432
  (52 shorter events, 22.0 us)
Async XLA Ops:
  4.5 10.4 %collective-permute-start.1 = (bf16[80,1792]{1,0:T(8,128)(2,1)S(1)}, bf16[80,1792]{1,0:T(8,128)(2,1)S(1)}, u32[]{:S(2)}, u32[]{:S(2)}) collective-permute-start(bf16[80,1792]{1,0:T(8,128)(2,1)S(1)} %get-tuple-element.56), channel_id=1, source_target_pairs={{0,2},{2,0},{4,6},{6,4},{1,3},{3,1},{5,7},{7,5},{8,10},{10,8},{12,... | collective-permute-start | bytes 860168 | tf_op jit(solution)/shard_map/ppermute | solution.py:22
  7.3 15.8 %collective-permute-start.2 = (bf16[80,1792]{1,0:T(8,128)(2,1)S(1)}, bf16[80,1792]{1,0:T(8,128)(2,1)S(1)}, u32[]{:S(2)}, u32[]{:S(2)}) collective-permute-start(bf16[80,1792]{1,0:T(8,128)(2,1)S(1)} %get-tuple-element.57), channel_id=1, source_target_pairs={{0,4},{2,6},{4,0},{6,2},{1,5},{3,7},{5,1},{7,3},{8,12},{10,14},{12... | collective-permute-start | bytes 860168 | tf_op jit(solution)/shard_map/ppermute | solution.py:22
  8.8 14.5 %collective-permute-start.3 = (bf16[80,1792]{1,0:T(8,128)(2,1)S(1)}, bf16[80,1792]{1,0:T(8,128)(2,1)S(1)}, u32[]{:S(2)}, u32[]{:S(2)}) collective-permute-start(bf16[80,1792]{1,0:T(8,128)(2,1)S(1)} %get-tuple-element.58), channel_id=1, source_target_pairs={{0,6},{2,4},{4,2},{6,0},{1,7},{3,5},{5,3},{7,1},{8,14},{10,12},{12... | collective-permute-start | bytes 860168 | tf_op jit(solution)/shard_map/ppermute | solution.py:22
  9.4 18.4 %collective-permute-start.6 = (bf16[80,1792]{1,0:T(8,128)(2,1)S(1)}, bf16[80,1792]{1,0:T(8,128)(2,1)S(1)}, u32[]{:S(2)}, u32[]{:S(2)}) collective-permute-start(bf16[80,1792]{1,0:T(8,128)(2,1)S(1)} %get-tuple-element.67), channel_id=1, source_target_pairs={{0,2},{2,0},{4,6},{6,4},{1,3},{3,1},{5,7},{7,5},{8,10},{10,8},{12,... | collective-permute-start | bytes 860168 | tf_op jit(solution)/shard_map/ppermute | solution.py:22
  11.5 24.0 %collective-permute-start.7 = (bf16[80,1792]{1,0:T(8,128)(2,1)S(1)}, bf16[80,1792]{1,0:T(8,128)(2,1)S(1)}, u32[]{:S(2)}, u32[]{:S(2)}) collective-permute-start(bf16[80,1792]{1,0:T(8,128)(2,1)S(1)} %get-tuple-element.68), channel_id=1, source_target_pairs={{0,4},{2,6},{4,0},{6,2},{1,5},{3,7},{5,1},{7,3},{8,12},{10,14},{12... | collective-permute-start | bytes 860168 | tf_op jit(solution)/shard_map/ppermute | solution.py:22
  14.9 20.5 %collective-permute-start.8 = (bf16[80,1792]{1,0:T(8,128)(2,1)S(1)}, bf16[80,1792]{1,0:T(8,128)(2,1)S(1)}, u32[]{:S(2)}, u32[]{:S(2)}) collective-permute-start(bf16[80,1792]{1,0:T(8,128)(2,1)S(1)} %get-tuple-element.69), channel_id=1, source_target_pairs={{0,6},{2,4},{4,2},{6,0},{1,7},{3,5},{5,3},{7,1},{8,14},{10,12},{12... | collective-permute-start | bytes 860168 | tf_op jit(solution)/shard_map/ppermute | solution.py:22
  23.2 19.5 %collective-permute-start.12 = (bf16[80,1792]{1,0:T(8,128)(2,1)S(1)}, bf16[80,1792]{1,0:T(8,128)(2,1)S(1)}, u32[]{:S(2)}, u32[]{:S(2)}) collective-permute-start(bf16[80,1792]{1,0:T(8,128)(2,1)S(1)} %get-tuple-element.74), channel_id=1, source_target_pairs={{0,2},{2,0},{4,6},{6,4},{1,3},{3,1},{5,7},{7,5},{8,10},{10,8},{12,... | collective-permute-start | bytes 860168 | tf_op jit(solution)/shard_map/ppermute | solution.py:22
  23.4 23.4 %collective-permute-start.13 = (bf16[80,1792]{1,0:T(8,128)(2,1)S(1)}, bf16[80,1792]{1,0:T(8,128)(2,1)S(1)}, u32[]{:S(2)}, u32[]{:S(2)}) collective-permute-start(bf16[80,1792]{1,0:T(8,128)(2,1)S(1)} %get-tuple-element.75), channel_id=1, source_target_pairs={{0,4},{2,6},{4,0},{6,2},{1,5},{3,7},{5,1},{7,3},{8,12},{10,14},{12... | collective-permute-start | bytes 860168 | tf_op jit(solution)/shard_map/ppermute | solution.py:22
  27.8 19.5 %collective-permute-start.14 = (bf16[80,1792]{1,0:T(8,128)(2,1)S(1)}, bf16[80,1792]{1,0:T(8,128)(2,1)S(1)}, u32[]{:S(2)}, u32[]{:S(2)}) collective-permute-start(bf16[80,1792]{1,0:T(8,128)(2,1)S(1)} %get-tuple-element.76), channel_id=1, source_target_pairs={{0,6},{2,4},{4,2},{6,0},{1,7},{3,5},{5,3},{7,1},{8,14},{10,12},{12... | collective-permute-start | bytes 860168 | tf_op jit(solution)/shard_map/ppermute | solution.py:22
  40.1 10.2 %collective-permute-start.9 = (bf16[40,1792]{1,0:T(8,128)(2,1)S(1)}, bf16[40,1792]{1,0:T(8,128)(2,1)S(1)}, u32[]{:S(2)}, u32[]{:S(2)}) collective-permute-start(bf16[40,1792]{1,0:T(8,128)(2,1)S(1)} %get-tuple-element.71), channel_id=1, source_target_pairs={{0,2},{2,0},{4,6},{6,4},{1,3},{3,1},{5,7},{7,5},{8,10},{10,8},{12,... | collective-permute-start | bytes 430088 | tf_op jit(solution)/shard_map/ppermute | solution.py:22
  40.8 12.1 %collective-permute-start.10 = (bf16[40,1792]{1,0:T(8,128)(2,1)S(1)}, bf16[40,1792]{1,0:T(8,128)(2,1)S(1)}, u32[]{:S(2)}, u32[]{:S(2)}) collective-permute-start(bf16[40,1792]{1,0:T(8,128)(2,1)S(1)} %get-tuple-element.72), channel_id=1, source_target_pairs={{0,4},{2,6},{4,0},{6,2},{1,5},{3,7},{5,1},{7,3},{8,12},{10,14},{12... | collective-permute-start | bytes 430088 | tf_op jit(solution)/shard_map/ppermute | solution.py:22
  42.7 11.7 %collective-permute-start.11 = (bf16[40,1792]{1,0:T(8,128)(2,1)S(1)}, bf16[40,1792]{1,0:T(8,128)(2,1)S(1)}, u32[]{:S(2)}, u32[]{:S(2)}) collective-permute-start(bf16[40,1792]{1,0:T(8,128)(2,1)S(1)} %get-tuple-element.73), channel_id=1, source_target_pairs={{0,6},{2,4},{4,2},{6,0},{1,7},{3,5},{5,3},{7,1},{8,14},{10,12},{12... | collective-permute-start | bytes 430088 | tf_op jit(solution)/shard_map/ppermute | solution.py:22
  48.8 11.7 %collective-permute-start.16 = (bf16[40,1792]{1,0:T(8,128)(2,1)S(1)}, bf16[40,1792]{1,0:T(8,128)(2,1)S(1)}, u32[]{:S(2)}, u32[]{:S(2)}) collective-permute-start(bf16[40,1792]{1,0:T(8,128)(2,1)S(1)} %get-tuple-element.79), channel_id=1, source_target_pairs={{0,2},{2,0},{4,6},{6,4},{1,3},{3,1},{5,7},{7,5},{8,10},{10,8},{12,... | collective-permute-start | bytes 430088 | tf_op jit(solution)/shard_map/ppermute | solution.py:22
  50.3 11.6 %collective-permute-start.17 = (bf16[40,1792]{1,0:T(8,128)(2,1)S(1)}, bf16[40,1792]{1,0:T(8,128)(2,1)S(1)}, u32[]{:S(2)}, u32[]{:S(2)}) collective-permute-start(bf16[40,1792]{1,0:T(8,128)(2,1)S(1)} %get-tuple-element.80), channel_id=1, source_target_pairs={{0,4},{2,6},{4,0},{6,2},{1,5},{3,7},{5,1},{7,3},{8,12},{10,14},{12... | collective-permute-start | bytes 430088 | tf_op jit(solution)/shard_map/ppermute | solution.py:22
  52.9 10.7 %collective-permute-start.18 = (bf16[40,1792]{1,0:T(8,128)(2,1)S(1)}, bf16[40,1792]{1,0:T(8,128)(2,1)S(1)}, u32[]{:S(2)}, u32[]{:S(2)}) collective-permute-start(bf16[40,1792]{1,0:T(8,128)(2,1)S(1)} %get-tuple-element.81), channel_id=1, source_target_pairs={{0,6},{2,4},{4,2},{6,0},{1,7},{3,5},{5,3},{7,1},{8,14},{10,12},{12... | collective-permute-start | bytes 430088 | tf_op jit(solution)/shard_map/ppermute | solution.py:22
  58.4 7.7 %collective-permute-start.21 = (bf16[40,1792]{1,0:T(8,128)(2,1)S(1)}, bf16[40,1792]{1,0:T(8,128)(2,1)S(1)}, u32[]{:S(2)}, u32[]{:S(2)}) collective-permute-start(bf16[40,1792]{1,0:T(8,128)(2,1)S(1)} %get-tuple-element.83), channel_id=1, source_target_pairs={{0,2},{2,0},{4,6},{6,4},{1,3},{3,1},{5,7},{7,5},{8,10},{10,8},{12,... | collective-permute-start | bytes 430088 | tf_op jit(solution)/shard_map/ppermute | solution.py:22
  60.4 10.2 %collective-permute-start.22 = (bf16[40,1792]{1,0:T(8,128)(2,1)S(1)}, bf16[40,1792]{1,0:T(8,128)(2,1)S(1)}, u32[]{:S(2)}, u32[]{:S(2)}) collective-permute-start(bf16[40,1792]{1,0:T(8,128)(2,1)S(1)} %get-tuple-element.84), channel_id=1, source_target_pairs={{0,4},{2,6},{4,0},{6,2},{1,5},{3,7},{5,1},{7,3},{8,12},{10,14},{12... | collective-permute-start | bytes 430088 | tf_op jit(solution)/shard_map/ppermute | solution.py:22
  60.4 10.2 %collective-permute-start.23 = (bf16[40,1792]{1,0:T(8,128)(2,1)S(1)}, bf16[40,1792]{1,0:T(8,128)(2,1)S(1)}, u32[]{:S(2)}, u32[]{:S(2)}) collective-permute-start(bf16[40,1792]{1,0:T(8,128)(2,1)S(1)} %get-tuple-element.85), channel_id=1, source_target_pairs={{0,6},{2,4},{4,2},{6,0},{1,7},{3,5},{5,3},{7,1},{8,14},{10,12},{12... | collective-permute-start | bytes 430088 | tf_op jit(solution)/shard_map/ppermute | solution.py:22
  62.0 9.1 %collective-permute-start.15 = (bf16[64,1792]{1,0:T(8,128)(2,1)S(1)}, bf16[64,1792]{1,0:T(8,128)(2,1)S(1)}, u32[]{:S(2)}, u32[]{:S(2)}) collective-permute-start(bf16[64,1792]{1,0:T(8,128)(2,1)S(1)} %shard_map.148.refs_0_), channel_id=1, source_target_pairs={{0,8},{1,9},{8,16},{9,17},{16,24},{17,25},{24,0},{25,1},{2,10},{3,... | collective-permute-start | bytes 688136 | tf_op jit(solution)/shard_map/ppermute | solution.py:32
  63.5 9.2 %collective-permute-start.25 = (bf16[40,1792]{1,0:T(8,128)(2,1)S(1)}, bf16[40,1792]{1,0:T(8,128)(2,1)S(1)}, u32[]{:S(2)}, u32[]{:S(2)}) collective-permute-start(bf16[40,1792]{1,0:T(8,128)(2,1)S(1)} %get-tuple-element.87), channel_id=1, source_target_pairs={{0,2},{2,0},{4,6},{6,4},{1,3},{3,1},{5,7},{7,5},{8,10},{10,8},{12,... | collective-permute-start | bytes 430088 | tf_op jit(solution)/shard_map/ppermute | solution.py:22
  66.1 6.7 %collective-permute-start.26 = (bf16[40,1792]{1,0:T(8,128)(2,1)S(1)}, bf16[40,1792]{1,0:T(8,128)(2,1)S(1)}, u32[]{:S(2)}, u32[]{:S(2)}) collective-permute-start(bf16[40,1792]{1,0:T(8,128)(2,1)S(1)} %get-tuple-element.88), channel_id=1, source_target_pairs={{0,4},{2,6},{4,0},{6,2},{1,5},{3,7},{5,1},{7,3},{8,12},{10,14},{12... | collective-permute-start | bytes 430088 | tf_op jit(solution)/shard_map/ppermute | solution.py:22
  70.6 9.2 %collective-permute-start.20 = (bf16[64,1792]{1,0:T(8,128)(2,1)S(1)}, bf16[64,1792]{1,0:T(8,128)(2,1)S(1)}, u32[]{:S(2)}, u32[]{:S(2)}) collective-permute-start(bf16[64,1792]{1,0:T(8,128)(2,1)S(1)} %shard_map.150.refs_4_), channel_id=1, source_target_pairs={{0,9},{1,8},{8,17},{9,16},{16,25},{17,24},{24,1},{25,0},{2,11},{3,... | collective-permute-start | bytes 688136 | tf_op jit(solution)/shard_map/ppermute | solution.py:32
  71.1 14.2 %collective-permute-start.24 = (bf16[64,1792]{1,0:T(8,128)(2,1)S(1)}, bf16[64,1792]{1,0:T(8,128)(2,1)S(1)}, u32[]{:S(2)}, u32[]{:S(2)}) collective-permute-start(bf16[64,1792]{1,0:T(8,128)(2,1)S(1)} %shard_map.151.refs_4_), channel_id=1, source_target_pairs={{0,8},{1,9},{8,16},{9,17},{16,24},{17,25},{24,0},{25,1},{2,10},{3,... | collective-permute-start | bytes 688136 | tf_op jit(solution)/shard_map/ppermute | solution.py:32
  80.3 12.3 %collective-permute-start.28 = (bf16[64,1792]{1,0:T(8,128)(2,1)S(1)}, bf16[64,1792]{1,0:T(8,128)(2,1)S(1)}, u32[]{:S(2)}, u32[]{:S(2)}) collective-permute-start(bf16[64,1792]{1,0:T(8,128)(2,1)S(1)} %shard_map.152.refs_0_), channel_id=1, source_target_pairs={{0,9},{1,8},{8,17},{9,16},{16,25},{17,24},{24,1},{25,0},{2,11},{3,... | collective-permute-start | bytes 688136 | tf_op jit(solution)/shard_map/ppermute | solution.py:32
  (5 other events, 21.7 us)

commit v13 on v11

--- a/solution.py
+++ b/solution.py
@@ -465,16 +465,16 @@
     ]
 
 
-def finish_kernel(*refs):
-    sources, outs, sems = refs[:4], refs[-3:-1], refs[-1]
-    width = sources[0].shape[1]
+def place_kernel(*refs, halves_of, count):
+    outs, sems = refs[-1 - count : -1], refs[-1]
+    width = refs[0].shape[1]
     core = lax.axis_index("dp")
     copies = []
-    for place, source in enumerate(sources):
-        half = core if place % 2 == 0 else 1 - core
+    for place, (out, own) in enumerate(halves_of):
+        half = core if own else 1 - core
         columns = pl.ds(pl.multiple_of(half * width, 128), width)
         copies.append(
-            pltpu.make_async_copy(source, outs[place // 2].at[:, columns], sems.at[place])
+            pltpu.make_async_copy(refs[place], outs[out].at[:, columns], sems.at[place])
         )
     for copy in copies:
         copy.start()
@@ -482,15 +482,16 @@
         copy.wait()
 
 
-def finish(y_mine, y_rest, dx_mine, dx_rest, after):
-    tokens, width = y_mine.shape
-    return call(
-        finish_kernel,
-        [pltpu.HBM((tokens, 2 * width), BF16)] * 2,
-        [VMEM] * 4 + [AFTER] * len(after),
-        [HBM] * 2,
-        [pltpu.SemaphoreType.DMA((4,))],
-    )(y_mine, y_rest, dx_mine, dx_rest, *after)
+def placed(sources, halves_of, count, into=(), after=()):
+    tokens, width = sources[0].shape
+    return call(
+        functools.partial(place_kernel, halves_of=halves_of, count=count),
+        [pltpu.HBM((tokens, 2 * width), BF16)] * count,
+        [VMEM] * len(sources) + [HBM] * len(into) + [AFTER] * len(after),
+        [HBM] * count,
+        [pltpu.SemaphoreType.DMA((len(sources),))],
+        aliases={len(sources) + place: place for place in range(len(into))},
+    )(*sources, *[in_hbm(value) for value in into], *after)
 
 
 def local(x_fwd, ids_fwd, route_fwd, x_bwd, ids_bwd, route_bwd, dy_bwd, w_gate, w_up, w_down):
@@ -575,7 +576,13 @@
     grad_g, grad_u = grad_in(
         d_gate, d_up, turned, after=(other_sum, in_vmem(dx_mine)), weight=100
     )
-    y_next, dx_next = finish(y_mine, y_rest, dx_mine, dx_rest, after=(in_hbm(grad_g),))
+    y_next, dx_next = placed(
+        [y_mine, y_rest, dx_mine],
+        ((0, True), (0, False), (1, True)),
+        2,
+        after=(in_hbm(grad_g),),
+    )
+    (dx_next,) = placed([dx_rest], ((0, False),), 1, into=(dx_next,))
     return (
         y_next[None],
         dx_next[None],

time: 87.6 us -> 87.4 us (level)
  transfers between devices with their start and end apart: 29 -> 29, of which waited for: 13 -> 13; matrix products, arithmetic and copies ran while one was open for 0% -> 0% of each run, Pallas kernels for 35% -> 36%
where the time goes in v13:
time: 87.4 us; the launch traced here: 87.2 us
  starting transfers between devices  33.7 us (39%)
  Pallas kernels  33.6 us (38%)
  waiting for transfers between devices  18.9 us (22%)
  between operations  0.99 us (1%)
    ppermute x25, starting transfers between devices, exchange(): lax.ppermute(value, axis, [(source, source ^ mask) for source in range(co...  29 us
    ppermute x25, waiting for transfers between devices, exchange(): lax.ppermute(value, axis, [(source, source ^ mask) for source in range(co...  17.1 us
    pallas_call x1, Pallas kernels, grad_in(): call(grad_in_kernel, [pltpu.HBM((width, units), BF16)] * 2, [VMEM] * 3 +...  5.82 us
    pallas_call x2, Pallas kernels, gate_up(): call(functools.partial(gate_up_kernel, blocks=blocks), array(planes, tota...  5.22 us
    ppermute x4, starting transfers between devices, section_shift(): return lax.ppermute(value, ('section', 'dp'), pairs)  4.72 us
    pallas_call x1, Pallas kernels, load(): call(functools.partial(load_kernel, count=len(weights)), [array(*weight.s...  4.23 us
    pallas_call x1, Pallas kernels, grad_down(): call(grad_down_kernel, pltpu.HBM((units, width), BF16), [VMEM] * 2 + [AFT...  3.9 us
    pallas_call x1, Pallas kernels, back(): call(functools.partial(back_kernel, blocks=plan.blocks), [array(total, un...  3.2 us
  transfers between devices with their start and end apart: 29, of which 13 were waited for; matrix products, arithmetic and copies ran while one was open for 0% of the time, Pallas kernels for 36%

profile of v13, /device:TPU:0, one launch (start us, length us, event | category | flops | bytes accessed | tf_op | source)
XLA Modules:
  0.0 87.2 jit_solution(3256591442210517094)
XLA Ops:
  4.5 2.8 %collective-permute-start.1 = (bf16[80,1792]{1,0:T(8,128)(2,1)S(1)}, bf16[80,1792]{1,0:T(8,128)(2,1)S(1)}, u32[]{:S(2)}, u32[]{:S(2)}) collective-permute-start(bf16[80,1792]{1,0:T(8,128)(2,1)S(1)} %get-tuple-element.55), channel_id=1, source_target_pairs={{0,2},{2,0},{4,6},{6,4},{1,3},{3,1},{5,7},{7,5},{8,10},{10,8},{12,... | collective-permute-start | bytes 860168 | tf_op jit(solution)/shard_map/ppermute | solution.py:22
  7.3 1.5 %collective-permute-start.2 = (bf16[80,1792]{1,0:T(8,128)(2,1)S(1)}, bf16[80,1792]{1,0:T(8,128)(2,1)S(1)}, u32[]{:S(2)}, u32[]{:S(2)}) collective-permute-start(bf16[80,1792]{1,0:T(8,128)(2,1)S(1)} %get-tuple-element.56), channel_id=1, source_target_pairs={{0,4},{2,6},{4,0},{6,2},{1,5},{3,7},{5,1},{7,3},{8,12},{10,14},{12... | collective-permute-start | bytes 860168 | tf_op jit(solution)/shard_map/ppermute | solution.py:22
  9.4 2.0 %collective-permute-start.6 = (bf16[80,1792]{1,0:T(8,128)(2,1)S(1)}, bf16[80,1792]{1,0:T(8,128)(2,1)S(1)}, u32[]{:S(2)}, u32[]{:S(2)}) collective-permute-start(bf16[80,1792]{1,0:T(8,128)(2,1)S(1)} %get-tuple-element.66), channel_id=1, source_target_pairs={{0,2},{2,0},{4,6},{6,4},{1,3},{3,1},{5,7},{7,5},{8,10},{10,8},{12,... | collective-permute-start | bytes 860168 | tf_op jit(solution)/shard_map/ppermute | solution.py:22
  13.0 1.9 %collective-permute-done.1.refs_1_ = bf16[80,1792]{1,0:T(8,128)(2,1)S(1)} collective-permute-done((bf16[80,1792]{1,0:T(8,128)(2,1)S(1)}, bf16[80,1792]{1,0:T(8,128)(2,1)S(1)}, u32[]{:S(2)}, u32[]{:S(2)}) %collective-permute-start.1) | collective-permute-done | bytes 286752 | tf_op jit(solution)/shard_map/ppermute | solution.py:22
  14.9 3.0 %collective-permute-start.8 = (bf16[80,1792]{1,0:T(8,128)(2,1)S(1)}, bf16[80,1792]{1,0:T(8,128)(2,1)S(1)}, u32[]{:S(2)}, u32[]{:S(2)}) collective-permute-start(bf16[80,1792]{1,0:T(8,128)(2,1)S(1)} %get-tuple-element.68), channel_id=1, source_target_pairs={{0,6},{2,4},{4,2},{6,0},{1,7},{3,5},{5,3},{7,1},{8,14},{10,12},{12... | collective-permute-start | bytes 860168 | tf_op jit(solution)/shard_map/ppermute | solution.py:22
  17.9 4.2 %shard_map.141 = (bf16[1792,1024]{1,0:T(8,128)(2,1)S(1)}, bf16[1792,1024]{1,0:T(8,128)(2,1)S(1)}, bf16[1024,1792]{1,0:T(8,128)(2,1)S(1)}) custom-call(bf16[1792,1024]{1,0:T(8,128)(2,1)} %bitcast.24, bf16[1792,1024]{1,0:T(8,128)(2,1)} %bitcast.25, bf16[1024,1792]{1,0:T(8,128)(2,1)} %bitcast.26, bf16[80,1792]{1,0:T(8,128)(2,1)S(1)} %get-tuple-element.60.refs_3_.refs_0_), custom_call_target="tpu_custom_call" | custom-call | flops 10000000 | bytes 1 | tf_op jit(solution)/shard_map/pallas_call | solution.py:164
  23.4 1.8 %collective-permute-start.13 = (bf16[80,1792]{1,0:T(8,128)(2,1)S(1)}, bf16[80,1792]{1,0:T(8,128)(2,1)S(1)}, u32[]{:S(2)}, u32[]{:S(2)}) collective-permute-start(bf16[80,1792]{1,0:T(8,128)(2,1)S(1)} %get-tuple-element.74), channel_id=1, source_target_pairs={{0,4},{2,6},{4,0},{6,2},{1,5},{3,7},{5,1},{7,3},{8,12},{10,14},{12... | collective-permute-start | bytes 860168 | tf_op jit(solution)/shard_map/ppermute | solution.py:22
  25.2 2.6 %shard_map.143.refs_6_.own_ref = bf16[2,320,1024]{2,1,0:T(8,128)(2,1)S(1)} custom-call(bf16[80,1792]{1,0:T(8,128)(2,1)S(1)} %get-tuple-element.54.refs_0_, bf16[80,1792]{1,0:T(8,128)(2,1)S(1)} %collective-permute-done.1.refs_1_, bf16[80,1792]{1,0:T(8,128)(2,1)S(1)} %collective-permute-done.2.refs_2_, bf16[80,1792]{1,0:T(8,128)(2,1)S(1)} %collective-permute-done.3.refs_3_, ...), custom_call_target="tpu_custom_call" | custom-call | flops 10000000 | bytes 1 | tf_op jit(solution)/shard_map/pallas_call | solution.py:298
  27.8 2.4 %collective-permute-start.14 = (bf16[80,1792]{1,0:T(8,128)(2,1)S(1)}, bf16[80,1792]{1,0:T(8,128)(2,1)S(1)}, u32[]{:S(2)}, u32[]{:S(2)}) collective-permute-start(bf16[80,1792]{1,0:T(8,128)(2,1)S(1)} %get-tuple-element.75), channel_id=1, source_target_pairs={{0,6},{2,4},{4,2},{6,0},{1,7},{3,5},{5,3},{7,1},{8,14},{10,12},{12... | collective-permute-start | bytes 860168 | tf_op jit(solution)/shard_map/ppermute | solution.py:22
  30.3 5.2 %collective-permute-done.7.refs_2_ = bf16[80,1792]{1,0:T(8,128)(2,1)S(1)} collective-permute-done((bf16[80,1792]{1,0:T(8,128)(2,1)S(1)}, bf16[80,1792]{1,0:T(8,128)(2,1)S(1)}, u32[]{:S(2)}, u32[]{:S(2)}) %collective-permute-start.7) | collective-permute-done | bytes 286752 | tf_op jit(solution)/shard_map/ppermute | solution.py:22
  35.4 2.6 %shard_map.144.refs_0_.refs_5_ = bf16[3,320,1024]{2,1,0:T(8,128)(2,1)S(1)} custom-call(bf16[80,1792]{1,0:T(8,128)(2,1)S(1)} %get-tuple-element.60.refs_3_.refs_0_, bf16[80,1792]{1,0:T(8,128)(2,1)S(1)} %collective-permute-done.6.refs_1_, bf16[80,1792]{1,0:T(8,128)(2,1)S(1)} %collective-permute-done.7.refs_2_, ...), custom_call_target="tpu_custom_call" | custom-call | flops 30000001024 | bytes 1 | tf_op jit(solution)/shard_map/pallas_call | solution.py:298
  38.5 1.7 %shard_map.145 = (bf16[40,1792]{1,0:T(8,128)(2,1)S(1)}, bf16[40,1792]{1,0:T(8,128)(2,1)S(1)}, bf16[40,1792]{1,0:T(8,128)(2,1)S(1)}, bf16[40,1792]{1,0:T(8,128)(2...) custom-call(bf16[2,320,1024]{2,1,0:T(8,128)(2,1)S(1)} %shard_map.143, ...), custom_call_target="tpu_custom_call" | custom-call | flops 10000000 | bytes 1 | tf_op jit(solution)/shard_map/pallas_call | solution.py:361
  44.2 2.6 %collective-permute-done.13.refs_2_ = bf16[80,1792]{1,0:T(8,128)(2,1)S(1)} collective-permute-done((bf16[80,1792]{1,0:T(8,128)(2,1)S(1)}, bf16[80,1792]{1,0:T(8,128)(2,1)S(1)}, u32[]{:S(2)}, u32[]{:S(2)}) %collective-permute-start.13) | collective-permute-done | bytes 286752 | tf_op jit(solution)/shard_map/ppermute | solution.py:22
  48.8 1.6 %collective-permute-start.16 = (bf16[40,1792]{1,0:T(8,128)(2,1)S(1)}, bf16[40,1792]{1,0:T(8,128)(2,1)S(1)}, u32[]{:S(2)}, u32[]{:S(2)}) collective-permute-start(bf16[40,1792]{1,0:T(8,128)(2,1)S(1)} %get-tuple-element.78), channel_id=1, source_target_pairs={{0,2},{2,0},{4,6},{6,4},{1,3},{3,1},{5,7},{7,5},{8,10},{10,8},{12,... | collective-permute-start | bytes 430088 | tf_op jit(solution)/shard_map/ppermute | solution.py:22
  50.9 1.9 %collective-permute-done.10.refs_2_ = bf16[40,1792]{1,0:T(8,128)(2,1)S(1)} collective-permute-done((bf16[40,1792]{1,0:T(8,128)(2,1)S(1)}, bf16[40,1792]{1,0:T(8,128)(2,1)S(1)}, u32[]{:S(2)}, u32[]{:S(2)}) %collective-permute-start.10) | collective-permute-done | bytes 143392 | tf_op jit(solution)/shard_map/ppermute | solution.py:22
  54.9 1.8 %collective-permute-start.15 = (bf16[64,1792]{1,0:T(8,128)(2,1)S(1)}, bf16[64,1792]{1,0:T(8,128)(2,1)S(1)}, u32[]{:S(2)}, u32[]{:S(2)}) collective-permute-start(bf16[64,1792]{1,0:T(8,128)(2,1)S(1)} %shard_map.148.refs_0_), channel_id=1, source_target_pairs={{0,8},{1,9},{8,16},{9,17},{16,24},{17,25},{24,0},{25,1},{2,10},{3,... | collective-permute-start | bytes 688136 | tf_op jit(solution)/shard_map/ppermute | solution.py:32
  56.7 3.2 %shard_map.149 = (bf16[320,1024]{1,0:T(8,128)(2,1)S(1)}, bf16[320,1024]{1,0:T(8,128)(2,1)S(1)}, bf16[320,1024]{1,0:T(8,128)(2,1)S(1)}, bf16[40,1792]{1,0:T(8,128...) custom-call(bf16[3,320,1024]{2,1,0:T(8,128)(2,1)S(1)} %get-tuple-ele, ...), custom_call_target="tpu_custom_call" | custom-call | flops 10000000 | bytes 1 | tf_op jit(solution)/shard_map/pallas_call | solution.py:394
  60.0 2.0 %collective-permute-start.21 = (bf16[40,1792]{1,0:T(8,128)(2,1)S(1)}, bf16[40,1792]{1,0:T(8,128)(2,1)S(1)}, u32[]{:S(2)}, u32[]{:S(2)}) collective-permute-start(bf16[40,1792]{1,0:T(8,128)(2,1)S(1)} %get-tuple-element.82), channel_id=1, source_target_pairs={{0,2},{2,0},{4,6},{6,4},{1,3},{3,1},{5,7},{7,5},{8,10},{10,8},{12,... | collective-permute-start | bytes 430088 | tf_op jit(solution)/shard_map/ppermute | solution.py:22
  62.0 1.5 %collective-permute-start.23 = (bf16[40,1792]{1,0:T(8,128)(2,1)S(1)}, bf16[40,1792]{1,0:T(8,128)(2,1)S(1)}, u32[]{:S(2)}, u32[]{:S(2)}) collective-permute-start(bf16[40,1792]{1,0:T(8,128)(2,1)S(1)} %get-tuple-element.84), channel_id=1, source_target_pairs={{0,6},{2,4},{4,2},{6,0},{1,7},{3,5},{5,3},{7,1},{8,14},{10,12},{12... | collective-permute-start | bytes 430088 | tf_op jit(solution)/shard_map/ppermute | solution.py:22
  64.3 1.9 %collective-permute-start.25 = (bf16[40,1792]{1,0:T(8,128)(2,1)S(1)}, bf16[40,1792]{1,0:T(8,128)(2,1)S(1)}, u32[]{:S(2)}, u32[]{:S(2)}) collective-permute-start(bf16[40,1792]{1,0:T(8,128)(2,1)S(1)} %get-tuple-element.88), channel_id=1, source_target_pairs={{0,2},{2,0},{4,6},{6,4},{1,3},{3,1},{5,7},{7,5},{8,10},{10,8},{12,... | collective-permute-start | bytes 430088 | tf_op jit(solution)/shard_map/ppermute | solution.py:22
  66.7 2.9 %collective-permute-done.22.refs_2_ = bf16[40,1792]{1,0:T(8,128)(2,1)S(1)} collective-permute-done((bf16[40,1792]{1,0:T(8,128)(2,1)S(1)}, bf16[40,1792]{1,0:T(8,128)(2,1)S(1)}, u32[]{:S(2)}, u32[]{:S(2)}) %collective-permute-start.22) | collective-permute-done | bytes 143392 | tf_op jit(solution)/shard_map/ppermute | solution.py:22
  70.1 1.6 %collective-permute-start.24 = (bf16[64,1792]{1,0:T(8,128)(2,1)S(1)}, bf16[64,1792]{1,0:T(8,128)(2,1)S(1)}, u32[]{:S(2)}, u32[]{:S(2)}) collective-permute-start(bf16[64,1792]{1,0:T(8,128)(2,1)S(1)} %shard_map.151.refs_0_), channel_id=1, source_target_pairs={{0,8},{1,9},{8,16},{9,17},{16,24},{17,25},{24,0},{25,1},{2,10},{3,... | collective-permute-start | bytes 688136 | tf_op jit(solution)/shard_map/ppermute | solution.py:32
  71.8 3.9 %shard_map.152.refs_4_ = bf16[1024,1792]{1,0:T(8,128)(2,1)} custom-call(bf16[320,1024]{1,0:T(8,128)(2,1)S(1)} %get-tuple-element.91.hidden, bf16[320,1792]{1,0:T(8,128)(2,1)S(1)} %get-tuple-element.92.cots, bf16[64,1792]{1,0:T(8,128)(2,1)S(1)} %shard_map.151.refs_0_), custom_call_target="tpu_custom_call" | custom-call | flops 10000000 | bytes 1 | tf_op jit(solution)/shard_map/pallas_call | solution.py:448
  78.6 5.8 %shard_map.154 = (bf16[1792,1024]{1,0:T(8,128)(2,1)}, bf16[1792,1024]{1,0:T(8,128)(2,1)}) custom-call(bf16[320,1024]{1,0:T(8,128)(2,1)S(1)} %get-tuple-element.85.d_gate, bf16[320,1024]{1,0:T(8,128)(2,1)S(1)} %get-tuple-element.86.d_up, bf16[1792,320]{1,0:T(8,128)(2,1)S(1)} %shard_map.146.refs_6_.turned, bf16[64,1792]{1,0:T(8,128)(2,1)S(1)} %shard_map.153.refs_0_, ...), custom_call_target="tpu_custom_call" | custom-call | flops 1000000000 | bytes 1 | tf_op jit(solution)/shard_map/pallas_call | solution.py:430
  (54 shorter events, 23.6 us)
Async XLA Ops:
  4.5 10.4 %collective-permute-start.1 = (bf16[80,1792]{1,0:T(8,128)(2,1)S(1)}, bf16[80,1792]{1,0:T(8,128)(2,1)S(1)}, u32[]{:S(2)}, u32[]{:S(2)}) collective-permute-start(bf16[80,1792]{1,0:T(8,128)(2,1)S(1)} %get-tuple-element.55), channel_id=1, source_target_pairs={{0,2},{2,0},{4,6},{6,4},{1,3},{3,1},{5,7},{7,5},{8,10},{10,8},{12,... | collective-permute-start | bytes 860168 | tf_op jit(solution)/shard_map/ppermute | solution.py:22
  7.3 15.8 %collective-permute-start.2 = (bf16[80,1792]{1,0:T(8,128)(2,1)S(1)}, bf16[80,1792]{1,0:T(8,128)(2,1)S(1)}, u32[]{:S(2)}, u32[]{:S(2)}) collective-permute-start(bf16[80,1792]{1,0:T(8,128)(2,1)S(1)} %get-tuple-element.56), channel_id=1, source_target_pairs={{0,4},{2,6},{4,0},{6,2},{1,5},{3,7},{5,1},{7,3},{8,12},{10,14},{12... | collective-permute-start | bytes 860168 | tf_op jit(solution)/shard_map/ppermute | solution.py:22
  8.8 14.5 %collective-permute-start.3 = (bf16[80,1792]{1,0:T(8,128)(2,1)S(1)}, bf16[80,1792]{1,0:T(8,128)(2,1)S(1)}, u32[]{:S(2)}, u32[]{:S(2)}) collective-permute-start(bf16[80,1792]{1,0:T(8,128)(2,1)S(1)} %get-tuple-element.57), channel_id=1, source_target_pairs={{0,6},{2,4},{4,2},{6,0},{1,7},{3,5},{5,3},{7,1},{8,14},{10,12},{12... | collective-permute-start | bytes 860168 | tf_op jit(solution)/shard_map/ppermute | solution.py:22
  9.4 18.4 %collective-permute-start.6 = (bf16[80,1792]{1,0:T(8,128)(2,1)S(1)}, bf16[80,1792]{1,0:T(8,128)(2,1)S(1)}, u32[]{:S(2)}, u32[]{:S(2)}) collective-permute-start(bf16[80,1792]{1,0:T(8,128)(2,1)S(1)} %get-tuple-element.66), channel_id=1, source_target_pairs={{0,2},{2,0},{4,6},{6,4},{1,3},{3,1},{5,7},{7,5},{8,10},{10,8},{12,... | collective-permute-start | bytes 860168 | tf_op jit(solution)/shard_map/ppermute | solution.py:22
  11.5 24.0 %collective-permute-start.7 = (bf16[80,1792]{1,0:T(8,128)(2,1)S(1)}, bf16[80,1792]{1,0:T(8,128)(2,1)S(1)}, u32[]{:S(2)}, u32[]{:S(2)}) collective-permute-start(bf16[80,1792]{1,0:T(8,128)(2,1)S(1)} %get-tuple-element.67), channel_id=1, source_target_pairs={{0,4},{2,6},{4,0},{6,2},{1,5},{3,7},{5,1},{7,3},{8,12},{10,14},{12... | collective-permute-start | bytes 860168 | tf_op jit(solution)/shard_map/ppermute | solution.py:22
  14.9 20.5 %collective-permute-start.8 = (bf16[80,1792]{1,0:T(8,128)(2,1)S(1)}, bf16[80,1792]{1,0:T(8,128)(2,1)S(1)}, u32[]{:S(2)}, u32[]{:S(2)}) collective-permute-start(bf16[80,1792]{1,0:T(8,128)(2,1)S(1)} %get-tuple-element.68), channel_id=1, source_target_pairs={{0,6},{2,4},{4,2},{6,0},{1,7},{3,5},{5,3},{7,1},{8,14},{10,12},{12... | collective-permute-start | bytes 860168 | tf_op jit(solution)/shard_map/ppermute | solution.py:22
  23.2 19.5 %collective-permute-start.12 = (bf16[80,1792]{1,0:T(8,128)(2,1)S(1)}, bf16[80,1792]{1,0:T(8,128)(2,1)S(1)}, u32[]{:S(2)}, u32[]{:S(2)}) collective-permute-start(bf16[80,1792]{1,0:T(8,128)(2,1)S(1)} %get-tuple-element.73), channel_id=1, source_target_pairs={{0,2},{2,0},{4,6},{6,4},{1,3},{3,1},{5,7},{7,5},{8,10},{10,8},{12,... | collective-permute-start | bytes 860168 | tf_op jit(solution)/shard_map/ppermute | solution.py:22
  23.4 23.4 %collective-permute-start.13 = (bf16[80,1792]{1,0:T(8,128)(2,1)S(1)}, bf16[80,1792]{1,0:T(8,128)(2,1)S(1)}, u32[]{:S(2)}, u32[]{:S(2)}) collective-permute-start(bf16[80,1792]{1,0:T(8,128)(2,1)S(1)} %get-tuple-element.74), channel_id=1, source_target_pairs={{0,4},{2,6},{4,0},{6,2},{1,5},{3,7},{5,1},{7,3},{8,12},{10,14},{12... | collective-permute-start | bytes 860168 | tf_op jit(solution)/shard_map/ppermute | solution.py:22
  27.8 19.5 %collective-permute-start.14 = (bf16[80,1792]{1,0:T(8,128)(2,1)S(1)}, bf16[80,1792]{1,0:T(8,128)(2,1)S(1)}, u32[]{:S(2)}, u32[]{:S(2)}) collective-permute-start(bf16[80,1792]{1,0:T(8,128)(2,1)S(1)} %get-tuple-element.75), channel_id=1, source_target_pairs={{0,6},{2,4},{4,2},{6,0},{1,7},{3,5},{5,3},{7,1},{8,14},{10,12},{12... | collective-permute-start | bytes 860168 | tf_op jit(solution)/shard_map/ppermute | solution.py:22
  40.1 10.2 %collective-permute-start.9 = (bf16[40,1792]{1,0:T(8,128)(2,1)S(1)}, bf16[40,1792]{1,0:T(8,128)(2,1)S(1)}, u32[]{:S(2)}, u32[]{:S(2)}) collective-permute-start(bf16[40,1792]{1,0:T(8,128)(2,1)S(1)} %get-tuple-element.70), channel_id=1, source_target_pairs={{0,2},{2,0},{4,6},{6,4},{1,3},{3,1},{5,7},{7,5},{8,10},{10,8},{12,... | collective-permute-start | bytes 430088 | tf_op jit(solution)/shard_map/ppermute | solution.py:22
  40.8 12.1 %collective-permute-start.10 = (bf16[40,1792]{1,0:T(8,128)(2,1)S(1)}, bf16[40,1792]{1,0:T(8,128)(2,1)S(1)}, u32[]{:S(2)}, u32[]{:S(2)}) collective-permute-start(bf16[40,1792]{1,0:T(8,128)(2,1)S(1)} %get-tuple-element.71), channel_id=1, source_target_pairs={{0,4},{2,6},{4,0},{6,2},{1,5},{3,7},{5,1},{7,3},{8,12},{10,14},{12... | collective-permute-start | bytes 430088 | tf_op jit(solution)/shard_map/ppermute | solution.py:22
  42.7 11.7 %collective-permute-start.11 = (bf16[40,1792]{1,0:T(8,128)(2,1)S(1)}, bf16[40,1792]{1,0:T(8,128)(2,1)S(1)}, u32[]{:S(2)}, u32[]{:S(2)}) collective-permute-start(bf16[40,1792]{1,0:T(8,128)(2,1)S(1)} %get-tuple-element.72), channel_id=1, source_target_pairs={{0,6},{2,4},{4,2},{6,0},{1,7},{3,5},{5,3},{7,1},{8,14},{10,12},{12... | collective-permute-start | bytes 430088 | tf_op jit(solution)/shard_map/ppermute | solution.py:22
  48.7 8.1 %collective-permute-start.19 = (bf16[3,320,1024]{2,1,0:T(8,128)(2,1)S(1)}, bf16[3,320,1024]{2,1,0:T(8,128)(2,1)S(1)}, u32[]{:S(2)}, u32[]{:S(2)}) collective-permute-start(bf16[3,320,1024]{2,1,0:T(8,128)(2,1)S(1)} %get-tuple-element.76.refs_4_.own_ref), channel_id=1, source_target_pairs={{0,1},{1,0},{2,3},{3,2},{4,5},{5,4},{6,7},{7,6},{8,9},{9,8},{10,11... | collective-permute-start | bytes 5898248 | tf_op jit(solution)/shard_map/ppermute | solution.py:22
  48.8 13.2 %collective-permute-start.16 = (bf16[40,1792]{1,0:T(8,128)(2,1)S(1)}, bf16[40,1792]{1,0:T(8,128)(2,1)S(1)}, u32[]{:S(2)}, u32[]{:S(2)}) collective-permute-start(bf16[40,1792]{1,0:T(8,128)(2,1)S(1)} %get-tuple-element.78), channel_id=1, source_target_pairs={{0,2},{2,0},{4,6},{6,4},{1,3},{3,1},{5,7},{7,5},{8,10},{10,8},{12,... | collective-permute-start | bytes 430088 | tf_op jit(solution)/shard_map/ppermute | solution.py:22
  50.3 11.7 %collective-permute-start.17 = (bf16[40,1792]{1,0:T(8,128)(2,1)S(1)}, bf16[40,1792]{1,0:T(8,128)(2,1)S(1)}, u32[]{:S(2)}, u32[]{:S(2)}) collective-permute-start(bf16[40,1792]{1,0:T(8,128)(2,1)S(1)} %get-tuple-element.79), channel_id=1, source_target_pairs={{0,4},{2,6},{4,0},{6,2},{1,5},{3,7},{5,1},{7,3},{8,12},{10,14},{12... | collective-permute-start | bytes 430088 | tf_op jit(solution)/shard_map/ppermute | solution.py:22
  52.9 10.7 %collective-permute-start.18 = (bf16[40,1792]{1,0:T(8,128)(2,1)S(1)}, bf16[40,1792]{1,0:T(8,128)(2,1)S(1)}, u32[]{:S(2)}, u32[]{:S(2)}) collective-permute-start(bf16[40,1792]{1,0:T(8,128)(2,1)S(1)} %get-tuple-element.80), channel_id=1, source_target_pairs={{0,6},{2,4},{4,2},{6,0},{1,7},{3,5},{5,3},{7,1},{8,14},{10,12},{12... | collective-permute-start | bytes 430088 | tf_op jit(solution)/shard_map/ppermute | solution.py:22
  54.9 9.4 %collective-permute-start.15 = (bf16[64,1792]{1,0:T(8,128)(2,1)S(1)}, bf16[64,1792]{1,0:T(8,128)(2,1)S(1)}, u32[]{:S(2)}, u32[]{:S(2)}) collective-permute-start(bf16[64,1792]{1,0:T(8,128)(2,1)S(1)} %shard_map.148.refs_0_), channel_id=1, source_target_pairs={{0,8},{1,9},{8,16},{9,17},{16,24},{17,25},{24,0},{25,1},{2,10},{3,... | collective-permute-start | bytes 688136 | tf_op jit(solution)/shard_map/ppermute | solution.py:32
  62.0 7.6 %collective-permute-start.22 = (bf16[40,1792]{1,0:T(8,128)(2,1)S(1)}, bf16[40,1792]{1,0:T(8,128)(2,1)S(1)}, u32[]{:S(2)}, u32[]{:S(2)}) collective-permute-start(bf16[40,1792]{1,0:T(8,128)(2,1)S(1)} %get-tuple-element.83), channel_id=1, source_target_pairs={{0,4},{2,6},{4,0},{6,2},{1,5},{3,7},{5,1},{7,3},{8,12},{10,14},{12... | collective-permute-start | bytes 430088 | tf_op jit(solution)/shard_map/ppermute | solution.py:22
  62.0 7.6 %collective-permute-start.23 = (bf16[40,1792]{1,0:T(8,128)(2,1)S(1)}, bf16[40,1792]{1,0:T(8,128)(2,1)S(1)}, u32[]{:S(2)}, u32[]{:S(2)}) collective-permute-start(bf16[40,1792]{1,0:T(8,128)(2,1)S(1)} %get-tuple-element.84), channel_id=1, source_target_pairs={{0,6},{2,4},{4,2},{6,0},{1,7},{3,5},{5,3},{7,1},{8,14},{10,12},{12... | collective-permute-start | bytes 430088 | tf_op jit(solution)/shard_map/ppermute | solution.py:22
  64.1 12.2 %collective-permute-start.20 = (bf16[64,1792]{1,0:T(8,128)(2,1)S(1)}, bf16[64,1792]{1,0:T(8,128)(2,1)S(1)}, u32[]{:S(2)}, u32[]{:S(2)}) collective-permute-start(bf16[64,1792]{1,0:T(8,128)(2,1)S(1)} %shard_map.150.refs_4_), channel_id=1, source_target_pairs={{0,9},{1,8},{8,17},{9,16},{16,25},{17,24},{24,1},{25,0},{2,11},{3,... | collective-permute-start | bytes 688136 | tf_op jit(solution)/shard_map/ppermute | solution.py:32
  64.3 11.3 %collective-permute-start.25 = (bf16[40,1792]{1,0:T(8,128)(2,1)S(1)}, bf16[40,1792]{1,0:T(8,128)(2,1)S(1)}, u32[]{:S(2)}, u32[]{:S(2)}) collective-permute-start(bf16[40,1792]{1,0:T(8,128)(2,1)S(1)} %get-tuple-element.88), channel_id=1, source_target_pairs={{0,2},{2,0},{4,6},{6,4},{1,3},{3,1},{5,7},{7,5},{8,10},{10,8},{12,... | collective-permute-start | bytes 430088 | tf_op jit(solution)/shard_map/ppermute | solution.py:22
  66.7 9.6 %collective-permute-start.26 = (bf16[40,1792]{1,0:T(8,128)(2,1)S(1)}, bf16[40,1792]{1,0:T(8,128)(2,1)S(1)}, u32[]{:S(2)}, u32[]{:S(2)}) collective-permute-start(bf16[40,1792]{1,0:T(8,128)(2,1)S(1)} %get-tuple-element.89), channel_id=1, source_target_pairs={{0,4},{2,6},{4,0},{6,2},{1,5},{3,7},{5,1},{7,3},{8,12},{10,14},{12... | collective-permute-start | bytes 430088 | tf_op jit(solution)/shard_map/ppermute | solution.py:22
  70.1 8.5 %collective-permute-start.24 = (bf16[64,1792]{1,0:T(8,128)(2,1)S(1)}, bf16[64,1792]{1,0:T(8,128)(2,1)S(1)}, u32[]{:S(2)}, u32[]{:S(2)}) collective-permute-start(bf16[64,1792]{1,0:T(8,128)(2,1)S(1)} %shard_map.151.refs_0_), channel_id=1, source_target_pairs={{0,8},{1,9},{8,16},{9,17},{16,24},{17,25},{24,0},{25,1},{2,10},{3,... | collective-permute-start | bytes 688136 | tf_op jit(solution)/shard_map/ppermute | solution.py:32
  76.8 9.6 %collective-permute-start.28 = (bf16[64,1792]{1,0:T(8,128)(2,1)S(1)}, bf16[64,1792]{1,0:T(8,128)(2,1)S(1)}, u32[]{:S(2)}, u32[]{:S(2)}) collective-permute-start(bf16[64,1792]{1,0:T(8,128)(2,1)S(1)} %shard_map.153.refs_0_), channel_id=1, source_target_pairs={{0,9},{1,8},{8,17},{9,16},{16,25},{17,24},{24,1},{25,0},{2,11},{3,... | collective-permute-start | bytes 688136 | tf_op jit(solution)/shard_map/ppermute | solution.py:32
  (5 other events, 22.9 us)
